TPU v7x, 32 devices: a whole 2x2x4 slice. The times are simulated.
32 devices in a mesh: dp: 4 (over y, x), seq: 8 (over z, core).
Axes of the slice: x: 2, y: 2, z: 4, core: 2. Of those that a mesh axis runs over, the one named last changes fastest.
Arguments:
- inputs: bfloat16 [2, 4, 2048, 1024], P(None, 'dp', 'seq'), may hold values from -6 to 6
- doc_flags: int32 [2, 4, 2048], P(None, 'dp', 'seq'), may hold values from 0 to 1, as said below
- first_gain: bfloat16 [1024], P(('dp', 'seq')), may hold values from 0.25 to 1.75
- first_bias: bfloat16 [1024], P(('dp', 'seq')), may hold values from -3 to 3
- w_query: bfloat16 [1024, 1024], P(('dp', 'seq')), may hold values from -0.1875 to 0.1875
- w_key: bfloat16 [1024, 1024], P(('dp', 'seq')), may hold values from -0.1875 to 0.1875
- w_value: bfloat16 [1024, 2048], P(('dp', 'seq')), may hold values from -0.1875 to 0.1875
- w_gate: bfloat16 [1024, 2048], P(('dp', 'seq')), may hold values from -0.1875 to 0.1875
- group_gain: bfloat16 [2048], P(('dp', 'seq')), may hold values from 0.25 to 1.75
- w_output: bfloat16 [2048, 1024], P(('dp', 'seq')), may hold values from -0.25 to 0.25
- second_gain: bfloat16 [1024], P(('dp', 'seq')), may hold values from 0.25 to 1.75
- second_bias: bfloat16 [1024], P(('dp', 'seq')), may hold values from -3 to 3
- w_up: bfloat16 [1024, 2048], P(('dp', 'seq')), may hold values from -0.1875 to 0.1875
- w_down: bfloat16 [2048, 1024], P(('dp', 'seq')), may hold values from -0.1875 to 0.1875
- cotangent: bfloat16 [2, 4, 2048, 1024], P(None, 'dp', 'seq'), may hold values from -6 to 6
Outputs:
- output: bfloat16 [2, 4, 2048, 1024], P(None, 'dp', 'seq')
- input_grad: float32 [2, 4, 2048, 1024], P(None, 'dp', 'seq')
- grad_first_gain: float32 [1024], P(('dp', 'seq'))
- grad_first_bias: float32 [1024], P(('dp', 'seq'))
- grad_w_query: float32 [1024, 1024], P(('dp', 'seq'))
- grad_w_key: float32 [1024, 1024], P(('dp', 'seq'))
- grad_w_value: float32 [1024, 2048], P(('dp', 'seq'))
- grad_w_gate: float32 [1024, 2048], P(('dp', 'seq'))
- grad_group_gain: float32 [2048], P(('dp', 'seq'))
- grad_w_output: float32 [2048, 1024], P(('dp', 'seq'))
- grad_second_gain: float32 [1024], P(('dp', 'seq'))
- grad_second_bias: float32 [1024], P(('dp', 'seq'))
- grad_w_up: float32 [1024, 2048], P(('dp', 'seq'))
- grad_w_down: float32 [2048, 1024], P(('dp', 'seq'))
Inputs may be any that keep to these rules, and one draw needn't show every extreme that they name: `doc_flags`: position 0 of every row holds 1. Of the 2 rows that one index of dp holds over all micro-batches, one holds no other 1, and each of the others holds one to three more.
All inputs are finite; a program needn't handle non-finite values.
Results may differ from a plain program's by a relative error of at most 0.013.
The roundings to bfloat16 on the way count: a program that leaves them out, or rounds other values in their place, can miss the bound.
Values may be sent and summed in bfloat16 or wider, within the bound.
No kernel may reach another device: no remote copies, remote signals or barrier semaphores. Data moves between devices by JAX's collectives and lax.ppermute only.
A program may use at most 320 MiB of HBM per device.

v0:
```python
import jax
import jax.numpy as jnp
from jax import lax
from jax.sharding import PartitionSpec as P

H = 4
QK = 256
VH = 512


def prefix(part, axis, combine, identity, reverse):
    count = lax.axis_size(axis)
    place = lax.axis_index(axis)
    ahead = count - 1 - place if reverse else place
    gathered = jax.tree.map(lambda a: lax.all_gather(a, axis), part)
    state = jax.tree.map(lambda a, e: jnp.zeros_like(a) + jnp.asarray(e, a.dtype), part, identity)

    def one(turn, state):
        source = count - 1 - turn if reverse else turn
        return combine(
            state, jax.tree.map(lambda a: lax.dynamic_index_in_dim(a, source, 0, False), gathered)
        )

    return lax.fori_loop(0, ahead, one, state)


def layer_norm(values, gain, shift):
    average = jnp.mean(values, axis=-1, keepdims=True)
    centred = values - average
    spread = jnp.mean(centred * centred, axis=-1, keepdims=True)
    return centred * lax.rsqrt(spread + 1e-05) * gain + shift


def rotate(values, positions):
    half = values.shape[-1] // 2
    frequency = 10000.0 ** (-jnp.arange(half, dtype=jnp.float32) / half)
    angles = positions.astype(jnp.float32)[:, None] * frequency[None, :]
    cosine = jnp.cos(angles)[:, None, :]
    sine = jnp.sin(angles)[:, None, :]
    first = values[..., :half]
    second = values[..., half:]
    return jnp.concatenate(
        [first * cosine - second * sine, second * cosine + first * sine], axis=-1
    )


def unrotate(grad, positions, factor):
    _, pull = jax.vjp(lambda values: rotate(values, positions) * factor, jnp.zeros_like(grad))
    return pull(grad)[0]


def norm_gate(retained, gate_pre, gain):
    grouped = retained.reshape(retained.shape[0], H, VH)
    average = jnp.mean(grouped, axis=-1, keepdims=True)
    centred = grouped - average
    spread = jnp.mean(centred * centred, axis=-1, keepdims=True)
    normal = (centred * lax.rsqrt(spread + 1.0)).reshape(retained.shape) * gain
    return jax.nn.silu(gate_pre) * normal


def decay_rates():
    return jnp.log1p(-(2.0 ** (-5.0 - 3.0 * jnp.arange(H, dtype=jnp.float32))))


def decay_tables(flags, rates):
    length = flags.shape[-1]
    counts = jnp.cumsum(flags, axis=-1, dtype=jnp.int32)
    index = jnp.arange(length, dtype=jnp.int32)
    spacing = (index[:, None] - index[None, :]).astype(jnp.float32)
    same = (counts[:, :, None] == counts[:, None, :]) & (index[:, None] >= index[None, :])[None]
    zero = jnp.zeros((), rates.dtype)
    mask = jnp.where(same[:, None], jnp.exp(spacing[None, None] * rates[None, :, None, None]), zero)
    enter = jnp.where(
        (counts == 0)[:, None, :],
        jnp.exp((index + 1).astype(jnp.float32)[None, None, :] * rates[None, :, None]),
        zero,
    )
    leave = jnp.where(
        (counts == counts[:, -1:])[:, None, :],
        jnp.exp((length - 1 - index).astype(jnp.float32)[None, None, :] * rates[None, :, None]),
        zero,
    )
    carry = jnp.where((counts[:, -1] == 0)[:, None], jnp.exp(rates * float(length))[None, :], zero)
    return (mask, enter, leave, carry)


def project(left, right):
    return jnp.dot(left, right, preferred_element_type=jnp.float32)


def weight_grad(left, right):
    return lax.dot_general(
        left, right, (((0,), (0,)), ((), ())), preferred_element_type=jnp.float32
    )


def back_project(grad, weight):
    return lax.dot_general(
        grad, weight, (((1,), (1,)), ((), ())), preferred_element_type=jnp.float32
    )


def chain(earlier, later):
    return (earlier[0] * later[0], earlier[1] * later[0][:, :, None, None] + later[1])


def to_heads(values, rows, width):
    return values.reshape(rows, -1, H, width).transpose(0, 2, 1, 3)


def from_heads(values):
    rows, heads, length, width = values.shape
    return values.transpose(0, 2, 1, 3).reshape(rows * length, heads * width)


def attention_forward(weights, inputs, flags, positions):
    first_gain, first_bias, w_query, w_key, w_value, w_gate, group_gain, w_output = weights
    rows = inputs.shape[0]
    flat = inputs.reshape(-1, inputs.shape[-1]).astype(jnp.float32)
    normed = layer_norm(
        flat, first_gain.astype(jnp.float32), first_bias.astype(jnp.float32)
    ).astype(jnp.bfloat16)
    query_pre = project(normed, w_query)
    key_pre = project(normed, w_key)
    value_r = to_heads(project(normed, w_value).astype(jnp.bfloat16), rows, VH)
    gate_pre = project(normed, w_gate)
    query_r = (
        rotate(query_pre.reshape(rows, -1, H, QK), positions)
        .astype(jnp.bfloat16)
        .transpose(0, 2, 1, 3)
    )
    key_r = (
        (rotate(key_pre.reshape(rows, -1, H, QK), positions) * QK ** (-0.5))
        .astype(jnp.bfloat16)
        .transpose(0, 2, 1, 3)
    )
    tables = decay_tables(flags, decay_rates())
    mask, enter, leave, carry = tables
    scores = jnp.einsum("rhcd,rhsd->rhcs", query_r, key_r, preferred_element_type=jnp.float32)
    mixing = (scores * mask).astype(jnp.bfloat16)
    inner = jnp.einsum("rhcs,rhse->rhce", mixing, value_r, preferred_element_type=jnp.float32)
    weighted_keys = (key_r.astype(jnp.float32) * leave[..., None]).astype(jnp.bfloat16)
    summary = jnp.einsum(
        "rhsd,rhse->rhde", weighted_keys, value_r, preferred_element_type=jnp.float32
    )
    identity = (jnp.ones_like(carry), jnp.zeros_like(summary))
    state_in = prefix((carry, summary), "seq", chain, identity, False)[1]
    query_entered = (query_r.astype(jnp.float32) * enter[..., None]).astype(jnp.bfloat16)
    state_low = state_in.astype(jnp.bfloat16)
    cross = jnp.einsum(
        "rhcd,rhde->rhce", query_entered, state_low, preferred_element_type=jnp.float32
    )
    retained = from_heads(inner + cross)
    mixed = norm_gate(retained, gate_pre, group_gain.astype(jnp.float32)).astype(jnp.bfloat16)
    hidden_in = flat + project(mixed, w_output)
    saved = (
        flat,
        normed,
        gate_pre,
        query_r,
        key_r,
        value_r,
        mixing,
        weighted_keys,
        query_entered,
        state_low,
        tables,
        retained,
        mixed,
    )
    return (hidden_in, saved)


def feed_forward(weights, hidden_in):
    second_gain, second_bias, w_up, w_down = weights
    normed = layer_norm(
        hidden_in, second_gain.astype(jnp.float32), second_bias.astype(jnp.float32)
    ).astype(jnp.bfloat16)
    upward = project(normed, w_up)
    activated = jax.nn.gelu(upward, approximate=True).astype(jnp.bfloat16)
    output = hidden_in + project(activated, w_down)
    return (output, (hidden_in, normed, upward, activated))


def feed_backward(weights, saved, grad_out):
    second_gain, second_bias, w_up, w_down = weights
    hidden_in, normed, upward, activated = saved
    grad_down = grad_out.astype(jnp.bfloat16)
    grad_w_down = weight_grad(activated, grad_down)
    grad_activated = back_project(grad_down, w_down)
    _, pull_gelu = jax.vjp(lambda values: jax.nn.gelu(values, approximate=True), upward)
    grad_upward = pull_gelu(grad_activated)[0].astype(jnp.bfloat16)
    grad_w_up = weight_grad(normed, grad_upward)
    grad_normed = back_project(grad_upward, w_up)
    _, pull_norm = jax.vjp(
        layer_norm, hidden_in, second_gain.astype(jnp.float32), second_bias.astype(jnp.float32)
    )
    grad_hidden, grad_gain, grad_bias = pull_norm(grad_normed)
    return (grad_out + grad_hidden, (grad_gain, grad_bias, grad_w_up, grad_w_down))


def attention_backward(weights, saved, grad_hidden, positions):
    first_gain, first_bias, w_query, w_key, w_value, w_gate, group_gain, w_output = weights
    (
        flat,
        normed,
        gate_pre,
        query_r,
        key_r,
        value_r,
        mixing,
        weighted_keys,
        query_entered,
        state_low,
        tables,
        retained,
        mixed,
    ) = saved
    mask, enter, leave, carry = tables
    rows = query_r.shape[0]
    grad_branch = grad_hidden.astype(jnp.bfloat16)
    grad_w_output = weight_grad(mixed, grad_branch)
    grad_mixed = back_project(grad_branch, w_output)
    _, pull_gate = jax.vjp(norm_gate, retained, gate_pre, group_gain.astype(jnp.float32))
    grad_retained, grad_gate, grad_group = pull_gate(grad_mixed)
    grad_ret = to_heads(grad_retained.astype(jnp.bfloat16), rows, VH)
    grad_mixing = jnp.einsum(
        "rhce,rhse->rhcs", grad_ret, value_r, preferred_element_type=jnp.float32
    )
    grad_scores = (grad_mixing * mask).astype(jnp.bfloat16)
    grad_query = jnp.einsum(
        "rhcs,rhsd->rhcd", grad_scores, key_r, preferred_element_type=jnp.float32
    )
    grad_key = jnp.einsum(
        "rhcs,rhcd->rhsd", grad_scores, query_r, preferred_element_type=jnp.float32
    )
    grad_value = jnp.einsum("rhcs,rhce->rhse", mixing, grad_ret, preferred_element_type=jnp.float32)
    grad_query = (
        grad_query
        + jnp.einsum("rhce,rhde->rhcd", grad_ret, state_low, preferred_element_type=jnp.float32)
        * enter[..., None]
    )
    grad_state = jnp.einsum(
        "rhcd,rhce->rhde", query_entered, grad_ret, preferred_element_type=jnp.float32
    )
    identity = (jnp.ones_like(carry), jnp.zeros_like(grad_state))
    grad_summary = prefix((carry, grad_state), "seq", chain, identity, True)[1]
    summary_low = grad_summary.astype(jnp.bfloat16)
    grad_value = grad_value + jnp.einsum(
        "rhsd,rhde->rhse", weighted_keys, summary_low, preferred_element_type=jnp.float32
    )
    grad_key = (
        grad_key
        + jnp.einsum("rhse,rhde->rhsd", value_r, summary_low, preferred_element_type=jnp.float32)
        * leave[..., None]
    )
    grad_q = (
        unrotate(grad_query.transpose(0, 2, 1, 3), positions, 1.0)
        .reshape(-1, H * QK)
        .astype(jnp.bfloat16)
    )
    grad_k = (
        unrotate(grad_key.transpose(0, 2, 1, 3), positions, QK ** (-0.5))
        .reshape(-1, H * QK)
        .astype(jnp.bfloat16)
    )
    grad_v = from_heads(grad_value).astype(jnp.bfloat16)
    grad_g = grad_gate.astype(jnp.bfloat16)
    grad_normed = (
        back_project(grad_q, w_query)
        + back_project(grad_k, w_key)
        + back_project(grad_v, w_value)
        + back_project(grad_g, w_gate)
    )
    _, pull_norm = jax.vjp(
        layer_norm, flat, first_gain.astype(jnp.float32), first_bias.astype(jnp.float32)
    )
    grad_flat, grad_gain, grad_bias = pull_norm(grad_normed)
    grads = (
        grad_gain,
        grad_bias,
        weight_grad(normed, grad_q),
        weight_grad(normed, grad_k),
        weight_grad(normed, grad_v),
        weight_grad(normed, grad_g),
        grad_group,
        grad_w_output,
    )
    return (grad_hidden + grad_flat, grads)


def per_device(
    inputs,
    doc_flags,
    first_gain,
    first_bias,
    w_query,
    w_key,
    w_value,
    w_gate,
    group_gain,
    w_output,
    second_gain,
    second_bias,
    w_up,
    w_down,
    cotangent,
):
    length = inputs.shape[2]
    width = inputs.shape[3]
    positions = lax.axis_index("seq") * length + jnp.arange(length, dtype=jnp.int32)
    outputs = []
    input_grads = []
    totals = None
    for batch_index in range(inputs.shape[0]):
        block_inputs = inputs[batch_index : batch_index + 1]
        rows = block_inputs.shape[0] * block_inputs.shape[1]
        merged = block_inputs.reshape(rows, length, width)
        merged_flags = doc_flags[batch_index : batch_index + 1].reshape(rows, length)
        gathered = (
            lax.all_gather(first_gain, ("dp", "seq"), axis=0, tiled=True),
            lax.all_gather(first_bias, ("dp", "seq"), axis=0, tiled=True),
            lax.all_gather(w_query, ("dp", "seq"), axis=0, tiled=True),
            lax.all_gather(w_key, ("dp", "seq"), axis=0, tiled=True),
            lax.all_gather(w_value, ("dp", "seq"), axis=0, tiled=True),
            lax.all_gather(w_gate, ("dp", "seq"), axis=0, tiled=True),
            lax.all_gather(group_gain, ("dp", "seq"), axis=0, tiled=True),
            lax.all_gather(w_output, ("dp", "seq"), axis=0, tiled=True),
        )
        hidden_in, attention_saved = attention_forward(gathered, merged, merged_flags, positions)
        feeding = (
            lax.all_gather(second_gain, ("dp", "seq"), axis=0, tiled=True),
            lax.all_gather(second_bias, ("dp", "seq"), axis=0, tiled=True),
            lax.all_gather(w_up, ("dp", "seq"), axis=0, tiled=True),
            lax.all_gather(w_down, ("dp", "seq"), axis=0, tiled=True),
        )
        train_output, feed_saved = feed_forward(feeding, hidden_in)
        feeding = (
            lax.all_gather(second_gain, ("dp", "seq"), axis=0, tiled=True),
            lax.all_gather(second_bias, ("dp", "seq"), axis=0, tiled=True),
            lax.all_gather(w_up, ("dp", "seq"), axis=0, tiled=True),
            lax.all_gather(w_down, ("dp", "seq"), axis=0, tiled=True),
        )
        grad_hidden, feed_terms = feed_backward(
            feeding,
            feed_saved,
            cotangent[batch_index : batch_index + 1].reshape(-1, width).astype(jnp.float32),
        )
        feed_parts = (
            lax.psum_scatter(feed_terms[0], ("dp", "seq"), scatter_dimension=0, tiled=True),
            lax.psum_scatter(feed_terms[1], ("dp", "seq"), scatter_dimension=0, tiled=True),
            lax.psum_scatter(feed_terms[2], ("dp", "seq"), scatter_dimension=0, tiled=True),
            lax.psum_scatter(feed_terms[3], ("dp", "seq"), scatter_dimension=0, tiled=True),
        )
        gathered = (
            lax.all_gather(first_gain, ("dp", "seq"), axis=0, tiled=True),
            lax.all_gather(first_bias, ("dp", "seq"), axis=0, tiled=True),
            lax.all_gather(w_query, ("dp", "seq"), axis=0, tiled=True),
            lax.all_gather(w_key, ("dp", "seq"), axis=0, tiled=True),
            lax.all_gather(w_value, ("dp", "seq"), axis=0, tiled=True),
            lax.all_gather(w_gate, ("dp", "seq"), axis=0, tiled=True),
            lax.all_gather(group_gain, ("dp", "seq"), axis=0, tiled=True),
            lax.all_gather(w_output, ("dp", "seq"), axis=0, tiled=True),
        )
        grad_inputs, retention_terms = attention_backward(
            gathered, attention_saved, grad_hidden, positions
        )
        retention_parts = (
            lax.psum_scatter(retention_terms[0], ("dp", "seq"), scatter_dimension=0, tiled=True),
            lax.psum_scatter(retention_terms[1], ("dp", "seq"), scatter_dimension=0, tiled=True),
            lax.psum_scatter(retention_terms[2], ("dp", "seq"), scatter_dimension=0, tiled=True),
            lax.psum_scatter(retention_terms[3], ("dp", "seq"), scatter_dimension=0, tiled=True),
            lax.psum_scatter(retention_terms[4], ("dp", "seq"), scatter_dimension=0, tiled=True),
            lax.psum_scatter(retention_terms[5], ("dp", "seq"), scatter_dimension=0, tiled=True),
            lax.psum_scatter(retention_terms[6], ("dp", "seq"), scatter_dimension=0, tiled=True),
            lax.psum_scatter(retention_terms[7], ("dp", "seq"), scatter_dimension=0, tiled=True),
        )
        shaped_output = train_output.reshape(block_inputs.shape).astype(jnp.bfloat16)
        grad_in = grad_inputs.reshape(block_inputs.shape)
        parts = tuple(retention_parts) + tuple(feed_parts)
        outputs.append(shaped_output)
        input_grads.append(grad_in)
        totals = (
            parts if totals is None else tuple((total + part for total, part in zip(totals, parts)))
        )
    output = jnp.concatenate(outputs, axis=0)
    input_grad = jnp.concatenate(input_grads, axis=0)
    return (
        output,
        input_grad,
        totals[0],
        totals[1],
        totals[2],
        totals[3],
        totals[4],
        totals[5],
        totals[6],
        totals[7],
        totals[8],
        totals[9],
        totals[10],
        totals[11],
    )


def solution(mesh):
    return jax.shard_map(
        per_device,
        mesh=mesh,
        in_specs=(
            P(None, "dp", "seq", None),
            P(None, "dp", "seq"),
            P(("dp", "seq")),
            P(("dp", "seq")),
            P(("dp", "seq"), None),
            P(("dp", "seq"), None),
            P(("dp", "seq"), None),
            P(("dp", "seq"), None),
            P(("dp", "seq")),
            P(("dp", "seq"), None),
            P(("dp", "seq")),
            P(("dp", "seq")),
            P(("dp", "seq"), None),
            P(("dp", "seq"), None),
            P(None, "dp", "seq", None),
        ),
        out_specs=(
            P(None, "dp", "seq", None),
            P(None, "dp", "seq", None),
            P(("dp", "seq")),
            P(("dp", "seq")),
            P(("dp", "seq"), None),
            P(("dp", "seq"), None),
            P(("dp", "seq"), None),
            P(("dp", "seq"), None),
            P(("dp", "seq")),
            P(("dp", "seq"), None),
            P(("dp", "seq")),
            P(("dp", "seq")),
            P(("dp", "seq"), None),
            P(("dp", "seq"), None),
        ),
        check_vma=False,
    )
```

profile of v0, /device:TPU:1, one launch (start us, length us, event | category | flops | bytes accessed | tf_op | source)
XLA Modules:
  0.0 2141.7 jit_solution(10603171388747906370)
XLA Ops:
  14.2 41.2 %all-reduce.19 = (bf16[1024]{0:T(1024)(128)(2,1)S(1)}, bf16[1024]{0:T(1024)(128)(2,1)S(1)}, bf16[2048]{0:T(1024)(128)(2,1)}, bf16[1024]{0:T(1024)(128)(2,1)}, bf16[1024]{0:T(1024)(128)(2,1)}) all-reduce(bf16[1024]{0:T(1024)(128)(2,1)S(1)} %dynamic-update-slice.1, ...), channel_id=1, replica_groups=mesh['dp'=4,'seq'=8] {'dp','seq'}, use_global_device_ids=true, to_apply=%add.9 | all-reduce | flops 6144 | bytes 24576
  72.9 55.5 %all-gather.18.cloned.1.call-done = bf16[1024,1024]{1,0:T(8,128)(2,1)} async-done(((bf16[32,1024]{1,0:T(8,128)(2,1)}), bf16[1024,1024]{1,0:T(8,128)(2,1)}) %all-gather.18.cloned.1.call-update) | async-done | bytes 2097168 | tf_op jit(solution)/shard_map/all_gather | solution.py:323
  128.4 3.9 copy.99
  138.4 54.1 %all-gather.22.cloned.1.call-done = bf16[1024,2048]{1,0:T(8,128)(2,1)} async-done(((bf16[32,2048]{1,0:T(8,128)(2,1)}), bf16[1024,2048]{1,0:T(8,128)(2,1)}) %all-gather.22.cloned.1.call-update) | async-done | bytes 4194320 | tf_op jit(solution)/shard_map/all_gather | solution.py:325
  192.5 4.5 convolution_convert_fusion
  202.7 4.5 convolution_convert_fusion.1
  209.1 3.3 fusion.126
  215.8 11.1 all_gather.59
  226.9 8.6 all_gather.50
  245.4 10.6 all-gather.16.cloned.1.call-done
  256.0 4.8 fusion.231
  260.9 146.3 %all-gather.32.cloned.1.call-done = f32[32,256,512]{2,1,0:T(8,128)} async-done(((f32[4,256,512]{2,1,0:T(8,128)}), f32[32,256,512]{2,1,0:T(8,128)}) %all-gather.32.cloned.1.call-update) | async-done | bytes 16777232 | tf_op jit(solution)/shard_map/all_gather | solution.py:15
  410.5 3.5 bitcast_reduce_fusion
  430.0 128.0 %all-gather.30.cloned.1.call-done = f32[32,256,512]{2,1,0:T(8,128)} async-done(((f32[4,256,512]{2,1,0:T(8,128)}), f32[32,256,512]{2,1,0:T(8,128)}) %all-gather.30.cloned.1.call-update) | async-done | bytes 16777232 | tf_op jit(solution)/shard_map/all_gather | solution.py:15
  559.6 5.0 while.52
  560.3 4.1 bitcast_add_fusion.12
  564.6 4.2 bitcast_reduce_fusion.1
  583.1 7.2 multiply_convert_fusion.3
  590.3 31.0 %all-gather.24.cloned.1.call-done = bf16[2048,1024]{1,0:T(8,128)(2,1)} async-done(((bf16[64,1024]{1,0:T(8,128)(2,1)}), bf16[2048,1024]{1,0:T(8,128)(2,1)}) %all-gather.24.cloned.1.call-update) | async-done | bytes 4194320 | tf_op jit(solution)/shard_map/all_gather | solution.py:328
  621.4 4.0 fusion.242
  628.3 56.8 %all-gather.26.cloned.1.call-done = bf16[1024,2048]{1,0:T(8,128)(2,1)} async-done(((bf16[32,2048]{1,0:T(8,128)(2,1)}), bf16[1024,2048]{1,0:T(8,128)(2,1)}) %all-gather.26.cloned.1.call-update) | async-done | bytes 4194320 | tf_op jit(solution)/shard_map/all_gather | solution.py:334
  685.1 5.3 fusion.218
  693.1 55.7 %all-gather.28.cloned.1.call-done = bf16[2048,1024]{1,0:T(8,128)(2,1)} async-done(((bf16[64,1024]{1,0:T(8,128)(2,1)}), bf16[2048,1024]{1,0:T(8,128)(2,1)}) %all-gather.28.cloned.1.call-update) | async-done | bytes 4194320 | tf_op jit(solution)/shard_map/all_gather | solution.py:335
  748.8 5.5 fusion.6
  766.1 4.0 multiply_reduce_fusion.1
  786.6 3.3 fusion.110
  790.1 7.5 multiply_reduce_fusion
  800.4 3.2 fusion.22
  822.1 4.8 convolution_add_fusion.1
  829.9 4.6 convolution_add_fusion.2
  838.0 4.8 convolution_add_fusion.3
  842.8 3.3 fusion.173
  846.2 5.1 convolution_add_fusion
  863.1 76.6 %all-gather.34.cloned.1.call-done = f32[32,256,512]{2,1,0:T(8,128)} async-done(((f32[4,256,512]{2,1,0:T(8,128)}), f32[32,256,512]{2,1,0:T(8,128)}) %all-gather.34.cloned.1.call-update) | async-done | bytes 16777232 | tf_op jit(solution)/shard_map/all_gather | solution.py:15
  939.9 18.2 while.54
  962.0 129.2 %all-gather.36.cloned.1.call-done = f32[32,256,512]{2,1,0:T(8,128)} async-done(((f32[4,256,512]{2,1,0:T(8,128)}), f32[32,256,512]{2,1,0:T(8,128)}) %all-gather.36.cloned.1.call-update) | async-done | bytes 16777232 | tf_op jit(solution)/shard_map/all_gather | solution.py:15
  1091.5 17.2 while.55
  1133.2 3.2 fusion.31
  1139.7 4.9 convolution_add_fusion.4
  1145.9 4.5 fusion.63
  1167.4 41.3 %all-reduce.18 = (f32[1024]{0:T(1024)S(1)}, f32[1024]{0:T(1024)S(1)}, f32[2048]{0:T(1024)S(1)}, f32[1024]{0:T(1024)S(1)}, f32[1024]{0:T(1024)S(1)}) all-reduce(f32[1024]{0:T(1024)S(1)} %add.535, f32[1024]{0:T(1024)S(1)} %add.536, f32[2048]{0:T(1024)S(1)} %add.541, ...), channel_id=18, replica_groups=mesh['dp'=4,'seq'=8] {'dp','seq'}, use_global_device_ids=true, to_apply=%region_37.38.clone | all-reduce | flops 6144 | bytes 49152
  1215.6 24.9 %reduce-scatter.18.cloned.1.call-done = f32[32,2048]{1,0:T(8,128)} async-done(((f32[1024,2048]{1,0:T(8,128)}), f32[32,2048]{1,0:T(8,128)}) %reduce-scatter.18.cloned.1.call-update) | async-done | bytes 262160 | tf_op jit(solution)/shard_map/reduce_scatter | solution.py:352
  1240.5 152.5 %reduce-scatter.16.cloned.1.call-done = f32[64,1024]{1,0:T(8,128)} async-done(((f32[2048,1024]{1,0:T(8,128)}), f32[64,1024]{1,0:T(8,128)}) %reduce-scatter.16.cloned.1.call-update) | async-done | bytes 262160 | tf_op jit(solution)/shard_map/reduce_scatter | solution.py:376
  1393.0 152.7 %reduce-scatter.14.cloned.1.call-done = f32[32,2048]{1,0:T(8,128)} async-done(((f32[1024,2048]{1,0:T(8,128)}), f32[32,2048]{1,0:T(8,128)}) %reduce-scatter.14.cloned.1.call-update) | async-done | bytes 262160 | tf_op jit(solution)/shard_map/reduce_scatter | solution.py:374
  1545.7 152.5 %reduce-scatter.20.cloned.1.call-done = f32[64,1024]{1,0:T(8,128)} async-done(((f32[2048,1024]{1,0:T(8,128)}), f32[64,1024]{1,0:T(8,128)}) %reduce-scatter.20.cloned.1.call-update) | async-done | bytes 262160 | tf_op jit(solution)/shard_map/reduce_scatter | solution.py:353
  1698.2 142.3 %reduce-scatter.10.cloned.1.call-done = f32[32,1024]{1,0:T(8,128)} async-done(((f32[1024,1024]{1,0:T(8,128)}), f32[32,1024]{1,0:T(8,128)}) %reduce-scatter.10.cloned.1.call-update) | async-done | bytes 131088 | tf_op jit(solution)/shard_map/reduce_scatter | solution.py:372
  1840.5 142.0 %reduce-scatter.8.cloned.1.call-done = f32[32,1024]{1,0:T(8,128)} async-done(((f32[1024,1024]{1,0:T(8,128)}), f32[32,1024]{1,0:T(8,128)}) %reduce-scatter.8.cloned.1.call-update) | async-done | bytes 131088 | tf_op jit(solution)/shard_map/reduce_scatter | solution.py:371
  1982.5 152.2 %reduce-scatter.12.cloned.1.call-done = f32[32,2048]{1,0:T(8,128)} async-done(((f32[1024,2048]{1,0:T(8,128)}), f32[32,2048]{1,0:T(8,128)}) %reduce-scatter.12.cloned.1.call-update) | async-done | bytes 262160 | tf_op jit(solution)/shard_map/reduce_scatter | solution.py:373
  (593 shorter events, 251.0 us)
Async XLA Ops:
  7.2 56.9 %copy-start.3 = (bf16[2,1,256,1024]{3,2,1,0:T(8,128)(2,1)S(1)}, bf16[2,1,256,1024]{3,2,1,0:T(8,128)(2,1)}, u32[]{:S(2)}) copy-start(bf16[2,1,256,1024]{3,2,1,0:T(8,128)(2,1)} %param.23) | copy-start | bytes 3145732
  7.2 62.9 %all-gather.20.cloned.1.call-start = ((), (), s32[]{:S(2)}) async-start(), calls=%async_computation.9 | async-start | bytes 2162688 | tf_op jit(solution)/shard_map/all_gather | solution.py:324
  7.9 120.5 %all-gather.18.cloned.1.call-start = ((), (), s32[]{:S(2)}) async-start(), calls=%async_computation.8 | async-start | bytes 2162688 | tf_op jit(solution)/shard_map/all_gather | solution.py:323
  8.7 183.8 %all-gather.22.cloned.1.call-start = ((), (), s32[]{:S(2)}) async-start(), calls=%async_computation.10 | async-start | bytes 4325376 | tf_op jit(solution)/shard_map/all_gather | solution.py:325
  9.4 246.6 %all-gather.16.cloned.1.call-start = ((), (), s32[]{:S(2)}) async-start(), calls=%async_computation.7 | async-start | bytes 4325376 | tf_op jit(solution)/shard_map/all_gather | solution.py:326
  10.0 397.2 %all-gather.32.cloned.1.call-start = ((), (), s32[]{:S(2)}) async-start(), calls=%async_computation.15 | async-start | bytes 18874368 | tf_op jit(solution)/shard_map/all_gather | solution.py:15
  64.1 69.2 %copy-start.104 = (f32[256]{0:T(256)}, f32[256]{0:T(256)S(1)}, u32[]{:S(2)}) copy-start(f32[256]{0:T(256)S(1)} %get-tuple-element.485) | copy-start | bytes 3076
  65.2 68.1 %copy-start.124 = (f32[256]{0:T(256)}, f32[256]{0:T(256)S(1)}, u32[]{:S(2)}) copy-start(f32[256]{0:T(256)S(1)} %fusion.209) | copy-start | bytes 3076
  65.2 137.5 %copy-start.99 = (f32[256]{0:T(256)}, f32[256]{0:T(256)S(1)}, u32[]{:S(2)}) copy-start(f32[256]{0:T(256)S(1)} %fusion.207) | copy-start | bytes 3076
  67.1 69.5 %copy-start.85 = (f32[256,128]{0,1:T(8,128)}, f32[256,128]{0,1:T(8,128)S(1)}, u32[]{:S(2)}) copy-start(f32[256,128]{0,1:T(8,128)S(1)} %get-tuple-element.470) | copy-start | bytes 393220
  136.6 55.8 %copy-start.105 = (f32[256]{0:T(256)S(1)}, f32[256]{0:T(256)}, u32[]{:S(2)}) copy-start(f32[256]{0:T(256)} %copy-done.104) | copy-start | bytes 3076
  136.6 55.8 %copy-start.125 = (f32[256]{0:T(256)S(1)}, f32[256]{0:T(256)}, u32[]{:S(2)}) copy-start(f32[256]{0:T(256)} %copy-done.124) | copy-start | bytes 3076
  138.4 60.5 %copy-start.44 = (bf16[1,256,4,256]{1,3,2,0:T(8,128)(2,1)}, bf16[1,256,4,256]{1,3,2,0:T(8,128)(2,1)S(1)}, u32[]{:S(2)}) copy-start(bf16[1,256,4,256]{1,3,2,0:T(8,128)(2,1)S(1)} %fusion.97) | copy-start | bytes 1572868
  198.8 42.8 %copy-start.18 = (bf16[1,256,4,512]{3,2,1,0:T(4,128)(2,1)}, bf16[1,256,4,512]{3,2,1,0:T(4,128)(2,1)S(1)}, u32[]{:S(2)}) copy-start(bf16[1,256,4,512]{3,2,1,0:T(4,128)(2,1)S(1)} %reshape.1822) | copy-start | bytes 3145732
  200.7 357.2 %all-gather.30.cloned.1.call-start = ((), (), s32[]{:S(2)}) async-start(), calls=%async_computation.14 | async-start | bytes 18874368 | tf_op jit(solution)/shard_map/all_gather | solution.py:15
  209.1 34.5 %copy-start.19 = (bf16[1,256,4,512]{3,2,1,0:T(4,128)(2,1)}, bf16[1,256,4,512]{3,2,1,0:T(4,128)(2,1)S(1)}, u32[]{:S(2)}) copy-start(bf16[1,256,4,512]{3,2,1,0:T(4,128)(2,1)S(1)} %reshape.1808) | copy-start | bytes 3145732
  212.5 408.9 %all-gather.24.cloned.1.call-start = ((), (), s32[]{:S(2)}) async-start(), calls=%async_computation.11 | async-start | bytes 4325376 | tf_op jit(solution)/shard_map/all_gather | solution.py:328
  213.2 471.9 %all-gather.26.cloned.1.call-start = ((), (), s32[]{:S(2)}) async-start(), calls=%async_computation.12 | async-start | bytes 4325376 | tf_op jit(solution)/shard_map/all_gather | solution.py:334
  214.0 534.8 %all-gather.28.cloned.1.call-start = ((), (), s32[]{:S(2)}) async-start(), calls=%async_computation.13 | async-start | bytes 4325376 | tf_op jit(solution)/shard_map/all_gather | solution.py:335
  214.7 725.0 %all-gather.34.cloned.1.call-start = ((), (), s32[]{:S(2)}) async-start(), calls=%async_computation.16 | async-start | bytes 18874368 | tf_op jit(solution)/shard_map/all_gather | solution.py:15
  214.9 26.8 %copy-start.109 = (pred[256,256]{1,0:T(8,128)(4,1)}, pred[256,256]{1,0:T(8,128)(4,1)S(1)}, u32[]{:S(2)}) copy-start(pred[256,256]{1,0:T(8,128)(4,1)S(1)} %fusion.199) | copy-start | bytes 196612
  215.6 24.9 %copy-start.46 = (bf16[1,256,4,256]{1,3,2,0:T(8,128)(2,1)S(1)}, bf16[1,256,4,256]{1,3,2,0:T(8,128)(2,1)}, u32[]{:S(2)}) copy-start(bf16[1,256,4,256]{1,3,2,0:T(8,128)(2,1)} %fusion.96) | copy-start | bytes 1572868
  215.6 24.9 %copy-start.65 = (bf16[1,256,4,128]{1,3,2,0:T(8,128)(2,1)S(1)}, bf16[1,256,4,128]{1,3,2,0:T(8,128)(2,1)}, u32[]{:S(2)}) copy-start(bf16[1,256,4,128]{1,3,2,0:T(8,128)(2,1)} %get-tuple-element.434) | copy-start | bytes 786436
  215.6 24.9 %copy-start.67 = (bf16[1,256,4,128]{1,3,2,0:T(8,128)(2,1)S(1)}, bf16[1,256,4,128]{1,3,2,0:T(8,128)(2,1)}, u32[]{:S(2)}) copy-start(bf16[1,256,4,128]{1,3,2,0:T(8,128)(2,1)} %get-tuple-element.435) | copy-start | bytes 786436
  215.6 24.9 %copy-start.95 = (f32[256,256]{1,0:T(8,128)S(1)}, f32[256,256]{1,0:T(8,128)}, u32[]{:S(2)}) copy-start(f32[256,256]{1,0:T(8,128)} %subtract_convert_fusion.2) | copy-start | bytes 786436
  215.7 26.0 %copy-start.111 = (pred[256,256]{1,0:T(8,128)(4,1)}, pred[256,256]{1,0:T(8,128)(4,1)S(1)}, u32[]{:S(2)}) copy-start(pred[256,256]{1,0:T(8,128)(4,1)S(1)} %fusion.200) | copy-start | bytes 196612
  243.6 12.5 copy-start.106
  243.6 12.5 copy-start.126
  625.4 135.8 %copy-start.137 = (f32[256]{0:T(256)}, f32[256]{0:T(256)S(1)}, u32[]{:S(2)}) copy-start(f32[256]{0:T(256)S(1)} %broadcast_multiply_fusion.6) | copy-start | bytes 3076
  625.7 59.4 %copy-start.97 = (f32[1024]{0:T(1024)S(1)}, f32[1024]{0:T(1024)}, u32[]{:S(2)}) copy-start(f32[1024]{0:T(1024)} %convert_element_type.444) | copy-start | bytes 12292
  627.1 134.1 %copy-start.145 = (f32[256]{0:T(256)}, f32[256]{0:T(256)S(1)}, u32[]{:S(2)}) copy-start(f32[256]{0:T(256)S(1)} %broadcast_multiply_fusion.4) | copy-start | bytes 3076
  628.3 132.9 %copy-start.143 = (f32[256]{0:T(256)}, f32[256]{0:T(256)S(1)}, u32[]{:S(2)}) copy-start(f32[256]{0:T(256)S(1)} %fusion.208) | copy-start | bytes 3076
  628.3 132.9 %copy-start.155 = (f32[256]{0:T(256)}, f32[256]{0:T(256)S(1)}, u32[]{:S(2)}) copy-start(f32[256]{0:T(256)S(1)} %fusion.210) | copy-start | bytes 3076
  789.9 301.3 %all-gather.36.cloned.1.call-start = ((), (), s32[]{:S(2)}) async-start(), calls=%async_computation.17 | async-start | bytes 18874368 | tf_op jit(solution)/shard_map/all_gather | solution.py:15
  790.1 7.5 copy-start.5
  790.1 7.5 copy-start.102
  818.8 421.7 %reduce-scatter.18.cloned.1.call-start = ((), (), s32[]{:S(2)}) async-start(), calls=%async_computation.23 | async-start | bytes 8650752 | tf_op jit(solution)/shard_map/reduce_scatter | solution.py:352
  826.9 566.1 %reduce-scatter.16.cloned.1.call-start = ((), (), s32[]{:S(2)}) async-start(), calls=%async_computation.22 | async-start | bytes 8650752 | tf_op jit(solution)/shard_map/reduce_scatter | solution.py:376
  834.5 711.1 %reduce-scatter.14.cloned.1.call-start = ((), (), s32[]{:S(2)}) async-start(), calls=%async_computation.21 | async-start | bytes 8650752 | tf_op jit(solution)/shard_map/reduce_scatter | solution.py:374
  842.7 855.4 %reduce-scatter.20.cloned.1.call-start = ((), (), s32[]{:S(2)}) async-start(), calls=%async_computation.24 | async-start | bytes 8650752 | tf_op jit(solution)/shard_map/reduce_scatter | solution.py:353
  851.3 989.2 %reduce-scatter.10.cloned.1.call-start = ((), (), s32[]{:S(2)}) async-start(), calls=%async_computation.19 | async-start | bytes 4325376 | tf_op jit(solution)/shard_map/reduce_scatter | solution.py:372
  939.9 18.2 copy-start.116
  1091.5 19.4 copy-start.86
  1118.4 864.1 %reduce-scatter.8.cloned.1.call-start = ((), (), s32[]{:S(2)}) async-start(), calls=%async_computation.18 | async-start | bytes 4325376 | tf_op jit(solution)/shard_map/reduce_scatter | solution.py:371
  1125.0 1009.6 %reduce-scatter.12.cloned.1.call-start = ((), (), s32[]{:S(2)}) async-start(), calls=%async_computation.20 | async-start | bytes 8650752 | tf_op jit(solution)/shard_map/reduce_scatter | solution.py:373
  1165.4 46.2 %copy-start.33 = (f32[256,1024]{1,0:T(8,128)S(1)}, f32[256,1024]{1,0:T(8,128)}, u32[]{:S(2)}) copy-start(f32[256,1024]{1,0:T(8,128)} %copy-done.32) | copy-start | bytes 3145732
  1165.4 46.2 %copy-start.152 = (f32[256]{0:T(256)S(1)}, f32[256]{0:T(256)}, u32[]{:S(2)}) copy-start(f32[256]{0:T(256)} %copy-done.151) | copy-start | bytes 3076
  1165.5 46.2 %copy-start.154 = (f32[256]{0:T(256)S(1)}, f32[256]{0:T(256)}, u32[]{:S(2)}) copy-start(f32[256]{0:T(256)} %copy-done.153) | copy-start | bytes 3076
  (141 other events, 314.3 us)
Sparse Core Ops, SparseCore 0:
  11.0 59.0 all-gather.19
  73.1 55.3 all-gather.17
  131.4 60.9 all-gather.21
  195.3 60.6 all-gather.15
  257.5 149.6 all-gather.31
  408.6 149.3 all-gather.29
  561.0 60.3 all-gather.23
  624.4 60.6 all-gather.25
  688.1 60.6 all-gather.27
  790.0 149.6 all-gather.33
  941.8 149.3 all-gather.35
  1093.9 146.5 reduce-scatter.17
  1243.4 149.5 reduce-scatter.15
  1395.7 149.9 reduce-scatter.13
  1548.4 149.7 reduce-scatter.19
  1700.9 139.5 reduce-scatter.9
  1843.2 139.2 reduce-scatter.7
  1985.2 149.4 reduce-scatter.11
where the time goes:
time: 2160 us; the launch traced here: 2140 us
  waiting for transfers between devices  1670 us (77%)
  matrix products  169 us (8%)
  blocking collectives  102 us (5%)
  local copies, waits for them, and re-layouts  101 us (5%)
  other arithmetic  77.1 us (4%)
    all_gather x4, waiting for transfers between devices, prefix(): gathered = jax.tree.map(lambda a: lax.all_gather(a, axis), part)  480 us
    reduce_scatter x1, waiting for transfers between devices, per_device(): lax.psum_scatter(retention_terms[5], ('dp', 'seq'), scatter_dimension=0,...  153 us
    reduce_scatter x1, waiting for transfers between devices, per_device(): lax.psum_scatter(retention_terms[7], ('dp', 'seq'), scatter_dimension=0,...  152 us
    reduce_scatter x1, waiting for transfers between devices, per_device(): lax.psum_scatter(feed_terms[3], ('dp', 'seq'), scatter_dimension=0, tiled...  152 us
    reduce_scatter x1, waiting for transfers between devices, per_device(): lax.psum_scatter(retention_terms[4], ('dp', 'seq'), scatter_dimension=0,...  152 us
    reduce_scatter x1, waiting for transfers between devices, per_device(): lax.psum_scatter(retention_terms[3], ('dp', 'seq'), scatter_dimension=0,...  142 us
    reduce_scatter x1, waiting for transfers between devices, per_device(): lax.psum_scatter(retention_terms[2], ('dp', 'seq'), scatter_dimension=0,...  142 us
    unnamed x2, blocking collectives  82.5 us
  transfers between devices with their start and end apart: 18, of which 18 were waited for; matrix products, arithmetic and copies ran while one was open for 13% of the time, Pallas kernels for 0%

commit v1 on v0

--- a/solution.py
+++ b/solution.py
@@ -8,20 +8,166 @@
 VH = 512
 
 
-def prefix(part, axis, combine, identity, reverse):
-    count = lax.axis_size(axis)
-    place = lax.axis_index(axis)
-    ahead = count - 1 - place if reverse else place
-    gathered = jax.tree.map(lambda a: lax.all_gather(a, axis), part)
-    state = jax.tree.map(lambda a, e: jnp.zeros_like(a) + jnp.asarray(e, a.dtype), part, identity)
-
-    def one(turn, state):
-        source = count - 1 - turn if reverse else turn
-        return combine(
-            state, jax.tree.map(lambda a: lax.dynamic_index_in_dim(a, source, 0, False), gathered)
+AXES = ("dp", "seq")
+
+
+def devices():
+    return lax.axis_size("dp") * lax.axis_size("seq")
+
+
+def place():
+    return lax.axis_index("dp") * lax.axis_size("seq") + lax.axis_index("seq")
+
+
+def swap(values, bit):
+    return lax.ppermute(values, AXES, [(i, i ^ bit) for i in range(devices())])
+
+
+def side(bit):
+    return (place() // bit) % 2 == 1
+
+
+def chip_bits():
+    return [1 << k for k in range(1, devices().bit_length() - 1)]
+
+
+def orders():
+    bits = chip_bits()
+    far = 4
+    near = [bit for bit in bits if bit != far and bit != 2] + [2]
+    return [near[turn:] + near[:turn] + [far] for turn in range(3)]
+
+
+def cut(width):
+    tiles = width // 128
+    sizes = [tiles // 3 + (1 if k < tiles % 3 else 0) for k in range(3)]
+    edges = [0]
+    for size in sizes:
+        edges.append(edges[-1] + 128 * size)
+    return list(zip(edges[:-1], edges[1:]))
+
+
+def halves(values):
+    half = values.shape[-1] // 2
+    upper = side(1)
+    low, high = values[..., :half], values[..., half:]
+    return jnp.where(upper, high, low), jnp.where(upper, low, high)
+
+
+def spread_class(piece, order):
+    held = []
+    for bit in order[::-1]:
+        spot = sum(1 for other in held if other > bit)
+        other = swap(piece, bit)
+        upper = side(bit)
+        piece = jnp.stack(
+            [jnp.where(upper, other, piece), jnp.where(upper, piece, other)], axis=spot
         )
-
-    return lax.fori_loop(0, ahead, one, state)
+        held.append(bit)
+    return piece
+
+
+def spread(shard):
+    rows, width = shard.shape
+    keep, give = halves(shard)
+    got = swap(give, 1)
+    upper = side(1)
+    piece = jnp.concatenate([jnp.where(upper, got, keep), jnp.where(upper, keep, got)], axis=0)
+    parts = []
+    others = []
+    for (start, stop), order in zip(cut(width // 2), orders()):
+        part = spread_class(piece[:, start:stop], order).reshape(-1, stop - start)
+        parts.append(part)
+        others.append(swap(part, 1))
+    upper = side(1)
+    first = [jnp.where(upper, b, a) for a, b in zip(parts, others)]
+    second = [jnp.where(upper, a, b) for a, b in zip(parts, others)]
+    return jnp.concatenate(first + second, axis=1)
+
+
+def collect_class(total, order):
+    count = devices() // 2
+    rows = total.shape[0] // count
+    held = sorted(order, reverse=True)
+    total = total.reshape((2,) * len(held) + (rows, total.shape[-1]))
+    for bit in order:
+        spot = held.index(bit)
+        upper = side(bit)
+        low = lax.index_in_dim(total, 0, spot, False)
+        high = lax.index_in_dim(total, 1, spot, False)
+        got = swap(jnp.where(upper, low, high), bit)
+        total = jnp.where(upper, high, low).astype(jnp.float32) + got.astype(jnp.float32)
+        held.remove(bit)
+        if held:
+            total = total.astype(jnp.bfloat16)
+    return total
+
+
+def collect(left, right):
+    keep, give = halves(right)
+    got = swap(weight_grad(left, give).astype(jnp.bfloat16), 1)
+    total = (weight_grad(left, keep) + got.astype(jnp.float32)).astype(jnp.bfloat16)
+    parts = [
+        collect_class(total[:, start:stop], order)
+        for (start, stop), order in zip(cut(total.shape[-1]), orders())
+    ]
+    whole = jnp.concatenate(parts, axis=1)
+    rows = whole.shape[0] // 2
+    upper = side(1)
+    mine = jnp.where(upper, whole[rows:], whole[:rows])
+    got = swap(jnp.where(upper, whole[:rows], whole[rows:]), 1)
+    return jnp.concatenate([jnp.where(upper, got, mine), jnp.where(upper, mine, got)], axis=1)
+
+
+def collect_vector(values):
+    count = devices()
+    total = values.reshape((2,) * (count.bit_length() - 1) + (-1,))
+    for bit in [1 << k for k in range(count.bit_length() - 1)][::-1]:
+        upper = side(bit)
+        got = swap(jnp.where(upper, total[0], total[1]), bit)
+        total = jnp.where(upper, total[1], total[0]) + got
+    return total
+
+
+def spread_vector(piece):
+    for bit in [1 << k for k in range(devices().bit_length() - 1)]:
+        other = swap(piece, bit)
+        upper = side(bit)
+        piece = jnp.concatenate(
+            [jnp.where(upper, other, piece), jnp.where(upper, piece, other)], axis=0
+        )
+    return piece
+
+
+def scaled(carry, state):
+    return carry[:, None, None] * state
+
+
+def pass_states(carry, part, reverse):
+    count = lax.axis_size("seq")
+    chips = count // 2
+    upper = lax.axis_index("seq") % 2 == 1
+    own_carry = jnp.where(upper, carry[1], carry[0])
+    near_carry = swap(jnp.where(upper, carry[0], carry[1])[None], 1)[0]
+    own = jnp.where(upper, part[1], part[0])
+    near = swap(jnp.where(upper, part[0], part[1]), 1)
+    turned = upper if not reverse else jnp.logical_not(upper)
+    first_carry = jnp.where(turned, near_carry, own_carry)
+    last_carry = jnp.where(turned, own_carry, near_carry)
+    first = jnp.where(turned, near, own)
+    last = jnp.where(turned, own, near)
+    joined = scaled(last_carry, first) + last
+    both = first_carry * last_carry
+    entering = jnp.zeros_like(joined)
+    for step in range(1, chips):
+        message = (joined + scaled(both, entering)).astype(jnp.bfloat16)
+        source, target = (step - 1, step) if not reverse else (chips - step, chips - step - 1)
+        pairs = [(2 * source + core, 2 * target + core) for core in range(2)]
+        entering = entering + lax.ppermute(message, "seq", pairs).astype(jnp.float32)
+    middle = scaled(first_carry, entering) + first
+    mine = jnp.where(turned, middle, entering).astype(jnp.bfloat16)
+    theirs = swap(jnp.where(turned, entering, middle).astype(jnp.bfloat16), 1)
+    return jnp.stack([jnp.where(upper, theirs, mine), jnp.where(upper, mine, theirs)])
 
 
 def layer_norm(values, gain, shift):
@@ -98,10 +244,6 @@
     return lax.dot_general(
         grad, weight, (((1,), (1,)), ((), ())), preferred_element_type=jnp.float32
     )
-
-
-def chain(earlier, later):
-    return (earlier[0] * later[0], earlier[1] * later[0][:, :, None, None] + later[1])
 
 
 def to_heads(values, rows, width):
@@ -143,10 +285,8 @@
     summary = jnp.einsum(
         "rhsd,rhse->rhde", weighted_keys, value_r, preferred_element_type=jnp.float32
     )
-    identity = (jnp.ones_like(carry), jnp.zeros_like(summary))
-    state_in = prefix((carry, summary), "seq", chain, identity, False)[1]
+    state_low = pass_states(carry, summary, False)
     query_entered = (query_r.astype(jnp.float32) * enter[..., None]).astype(jnp.bfloat16)
-    state_low = state_in.astype(jnp.bfloat16)
     cross = jnp.einsum(
         "rhcd,rhde->rhce", query_entered, state_low, preferred_element_type=jnp.float32
     )
@@ -186,11 +326,11 @@
     second_gain, second_bias, w_up, w_down = weights
     hidden_in, normed, upward, activated = saved
     grad_down = grad_out.astype(jnp.bfloat16)
-    grad_w_down = weight_grad(activated, grad_down)
+    grad_w_down = collect(activated, grad_down)
     grad_activated = back_project(grad_down, w_down)
     _, pull_gelu = jax.vjp(lambda values: jax.nn.gelu(values, approximate=True), upward)
     grad_upward = pull_gelu(grad_activated)[0].astype(jnp.bfloat16)
-    grad_w_up = weight_grad(normed, grad_upward)
+    grad_w_up = collect(normed, grad_upward)
     grad_normed = back_project(grad_upward, w_up)
     _, pull_norm = jax.vjp(
         layer_norm, hidden_in, second_gain.astype(jnp.float32), second_bias.astype(jnp.float32)
@@ -219,7 +359,7 @@
     mask, enter, leave, carry = tables
     rows = query_r.shape[0]
     grad_branch = grad_hidden.astype(jnp.bfloat16)
-    grad_w_output = weight_grad(mixed, grad_branch)
+    grad_w_output = collect(mixed, grad_branch)
     grad_mixed = back_project(grad_branch, w_output)
     _, pull_gate = jax.vjp(norm_gate, retained, gate_pre, group_gain.astype(jnp.float32))
     grad_retained, grad_gate, grad_group = pull_gate(grad_mixed)
@@ -243,9 +383,7 @@
     grad_state = jnp.einsum(
         "rhcd,rhce->rhde", query_entered, grad_ret, preferred_element_type=jnp.float32
     )
-    identity = (jnp.ones_like(carry), jnp.zeros_like(grad_state))
-    grad_summary = prefix((carry, grad_state), "seq", chain, identity, True)[1]
-    summary_low = grad_summary.astype(jnp.bfloat16)
+    summary_low = pass_states(carry, grad_state, True)
     grad_value = grad_value + jnp.einsum(
         "rhsd,rhde->rhse", weighted_keys, summary_low, preferred_element_type=jnp.float32
     )
@@ -279,10 +417,10 @@
     grads = (
         grad_gain,
         grad_bias,
-        weight_grad(normed, grad_q),
-        weight_grad(normed, grad_k),
-        weight_grad(normed, grad_v),
-        weight_grad(normed, grad_g),
+        collect(normed, grad_q),
+        collect(normed, grad_k),
+        collect(normed, grad_v),
+        collect(normed, grad_g),
         grad_group,
         grad_w_output,
     )
@@ -306,100 +444,54 @@
     w_down,
     cotangent,
 ):
-    length = inputs.shape[2]
-    width = inputs.shape[3]
+    batches, rows, length, width = inputs.shape
     positions = lax.axis_index("seq") * length + jnp.arange(length, dtype=jnp.int32)
-    outputs = []
-    input_grads = []
-    totals = None
-    for batch_index in range(inputs.shape[0]):
-        block_inputs = inputs[batch_index : batch_index + 1]
-        rows = block_inputs.shape[0] * block_inputs.shape[1]
-        merged = block_inputs.reshape(rows, length, width)
-        merged_flags = doc_flags[batch_index : batch_index + 1].reshape(rows, length)
-        gathered = (
-            lax.all_gather(first_gain, ("dp", "seq"), axis=0, tiled=True),
-            lax.all_gather(first_bias, ("dp", "seq"), axis=0, tiled=True),
-            lax.all_gather(w_query, ("dp", "seq"), axis=0, tiled=True),
-            lax.all_gather(w_key, ("dp", "seq"), axis=0, tiled=True),
-            lax.all_gather(w_value, ("dp", "seq"), axis=0, tiled=True),
-            lax.all_gather(w_gate, ("dp", "seq"), axis=0, tiled=True),
-            lax.all_gather(group_gain, ("dp", "seq"), axis=0, tiled=True),
-            lax.all_gather(w_output, ("dp", "seq"), axis=0, tiled=True),
-        )
-        hidden_in, attention_saved = attention_forward(gathered, merged, merged_flags, positions)
-        feeding = (
-            lax.all_gather(second_gain, ("dp", "seq"), axis=0, tiled=True),
-            lax.all_gather(second_bias, ("dp", "seq"), axis=0, tiled=True),
-            lax.all_gather(w_up, ("dp", "seq"), axis=0, tiled=True),
-            lax.all_gather(w_down, ("dp", "seq"), axis=0, tiled=True),
-        )
-        train_output, feed_saved = feed_forward(feeding, hidden_in)
-        feeding = (
-            lax.all_gather(second_gain, ("dp", "seq"), axis=0, tiled=True),
-            lax.all_gather(second_bias, ("dp", "seq"), axis=0, tiled=True),
-            lax.all_gather(w_up, ("dp", "seq"), axis=0, tiled=True),
-            lax.all_gather(w_down, ("dp", "seq"), axis=0, tiled=True),
-        )
-        grad_hidden, feed_terms = feed_backward(
-            feeding,
-            feed_saved,
-            cotangent[batch_index : batch_index + 1].reshape(-1, width).astype(jnp.float32),
-        )
-        feed_parts = (
-            lax.psum_scatter(feed_terms[0], ("dp", "seq"), scatter_dimension=0, tiled=True),
-            lax.psum_scatter(feed_terms[1], ("dp", "seq"), scatter_dimension=0, tiled=True),
-            lax.psum_scatter(feed_terms[2], ("dp", "seq"), scatter_dimension=0, tiled=True),
-            lax.psum_scatter(feed_terms[3], ("dp", "seq"), scatter_dimension=0, tiled=True),
-        )
-        gathered = (
-            lax.all_gather(first_gain, ("dp", "seq"), axis=0, tiled=True),
-            lax.all_gather(first_bias, ("dp", "seq"), axis=0, tiled=True),
-            lax.all_gather(w_query, ("dp", "seq"), axis=0, tiled=True),
-            lax.all_gather(w_key, ("dp", "seq"), axis=0, tiled=True),
-            lax.all_gather(w_value, ("dp", "seq"), axis=0, tiled=True),
-            lax.all_gather(w_gate, ("dp", "seq"), axis=0, tiled=True),
-            lax.all_gather(group_gain, ("dp", "seq"), axis=0, tiled=True),
-            lax.all_gather(w_output, ("dp", "seq"), axis=0, tiled=True),
-        )
-        grad_inputs, retention_terms = attention_backward(
-            gathered, attention_saved, grad_hidden, positions
-        )
-        retention_parts = (
-            lax.psum_scatter(retention_terms[0], ("dp", "seq"), scatter_dimension=0, tiled=True),
-            lax.psum_scatter(retention_terms[1], ("dp", "seq"), scatter_dimension=0, tiled=True),
-            lax.psum_scatter(retention_terms[2], ("dp", "seq"), scatter_dimension=0, tiled=True),
-            lax.psum_scatter(retention_terms[3], ("dp", "seq"), scatter_dimension=0, tiled=True),
-            lax.psum_scatter(retention_terms[4], ("dp", "seq"), scatter_dimension=0, tiled=True),
-            lax.psum_scatter(retention_terms[5], ("dp", "seq"), scatter_dimension=0, tiled=True),
-            lax.psum_scatter(retention_terms[6], ("dp", "seq"), scatter_dimension=0, tiled=True),
-            lax.psum_scatter(retention_terms[7], ("dp", "seq"), scatter_dimension=0, tiled=True),
-        )
-        shaped_output = train_output.reshape(block_inputs.shape).astype(jnp.bfloat16)
-        grad_in = grad_inputs.reshape(block_inputs.shape)
-        parts = tuple(retention_parts) + tuple(feed_parts)
-        outputs.append(shaped_output)
-        input_grads.append(grad_in)
-        totals = (
-            parts if totals is None else tuple((total + part for total, part in zip(totals, parts)))
-        )
-    output = jnp.concatenate(outputs, axis=0)
-    input_grad = jnp.concatenate(input_grads, axis=0)
+    merged = inputs.reshape(batches * rows, length, width)
+    flags = doc_flags.reshape(batches * rows, length)
+    vectors = [first_gain, first_bias, group_gain, second_gain, second_bias]
+    sizes = [vector.shape[0] for vector in vectors]
+    edges = [sum(sizes[:k]) for k in range(len(sizes) + 1)]
+    table = spread_vector(jnp.concatenate(vectors)[None])
+    full = [table[:, a:b].reshape(-1) for a, b in zip(edges[:-1], edges[1:])]
+    first_gain, first_bias, group_gain, second_gain, second_bias = full
+    gathered = (
+        first_gain,
+        first_bias,
+        spread(w_query),
+        spread(w_key),
+        spread(w_value),
+        spread(w_gate),
+        group_gain,
+        spread(w_output),
+    )
+    hidden_in, attention_saved = attention_forward(gathered, merged, flags, positions)
+    feeding = (second_gain, second_bias, spread(w_up), spread(w_down))
+    train_output, feed_saved = feed_forward(feeding, hidden_in)
+    grad_hidden, feed_parts = feed_backward(
+        feeding, feed_saved, cotangent.reshape(-1, width).astype(jnp.float32)
+    )
+    grad_inputs, retention_parts = attention_backward(
+        gathered, attention_saved, grad_hidden, positions
+    )
+    small = [retention_parts[0], retention_parts[1], retention_parts[6], feed_parts[0], feed_parts[1]]
+    count = devices()
+    summed = collect_vector(jnp.concatenate([part.reshape(count, -1) for part in small], axis=1))
+    small = [summed[a:b] for a, b in zip(edges[:-1], edges[1:])]
     return (
-        output,
-        input_grad,
-        totals[0],
-        totals[1],
-        totals[2],
-        totals[3],
-        totals[4],
-        totals[5],
-        totals[6],
-        totals[7],
-        totals[8],
-        totals[9],
-        totals[10],
-        totals[11],
+        train_output.reshape(inputs.shape).astype(jnp.bfloat16),
+        grad_inputs.reshape(inputs.shape),
+        small[0],
+        small[1],
+        retention_parts[2],
+        retention_parts[3],
+        retention_parts[4],
+        retention_parts[5],
+        small[2],
+        retention_parts[7],
+        small[3],
+        small[4],
+        feed_parts[2],
+        feed_parts[3],
     )
 
 

time: 2160 us -> 999 us (0.46)
  waiting for transfers between devices: 1670 us -> 269 us
  starting transfers between devices: 1.63 us -> 376 us
  blocking collectives: 102 us -> 0 us
  matrix products: 169 us -> 112 us
  other arithmetic: 77.1 us -> 119 us
    reduce_scatter x7 -> x0, waiting for transfers between devices: 919 us -> none  [the longest x1 153 us: per_device(): lax.psum_scatter(retention_terms[5], ('dp', 'seq'), scatter_dimension=0,...]
    all_gather x11 -> x0, waiting for transfers between devices: 747 us -> none  [the longest x4 480 us: prefix(): gathered = jax.tree.map(lambda a: lax.all_gather(a, axis), part)]
    ppermute x0 -> x231, starting transfers between devices: none -> 376 us  [the longest x225 370 us: swap(): return lax.ppermute(values, AXES, [(i, i ^ bit) for i in range(devices())])]
    ppermute x0 -> x231, waiting for transfers between devices: none -> 269 us  [the longest x225 227 us: swap(): return lax.ppermute(values, AXES, [(i, i ^ bit) for i in range(devices())])]
    unnamed x2 -> x0, blocking collectives: 82.5 us -> none
    unnamed x0 -> x37, other arithmetic: none -> 36.6 us
    add x19 -> x28, other arithmetic: 33.3 us -> 4.61 us  [the longest x1 4.24 us: attention_backward(): return (grad_hidden + grad_flat, grads)]
    dot_general x14 -> x7, matrix products: 44 us -> 32.1 us  [project(): return jnp.dot(left, right, preferred_element_type=jnp.float32)]
  transfers between devices with their start and end apart: 18 -> 231, of which waited for: 18 -> 102; matrix products, arithmetic and copies ran while one was open for 13% -> 16% of each run, Pallas kernels for 0% -> 0%
where the time goes in v1:
time: 999 us; the launch traced here: 988 us
  starting transfers between devices  376 us (38%)
  waiting for transfers between devices  269 us (27%)
  other arithmetic  119 us (12%)
  matrix products  112 us (11%)
  local copies, waits for them, and re-layouts  106 us (11%)
    ppermute x225, starting transfers between devices, swap(): return lax.ppermute(values, AXES, [(i, i ^ bit) for i in range(devices())])  370 us
    ppermute x225, waiting for transfers between devices, swap(): return lax.ppermute(values, AXES, [(i, i ^ bit) for i in range(devices())])  227 us
    unnamed x323, local copies, waits for them, and re-layouts  48.4 us
    ppermute x6, waiting for transfers between devices, pass_states(): lax.ppermute(message, 'seq', pairs).astype(jnp.float32)  42.4 us
    unnamed x37, other arithmetic  36.6 us
    dot_general x7, matrix products, project(): return jnp.dot(left, right, preferred_element_type=jnp.float32)  32.1 us
    dot_general x7, matrix products, back_project(): lax.dot_general(grad, weight, (((1,), (1,)), ((), ())), preferred_element...  28.2 us
    dot_general x14, matrix products, weight_grad(): lax.dot_general(left, right, (((0,), (0,)), ((), ())), preferred_element_...  26.9 us
  transfers between devices with their start and end apart: 231, of which 102 were waited for; matrix products, arithmetic and copies ran while one was open for 16% of the time, Pallas kernels for 0%

profile of v1, /device:TPU:1, one launch (start us, length us, event | category | flops | bytes accessed | tf_op | source)
XLA Modules:
  0.0 988.2 jit_solution(820300845400582424)
XLA Ops:
  52.3 4.8 collective-permute-start.53
  77.1 6.7 collective-permute-done.81
  101.8 4.3 collective-permute-done.6
  106.2 4.0 collective-permute-done.11
  156.4 4.6 collective-permute-done.66
  164.3 8.4 collective-permute-done.56
  180.9 27.9 %collective-permute-start.31 = (bf16[1024,128]{1,0:T(8,128)(2,1)S(1)}, bf16[1024,128]{1,0:T(8,128)(2,1)}, u32[]{:S(2)}, u32[]{:S(2)}) collective-permute-start(bf16[1024,128]{1,0:T(8,128)(2,1)S(1)} %bitcast.1129), channel_id=1, source_target_pairs={{0,1},{1,0},{2,3},{3,2},{4,5},{5,4},{6,7},{7,6},{8,9},{9,8},{10,11... | collective-permute-start | bytes 786440 | tf_op jit(solution)/shard_map/ppermute | solution.py:23
  216.8 4.2 collective-permute-done.121
  222.6 5.4 collective-permute-done.105
  228.5 5.2 collective-permute-done.89
  235.5 4.3 collective-permute-done.19
  240.2 5.2 collective-permute-done.67
  254.8 6.0 collective-permute-done.14
  261.1 8.1 collective-permute-done.62
  269.4 9.9 %collective-permute-start.42 = (bf16[1024,256]{1,0:T(8,128)(2,1)S(1)}, bf16[1024,256]{1,0:T(8,128)(2,1)S(1)}, u32[]{:S(2)}, u32[]{:S(2)}) collective-permute-start(bf16[1024,256]{1,0:T(8,128)(2,1)S(1)} %bitcast.1108), channel_id=1, source_target_pairs={{0,1},{1,0},{2,3},{3,2},{4,5},{5,4},{6,7},{7,6},{8,9},{9,8},{10,11... | collective-permute-start | bytes 1572872 | tf_op jit(solution)/shard_map/ppermute | solution.py:23
  294.3 4.0 copy.112
  304.5 4.6 copy.108
  336.5 4.6 reshape.1368
  369.6 20.7 %collective-permute-done.71 = bf16[4,256,512]{2,1,0:T(8,128)(2,1)S(1)} collective-permute-done((bf16[4,256,512]{2,1,0:T(8,128)(2,1)S(1)}, bf16[4,256,512]{2,1,0:T(8,128)(2,1)S(1)}, u32[]{:S(2)}, u32[]{:S(2)}) %collective-permute-start.71) | collective-permute-done | bytes 1048608 | tf_op jit(solution)/shard_map/ppermute | solution.py:166
  408.7 4.6 copy.121
  426.0 8.6 multiply_convert_fusion.1
  434.5 5.2 fusion.285
  440.5 4.8 fusion.286
  445.3 4.9 fusion.6
  450.3 6.4 multiply_reduce_fusion.2
  463.5 4.3 multiply_reduce_fusion
  472.3 4.6 convolution_convert_fusion.2
  488.6 3.9 copy.256
  492.5 9.5 fusion.8
  502.1 4.9 reshape.1380
  528.6 6.1 add_convert_fusion.12
  551.5 24.2 %collective-permute-start.226 = (bf16[2,2,2,128,128]{4,3,2,0,1:T(8,128)(2,1)S(1)}, bf16[2,2,2,128,128]{4,3,2,0,1:T(8,128)(2,1)S(1)}, u32[]{:S(2)}, u32[]{:S(2)}) collective-permute-start(bf16[2,2,2,128,128]{4,3,2,0,1:T(8,128)(2,1)S(1)} %select_bitcast_fusion.27), channel_id=1, source_target_pairs={{0,2},{1,3},{2,0},{3,1},{4,6},{5,7},{6,4},{7,5},{8,10},{9,11},{10,... | collective-permute-start | bytes 786440 | tf_op jit(solution)/shard_map/ppermute | solution.py:23
  589.2 4.2 collective-permute-done.198
  594.9 5.7 collective-permute-done.184
  603.9 16.9 %collective-permute-done.176 = bf16[2,2,2,64,384]{4,3,1,2,0:T(8,128)(2,1)S(1)} collective-permute-done((bf16[2,2,2,64,384]{4,3,1,2,0:T(8,128)(2,1)S(1)}, bf16[2,2,2,64,384]{4,3,1,2,0:T(8,128)(2,1)S(1)}, u32[]{:S(2)}, u32[]{:S(2)}) %collective-permute-start.176) | collective-permute-done | bytes 393248 | tf_op jit(solution)/shard_map/ppermute | solution.py:23
  642.6 3.9 collective-permute-done.200
  653.5 42.8 %collective-permute-start.229 = (bf16[128,128]{1,0:T(8,128)(2,1)S(1)}, bf16[128,128]{1,0:T(8,128)(2,1)S(1)}, u32[]{:S(2)}, u32[]{:S(2)}) collective-permute-start(bf16[128,128]{1,0:T(8,128)(2,1)S(1)} %select_bitcast_fusion.200), channel_id=1, source_target_pairs={{0,4},{1,5},{2,6},{3,7},{4,0},{5,1},{6,2},{7,3},{8,12},{9,13},{10,... | collective-permute-start | bytes 98312 | tf_op jit(solution)/shard_map/ppermute | solution.py:23
  737.2 22.9 %collective-permute-start.216 = (f32[32,1024]{1,0:T(8,128)S(1)}, f32[32,1024]{1,0:T(8,128)S(1)}, u32[]{:S(2)}, u32[]{:S(2)}) collective-permute-start(f32[32,1024]{1,0:T(8,128)S(1)} %slice_select_fusion.5), channel_id=1, source_target_pairs={{0,1},{1,0},{2,3},{3,2},{4,5},{5,4},{6,7},{7,6},{8,9},{9,8},{10,11... | collective-permute-start | bytes 393224 | tf_op jit(solution)/shard_map/ppermute | solution.py:23
  772.7 21.4 %collective-permute-start.193 = (bf16[128,256]{1,0:T(8,128)(2,1)S(1)}, bf16[128,256]{1,0:T(8,128)(2,1)S(1)}, u32[]{:S(2)}, u32[]{:S(2)}) collective-permute-start(bf16[128,256]{1,0:T(8,128)(2,1)S(1)} %select_bitcast_fusion.143), channel_id=1, source_target_pairs={{0,4},{1,5},{2,6},{3,7},{4,0},{5,1},{6,2},{7,3},{8,12},{9,13},{10,... | collective-permute-start | bytes 196616 | tf_op jit(solution)/shard_map/ppermute | solution.py:23
  796.4 21.7 %collective-permute-done.126 = bf16[4,256,512]{2,1,0:T(8,128)(2,1)S(1)} collective-permute-done((bf16[4,256,512]{2,1,0:T(8,128)(2,1)S(1)}, bf16[4,256,512]{2,1,0:T(8,128)(2,1)S(1)}, u32[]{:S(2)}, u32[]{:S(2)}) %collective-permute-start.126) | collective-permute-done | bytes 1048608 | tf_op jit(solution)/shard_map/ppermute | solution.py:166
  834.9 4.3 fusion.290
  853.8 5.2 fusion.261
  864.4 4.2 add_add_fusion.4
  893.0 6.8 collective-permute-done.143
  928.9 11.0 %collective-permute-start.146 = (f32[32,512]{1,0:T(8,128)S(1)}, f32[32,512]{1,0:T(8,128)S(1)}, u32[]{:S(2)}, u32[]{:S(2)}) collective-permute-start(f32[32,512]{1,0:T(8,128)S(1)} %slice_select_fusion.15), channel_id=1, source_target_pairs={{0,1},{1,0},{2,3},{3,2},{4,5},{5,4},{6,7},{7,6},{8,9},{9,8},{10,11... | collective-permute-start | bytes 196616 | tf_op jit(solution)/shard_map/ppermute | solution.py:23
  944.6 6.9 collective-permute-done.170
  956.3 7.7 collective-permute-done.162
  979.4 6.4 collective-permute-start.174
  (1400 shorter events, 554.2 us)
Async XLA Ops:
  2.9 24.5 %collective-permute-start.69 = (f32[1,4]{1,0:T(1,128)S(1)}, f32[1,4]{1,0:T(1,128)S(1)}, u32[]{:S(2)}, u32[]{:S(2)}) collective-permute-start(f32[1,4]{1,0:T(1,128)S(1)} %broadcast_select_fusion.77), channel_id=1, source_target_pairs={{0,1},{1,0},{2,3},{3,2},{4,5},{5,4},{6,7},{7,6},{8,9},{9,8},{10,11... | collective-permute-start | bytes 56 | tf_op jit(solution)/shard_map/ppermute | solution.py:23
  7.6 30.3 %collective-permute-start.37 = (bf16[32,512]{1,0:T(8,128)(2,1)S(1)}, bf16[32,512]{1,0:T(8,128)(2,1)S(1)}, u32[]{:S(2)}, u32[]{:S(2)}) collective-permute-start(bf16[32,512]{1,0:T(8,128)(2,1)S(1)} %broadcast_select_fusion.51), channel_id=1, source_target_pairs={{0,1},{1,0},{2,3},{3,2},{4,5},{5,4},{6,7},{7,6},{8,9},{9,8},{10,11... | collective-permute-start | bytes 98312 | tf_op jit(solution)/shard_map/ppermute | solution.py:23
  8.5 29.5 %collective-permute-start.21 = (bf16[32,512]{1,0:T(8,128)(2,1)S(1)}, bf16[32,512]{1,0:T(8,128)(2,1)S(1)}, u32[]{:S(2)}, u32[]{:S(2)}) collective-permute-start(bf16[32,512]{1,0:T(8,128)(2,1)S(1)} %broadcast_select_fusion.55), channel_id=1, source_target_pairs={{0,1},{1,0},{2,3},{3,2},{4,5},{5,4},{6,7},{7,6},{8,9},{9,8},{10,11... | collective-permute-start | bytes 98312 | tf_op jit(solution)/shard_map/ppermute | solution.py:23
  9.8 47.3 %collective-permute-start.107 = (bf16[64,512]{1,0:T(8,128)(2,1)S(1)}, bf16[64,512]{1,0:T(8,128)(2,1)S(1)}, u32[]{:S(2)}, u32[]{:S(2)}) collective-permute-start(bf16[64,512]{1,0:T(8,128)(2,1)S(1)} %broadcast_select_fusion.21), channel_id=1, source_target_pairs={{0,1},{1,0},{2,3},{3,2},{4,5},{5,4},{6,7},{7,6},{8,9},{9,8},{10,11... | collective-permute-start | bytes 196616 | tf_op jit(solution)/shard_map/ppermute | solution.py:23
  25.3 37.5 %collective-permute-start.91 = (bf16[32,1024]{1,0:T(8,128)(2,1)S(1)}, bf16[32,1024]{1,0:T(8,128)(2,1)S(1)}, u32[]{:S(2)}, u32[]{:S(2)}) collective-permute-start(bf16[32,1024]{1,0:T(8,128)(2,1)S(1)} %broadcast_select_fusion.35), channel_id=1, source_target_pairs={{0,1},{1,0},{2,3},{3,2},{4,5},{5,4},{6,7},{7,6},{8,9},{9,8},{10,11... | collective-permute-start | bytes 196616 | tf_op jit(solution)/shard_map/ppermute | solution.py:23
  32.6 27.3 %collective-permute-start.75 = (bf16[64,512]{1,0:T(8,128)(2,1)S(1)}, bf16[64,512]{1,0:T(8,128)(2,1)S(1)}, u32[]{:S(2)}, u32[]{:S(2)}) collective-permute-start(bf16[64,512]{1,0:T(8,128)(2,1)S(1)} %broadcast_select_fusion.25), channel_id=1, source_target_pairs={{0,1},{1,0},{2,3},{3,2},{4,5},{5,4},{6,7},{7,6},{8,9},{9,8},{10,11... | collective-permute-start | bytes 196616 | tf_op jit(solution)/shard_map/ppermute | solution.py:23
  37.9 26.2 %collective-permute-start.5 = (bf16[32,1024]{1,0:T(8,128)(2,1)S(1)}, bf16[32,1024]{1,0:T(8,128)(2,1)S(1)}, u32[]{:S(2)}, u32[]{:S(2)}) collective-permute-start(bf16[32,1024]{1,0:T(8,128)(2,1)S(1)} %broadcast_select_fusion.43), channel_id=1, source_target_pairs={{0,1},{1,0},{2,3},{3,2},{4,5},{5,4},{6,7},{7,6},{8,9},{9,8},{10,11... | collective-permute-start | bytes 196616 | tf_op jit(solution)/shard_map/ppermute | solution.py:23
  69.4 46.8 %collective-permute-start.108 = (bf16[128,256]{1,0:T(8,128)(2,1)S(1)}, bf16[128,256]{1,0:T(8,128)(2,1)S(1)}, u32[]{:S(2)}, u32[]{:S(2)}) collective-permute-start(bf16[128,256]{1,0:T(8,128)(2,1)S(1)} %fusion.220), channel_id=1, source_target_pairs={{0,4},{1,5},{2,6},{3,7},{4,0},{5,1},{6,2},{7,3},{8,12},{9,13},{10,... | collective-permute-start | bytes 196616 | tf_op jit(solution)/shard_map/ppermute | solution.py:23
  72.0 39.8 %collective-permute-start.97 = (bf16[64,384]{1,0:T(8,128)(2,1)S(1)}, bf16[64,384]{1,0:T(8,128)(2,1)S(1)}, u32[]{:S(2)}, u32[]{:S(2)}) collective-permute-start(bf16[64,384]{1,0:T(8,128)(2,1)S(1)} %get-tuple-element.248), channel_id=1, source_target_pairs={{0,4},{1,5},{2,6},{3,7},{4,0},{5,1},{6,2},{7,3},{8,12},{9,13},{10,... | collective-permute-start | bytes 147464 | tf_op jit(solution)/shard_map/ppermute | solution.py:23
  72.9 37.4 %collective-permute-start.92 = (bf16[64,384]{1,0:T(8,128)(2,1)S(1)}, bf16[64,384]{1,0:T(8,128)(2,1)S(1)}, u32[]{:S(2)}, u32[]{:S(2)}) collective-permute-start(bf16[64,384]{1,0:T(8,128)(2,1)S(1)} %get-tuple-element.249), channel_id=1, source_target_pairs={{0,4},{1,5},{2,6},{3,7},{4,0},{5,1},{6,2},{7,3},{8,12},{9,13},{10,... | collective-permute-start | bytes 147464 | tf_op jit(solution)/shard_map/ppermute | solution.py:23
  83.8 31.7 %collective-permute-start.76 = (bf16[128,256]{1,0:T(8,128)(2,1)S(1)}, bf16[128,256]{1,0:T(8,128)(2,1)S(1)}, u32[]{:S(2)}, u32[]{:S(2)}) collective-permute-start(bf16[128,256]{1,0:T(8,128)(2,1)S(1)} %fusion.221), channel_id=1, source_target_pairs={{0,4},{1,5},{2,6},{3,7},{4,0},{5,1},{6,2},{7,3},{8,12},{9,13},{10,... | collective-permute-start | bytes 196616 | tf_op jit(solution)/shard_map/ppermute | solution.py:23
  156.4 22.8 %collective-permute-start.99 = (bf16[2,2,64,384]{3,2,1,0:T(8,128)(2,1)S(1)}, bf16[2,2,64,384]{3,2,1,0:T(8,128)(2,1)S(1)}, u32[]{:S(2)}, u32[]{:S(2)}) collective-permute-start(bf16[2,2,64,384]{3,2,1,0:T(8,128)(2,1)S(1)} %pad_maximum_fusion.61), channel_id=1, source_target_pairs={{0,2},{1,3},{2,0},{3,1},{4,6},{5,7},{6,4},{7,5},{8,10},{9,11},{10,... | collective-permute-start | bytes 589832 | tf_op jit(solution)/shard_map/ppermute | solution.py:23
  174.2 34.8 %collective-permute-start.110 = (bf16[2,2,128,256]{3,2,0,1:T(8,128)(2,1)S(1)}, bf16[2,2,128,256]{3,2,0,1:T(8,128)(2,1)S(1)}, u32[]{:S(2)}, u32[]{:S(2)}) collective-permute-start(bf16[2,2,128,256]{3,2,0,1:T(8,128)(2,1)S(1)} %pad_maximum_fusion.43), channel_id=1, source_target_pairs={{0,16},{1,17},{2,18},{3,19},{4,20},{5,21},{6,22},{7,23},{8,24},{9,... | collective-permute-start | bytes 786440 | tf_op jit(solution)/shard_map/ppermute | solution.py:23
  177.5 35.5 %collective-permute-start.78 = (bf16[2,2,128,256]{3,2,1,0:T(8,128)(2,1)S(1)}, bf16[2,2,128,256]{3,2,1,0:T(8,128)(2,1)S(1)}, u32[]{:S(2)}, u32[]{:S(2)}) collective-permute-start(bf16[2,2,128,256]{3,2,1,0:T(8,128)(2,1)S(1)} %pad_maximum_fusion.39), channel_id=1, source_target_pairs={{0,16},{1,17},{2,18},{3,19},{4,20},{5,21},{6,22},{7,23},{8,24},{9,... | collective-permute-start | bytes 786440 | tf_op jit(solution)/shard_map/ppermute | solution.py:23
  179.2 30.0 %collective-permute-start.41 = (bf16[2,2,2,64,256]{4,3,1,2,0:T(8,128)(2,1)S(1)}, bf16[2,2,2,64,256]{4,3,1,2,0:T(8,128)(2,1)S(1)}, u32[]{:S(2)}, u32[]{:S(2)}) collective-permute-start(bf16[2,2,2,64,256]{4,3,1,2,0:T(8,128)(2,1)S(1)} %pad_maximum_fusion.35), channel_id=1, source_target_pairs={{0,8},{1,9},{2,10},{3,11},{4,12},{5,13},{6,14},{7,15},{8,0},{9,1},... | collective-permute-start | bytes 786440 | tf_op jit(solution)/shard_map/ppermute | solution.py:23
  179.6 33.7 %collective-permute-start.25 = (bf16[2,2,2,64,256]{4,3,1,2,0:T(8,128)(2,1)S(1)}, bf16[2,2,2,64,256]{4,3,1,2,0:T(8,128)(2,1)S(1)}, u32[]{:S(2)}, u32[]{:S(2)}) collective-permute-start(bf16[2,2,2,64,256]{4,3,1,2,0:T(8,128)(2,1)S(1)} %pad_maximum_fusion.32), channel_id=1, source_target_pairs={{0,8},{1,9},{2,10},{3,11},{4,12},{5,13},{6,14},{7,15},{8,0},{9,1},... | collective-permute-start | bytes 786440 | tf_op jit(solution)/shard_map/ppermute | solution.py:23
  180.9 117.4 %collective-permute-start.31 = (bf16[1024,128]{1,0:T(8,128)(2,1)S(1)}, bf16[1024,128]{1,0:T(8,128)(2,1)}, u32[]{:S(2)}, u32[]{:S(2)}) collective-permute-start(bf16[1024,128]{1,0:T(8,128)(2,1)S(1)} %bitcast.1129), channel_id=1, source_target_pairs={{0,1},{1,0},{2,3},{3,2},{4,5},{5,4},{6,7},{7,6},{8,9},{9,8},{10,11... | collective-permute-start | bytes 786440 | tf_op jit(solution)/shard_map/ppermute | solution.py:23
  209.0 91.2 %collective-permute-start.36 = (bf16[1024,128]{1,0:T(8,128)(2,1)S(1)}, bf16[1024,128]{1,0:T(8,128)(2,1)}, u32[]{:S(2)}, u32[]{:S(2)}) collective-permute-start(bf16[1024,128]{1,0:T(8,128)(2,1)S(1)} %bitcast.1126), channel_id=1, source_target_pairs={{0,1},{1,0},{2,3},{3,2},{4,5},{5,4},{6,7},{7,6},{8,9},{9,8},{10,11... | collective-permute-start | bytes 786440 | tf_op jit(solution)/shard_map/ppermute | solution.py:23
  209.2 77.5 %collective-permute-start.47 = (bf16[1024,128]{1,0:T(8,128)(2,1)S(1)}, bf16[1024,128]{1,0:T(8,128)(2,1)S(1)}, u32[]{:S(2)}, u32[]{:S(2)}) collective-permute-start(bf16[1024,128]{1,0:T(8,128)(2,1)S(1)} %bitcast.1135), channel_id=1, source_target_pairs={{0,1},{1,0},{2,3},{3,2},{4,5},{5,4},{6,7},{7,6},{8,9},{9,8},{10,11... | collective-permute-start | bytes 786440 | tf_op jit(solution)/shard_map/ppermute | solution.py:23
  285.7 30.7 %collective-permute-start.111 = (bf16[2,2,2,128,256]{4,3,1,2,0:T(8,128)(2,1)}, bf16[2,2,2,128,256]{4,3,1,2,0:T(8,128)(2,1)}, u32[]{:S(2)}, u32[]{:S(2)}) collective-permute-start(bf16[2,2,2,128,256]{4,3,1,2,0:T(8,128)(2,1)} %pad_maximum_fusion.22), channel_id=1, source_target_pairs={{0,8},{1,9},{2,10},{3,11},{4,12},{5,13},{6,14},{7,15},{8,0},{9,1},... | collective-permute-start | bytes 1572872 | tf_op jit(solution)/shard_map/ppermute | solution.py:23
  288.2 30.8 %collective-permute-start.79 = (bf16[2,2,2,128,256]{4,3,2,1,0:T(8,128)(2,1)}, bf16[2,2,2,128,256]{4,3,2,1,0:T(8,128)(2,1)}, u32[]{:S(2)}, u32[]{:S(2)}) collective-permute-start(bf16[2,2,2,128,256]{4,3,2,1,0:T(8,128)(2,1)} %pad_maximum_fusion.18), channel_id=1, source_target_pairs={{0,8},{1,9},{2,10},{3,11},{4,12},{5,13},{6,14},{7,15},{8,0},{9,1},... | collective-permute-start | bytes 1572872 | tf_op jit(solution)/shard_map/ppermute | solution.py:23
  291.5 34.9 %collective-permute-start.68 = (bf16[1024,256]{1,0:T(8,128)(2,1)}, bf16[1024,256]{1,0:T(8,128)(2,1)}, u32[]{:S(2)}, u32[]{:S(2)}) collective-permute-start(bf16[1024,256]{1,0:T(8,128)(2,1)} %bitcast.123), channel_id=1, source_target_pairs={{0,1},{1,0},{2,3},{3,2},{4,5},{5,4},{6,7},{7,6},{8,9},{9,8},{10,11... | collective-permute-start | bytes 1572872 | tf_op jit(solution)/shard_map/ppermute | solution.py:23
  298.3 57.7 %collective-permute-start.20 = (bf16[1024,256]{1,0:T(8,128)(2,1)}, bf16[1024,256]{1,0:T(8,128)(2,1)}, u32[]{:S(2)}, u32[]{:S(2)}) collective-permute-start(bf16[1024,256]{1,0:T(8,128)(2,1)} %bitcast.29), channel_id=1, source_target_pairs={{0,1},{1,0},{2,3},{3,2},{4,5},{5,4},{6,7},{7,6},{8,9},{9,8},{10,11... | collective-permute-start | bytes 1572872 | tf_op jit(solution)/shard_map/ppermute | solution.py:23
  300.3 23.9 %collective-permute-start.58 = (bf16[1024,384]{1,0:T(8,128)(2,1)}, bf16[1024,384]{1,0:T(8,128)(2,1)}, u32[]{:S(2)}, u32[]{:S(2)}) collective-permute-start(bf16[1024,384]{1,0:T(8,128)(2,1)} %bitcast.105), channel_id=1, source_target_pairs={{0,1},{1,0},{2,3},{3,2},{4,5},{5,4},{6,7},{7,6},{8,9},{9,8},{10,11... | collective-permute-start | bytes 2359304 | tf_op jit(solution)/shard_map/ppermute | solution.py:23
  322.6 71.1 %collective-permute-start.85 = (bf16[2048,128]{1,0:T(8,128)(2,1)}, bf16[2048,128]{1,0:T(8,128)(2,1)}, u32[]{:S(2)}, u32[]{:S(2)}) collective-permute-start(bf16[2048,128]{1,0:T(8,128)(2,1)} %bitcast.155), channel_id=1, source_target_pairs={{0,1},{1,0},{2,3},{3,2},{4,5},{5,4},{6,7},{7,6},{8,9},{9,8},{10,11... | collective-permute-start | bytes 1572872 | tf_op jit(solution)/shard_map/ppermute | solution.py:23
  324.2 70.9 %collective-permute-start.90 = (bf16[2048,128]{1,0:T(8,128)(2,1)}, bf16[2048,128]{1,0:T(8,128)(2,1)}, u32[]{:S(2)}, u32[]{:S(2)}) collective-permute-start(bf16[2048,128]{1,0:T(8,128)(2,1)} %bitcast.164), channel_id=1, source_target_pairs={{0,1},{1,0},{2,3},{3,2},{4,5},{5,4},{6,7},{7,6},{8,9},{9,8},{10,11... | collective-permute-start | bytes 1572872 | tf_op jit(solution)/shard_map/ppermute | solution.py:23
  366.1 24.3 %collective-permute-start.71 = (bf16[4,256,512]{2,1,0:T(8,128)(2,1)S(1)}, bf16[4,256,512]{2,1,0:T(8,128)(2,1)S(1)}, u32[]{:S(2)}, u32[]{:S(2)}) collective-permute-start(bf16[4,256,512]{2,1,0:T(8,128)(2,1)S(1)} %get-tuple-element.67), channel_id=1, source_target_pairs={{0,2},{1,3},{8,10},{9,11},{16,18},{17,19},{24,26},{25,27}} | collective-permute-start | bytes 3145736 | tf_op jit(solution)/shard_map/ppermute | solution.py:166
  368.4 23.4 %collective-permute-start.80 = (bf16[2048,256]{1,0:T(8,128)(2,1)S(1)}, bf16[2048,256]{1,0:T(8,128)(2,1)S(1)}, u32[]{:S(2)}, u32[]{:S(2)}) collective-permute-start(bf16[2048,256]{1,0:T(8,128)(2,1)S(1)} %bitcast.1080), channel_id=1, source_target_pairs={{0,1},{1,0},{2,3},{3,2},{4,5},{5,4},{6,7},{7,6},{8,9},{9,8},{10,11... | collective-permute-start | bytes 3145736 | tf_op jit(solution)/shard_map/ppermute | solution.py:23
  520.4 26.9 %collective-permute-start.175 = (bf16[1024,1024]{1,0:T(8,128)(2,1)}, bf16[1024,1024]{1,0:T(8,128)(2,1)S(1)}, u32[]{:S(2)}, u32[]{:S(2)}) collective-permute-start(bf16[1024,1024]{1,0:T(8,128)(2,1)} %convolution_convert_fusion.4), channel_id=1, source_target_pairs={{0,1},{1,0},{2,3},{3,2},{4,5},{5,4},{6,7},{7,6},{8,9},{9,8},{10,11... | collective-permute-start | bytes 6291464 | tf_op jit(solution)/shard_map/ppermute | solution.py:23
  524.3 56.9 %collective-permute-start.123 = (f32[4,256,512]{2,1,0:T(8,128)S(1)}, f32[4,256,512]{2,1,0:T(8,128)S(1)}, u32[]{:S(2)}, u32[]{:S(2)}) collective-permute-start(f32[4,256,512]{2,1,0:T(8,128)S(1)} %select_bitcast_fusion), channel_id=1, source_target_pairs={{0,1},{1,0},{2,3},{3,2},{4,5},{5,4},{6,7},{7,6},{8,9},{9,8},{10,11... | collective-permute-start | bytes 6291464 | tf_op jit(solution)/shard_map/ppermute | solution.py:23
  551.5 31.7 %collective-permute-start.226 = (bf16[2,2,2,128,128]{4,3,2,0,1:T(8,128)(2,1)S(1)}, bf16[2,2,2,128,128]{4,3,2,0,1:T(8,128)(2,1)S(1)}, u32[]{:S(2)}, u32[]{:S(2)}) collective-permute-start(bf16[2,2,2,128,128]{4,3,2,0,1:T(8,128)(2,1)S(1)} %select_bitcast_fusion.27), channel_id=1, source_target_pairs={{0,2},{1,3},{2,0},{3,1},{4,6},{5,7},{6,4},{7,5},{8,10},{9,11},{10,... | collective-permute-start | bytes 786440 | tf_op jit(solution)/shard_map/ppermute | solution.py:23
  578.0 138.6 %collective-permute-start.218 = (bf16[2,2,2,128,256]{4,3,1,2,0:T(8,128)(2,1)S(1)}, bf16[2,2,2,128,256]{4,3,1,2,0:T(8,128)(2,1)S(1)}, u32[]{:S(2)}, u32[]{:S(2)}) collective-permute-start(bf16[2,2,2,128,256]{4,3,1,2,0:T(8,128)(2,1)S(1)} %select_bitcast_fusion.6), channel_id=1, source_target_pairs={{0,8},{1,9},{2,10},{3,11},{4,12},{5,13},{6,14},{7,15},{8,0},{9,1},... | collective-permute-start | bytes 1572872 | tf_op jit(solution)/shard_map/ppermute | solution.py:23
  583.3 38.7 %collective-permute-start.208 = (bf16[2,2,2,64,384]{4,3,1,0,2:T(8,128)(2,1)S(1)}, bf16[2,2,2,64,384]{4,3,1,0,2:T(8,128)(2,1)S(1)}, u32[]{:S(2)}, u32[]{:S(2)}) collective-permute-start(bf16[2,2,2,64,384]{4,3,1,0,2:T(8,128)(2,1)S(1)} %copy.189), channel_id=1, source_target_pairs={{0,16},{1,17},{2,18},{3,19},{4,20},{5,21},{6,22},{7,23},{8,24},{9,... | collective-permute-start | bytes 1179656 | tf_op jit(solution)/shard_map/ppermute | solution.py:23
  600.6 116.5 %collective-permute-start.190 = (bf16[2,2,2,128,256]{4,3,1,2,0:T(8,128)(2,1)S(1)}, bf16[2,2,2,128,256]{4,3,1,2,0:T(8,128)(2,1)S(1)}, u32[]{:S(2)}, u32[]{:S(2)}) collective-permute-start(bf16[2,2,2,128,256]{4,3,1,2,0:T(8,128)(2,1)S(1)} %select_bitcast_fusion.7), channel_id=1, source_target_pairs={{0,8},{1,9},{2,10},{3,11},{4,12},{5,13},{6,14},{7,15},{8,0},{9,1},... | collective-permute-start | bytes 1572872 | tf_op jit(solution)/shard_map/ppermute | solution.py:23
  620.8 144.2 %collective-permute-start.124 = (bf16[4,256,512]{2,1,0:T(8,128)(2,1)S(1)}, bf16[4,256,512]{2,1,0:T(8,128)(2,1)S(1)}, u32[]{:S(2)}, u32[]{:S(2)}) collective-permute-start(bf16[4,256,512]{2,1,0:T(8,128)(2,1)S(1)} %get-tuple-element.52), channel_id=1, source_target_pairs={{6,4},{7,5},{14,12},{15,13},{22,20},{23,21},{30,28},{31,29}} | collective-permute-start | bytes 3145736 | tf_op jit(solution)/shard_map/ppermute | solution.py:166
  640.3 78.6 %collective-permute-start.205 = (bf16[2,2,64,384]{3,2,0,1:T(8,128)(2,1)S(1)}, bf16[2,2,64,384]{3,2,0,1:T(8,128)(2,1)S(1)}, u32[]{:S(2)}, u32[]{:S(2)}) collective-permute-start(bf16[2,2,64,384]{3,2,0,1:T(8,128)(2,1)S(1)} %select_bitcast_fusion.59), channel_id=1, source_target_pairs={{0,16},{1,17},{2,18},{3,19},{4,20},{5,21},{6,22},{7,23},{8,24},{9,... | collective-permute-start | bytes 589832 | tf_op jit(solution)/shard_map/ppermute | solution.py:23
  653.5 44.1 %collective-permute-start.229 = (bf16[128,128]{1,0:T(8,128)(2,1)S(1)}, bf16[128,128]{1,0:T(8,128)(2,1)S(1)}, u32[]{:S(2)}, u32[]{:S(2)}) collective-permute-start(bf16[128,128]{1,0:T(8,128)(2,1)S(1)} %select_bitcast_fusion.200), channel_id=1, source_target_pairs={{0,4},{1,5},{2,6},{3,7},{4,0},{5,1},{6,2},{7,3},{8,12},{9,13},{10,... | collective-permute-start | bytes 98312 | tf_op jit(solution)/shard_map/ppermute | solution.py:23
  718.9 44.3 %collective-permute-start.219 = (bf16[2,2,128,256]{3,2,0,1:T(8,128)(2,1)S(1)}, bf16[2,2,128,256]{3,2,0,1:T(8,128)(2,1)S(1)}, u32[]{:S(2)}, u32[]{:S(2)}) collective-permute-start(bf16[2,2,128,256]{3,2,0,1:T(8,128)(2,1)S(1)} %select_bitcast_fusion.28), channel_id=1, source_target_pairs={{0,16},{1,17},{2,18},{3,19},{4,20},{5,21},{6,22},{7,23},{8,24},{9,... | collective-permute-start | bytes 786440 | tf_op jit(solution)/shard_map/ppermute | solution.py:23
  721.1 42.3 %collective-permute-start.191 = (bf16[2,2,128,256]{3,2,0,1:T(8,128)(2,1)S(1)}, bf16[2,2,128,256]{3,2,0,1:T(8,128)(2,1)S(1)}, u32[]{:S(2)}, u32[]{:S(2)}) collective-permute-start(bf16[2,2,128,256]{3,2,0,1:T(8,128)(2,1)S(1)} %select_bitcast_fusion.31), channel_id=1, source_target_pairs={{0,16},{1,17},{2,18},{3,19},{4,20},{5,21},{6,22},{7,23},{8,24},{9,... | collective-permute-start | bytes 786440 | tf_op jit(solution)/shard_map/ppermute | solution.py:23
  735.4 24.7 %collective-permute-start.183 = (bf16[64,384]{1,0:T(8,128)(2,1)S(1)}, bf16[64,384]{1,0:T(8,128)(2,1)S(1)}, u32[]{:S(2)}, u32[]{:S(2)}) collective-permute-start(bf16[64,384]{1,0:T(8,128)(2,1)S(1)} %select_bitcast_fusion.184), channel_id=1, source_target_pairs={{0,4},{1,5},{2,6},{3,7},{4,0},{5,1},{6,2},{7,3},{8,12},{9,13},{10,... | collective-permute-start | bytes 147464 | tf_op jit(solution)/shard_map/ppermute | solution.py:23
  737.2 27.8 %collective-permute-start.216 = (f32[32,1024]{1,0:T(8,128)S(1)}, f32[32,1024]{1,0:T(8,128)S(1)}, u32[]{:S(2)}, u32[]{:S(2)}) collective-permute-start(f32[32,1024]{1,0:T(8,128)S(1)} %slice_select_fusion.5), channel_id=1, source_target_pairs={{0,1},{1,0},{2,3},{3,2},{4,5},{5,4},{6,7},{7,6},{8,9},{9,8},{10,11... | collective-permute-start | bytes 393224 | tf_op jit(solution)/shard_map/ppermute | solution.py:23
  768.6 25.5 %collective-permute-start.221 = (bf16[128,256]{1,0:T(8,128)(2,1)S(1)}, bf16[128,256]{1,0:T(8,128)(2,1)S(1)}, u32[]{:S(2)}, u32[]{:S(2)}) collective-permute-start(bf16[128,256]{1,0:T(8,128)(2,1)S(1)} %select_bitcast_fusion.139), channel_id=1, source_target_pairs={{0,4},{1,5},{2,6},{3,7},{4,0},{5,1},{6,2},{7,3},{8,12},{9,13},{10,... | collective-permute-start | bytes 196616 | tf_op jit(solution)/shard_map/ppermute | solution.py:23
  770.9 47.3 %collective-permute-start.126 = (bf16[4,256,512]{2,1,0:T(8,128)(2,1)S(1)}, bf16[4,256,512]{2,1,0:T(8,128)(2,1)S(1)}, u32[]{:S(2)}, u32[]{:S(2)}) collective-permute-start(bf16[4,256,512]{2,1,0:T(8,128)(2,1)S(1)} %add_convert_fusion.9), channel_id=1, source_target_pairs={{2,0},{3,1},{10,8},{11,9},{18,16},{19,17},{26,24},{27,25}} | collective-permute-start | bytes 3145736 | tf_op jit(solution)/shard_map/ppermute | solution.py:166
  772.7 23.7 %collective-permute-start.193 = (bf16[128,256]{1,0:T(8,128)(2,1)S(1)}, bf16[128,256]{1,0:T(8,128)(2,1)S(1)}, u32[]{:S(2)}, u32[]{:S(2)}) collective-permute-start(bf16[128,256]{1,0:T(8,128)(2,1)S(1)} %select_bitcast_fusion.143), channel_id=1, source_target_pairs={{0,4},{1,5},{2,6},{3,7},{4,0},{5,1},{6,2},{7,3},{8,12},{9,13},{10,... | collective-permute-start | bytes 196616 | tf_op jit(solution)/shard_map/ppermute | solution.py:23
  794.2 26.8 %collective-permute-start.230 = (f32[64,512]{1,0:T(8,128)S(1)}, f32[64,512]{1,0:T(8,128)S(1)}, u32[]{:S(2)}, u32[]{:S(2)}) collective-permute-start(f32[64,512]{1,0:T(8,128)S(1)} %slice_select_fusion.3), channel_id=1, source_target_pairs={{0,1},{1,0},{2,3},{3,2},{4,5},{5,4},{6,7},{7,6},{8,9},{9,8},{10,11... | collective-permute-start | bytes 393224 | tf_op jit(solution)/shard_map/ppermute | solution.py:23
  879.8 62.6 %collective-permute-start.161 = (bf16[1024,1024]{1,0:T(8,128)(2,1)S(1)}, bf16[1024,1024]{1,0:T(8,128)(2,1)S(1)}, u32[]{:S(2)}, u32[]{:S(2)}) collective-permute-start(bf16[1024,1024]{1,0:T(8,128)(2,1)S(1)} %convolution_convert_fusion.5), channel_id=1, source_target_pairs={{0,1},{1,0},{2,3},{3,2},{4,5},{5,4},{6,7},{7,6},{8,9},{9,8},{10,11... | collective-permute-start | bytes 6291464 | tf_op jit(solution)/shard_map/ppermute | solution.py:23
  885.4 32.1 %collective-permute-start.134 = (bf16[2,2,2,64,256]{4,3,1,2,0:T(8,128)(2,1)S(1)}, bf16[2,2,2,64,256]{4,3,1,2,0:T(8,128)(2,1)S(1)}, u32[]{:S(2)}, u32[]{:S(2)}) collective-permute-start(bf16[2,2,2,64,256]{4,3,1,2,0:T(8,128)(2,1)S(1)} %select_bitcast_fusion.35), channel_id=1, source_target_pairs={{0,8},{1,9},{2,10},{3,11},{4,12},{5,13},{6,14},{7,15},{8,0},{9,1},... | collective-permute-start | bytes 786440 | tf_op jit(solution)/shard_map/ppermute | solution.py:23
  889.0 29.2 %collective-permute-start.148 = (bf16[2,2,2,64,256]{4,3,1,2,0:T(8,128)(2,1)S(1)}, bf16[2,2,2,64,256]{4,3,1,2,0:T(8,128)(2,1)S(1)}, u32[]{:S(2)}, u32[]{:S(2)}) collective-permute-start(bf16[2,2,2,64,256]{4,3,1,2,0:T(8,128)(2,1)S(1)} %select_bitcast_fusion.34), channel_id=1, source_target_pairs={{0,8},{1,9},{2,10},{3,11},{4,12},{5,13},{6,14},{7,15},{8,0},{9,1},... | collective-permute-start | bytes 786440 | tf_op jit(solution)/shard_map/ppermute | solution.py:23
  (347 other events, 2749.5 us)

commit v2 on v0

v2 whole, which is shorter than its diff:
```python
import functools

import jax
import jax.numpy as jnp
from jax import lax
from jax.experimental import pallas as pl
from jax.experimental.pallas import tpu as pltpu
from jax.sharding import PartitionSpec as P

H = 4
QK = 256
VH = 512
AXES = ("dp", "seq")
F32 = jnp.float32
BF16 = jnp.bfloat16
FAR = 4
VMEM = 56 * 1024 * 1024


def mm(left, right):
    return lax.dot_general(left, right, (((1,), (0,)), ((), ())), preferred_element_type=F32)


def nt(left, right):
    return lax.dot_general(left, right, (((1,), (1,)), ((), ())), preferred_element_type=F32)


def tn(left, right):
    return lax.dot_general(left, right, (((0,), (0,)), ((), ())), preferred_element_type=F32)


def devices():
    return lax.axis_size("dp") * lax.axis_size("seq")


def place():
    return lax.axis_index("dp") * lax.axis_size("seq") + lax.axis_index("seq")


def swap(values, bit):
    return lax.ppermute(values, AXES, [(i, i ^ bit) for i in range(devices())])


def upper_core():
    return lax.axis_index("seq") % 2 == 1


def orders():
    bits = [1 << k for k in range(1, devices().bit_length() - 1)]
    near = [bit for bit in bits if bit not in (2, FAR)] + [2]
    return [near[turn:] + near[:turn] for turn in range(3)]


def cut(width):
    tiles = width // 128
    third = tiles // 4
    first = (tiles - third + 1) // 2
    edges = [0, first * 128, (tiles - third) * 128, width]
    return list(zip(edges[:-1], edges[1:]))


def halves(values):
    half = values.shape[-1] // 2
    upper = upper_core()
    low, high = values[..., :half], values[..., half:]
    return jnp.where(upper, high, low), jnp.where(upper, low, high)


def ordered(mine, other, axis):
    upper = upper_core()
    return jnp.concatenate(
        [jnp.where(upper, other, mine), jnp.where(upper, mine, other)], axis=axis
    )


def settle(info, parts, cuts, held, width):
    chips = devices() // 2
    rows = parts[0].shape[1]

    def body(info_ref, *refs):
        sources, target = refs[:-1], refs[-1]
        me = info_ref[0]
        for turn, ((start, stop), bits) in enumerate(zip(cuts, held)):
            for far in range(chips):
                at = sum((1 << k) for k, bit in enumerate(bits[:-1]) if far & (bit >> 1))
                source = sources[2 * turn + (1 if far & (bits[-1] >> 1) else 0)]
                target[far ^ me, :, start:stop] = source[at]

    return pl.pallas_call(
        body,
        out_shape=jax.ShapeDtypeStruct((chips, rows, width), BF16),
        in_specs=[pl.BlockSpec(memory_space=pltpu.SMEM)]
        + [pl.BlockSpec(memory_space=pltpu.VMEM)] * len(parts),
        out_specs=pl.BlockSpec(memory_space=pltpu.VMEM),
        compiler_params=pltpu.CompilerParams(vmem_limit_bytes=20 * 1024 * 1024),
        cost_estimate=pl.CostEstimate(
            flops=0, bytes_accessed=4 * chips * rows * width, transcendentals=0
        ),
        name="settle",
    )(info, *parts)


def sync(*values):
    return lax.optimization_barrier(values)


def classes(piece, got):
    pair = jnp.stack([piece, got])
    return [pair[:, :, start:stop] for start, stop in cut(piece.shape[-1])]


def grow(parts, turn):
    return [swap(part, order[::-1][turn]) for part, order in zip(parts, orders())]


def join(parts, gots):
    return [jnp.concatenate([part, got], axis=0) for part, got in zip(parts, gots)]


def settled(info, parts, gots, width):
    held = [[FAR] + order[::-1] for order in orders()]
    both = [value for pair in zip(parts, gots) for value in pair]
    return settle(info, both, cut(width), held, width)


def total_of(mine, got):
    return mine.astype(F32) + got.astype(F32)


def split_first(own, got):
    chips, rows, width = own.shape
    levels = chips.bit_length() - 1
    dims = (2,) * levels + (rows, width)
    own, got = own.reshape(dims), got.reshape(dims)
    bits = [1 << k for k in range(levels, 0, -1)]
    return [
        (own[..., start:stop], got[..., start:stop], list(bits)) for start, stop in cut(width)
    ]


def shrink(parts, turn):
    after = []
    for (mine, theirs, bits), order in zip(parts, orders()):
        bit = order[turn]
        spot = bits.index(bit)

        def pick(values, side):
            return lax.index_in_dim(values, side, spot, False)

        send = total_of(pick(mine, 1), pick(theirs, 1)).astype(BF16)
        keep = total_of(pick(mine, 0), pick(theirs, 0)).astype(BF16)
        after.append((keep, swap(send, bit), [other for other in bits if other != bit]))
    return after


def shrink_far(parts):
    send = jnp.concatenate([total_of(m[1], t[1]).astype(BF16) for m, t, _ in parts], axis=1)
    mine = jnp.concatenate([total_of(m[0], t[0]) for m, t, _ in parts], axis=1)
    return mine, swap(send, FAR)


def hold(parts, *others):
    arrays = [(mine, theirs) for mine, theirs, _ in parts]
    arrays, others = lax.optimization_barrier((arrays, others))
    return ([(m, t, bits) for (m, t), (_, _, bits) in zip(arrays, parts)],) + tuple(others)


def finish_wide(values):
    rows = values.shape[0] // 2
    upper = upper_core()
    low, high = values[:rows], values[rows:]
    mine, give = jnp.where(upper, high, low), jnp.where(upper, low, high)
    return mine, swap(give, 1)


def finish_tall(values):
    half = values.shape[1] // 2
    upper = upper_core()
    low, high = values[:, :half], values[:, half:]
    mine, give = jnp.where(upper, high, low), jnp.where(upper, low, high)
    return ordered(mine, swap(give, 1), 1)


def begin_states(carry, near_carry, own, near, reverse):
    upper = upper_core()
    turned = jnp.logical_not(upper) if reverse else upper
    first_carry = jnp.where(turned, near_carry, carry)[:, :, None, None]
    last_carry = jnp.where(turned, carry, near_carry)[:, :, None, None]
    first = jnp.where(turned, near, own)
    last = jnp.where(turned, own, near)
    joined = last_carry * first + last
    both = first_carry * last_carry
    rows = own.shape[1]
    entering = [jnp.zeros_like(joined[:, 0]) for _ in range(rows)]
    return (turned, first_carry, first, joined, both, entering)


def hop(states, phase, reverse):
    turned, first_carry, first, joined, both, entering = states
    chips = lax.axis_size("seq") // 2
    arrived = []
    for row in range(len(entering)):
        step = phase - row
        if not 1 <= step < chips:
            arrived.append(None)
            continue
        message = (joined[:, row] + both[:, row] * entering[row]).astype(BF16)
        source, target = (step - 1, step) if not reverse else (chips - step, chips - step - 1)
        pairs = [(2 * source + core, 2 * target + core) for core in range(2)]
        arrived.append(lax.ppermute(message, "seq", pairs))
    return arrived


def land(states, arrived):
    turned, first_carry, first, joined, both, entering = states
    entering = [
        e if a is None else e + a.astype(F32)
        for e, a in zip(entering, arrived)
    ]
    return (turned, first_carry, first, joined, both, entering)


def end_states(states):
    turned, first_carry, first, joined, both, entering = states
    entering = jnp.stack(entering, axis=1)
    middle = (first_carry * entering + first).astype(BF16)
    entering = entering.astype(BF16)
    mine = jnp.where(turned, middle, entering)
    theirs = swap(jnp.where(turned, entering, middle), 1)
    return mine, theirs


def call(body, grid, info, ins, outs, scratch, flops, name):
    def spec(block, index):
        if block is None:
            return pl.BlockSpec(memory_space=pltpu.SMEM)
        return pl.BlockSpec(block, index)

    moved = sum(a.size * a.dtype.itemsize for a, _, _ in ins)
    for shape, dtype, _, _ in outs:
        size = jnp.dtype(dtype).itemsize
        for extent in shape:
            size *= extent
        moved += size
    return pl.pallas_call(
        body,
        grid_spec=pltpu.PrefetchScalarGridSpec(
            num_scalar_prefetch=1,
            grid=(grid,),
            in_specs=[spec(block, index) for _, block, index in ins],
            out_specs=[spec(block, index) for _, _, block, index in outs],
            scratch_shapes=scratch,
        ),
        out_shape=[jax.ShapeDtypeStruct(shape, dtype) for shape, dtype, _, _ in outs],
        compiler_params=pltpu.CompilerParams(
            vmem_limit_bytes=VMEM, dimension_semantics=("arbitrary",)
        ),
        cost_estimate=pl.CostEstimate(flops=int(flops), bytes_accessed=int(moved), transcendentals=0),
        name=name,
    )(info, *[a for a, _, _ in ins])


def whole(array):
    zeros = (0,) * array.ndim
    return (array, array.shape, lambda h, info: zeros)


def whole_out(shape, dtype):
    zeros = (0,) * len(shape)
    return (shape, dtype, shape, lambda h, info: zeros)


def head_in(array):
    rest = (0,) * (array.ndim - 1)
    return (array, (1,) + array.shape[1:], lambda h, info: (h,) + rest)


def head_out(shape, dtype):
    rest = (0,) * (len(shape) - 1)
    return (shape, dtype, (1,) + shape[1:], lambda h, info: (h,) + rest)


def own_in(array):
    rest = (0,) * (array.ndim - 1)
    return (array, (1,) + array.shape[1:], lambda h, info: (jnp.minimum(h, 1),) + rest)


def other_in(array):
    rest = (0,) * (array.ndim - 1)
    return (array, (1,) + array.shape[1:], lambda h, info: (jnp.maximum(h - 2, 0),) + rest)


def own_out(shape, dtype):
    rest = (0,) * (len(shape) - 1)
    return (shape, dtype, (1,) + shape[1:], lambda h, info: (jnp.minimum(h, 1),) + rest)


def other_out(shape, dtype):
    rest = (0,) * (len(shape) - 1)
    return (shape, dtype, (1,) + shape[1:], lambda h, info: (jnp.maximum(h - 2, 0),) + rest)


def real(h, info):
    return lax.rem(h + 2 * info[1], 4)


def real_in(array):
    rest = (0,) * (array.ndim - 1)
    return (array, (1,) + array.shape[1:], lambda h, info: (real(h, info),) + rest)


def columns(array, width, first, own):
    block = array.shape[:2] + (width,)
    if own:
        return (array, block, lambda h, info: (0, 0, first + jnp.minimum(h, 1)))
    return (array, block, lambda h, info: (0, 0, first + jnp.maximum(h - 2, 0)))


def tall(array):
    block = (array.shape[0] // 4, array.shape[1], 1024)
    return (array, block, lambda h, info: (real(h, info), 0, 1))


def tall_rows(ref):
    chips = ref.shape[0]
    pieces = []
    for chip in range(chips):
        pieces += [ref[chip, :, :512], ref[chip, :, 512:]]
    return jnp.concatenate(pieces, axis=0)


def flat(ref):
    chips, rows, width = ref.shape
    return ref[...].reshape(chips * rows, width)


def side(info, own):
    return pl.multiple_of(512 * (info[1] if own else 1 - info[1]), 512)


def put_wide(target, info, values, start):
    chips, rows, _ = target.shape
    width = values.shape[1]
    values = values.astype(BF16)
    for chip in range(chips):
        target[chip ^ info[0], :, start : start + width] = values[chip * rows : (chip + 1) * rows]


def put_tall(target, info, values, block, start):
    chips, rows, _ = target.shape
    values = values.astype(BF16)
    share = chips // 4
    for chip in range(share):
        at = (block * share + chip) ^ info[0]
        base = 2 * rows * chip
        target[at, :, start : start + 512] = values[base : base + rows]
        target[at, :, start + 512 : start + 1024] = values[base + rows : base + 2 * rows]


def rotated(values, cosine, sine):
    a, b = values[:, :128], values[:, 128:]
    return jnp.concatenate([a * cosine - b * sine, b * cosine + a * sine], axis=1)


def unrotated(values, cosine, sine):
    a, b = values[:, :128], values[:, 128:]
    return jnp.concatenate([a * cosine + b * sine, b * cosine - a * sine], axis=1)


def mask_of(rate, tall_count, wide_count):
    length = tall_count.shape[0]
    i = lax.broadcasted_iota(jnp.int32, (length, length), 0)
    s = lax.broadcasted_iota(jnp.int32, (length, length), 1)
    decay = jnp.exp((i - s).astype(F32) * rate)
    return jnp.where((tall_count == wide_count) & (i >= s), decay, 0.0)


def enter_of(rate, tall_count):
    i = lax.broadcasted_iota(jnp.int32, tall_count.shape, 0)
    return jnp.where(tall_count == 0, jnp.exp((i + 1).astype(F32) * rate), 0.0)


def leave_of(rate, tall_count):
    length = tall_count.shape[0]
    i = lax.broadcasted_iota(jnp.int32, tall_count.shape, 0)
    last = tall_count[length - 1 :, :]
    return jnp.where(tall_count == last, jnp.exp((length - 1 - i).astype(F32) * rate), 0.0)


def norm_parts(values, eps):
    average = jnp.mean(values, axis=-1, keepdims=True)
    centred = values - average
    spread_ = jnp.mean(centred * centred, axis=-1, keepdims=True)
    scale = lax.rsqrt(spread_ + eps)
    return centred * scale, scale


def norm_back(grad, normal, scale):
    first = jnp.mean(grad, axis=-1, keepdims=True)
    second = jnp.mean(grad * normal, axis=-1, keepdims=True)
    return scale * (grad - first - normal * second)


CHUNK = 64


def norm_kernel(info, x, gain, bias, normed, normed_t):
    @pl.loop(0, x.shape[0] // CHUNK)
    def _(k):
        at = pl.ds(pl.multiple_of(k * CHUNK, CHUNK), CHUNK)
        normal, _ = norm_parts(x[at, :].astype(F32), 1e-05)
        normed[at, :] = (normal * gain[...].astype(F32) + bias[...].astype(F32)).astype(BF16)

    normed_t[...] = normed[...].T


def project_kernel(
    info, rates, normed, cosine, sine, tall_count, wide_count,
    q_own, k_own, v_own, q_oth, k_oth, v_oth,
    q_out, k_out, v_out, mix_out, inner_out, sum_own, sum_oth, pre,
):
    h = pl.program_id(0)

    def fill(wq, wk, wv):
        left = normed[...]
        pre[:, :256] = mm(left, flat(wq))
        pre[:, 256:512] = mm(left, flat(wk))
        pre[:, 512:] = mm(left, flat(wv))

    @pl.when(h < 2)
    def _():
        fill(q_own, k_own, v_own)

    @pl.when(h >= 2)
    def _():
        fill(q_oth, k_oth, v_oth)

    rate = rates[h]
    length = cosine.shape[0]
    for row in range(tall_count.shape[0]):
        at = slice(row * length, (row + 1) * length)
        count = tall_count[row]
        query = rotated(pre[at, :256], cosine[...], sine[...]).astype(BF16)
        key = (rotated(pre[at, 256:512], cosine[...], sine[...]) * QK**-0.5).astype(BF16)
        value = pre[at, 512:].astype(BF16)
        q_out[0, at] = query
        k_out[0, at] = key
        v_out[0, at] = value
        mixing = (nt(query, key) * mask_of(rate, count, wide_count[row])).astype(BF16)
        mix_out[0, at] = mixing
        inner_out[0, at] = mm(mixing, value)
        weighted = (key.astype(F32) * leave_of(rate, count)).astype(BF16)
        summary = tn(weighted, value)

        @pl.when(h < 2)
        def _():
            sum_own[0, row] = summary

        @pl.when(h >= 2)
        def _():
            sum_oth[0, row] = summary


def gate_kernel(info, normed, own, oth, out):
    h = pl.program_id(0)

    @pl.when(h < 2)
    def _():
        out[0] = mm(normed[...], flat(own))

    @pl.when(h >= 2)
    def _():
        out[0] = mm(normed[...], flat(oth))


def mix_kernel(
    info, rates, x, gain, second_gain, second_bias, tall_count, query, inner, gate,
    state_own, state_oth, wo_own, wo_oth,
    retained, mixed_t, hidden, normed, normed_t,
):
    h = pl.program_id(0)
    rate = rates[h]
    length = tall_count.shape[1]

    @pl.when(h == 0)
    def _():
        hidden[...] = x[...].astype(F32)

    for row in range(tall_count.shape[0]):
        at = slice(row * length, (row + 1) * length)
        entered = (query[0, at].astype(F32) * enter_of(rate, tall_count[row])).astype(BF16)

        @pl.when(h < 2)
        def _():
            retained[0, at] = inner[0, at] + mm(entered, state_own[0, row])

        @pl.when(h >= 2)
        def _():
            retained[0, at] = inner[0, at] + mm(entered, state_oth[0, row])

    normal, _ = norm_parts(retained[0], 1.0)
    pre = gate[0]
    mixed = (pre / (1.0 + jnp.exp(-pre)) * (normal * gain[0].astype(F32))).astype(BF16)
    mixed_t[0] = mixed.T
    hidden[:, pl.ds(side(info, True), 512)] += mm(mixed, tall_rows(wo_own))
    hidden[:, pl.ds(side(info, False), 512)] += mm(mixed, tall_rows(wo_oth))

    @pl.when(h == 3)
    def _():
        @pl.loop(0, x.shape[0] // CHUNK)
        def _(k):
            at = pl.ds(pl.multiple_of(k * CHUNK, CHUNK), CHUNK)
            normal, _ = norm_parts(hidden[at, :], 1e-05)
            normed[at, :] = (
                normal * second_gain[...].astype(F32) + second_bias[...].astype(F32)
            ).astype(BF16)

        normed_t[...] = normed[...].T


def feed_kernel(
    info, hidden, normed, normed_t, cot, second_gain,
    up_own, up_oth, down_own, down_oth,
    output, grad_hidden, grad_low, grad_gain, grad_bias, g_own, g_oth,
    upward, out_sum, norm_sum,
):
    f = pl.program_id(0)
    own_at = pl.ds(side(info, True), 512)
    oth_at = pl.ds(side(info, False), 512)

    @pl.when(f == 0)
    def _():
        out_sum[...] = hidden[...]
        norm_sum[...] = jnp.zeros_like(norm_sum)

    @pl.when(f < 2)
    def _():
        upward[...] = mm(normed[...], flat(up_own))

    @pl.when(f >= 2)
    def _():
        upward[...] = mm(normed[...], flat(up_oth))

    up = upward[...]
    root = 0.7978845608028654
    squared = up * up
    bent = jnp.tanh(root * (up + 0.044715 * (squared * up)))
    activated = (0.5 * up * (1.0 + bent)).astype(BF16)
    slope = 0.5 * (1.0 + bent) + 0.5 * up * (1.0 - bent * bent) * (
        root * (1.0 + 3 * 0.044715 * squared)
    )
    own, oth = tall_rows(down_own), tall_rows(down_oth)
    out_sum[:, own_at] += mm(activated, own)
    out_sum[:, oth_at] += mm(activated, oth)
    grad_up = (slope * (nt(cot[:, own_at], own) + nt(cot[:, oth_at], oth))).astype(BF16)
    block = real(f, info)
    act_t = activated.T
    put_tall(g_own, info, mm(act_t, cot[:, own_at]), block, 1024)
    put_tall(g_oth, info, mm(act_t, cot[:, oth_at]), block, 1024)
    grad_w = mm(normed_t[...], grad_up)
    for step in range(4):

        @pl.when(f == step)
        def _():
            put_wide(g_own if step < 2 else g_oth, info, grad_w, 512 * (step % 2))

    @pl.when(f < 2)
    def _():
        norm_sum[...] += nt(grad_up, flat(up_own))

    @pl.when(f >= 2)
    def _():
        norm_sum[...] += nt(grad_up, flat(up_oth))

    @pl.when(f == 3)
    def _():
        grad_gain[...] = jnp.zeros_like(grad_gain)
        grad_bias[...] = jnp.zeros_like(grad_bias)

        @pl.loop(0, hidden.shape[0] // CHUNK)
        def _(k):
            at = pl.ds(pl.multiple_of(k * CHUNK, CHUNK), CHUNK)
            output[at, :] = out_sum[at, :].astype(BF16)
            normal, scale = norm_parts(hidden[at, :], 1e-05)
            grad = norm_sum[at, :]
            grad_gain[...] += jnp.sum(grad * normal, axis=0, keepdims=True)
            grad_bias[...] += jnp.sum(grad, axis=0, keepdims=True)
            total = cot[at, :].astype(F32) + norm_back(
                grad * second_gain[...].astype(F32), normal, scale
            )
            grad_hidden[at, :] = total
            grad_low[at, :] = total.astype(BF16)


def unmix_kernel(
    info, rates, grad_low, gain, tall_count, query, retained, gate, wo_own, wo_oth,
    grad_ret, grad_gate, grad_gain, state_own, state_oth,
):
    h = pl.program_id(0)
    rate = rates[h]
    length = tall_count.shape[1]
    grad = nt(grad_low[:, pl.ds(side(info, True), 512)], tall_rows(wo_own)) + nt(
        grad_low[:, pl.ds(side(info, False), 512)], tall_rows(wo_oth)
    )
    normal, scale = norm_parts(retained[0], 1.0)
    pre = gate[0]
    share = 1.0 / (1.0 + jnp.exp(-pre))
    curve = pre * share
    scaled = gain[0].astype(F32)
    grad_gate[0] = (grad * (normal * scaled) * (share * (1.0 + pre * (1.0 - share)))).astype(BF16)
    grad_normal = grad * curve
    grad_gain[0] = jnp.sum(grad_normal * normal, axis=0, keepdims=True)
    grad_ret[0] = norm_back(grad_normal * scaled, normal, scale).astype(BF16)
    for row in range(tall_count.shape[0]):
        at = slice(row * length, (row + 1) * length)
        entered = (query[0, at].astype(F32) * enter_of(rate, tall_count[row])).astype(BF16)
        state = tn(entered, grad_ret[0, at])

        @pl.when(h < 2)
        def _():
            state_own[0, row] = state

        @pl.when(h >= 2)
        def _():
            state_oth[0, row] = state


def outer_kernel(
    info, grad_low, normed_t, mixed_t, grad_gate, g_own, g_oth,
    norm_part, out_own, out_oth,
):
    h = pl.program_id(0)

    @pl.when(h == 0)
    def _():
        norm_part[...] = jnp.zeros_like(norm_part)

    block = real(h, info)
    left = mixed_t[0]
    put_tall(out_own, info, mm(left, grad_low[:, pl.ds(side(info, True), 512)]), block, 1024)
    put_tall(out_oth, info, mm(left, grad_low[:, pl.ds(side(info, False), 512)]), block, 1024)
    grad_wg = mm(normed_t[...], grad_gate[0])
    for step in range(4):

        @pl.when(h == step)
        def _():
            put_wide(out_own if step < 2 else out_oth, info, grad_wg, 512 * (step % 2))

    @pl.when(h < 2)
    def _():
        norm_part[...] += nt(grad_gate[0], flat(g_own))

    @pl.when(h >= 2)
    def _():
        norm_part[...] += nt(grad_gate[0], flat(g_oth))


def inside_kernel(
    info, rates, normed_t, grad_ret, query, key, value, mixing,
    cosine, sine, tall_count, wide_count, state_own, state_oth,
    q_own, q_oth, norm_before,
    key_part, value_part, norm_part, out_own, out_oth,
    grad_q,
):
    h = pl.program_id(0)
    rate = rates[h]
    length = cosine.shape[0]

    @pl.when(h == 0)
    def _():
        norm_part[...] = norm_before[...]

    for row in range(tall_count.shape[0]):
        at = slice(row * length, (row + 1) * length)
        grad = grad_ret[0, at]
        mask = mask_of(rate, tall_count[row], wide_count[row])
        scores = (nt(grad, value[0, at]) * mask).astype(BF16)
        enter = enter_of(rate, tall_count[row])

        def set_query(state):
            total = mm(scores, key[0, at]) + nt(grad, state[0, row]) * enter
            grad_q[at, :] = unrotated(total, cosine[...], sine[...]).astype(BF16)

        @pl.when(h < 2)
        def _():
            set_query(state_own)

        @pl.when(h >= 2)
        def _():
            set_query(state_oth)

        key_part[0, at] = tn(scores, query[0, at])
        value_part[0, at] = tn(mixing[0, at], grad)

    grad_wq = mm(normed_t[...], grad_q[...])
    for step in range(4):

        @pl.when(h == step)
        def _():
            put_wide(out_own if step < 2 else out_oth, info, grad_wq, 256 * (step % 2))

    @pl.when(h < 2)
    def _():
        norm_part[...] += nt(grad_q[...], flat(q_own))

    @pl.when(h >= 2)
    def _():
        norm_part[...] += nt(grad_q[...], flat(q_oth))


def last_kernel(
    info, rates, normed_t, key, value, key_part, value_part, cosine, sine, tall_count,
    state_own, state_oth,
    grad_k, grad_v, out_own, out_oth,
):
    h = pl.program_id(0)
    rate = rates[h]
    length = cosine.shape[0]
    for row in range(tall_count.shape[0]):
        at = slice(row * length, (row + 1) * length)
        leave = leave_of(rate, tall_count[row])
        weighted = (key[0, at].astype(F32) * leave).astype(BF16)

        def set_both(state):
            low = state[0, row]
            grad_v[0, at] = (value_part[0, at] + mm(weighted, low)).astype(BF16)
            total = key_part[0, at] + nt(value[0, at], low) * leave
            grad_k[0, at] = (unrotated(total, cosine[...], sine[...]) * QK**-0.5).astype(BF16)

        @pl.when(h < 2)
        def _():
            set_both(state_own)

        @pl.when(h >= 2)
        def _():
            set_both(state_oth)

    grad_wk = mm(normed_t[...], grad_k[0])
    grad_wv = mm(normed_t[...], grad_v[0])
    for step in range(4):

        @pl.when(h == step)
        def _():
            target = out_own if step < 2 else out_oth
            put_wide(target, info, grad_wk, 256 * (step % 2))
            put_wide(target, info, grad_wv, 512 + 512 * (step % 2))


def input_kernel(
    info, x, gain, grad_hidden, norm_part, grad_k, grad_v, k_own, k_oth, v_own, v_oth,
    input_grad, grad_gain, grad_bias, norm_sum,
):
    h = pl.program_id(0)

    @pl.when(h == 0)
    def _():
        norm_sum[...] = norm_part[...]

    @pl.when(h < 2)
    def _():
        norm_sum[...] += nt(grad_k[0], flat(k_own)) + nt(grad_v[0], flat(v_own))

    @pl.when(h >= 2)
    def _():
        norm_sum[...] += nt(grad_k[0], flat(k_oth)) + nt(grad_v[0], flat(v_oth))

    @pl.when(h == 3)
    def _():
        grad_gain[...] = jnp.zeros_like(grad_gain)
        grad_bias[...] = jnp.zeros_like(grad_bias)

        @pl.loop(0, x.shape[0] // CHUNK)
        def _(k):
            at = pl.ds(pl.multiple_of(k * CHUNK, CHUNK), CHUNK)
            normal, scale = norm_parts(x[at, :].astype(F32), 1e-05)
            grad = norm_sum[at, :]
            grad_gain[...] += jnp.sum(grad * normal, axis=0, keepdims=True)
            grad_bias[...] += jnp.sum(grad, axis=0, keepdims=True)
            input_grad[at, :] = grad_hidden[at, :] + norm_back(
                grad * gain[...].astype(F32), normal, scale
            )


def per_device(
    inputs,
    doc_flags,
    first_gain,
    first_bias,
    w_query,
    w_key,
    w_value,
    w_gate,
    group_gain,
    w_output,
    second_gain,
    second_bias,
    w_up,
    w_down,
    cotangent,
):
    batches, row_count, length, width = inputs.shape
    rows = batches * row_count
    tokens = rows * length
    count = devices()
    chips = count // 2
    core = lax.axis_index("seq") % 2
    info = jnp.stack([place() // 2, core]).astype(jnp.int32)
    x = inputs.reshape(tokens, width)
    cot = cotangent.reshape(tokens, width)

    share = w_query.shape[0]
    upper = upper_core()

    def rows_of(values):
        return values.reshape(1, -1)

    def both_cores(keep, got, axis):
        return jnp.concatenate(
            [jnp.where(upper, got, keep), jnp.where(upper, keep, got)], axis=axis
        )

    def top_piece(*weights):
        pairs = [halves(w) for w in weights]
        keep = jnp.concatenate([a for a, _ in pairs], axis=1)
        got = swap(jnp.concatenate([b for _, b in pairs], axis=1), 1)
        return both_cores(keep, got, 0)

    def side_piece(weight):
        keep, give = halves(weight)
        return both_cores(keep, swap(give, 1), 1)

    vectors = [first_gain, first_bias, second_gain, second_bias, group_gain]
    vector = jnp.concatenate(vectors)[None]
    sizes = [v.shape[0] for v in vectors]
    edges = [sum(sizes[:k]) for k in range(len(sizes) + 1)]
    vector = jnp.concatenate([vector, jnp.zeros((15, vector.shape[1]), BF16)], axis=0)

    qkv = top_piece(w_query, w_key, w_value)
    go = jnp.concatenate([top_piece(w_gate), side_piece(w_output)], axis=1)
    ff = jnp.concatenate([top_piece(w_up), side_piece(w_down)], axis=1)
    got_qkv = swap(qkv, FAR)
    table = vector[None]
    for bit in [1 << k for k in range(count.bit_length() - 1)]:
        table = both_cores(table, swap(table, bit), 0) if bit == 1 else jnp.concatenate(
            [
                jnp.where((place() // bit) % 2 == 1, swapped, table)
                if first
                else jnp.where((place() // bit) % 2 == 1, table, swapped)
                for swapped in [swap(table, bit)]
                for first in (True, False)
            ],
            axis=0,
        )
    table = table[:, 0]
    first_gain, first_bias, second_gain, second_bias, group_gain = [
        table[:, a:b].reshape(1, -1) for a, b in zip(edges[:-1], edges[1:])
    ]
    group_gain = group_gain.reshape(H, 1, VH)

    positions = lax.axis_index("seq") * length + jnp.arange(length, dtype=jnp.int32)
    frequency = 10000.0 ** (-jnp.arange(QK // 2, dtype=F32) / (QK // 2))
    angles = positions.astype(F32)[:, None] * frequency[None, :]
    cosine, sine = jnp.cos(angles), jnp.sin(angles)
    rates = jnp.log1p(-(2.0 ** (-5.0 - 3.0 * jnp.arange(H, dtype=F32))))
    rates = jnp.where(upper, jnp.roll(rates, 2), rates)
    counts = jnp.cumsum(doc_flags.reshape(rows, length), axis=-1, dtype=jnp.int32)
    tall_count, wide_count = counts[:, :, None], counts[:, None, :]
    open_row = (counts[:, -1] == 0).astype(F32)
    near_row = swap(open_row, 1)
    decay = jnp.exp(rates[:2] * float(length))
    carry, near_carry = decay[:, None] * open_row[None], decay[:, None] * near_row[None]

    per_head = (H, tokens)
    state_shape = (2, rows, QK, VH)
    grad_shape = (chips, 2 * share)
    rates_in = (rates, None, None)
    unit = 2.0 * tokens * width * 512

    got_qkv, go, ff, gains, tables = sync(
        got_qkv, go, ff, (first_gain, first_bias, second_gain, second_bias, group_gain),
        (cosine, sine, tall_count, wide_count, carry, near_carry),
    )
    first_gain, first_bias, second_gain, second_bias, group_gain = gains
    cosine, sine, tall_count, wide_count, carry, near_carry = tables
    qkv_parts = classes(qkv, got_qkv)
    qkv_gots = grow(qkv_parts, 0)
    qkv_parts, qkv_gots, go = sync(qkv_parts, qkv_gots, go)
    qkv_parts = join(qkv_parts, qkv_gots)
    qkv_gots = grow(qkv_parts, 1)
    got_go = swap(go, FAR)
    qkv_parts, qkv_gots, got_go, go, ff = sync(qkv_parts, qkv_gots, got_go, go, ff)
    levels = len(orders()[0])
    for turn in range(2, levels - 1):
        qkv_parts = join(qkv_parts, qkv_gots)
        qkv_gots = grow(qkv_parts, turn)
        qkv_parts, qkv_gots = sync(qkv_parts, qkv_gots)
    qkv_parts = join(qkv_parts, qkv_gots)
    qkv_gots = grow(qkv_parts, levels - 1)
    go_parts = classes(go, got_go)
    go_gots = grow(go_parts, 0)
    got_ff = swap(ff, FAR)
    normed, normed_t = call(
        norm_kernel,
        1,
        info,
        [whole(x), whole(first_gain), whole(first_bias)],
        [whole_out((tokens, width), BF16), whole_out((width, tokens), BF16)],
        [],
        unit / 100,
        "norm",
    )
    qkv_parts, qkv_gots, go_parts, go_gots, got_ff, ff, normed, normed_t = sync(
        qkv_parts, qkv_gots, go_parts, go_gots, got_ff, ff, normed, normed_t
    )

    qkv_own = settled(info, qkv_parts, qkv_gots, 2048)
    qkv_oth = swap(qkv_own, 1)
    for turn in range(1, levels - 2):
        go_parts = join(go_parts, go_gots)
        go_gots = grow(go_parts, turn)
        go_parts, go_gots = sync(go_parts, go_gots)
    go_parts = join(go_parts, go_gots)
    go_gots = grow(go_parts, levels - 2)
    ff_parts = classes(ff, got_ff)
    ff_gots = grow(ff_parts, 0)
    (query, key, value, mixing, inner, sum_own, sum_oth) = call(
        project_kernel,
        H,
        info,
        [
            rates_in, whole(normed), whole(cosine), whole(sine),
            whole(tall_count), whole(wide_count),
            columns(qkv_own, 256, 0, True), columns(qkv_own, 256, 2, True),
            columns(qkv_own, 512, 2, True),
            columns(qkv_oth, 256, 0, False), columns(qkv_oth, 256, 2, False),
            columns(qkv_oth, 512, 2, False),
        ],
        [
            head_out(per_head + (QK,), BF16), head_out(per_head + (QK,), BF16),
            head_out(per_head + (VH,), BF16), head_out(per_head + (length,), BF16),
            head_out(per_head + (VH,), F32),
            own_out(state_shape, F32), other_out(state_shape, F32),
        ],
        [pltpu.VMEM((tokens, 1024), F32)],
        10 * unit,
        "project",
    )
    sum_near = swap(sum_oth, 1)
    go_parts, go_gots, ff_parts, ff_gots, sum_own, sum_near = sync(
        go_parts, go_gots, ff_parts, ff_gots, sum_own, sum_near
    )

    states = begin_states(carry, near_carry, sum_own, sum_near, False)
    arrived = hop(states, 1, False)
    go_parts = join(go_parts, go_gots)
    go_gots = grow(go_parts, levels - 1)
    for turn in range(1, levels - 2):
        ff_parts = join(ff_parts, ff_gots)
        ff_gots = grow(ff_parts, turn)
        ff_parts, ff_gots = sync(ff_parts, ff_gots)
    states, arrived, go_parts, go_gots = sync(states, arrived, go_parts, go_gots)
    states = land(states, arrived)

    arrived = hop(states, 2, False)
    go_own = settled(info, go_parts, go_gots, 2048)
    go_oth = swap(go_own, 1)
    ff_parts = join(ff_parts, ff_gots)
    ff_gots = grow(ff_parts, levels - 2)
    states, arrived, go_own, go_oth, ff_parts, ff_gots = sync(
        states, arrived, go_own, go_oth, ff_parts, ff_gots
    )
    states = land(states, arrived)

    arrived = hop(states, 3, False)
    ff_parts = join(ff_parts, ff_gots)
    ff_gots = grow(ff_parts, levels - 1)
    (gate,) = call(
        gate_kernel,
        H,
        info,
        [whole(normed), columns(go_own, 512, 0, True), columns(go_oth, 512, 0, False)],
        [head_out(per_head + (VH,), F32)],
        [],
        4 * unit,
        "gate",
    )
    states, arrived, gate, ff_parts, ff_gots = sync(states, arrived, gate, ff_parts, ff_gots)
    states = land(states, arrived)

    phases = lax.axis_size("seq") // 2 - 1 + rows - 1
    ff_own = settled(info, ff_parts, ff_gots, 2048)
    ff_oth = swap(ff_own, 1)
    for phase in range(4, phases + 1):
        arrived = hop(states, phase, False)
        states, arrived = sync(states, arrived)
        states = land(states, arrived)
    state_own, state_oth = end_states(states)

    retained, mixed_t, hidden, normed_second, normed_second_t = call(
        mix_kernel,
        H,
        info,
        [
            rates_in, whole(x), real_in(group_gain), whole(second_gain), whole(second_bias),
            whole(tall_count), head_in(query), head_in(inner), head_in(gate),
            own_in(state_own), other_in(state_oth), tall(go_own), tall(go_oth),
        ],
        [
            head_out(per_head + (VH,), F32), head_out((H, VH, tokens), BF16),
            whole_out((tokens, width), F32), whole_out((tokens, width), BF16),
            whole_out((width, tokens), BF16),
        ],
        [],
        5 * unit,
        "mix",
    )
    output, grad_hidden, grad_low, grad_second_gain, grad_second_bias, ff_g_own, ff_g_oth = call(
        feed_kernel,
        4,
        info,
        [
            whole(hidden), whole(normed_second), whole(normed_second_t), whole(cot),
            whole(second_gain),
            columns(ff_own, 512, 0, True), columns(ff_oth, 512, 0, False),
            tall(ff_own), tall(ff_oth),
        ],
        [
            whole_out((tokens, width), BF16), whole_out((tokens, width), F32),
            whole_out((tokens, width), BF16), whole_out((1, width), F32),
            whole_out((1, width), F32),
            whole_out(grad_shape + (2048,), BF16), whole_out(grad_shape + (2048,), BF16),
        ],
        [
            pltpu.VMEM((tokens, 512), F32), pltpu.VMEM((tokens, width), F32),
            pltpu.VMEM((tokens, width), F32),
        ],
        24 * unit,
        "feed",
    )

    ff_g_got = swap(ff_g_oth, 1)
    grad_ret, grad_gate, grad_group_gain, gstate_own, gstate_oth = call(
        unmix_kernel,
        H,
        info,
        [
            rates_in, whole(grad_low), real_in(group_gain), whole(tall_count), head_in(query),
            head_in(retained), head_in(gate), tall(go_own), tall(go_oth),
        ],
        [
            head_out(per_head + (VH,), BF16), head_out(per_head + (VH,), BF16),
            (
                (H, 1, VH), F32, (1, 1, VH),
                lambda h, info: (real(h, info), 0, 0),
            ),
            own_out(state_shape, F32), other_out(state_shape, F32),
        ],
        [],
        5 * unit,
        "unmix",
    )
    gstate_near = swap(gstate_oth, 1)
    gstate_own, gstate_near, ff_g_own, ff_g_got, grad_gate, grad_ret = sync(
        gstate_own, gstate_near, ff_g_own, ff_g_got, grad_gate, grad_ret
    )

    states = begin_states(carry, near_carry, gstate_own, gstate_near, True)
    arrived = hop(states, 1, True)
    ff_sums = shrink(split_first(ff_g_own, ff_g_got), 0)
    norm_part, go_g_own, go_g_oth = call(
        outer_kernel,
        H,
        info,
        [
            whole(grad_low), whole(normed_t), head_in(mixed_t), head_in(grad_gate),
            columns(go_own, 512, 0, True), columns(go_oth, 512, 0, False),
        ],
        [
            whole_out((tokens, width), F32),
            whole_out(grad_shape + (2048,), BF16), whole_out(grad_shape + (2048,), BF16),
        ],
        [],
        12 * unit,
        "outer",
    )
    ff_sums, states, arrived, norm_part, go_g_own, go_g_oth = hold(
        ff_sums, states, arrived, norm_part, go_g_own, go_g_oth
    )
    states = land(states, arrived)

    arrived = hop(states, 2, True)
    ff_sums = shrink(ff_sums, 1)
    key_part, value_part, norm_part, q_g_own, q_g_oth = call(
        inside_kernel,
        H,
        info,
        [
            rates_in, whole(normed_t), head_in(grad_ret),
            head_in(query), head_in(key), head_in(value), head_in(mixing),
            whole(cosine), whole(sine), whole(tall_count), whole(wide_count),
            own_in(state_own), other_in(state_oth),
            columns(qkv_own, 256, 0, True), columns(qkv_oth, 256, 0, False), whole(norm_part),
        ],
        [
            head_out(per_head + (QK,), F32), head_out(per_head + (VH,), F32),
            whole_out((tokens, width), F32),
            whole_out(grad_shape + (512,), BF16), whole_out(grad_shape + (512,), BF16),
        ],
        [pltpu.VMEM((tokens, QK), BF16)],
        7 * unit,
        "inside",
    )
    go_g_own = jnp.concatenate([go_g_own, q_g_own], axis=2)
    go_g_oth = jnp.concatenate([go_g_oth, q_g_oth], axis=2)
    ff_sums, states, arrived, key_part, value_part, norm_part, go_g_own, go_g_oth = hold(
        ff_sums, states, arrived, key_part, value_part, norm_part, go_g_own, go_g_oth
    )
    states = land(states, arrived)

    arrived = hop(states, 3, True)
    go_g_got = swap(go_g_oth, 1)
    for turn in range(2, levels):
        ff_sums = shrink(ff_sums, turn)
    ff_sums, states, arrived, go_g_own, go_g_got = hold(
        ff_sums, states, arrived, go_g_own, go_g_got
    )
    states = land(states, arrived)

    ff_far = shrink_far(ff_sums)
    go_sums = shrink(split_first(go_g_own, go_g_got), 0)
    for phase in range(4, phases + 1):
        arrived = hop(states, phase, True)
        states, arrived = sync(states, arrived)
        states = land(states, arrived)
    after_own, after_oth = end_states(states)
    go_sums, ff_far, after_own, after_oth = hold(go_sums, ff_far, after_own, after_oth)

    go_sums = shrink(go_sums, 1)
    grad_k, grad_v, kv_g_own, kv_g_oth = call(
        last_kernel,
        H,
        info,
        [
            rates_in, whole(normed_t), head_in(key), head_in(value), head_in(key_part),
            head_in(value_part), whole(cosine), whole(sine), whole(tall_count),
            own_in(after_own), other_in(after_oth),
        ],
        [
            head_out(per_head + (QK,), BF16), head_out(per_head + (VH,), BF16),
            whole_out(grad_shape + (1536,), BF16), whole_out(grad_shape + (1536,), BF16),
        ],
        [],
        8 * unit,
        "last",
    )
    go_sums, kv_g_own, kv_g_oth, grad_k, grad_v = hold(
        go_sums, kv_g_own, kv_g_oth, grad_k, grad_v
    )
    kv_g_got = swap(kv_g_oth, 1)
    for turn in range(2, levels):
        go_sums = shrink(go_sums, turn)
    go_sums, kv_g_own, kv_g_got = hold(go_sums, kv_g_own, kv_g_got)
    kv_sums = shrink(split_first(kv_g_own, kv_g_got), 0)
    go_far = shrink_far(go_sums)
    input_grad, grad_first_gain, grad_first_bias = call(
        input_kernel,
        H,
        info,
        [
            whole(x), whole(first_gain), whole(grad_hidden), whole(norm_part),
            head_in(grad_k), head_in(grad_v),
            columns(qkv_own, 256, 2, True), columns(qkv_oth, 256, 2, False),
            columns(qkv_own, 512, 2, True), columns(qkv_oth, 512, 2, False),
        ],
        [
            whole_out((tokens, width), F32), whole_out((1, width), F32),
            whole_out((1, width), F32),
        ],
        [pltpu.VMEM((tokens, width), F32)],
        6 * unit,
        "input",
    )
    kv_sums, go_far, input_grad, grad_first_gain, grad_first_bias = hold(
        kv_sums, go_far, input_grad, grad_first_gain, grad_first_bias
    )
    small = [grad_first_gain, grad_first_bias, grad_second_gain, grad_second_bias, grad_group_gain]
    small = jnp.concatenate([part.reshape(count, -1) for part in small], axis=1)
    small = jnp.pad(small, ((0, 0), (0, 1024 - edges[-1]))).reshape(count, 8, 128)
    kv_sums = shrink(kv_sums, 1)
    spread_small = lax.all_to_all(small, AXES, 0, 0, tiled=True)
    kv_sums, spread_small = hold(kv_sums, spread_small)
    for turn in range(2, levels):
        kv_sums = shrink(kv_sums, turn)
    summed = jnp.sum(spread_small, axis=0).reshape(-1)
    small = [summed[a:b] for a, b in zip(edges[:-1], edges[1:])]
    kv_far = shrink_far(kv_sums)

    def whole_sum(far):
        return far[0] + far[1].astype(F32)

    ff_grad, go_grad, kv_grad = whole_sum(ff_far), whole_sum(go_far), whole_sum(kv_far)
    ff_mine, ff_got = finish_wide(ff_grad[:, :1024])
    go_mine, go_got = finish_wide(jnp.concatenate([go_grad[:, :1024], go_grad[:, 2048:]], axis=1))
    kv_mine, kv_got = finish_wide(kv_grad)

    def wide(mine, got, start, stop):
        return ordered(mine[:, start:stop], got[:, start:stop], 1)

    return (
        output.reshape(inputs.shape),
        input_grad.reshape(inputs.shape),
        small[0],
        small[1],
        wide(go_mine, go_got, 1024, 1536),
        wide(kv_mine, kv_got, 0, 512),
        wide(kv_mine, kv_got, 512, 1536),
        wide(go_mine, go_got, 0, 1024),
        small[4],
        finish_tall(go_grad[:, 1024:2048]),
        small[2],
        small[3],
        wide(ff_mine, ff_got, 0, 1024),
        finish_tall(ff_grad[:, 1024:2048]),
    )


def solution(mesh):
    return jax.shard_map(
        per_device,
        mesh=mesh,
        in_specs=(
            P(None, "dp", "seq", None),
            P(None, "dp", "seq"),
            P(("dp", "seq")),
            P(("dp", "seq")),
            P(("dp", "seq"), None),
            P(("dp", "seq"), None),
            P(("dp", "seq"), None),
            P(("dp", "seq"), None),
            P(("dp", "seq")),
            P(("dp", "seq"), None),
            P(("dp", "seq")),
            P(("dp", "seq")),
            P(("dp", "seq"), None),
            P(("dp", "seq"), None),
            P(None, "dp", "seq", None),
        ),
        out_specs=(
            P(None, "dp", "seq", None),
            P(None, "dp", "seq", None),
            P(("dp", "seq")),
            P(("dp", "seq")),
            P(("dp", "seq"), None),
            P(("dp", "seq"), None),
            P(("dp", "seq"), None),
            P(("dp", "seq"), None),
            P(("dp", "seq")),
            P(("dp", "seq"), None),
            P(("dp", "seq")),
            P(("dp", "seq")),
            P(("dp", "seq"), None),
            P(("dp", "seq"), None),
        ),
        check_vma=False,
    )
```

time: 2160 us -> 583 us (0.27)
  waiting for transfers between devices: 1670 us -> 157 us
  matrix products: 169 us -> 0 us
  Pallas kernels: 0 us -> 156 us
  starting transfers between devices: 1.63 us -> 139 us
  blocking collectives: 102 us -> 0 us
  local copies, waits for them, and re-layouts: 101 us -> 39.8 us
    reduce_scatter x7 -> x0, waiting for transfers between devices: 919 us -> none  [the longest x1 153 us: per_device(): lax.psum_scatter(retention_terms[5], ('dp', 'seq'), scatter_dimension=0,...]
    all_gather x11 -> x0, waiting for transfers between devices: 747 us -> none  [the longest x4 480 us: prefix(): gathered = jax.tree.map(lambda a: lax.all_gather(a, axis), part)]
    dot_general x66 -> x0, matrix products: 169 us -> none  [the longest x14 45.2 us: weight_grad(): lax.dot_general(left, right, (((0,), (0,)), ((), ())), preferred_element_...]
    ppermute x0 -> x98, waiting for transfers between devices: none -> 157 us  [the longest x86 129 us: swap(): return lax.ppermute(values, AXES, [(i, i ^ bit) for i in range(devices())])]
    pallas_call x0 -> x13, Pallas kernels: none -> 156 us  [the longest x10 150 us: call(): pl.pallas_call(body, grid_spec=pltpu.PrefetchScalarGridSpec(num_scalar_pr...]
    ppermute x0 -> x98, starting transfers between devices: none -> 136 us  [the longest x86 107 us: swap(): return lax.ppermute(values, AXES, [(i, i ^ bit) for i in range(devices())])]
    unnamed x2 -> x0, blocking collectives: 82.5 us -> none
    unnamed x373 -> x147, local copies, waits for them, and re-layouts: 54.1 us -> 9.31 us
  transfers between devices with their start and end apart: 18 -> 99, of which waited for: 18 -> 38; matrix products, arithmetic and copies ran while one was open for 13% -> 16% of each run, Pallas kernels for 0% -> 18%
where the time goes in v2:
time: 583 us; the launch traced here: 573 us
  waiting for transfers between devices  157 us (27%)
  Pallas kernels  156 us (27%)
  starting transfers between devices  139 us (24%)
  other arithmetic  78 us (13%)
  local copies, waits for them, and re-layouts  39.8 us (7%)
    pallas_call x10, Pallas kernels, call(): pl.pallas_call(body, grid_spec=pltpu.PrefetchScalarGridSpec(num_scalar_pr...  150 us
    ppermute x86, waiting for transfers between devices, swap(): return lax.ppermute(values, AXES, [(i, i ^ bit) for i in range(devices())])  129 us
    ppermute x86, starting transfers between devices, swap(): return lax.ppermute(values, AXES, [(i, i ^ bit) for i in range(devices())])  107 us
    ppermute x12, starting transfers between devices, hop(): arrived.append(lax.ppermute(message, 'seq', pairs))  28.9 us
    ppermute x12, waiting for transfers between devices, hop(): arrived.append(lax.ppermute(message, 'seq', pairs))  27.5 us
    convert_element_type x24, other arithmetic, shrink(): send = total_of(pick(mine, 1), pick(theirs, 1)).astype(BF16)  21.8 us
  transfers between devices with their start and end apart: 99, of which 38 were waited for; matrix products, arithmetic and copies ran while one was open for 16% of the time, Pallas kernels for 18%

profile of v2, /device:TPU:1, one launch (start us, length us, event | category | flops | bytes accessed | tf_op | source)
XLA Modules:
  0.0 572.7 jit_solution(5618935987815292563)
XLA Ops:
  0.7 3.5 concatenate.159
  14.2 2.8 collective-permute-start.7
  19.9 2.8 collective-permute-start.8
  36.6 7.7 %collective-permute-done.1 = bf16[64,2048]{1,0:T(8,128)(2,1)S(1)} collective-permute-done((bf16[64,2048]{1,0:T(8,128)(2,1)S(1)}, bf16[64,2048]{1,0:T(8,128)(2,1)S(1)}, u32[]{:S(2)}, u32[]{:S(2)}) %collective-permute-start.1) | collective-permute-done | bytes 262176 | tf_op jit(solution)/shard_map/ppermute | solution.py:41
  47.6 3.9 collective-permute-done.14
  53.8 3.2 collective-permute-start.18
  58.1 5.7 collective-permute-done.18
  68.2 3.2 collective-permute-start.21
  72.8 13.0 %collective-permute-done.24 = bf16[2,64,512]{2,1,0:T(8,128)(2,1)} collective-permute-done((bf16[2,64,512]{2,1,0:T(8,128)(2,1)S(1)}, bf16[2,64,512]{2,1,0:T(8,128)(2,1)}, u32[]{:S(2)}, u32[]{:S(2)}) %collective-permute-start.24) | collective-permute-done | bytes 131104 | tf_op jit(solution)/shard_map/ppermute | solution.py:41
  85.8 2.7 collective-permute-start.23
  89.1 5.0 norm.1
  94.8 2.8 settle.3.q_own.k_own.v_own
  97.6 7.0 %collective-permute-start.26 = (bf16[16,64,2048]{2,1,0:T(8,128)(2,1)}, bf16[16,64,2048]{2,1,0:T(8,128)(2,1)}, u32[]{:S(2)}, u32[]{:S(2)}) collective-permute-start(bf16[16,64,2048]{2,1,0:T(8,128)(2,1)} %settle.3.q_own.k_own.v_own), channel_id=1, source_target_pairs={{0,1},{1,0},{2,3},{3,2},{4,5},{5,4},{6,7},{7,6},{8,9},{9,8},{10,11... | collective-permute-start | bytes 12582920 | tf_op jit(solution)/shard_map/ppermute | solution.py:41
  105.4 6.3 %collective-permute-done.26.q_oth.k_oth.v_oth = bf16[16,64,2048]{2,1,0:T(8,128)(2,1)} collective-permute-done((bf16[16,64,2048]{2,1,0:T(8,128)(2,1)}, bf16[16,64,2048]{2,1,0:T(8,128)(2,1)}, u32[]{:S(2)}, u32[]{:S(2)}) %collective-permute-start.26) | collective-permute-done | bytes 4194336 | tf_op jit(solution)/shard_map/ppermute | solution.py:41
  111.7 15.4 %project.1 = (bf16[4,512,256]{2,1,0:T(8,128)(2,1)}, bf16[4,512,256]{2,1,0:T(8,128)(2,1)}, bf16[4,512,512]{2,1,0:T(8,128)(2,1)}, bf16[4,512,256]{2,1,0:T(8,128)(2...) custom-call(s32[2]{0:T(128)} %pad_add_fusion.info.info_ref, f32[4]{0:T(128)} %copy-done.53, ...), custom_call_target="tpu_custom_call" | custom-call | flops 5368709120 | bytes 40112144 | tf_op jit(solution)/shard_map/project/pallas_call | solution.py:245
  127.1 3.1 copy.148
  138.1 6.0 %collective-permute-done.32 = bf16[2,64,512]{2,1,0:T(8,128)(2,1)} collective-permute-done((bf16[2,64,512]{2,1,0:T(8,128)(2,1)S(1)}, bf16[2,64,512]{2,1,0:T(8,128)(2,1)}, u32[]{:S(2)}, u32[]{:S(2)}) %collective-permute-start.32) | collective-permute-done | bytes 131104 | tf_op jit(solution)/shard_map/ppermute | solution.py:41
  145.3 2.9 collective-permute-done.30
  151.9 3.7 collective-permute-done.31
  167.5 9.3 %collective-permute-done.34 = bf16[2,256,512]{2,1,0:T(8,128)(2,1)S(1)} collective-permute-done((bf16[2,256,512]{2,1,0:T(8,128)(2,1)S(1)}, bf16[2,256,512]{2,1,0:T(8,128)(2,1)S(1)}, u32[]{:S(2)}, u32[]{:S(2)}) %collective-permute-start.34) | collective-permute-done | bytes 524320 | tf_op jit(solution)/shard_map/ppermute | solution.py:210
  188.0 3.3 collective-permute-start.39
  192.4 2.8 collective-permute-done.42
  195.2 5.5 collective-permute-done.41
  200.7 4.6 collective-permute-done.39
  214.0 7.3 %gate.1 = f32[4,512,512]{2,1,0:T(8,128)} custom-call(s32[2]{0:T(128)} %pad_add_fusion.info.info_ref, bf16[512,1024]{1,0:T(8,128)(2,1)} %get-tuple-element.307.normed, bf16[16,64,2048]{2,1,0:T(8,128)(2,1)} %copy-done, bf16[16,64,2048]{2,1,0:T(8,128)(2,1)} %copy-done.4), custom_call_target="tpu_custom_call" | custom-call | flops 2147483648 | bytes 13631488 | tf_op jit(solution)/shard_map/gate/pallas_call | solution.py:245
  221.4 4.0 collective-permute-done.47.refs_3_
  226.6 2.8 settle.5.up_own.down_own
  229.4 2.8 collective-permute-start.51
  243.9 16.7 %mix.1 = (f32[4,512,512]{2,1,0:T(8,128)}, bf16[4,512,512]{2,1,0:T(8,128)(2,1)}, f32[512,1024]{1,0:T(8,128)}, bf16[512,1024]{1,0:T(8,128)(2,1)}, bf16[1024,512]{1,0:T(8,128)(2,1)}) custom-call(s32[2]{0:T(128)} %pad_add_fusion.info.info_ref, f32[4]{0:T(128)} %copy-done.53, bf16[512,1024]{1,0:T(8,128)(2,1)} %bitcast.312, bf16[4,1,512]{2,1,0:T(2,128)(2,1)} %copy.153.gain, ...), custom_call_target="tpu_custom_call" | custom-call | flops 2684354560 | bytes 31467536 | tf_op jit(solution)/shard_map/mix/pallas_call | solution.py:245
  260.6 28.7 %feed.1 = (bf16[512,1024]{1,0:T(8,128)(2,1)}, f32[512,1024]{1,0:T(8,128)}, bf16[512,1024]{1,0:T(8,128)(2,1)}, f32[1,1024]{1,0:T(1,128)}, f32[1,1024]{1,0:T(1,128...) custom-call(s32[2]{0:T(128)} %pad_add_fusion.info.info_ref, f32[512,1024]{1,0:T(8,128)} %get-tuple-element.392.hidden, ...), custom_call_target="tpu_custom_call" | custom-call | flops 12884901888 | bytes 34613248 | tf_op jit(solution)/shard_map/feed/pallas_call | solution.py:245
  289.6 14.7 %unmix.1 = (bf16[4,512,512]{2,1,0:T(8,128)(2,1)}, bf16[4,512,512]{2,1,0:T(8,128)(2,1)}, f32[4,1,512]{2,1,0:T(1,128)}, f32[2,2,256,512]{3,2,1,0:T(8,128)}, f32[2,2,256,512]{3,2,1,0:T(8,128)}) custom-call(s32[2]{0:T(128)} %pad_add_fusion.info.info_ref, f32[4]{0:T(128)} %copy-done.53, bf16[512,1024]{1,0:T(8,128)(2,1)} %get-tuple-element.402.grad_low, ...), custom_call_target="tpu_custom_call" | custom-call | flops 2684354560 | bytes 27277328 | tf_op jit(solution)/shard_map/unmix/pallas_call | solution.py:245
  304.7 4.0 collective-permute-done.52
  315.9 12.8 %collective-permute-start.57 = (bf16[2,256,512]{2,1,0:T(8,128)(2,1)}, bf16[2,256,512]{2,1,0:T(8,128)(2,1)}, u32[]{:S(2)}, u32[]{:S(2)}) collective-permute-start(bf16[2,256,512]{2,1,0:T(8,128)(2,1)} %fusion.13), channel_id=1, source_target_pairs={{6,4},{7,5},{14,12},{15,13},{22,20},{23,21},{30,28},{31,29}} | collective-permute-start | bytes 1572872 | tf_op jit(solution)/shard_map/ppermute | solution.py:210
  334.9 16.1 %outer.1 = (f32[512,1024]{1,0:T(8,128)}, bf16[16,64,2048]{2,1,0:T(8,128)(2,1)}, bf16[16,64,2048]{2,1,0:T(8,128)(2,1)}) custom-call(s32[2]{0:T(128)} %pad_add_fusion.info.info_ref, bf16[512,1024]{1,0:T(8,128)(2,1)} %get-tuple-element.402.grad_low, bf16[1024,512]{1,0:T(8,128)(2,1)} %get-tuple-element.414.normed_t, ...), custom_call_target="tpu_custom_call" | custom-call | flops 6442450944 | bytes 25165824 | tf_op jit(solution)/shard_map/outer/pallas_call | solution.py:245
  365.4 17.0 %inside.1 = (f32[4,512,256]{2,1,0:T(8,128)}, f32[4,512,512]{2,1,0:T(8,128)}, f32[512,1024]{1,0:T(8,128)}, bf16[16,64,512]{2,1,0:T(8,128)(2,1)}, bf16[16,64,512]{2,1,0:T(8,128)(2,1)}) custom-call(s32[2]{0:T(128)} %pad_add_fusion.info.info_ref, f32[4]{0:T(128)} %copy-done.53, bf16[1024,512]{1,0:T(8,128)(2,1)} %get-tuple-element.414.normed_t, ...), custom_call_target="tpu_custom_call" | custom-call | flops 3758096384 | bytes 31723536 | tf_op jit(solution)/shard_map/inside/pallas_call | solution.py:245
  382.5 5.4 pad_maximum_fusion.1
  387.8 2.7 pad_maximum_fusion
  405.3 8.8 %collective-permute-done.63 = bf16[2,64,768]{2,1,0:T(8,128)(2,1)S(1)} collective-permute-done((bf16[2,64,768]{2,1,0:T(8,128)(2,1)S(1)}, bf16[2,64,768]{2,1,0:T(8,128)(2,1)S(1)}, u32[]{:S(2)}, u32[]{:S(2)}) %collective-permute-start.63) | collective-permute-done | bytes 196640 | tf_op jit(solution)/shard_map/ppermute | solution.py:41
  417.2 10.2 %collective-permute-start.72 = (bf16[64,2048]{1,0:T(8,128)(2,1)S(1)}, bf16[64,2048]{1,0:T(8,128)(2,1)S(1)}, u32[]{:S(2)}, u32[]{:S(2)}) collective-permute-start(bf16[64,2048]{1,0:T(8,128)(2,1)S(1)} %pad_maximum_fusion.10), channel_id=1, source_target_pairs={{0,4},{1,5},{2,6},{3,7},{4,0},{5,1},{6,2},{7,3},{8,12},{9,13},{10,... | collective-permute-start | bytes 786440 | tf_op jit(solution)/shard_map/ppermute | solution.py:41
  431.8 13.6 %collective-permute-done.73 = bf16[2,256,512]{2,1,0:T(8,128)(2,1)S(1)} collective-permute-done((bf16[2,256,512]{2,1,0:T(8,128)(2,1)S(1)}, bf16[2,256,512]{2,1,0:T(8,128)(2,1)S(1)}, u32[]{:S(2)}, u32[]{:S(2)}) %collective-permute-start.73) | collective-permute-done | bytes 524320 | tf_op jit(solution)/shard_map/ppermute | solution.py:210
  449.5 9.9 %collective-permute-done.71 = bf16[2,2,2,64,640]{4,3,2,0,1:T(8,128)(2,1)S(1)} collective-permute-done((bf16[2,2,2,64,640]{4,3,2,0,1:T(8,128)(2,1)S(1)}, bf16[2,2,2,64,640]{4,3,2,0,1:T(8,128)(2,1)S(1)}, u32[]{:S(2)}, u32[]{:S(2)}) %collective-permute-start.71) | collective-permute-done | bytes 655392 | tf_op jit(solution)/shard_map/ppermute | solution.py:41
  463.6 15.0 %last.1 = (bf16[4,512,256]{2,1,0:T(8,128)(2,1)}, bf16[4,512,512]{2,1,0:T(8,128)(2,1)}, bf16[16,64,1536]{2,1,0:T(8,128)(2,1)}, bf16[16,64,1536]{2,1,0:T(8,128)(2,1)}) custom-call(s32[2]{0:T(128)} %pad_add_fusion.info.info_ref, f32[4]{0:T(128)} %copy-done.53, bf16[1024,512]{1,0:T(8,128)(2,1)} %get-tuple-element.414.normed_t, ...), custom_call_target="tpu_custom_call" | custom-call | flops 4294967296 | bytes 22284304 | tf_op jit(solution)/shard_map/last/pallas_call | solution.py:245
  492.7 13.7 %input.1 = (f32[512,1024]{1,0:T(8,128)}, f32[1,1024]{1,0:T(1,128)}, f32[1,1024]{1,0:T(1,128)}) custom-call(s32[2]{0:T(128)} %pad_add_fusion.info.info_ref, bf16[512,1024]{1,0:T(8,128)(2,1)} %bitcast.313, bf16[1,1024]{1,0:T(2,128)(2,1)} %reshape.486.gain, f32[512,1024]{1,0:T(8,128)} %get-tuple-element.516.grad_hidden, ...), custom_call_target="tpu_custom_call" | custom-call | flops 3221225472 | bytes 27273216 | tf_op jit(solution)/shard_map/input/pallas_call | solution.py:245
  511.5 15.1 %collective-permute-done.85 = bf16[64,2560]{1,0:T(8,128)(2,1)S(1)} collective-permute-done((bf16[64,2560]{1,0:T(8,128)(2,1)S(1)}, bf16[64,2560]{1,0:T(8,128)(2,1)S(1)}, u32[]{:S(2)}, u32[]{:S(2)}) %collective-permute-start.85) | collective-permute-done | bytes 327712 | tf_op jit(solution)/shard_map/ppermute | solution.py:41
  532.0 3.4 all-to-all-start
  547.4 3.1 collective-permute-done.86
  560.1 5.5 collective-permute-done.93
  565.7 4.1 collective-permute-start.94
  (522 shorter events, 206.7 us)
Async XLA Ops:
  5.2 20.0 %collective-permute-start.4 = (bf16[32,1024]{1,0:T(8,128)(2,1)S(1)}, bf16[32,1024]{1,0:T(8,128)(2,1)S(1)}, u32[]{:S(2)}, u32[]{:S(2)}) collective-permute-start(bf16[32,1024]{1,0:T(8,128)(2,1)S(1)} %broadcast_select_fusion.30), channel_id=1, source_target_pairs={{0,1},{1,0},{2,3},{3,2},{4,5},{5,4},{6,7},{7,6},{8,9},{9,8},{10,11... | collective-permute-start | bytes 196616 | tf_op jit(solution)/shard_map/ppermute | solution.py:41
  6.6 20.2 %collective-permute-start.5 = (bf16[64,512]{1,0:T(8,128)(2,1)S(1)}, bf16[64,512]{1,0:T(8,128)(2,1)S(1)}, u32[]{:S(2)}, u32[]{:S(2)}) collective-permute-start(bf16[64,512]{1,0:T(8,128)(2,1)S(1)} %broadcast_select_fusion.20), channel_id=1, source_target_pairs={{0,1},{1,0},{2,3},{3,2},{4,5},{5,4},{6,7},{7,6},{8,9},{9,8},{10,11... | collective-permute-start | bytes 196616 | tf_op jit(solution)/shard_map/ppermute | solution.py:41
  7.6 19.3 %collective-permute-start.2 = (bf16[32,1024]{1,0:T(8,128)(2,1)S(1)}, bf16[32,1024]{1,0:T(8,128)(2,1)S(1)}, u32[]{:S(2)}, u32[]{:S(2)}) collective-permute-start(bf16[32,1024]{1,0:T(8,128)(2,1)S(1)} %broadcast_select_fusion.34), channel_id=1, source_target_pairs={{0,1},{1,0},{2,3},{3,2},{4,5},{5,4},{6,7},{7,6},{8,9},{9,8},{10,11... | collective-permute-start | bytes 196616 | tf_op jit(solution)/shard_map/ppermute | solution.py:41
  9.0 17.9 %collective-permute-start.3 = (bf16[64,512]{1,0:T(8,128)(2,1)S(1)}, bf16[64,512]{1,0:T(8,128)(2,1)S(1)}, u32[]{:S(2)}, u32[]{:S(2)}) collective-permute-start(bf16[64,512]{1,0:T(8,128)(2,1)S(1)} %broadcast_select_fusion.24), channel_id=1, source_target_pairs={{0,1},{1,0},{2,3},{3,2},{4,5},{5,4},{6,7},{7,6},{8,9},{9,8},{10,11... | collective-permute-start | bytes 196616 | tf_op jit(solution)/shard_map/ppermute | solution.py:41
  66.5 27.6 %collective-permute-start.20 = (bf16[8,64,768]{2,1,0:T(8,128)(2,1)S(1)}, bf16[8,64,768]{2,1,0:T(8,128)(2,1)S(1)}, u32[]{:S(2)}, u32[]{:S(2)}) collective-permute-start(bf16[8,64,768]{2,1,0:T(8,128)(2,1)S(1)} %constant_dynamic-update-slice_fusion.8.refs_2_), channel_id=1, source_target_pairs={{0,16},{1,17},{2,18},{3,19},{4,20},{5,21},{6,22},{7,23},{8,24},{9,... | collective-permute-start | bytes 2359304 | tf_op jit(solution)/shard_map/ppermute | solution.py:41
  66.8 27.2 %collective-permute-start.19 = (bf16[8,64,768]{2,1,0:T(8,128)(2,1)S(1)}, bf16[8,64,768]{2,1,0:T(8,128)(2,1)S(1)}, u32[]{:S(2)}, u32[]{:S(2)}) collective-permute-start(bf16[8,64,768]{2,1,0:T(8,128)(2,1)S(1)} %constant_dynamic-update-slice_fusion.6.refs_0_), channel_id=1, source_target_pairs={{0,8},{1,9},{2,10},{3,11},{4,12},{5,13},{6,14},{7,15},{8,0},{9,1},... | collective-permute-start | bytes 2359304 | tf_op jit(solution)/shard_map/ppermute | solution.py:41
  68.2 25.9 %collective-permute-start.21 = (bf16[8,64,512]{2,1,0:T(8,128)(2,1)S(1)}, bf16[8,64,512]{2,1,0:T(8,128)(2,1)S(1)}, u32[]{:S(2)}, u32[]{:S(2)}) collective-permute-start(bf16[8,64,512]{2,1,0:T(8,128)(2,1)S(1)} %constant_dynamic-update-slice_fusion.10.refs_4_), channel_id=1, source_target_pairs={{0,2},{1,3},{2,0},{3,1},{4,6},{5,7},{6,4},{7,5},{8,10},{9,11},{10,... | collective-permute-start | bytes 1572872 | tf_op jit(solution)/shard_map/ppermute | solution.py:41
  130.1 25.4 %collective-permute-start.33 = (f32[2,2,256,512]{3,2,0,1:T(8,128)}, f32[2,2,256,512]{3,2,0,1:T(8,128)S(1)}, u32[]{:S(2)}, u32[]{:S(2)}) collective-permute-start(f32[2,2,256,512]{3,2,0,1:T(8,128)} %copy.148), channel_id=1, source_target_pairs={{0,1},{1,0},{2,3},{3,2},{4,5},{5,4},{6,7},{7,6},{8,9},{9,8},{10,11... | collective-permute-start | bytes 6291464 | tf_op jit(solution)/shard_map/ppermute | solution.py:41
  130.5 25.0 %collective-permute-start.27 = (bf16[4,64,768]{2,1,0:T(8,128)(2,1)S(1)}, bf16[4,64,768]{2,1,0:T(8,128)(2,1)}, u32[]{:S(2)}, u32[]{:S(2)}) collective-permute-start(bf16[4,64,768]{2,1,0:T(8,128)(2,1)S(1)} %constant_dynamic-update-slice_fusion.12), channel_id=1, source_target_pairs={{0,16},{1,17},{2,18},{3,19},{4,20},{5,21},{6,22},{7,23},{8,24},{9,... | collective-permute-start | bytes 1179656 | tf_op jit(solution)/shard_map/ppermute | solution.py:41
  133.7 21.9 %collective-permute-start.28 = (bf16[4,64,768]{2,1,0:T(8,128)(2,1)S(1)}, bf16[4,64,768]{2,1,0:T(8,128)(2,1)}, u32[]{:S(2)}, u32[]{:S(2)}) collective-permute-start(bf16[4,64,768]{2,1,0:T(8,128)(2,1)S(1)} %constant_dynamic-update-slice_fusion.14), channel_id=1, source_target_pairs={{0,2},{1,3},{2,0},{3,1},{4,6},{5,7},{6,4},{7,5},{8,10},{9,11},{10,... | collective-permute-start | bytes 1179656 | tf_op jit(solution)/shard_map/ppermute | solution.py:41
  156.9 20.0 %collective-permute-start.36 = (bf16[8,64,768]{2,1,0:T(8,128)(2,1)S(1)}, bf16[8,64,768]{2,1,0:T(8,128)(2,1)S(1)}, u32[]{:S(2)}, u32[]{:S(2)}) collective-permute-start(bf16[8,64,768]{2,1,0:T(8,128)(2,1)S(1)} %constant_dynamic-update-slice_fusion.20.refs_2_), channel_id=1, source_target_pairs={{0,16},{1,17},{2,18},{3,19},{4,20},{5,21},{6,22},{7,23},{8,24},{9,... | collective-permute-start | bytes 2359304 | tf_op jit(solution)/shard_map/ppermute | solution.py:41
  159.0 17.9 %collective-permute-start.35 = (bf16[8,64,768]{2,1,0:T(8,128)(2,1)S(1)}, bf16[8,64,768]{2,1,0:T(8,128)(2,1)S(1)}, u32[]{:S(2)}, u32[]{:S(2)}) collective-permute-start(bf16[8,64,768]{2,1,0:T(8,128)(2,1)S(1)} %constant_dynamic-update-slice_fusion.18.refs_0_), channel_id=1, source_target_pairs={{0,8},{1,9},{2,10},{3,11},{4,12},{5,13},{6,14},{7,15},{8,0},{9,1},... | collective-permute-start | bytes 2359304 | tf_op jit(solution)/shard_map/ppermute | solution.py:41
  177.7 27.6 %collective-permute-start.40 = (bf16[16,64,2048]{2,1,0:T(8,128)(2,1)S(1)}, bf16[16,64,2048]{2,1,0:T(8,128)(2,1)S(1)}, u32[]{:S(2)}, u32[]{:S(2)}) collective-permute-start(bf16[16,64,2048]{2,1,0:T(8,128)(2,1)S(1)} %settle.4.own.wo_own.g_own), channel_id=1, source_target_pairs={{0,1},{1,0},{2,3},{3,2},{4,5},{5,4},{6,7},{7,6},{8,9},{9,8},{10,11... | collective-permute-start | bytes 12582920 | tf_op jit(solution)/shard_map/ppermute | solution.py:41
  188.0 17.4 %collective-permute-start.39 = (bf16[2,256,512]{2,1,0:T(8,128)(2,1)S(1)}, bf16[2,256,512]{2,1,0:T(8,128)(2,1)S(1)}, u32[]{:S(2)}, u32[]{:S(2)}) collective-permute-start(bf16[2,256,512]{2,1,0:T(8,128)(2,1)S(1)} %get-tuple-element.665), channel_id=1, source_target_pairs={{0,2},{1,3},{8,10},{9,11},{16,18},{17,19},{24,26},{25,27}} | collective-permute-start | bytes 1572872 | tf_op jit(solution)/shard_map/ppermute | solution.py:210
  205.4 15.9 %collective-permute-start.48 = (bf16[8,64,512]{2,1,0:T(8,128)(2,1)S(1)}, bf16[8,64,512]{2,1,0:T(8,128)(2,1)S(1)}, u32[]{:S(2)}, u32[]{:S(2)}) collective-permute-start(bf16[8,64,512]{2,1,0:T(8,128)(2,1)S(1)} %constant_dynamic-update-slice_fusion.34.refs_4_), channel_id=1, source_target_pairs={{0,2},{1,3},{2,0},{3,1},{4,6},{5,7},{6,4},{7,5},{8,10},{9,11},{10,... | collective-permute-start | bytes 1572872 | tf_op jit(solution)/shard_map/ppermute | solution.py:41
  207.7 17.6 %collective-permute-start.47 = (bf16[8,64,768]{2,1,0:T(8,128)(2,1)S(1)}, bf16[8,64,768]{2,1,0:T(8,128)(2,1)S(1)}, u32[]{:S(2)}, u32[]{:S(2)}) collective-permute-start(bf16[8,64,768]{2,1,0:T(8,128)(2,1)S(1)} %constant_dynamic-update-slice_fusion.32.refs_2_), channel_id=1, source_target_pairs={{0,16},{1,17},{2,18},{3,19},{4,20},{5,21},{6,22},{7,23},{8,24},{9,... | collective-permute-start | bytes 2359304 | tf_op jit(solution)/shard_map/ppermute | solution.py:41
  209.4 17.2 %collective-permute-start.46 = (bf16[8,64,768]{2,1,0:T(8,128)(2,1)S(1)}, bf16[8,64,768]{2,1,0:T(8,128)(2,1)S(1)}, u32[]{:S(2)}, u32[]{:S(2)}) collective-permute-start(bf16[8,64,768]{2,1,0:T(8,128)(2,1)S(1)} %constant_dynamic-update-slice_fusion.30.refs_0_), channel_id=1, source_target_pairs={{0,8},{1,9},{2,10},{3,11},{4,12},{5,13},{6,14},{7,15},{8,0},{9,1},... | collective-permute-start | bytes 2359304 | tf_op jit(solution)/shard_map/ppermute | solution.py:41
  229.4 31.2 %collective-permute-start.51 = (bf16[16,64,2048]{2,1,0:T(8,128)(2,1)}, bf16[16,64,2048]{2,1,0:T(8,128)(2,1)}, u32[]{:S(2)}, u32[]{:S(2)}) collective-permute-start(bf16[16,64,2048]{2,1,0:T(8,128)(2,1)} %settle.5.up_own.down_own), channel_id=1, source_target_pairs={{0,1},{1,0},{2,3},{3,2},{4,5},{5,4},{6,7},{7,6},{8,9},{9,8},{10,11... | collective-permute-start | bytes 12582920 | tf_op jit(solution)/shard_map/ppermute | solution.py:41
  289.3 19.4 %collective-permute-start.53 = (bf16[16,64,2048]{2,1,0:T(8,128)(2,1)}, bf16[16,64,2048]{2,1,0:T(8,128)(2,1)}, u32[]{:S(2)}, u32[]{:S(2)}) collective-permute-start(bf16[16,64,2048]{2,1,0:T(8,128)(2,1)} %get-tuple-element.407), channel_id=1, source_target_pairs={{0,1},{1,0},{2,3},{3,2},{4,5},{5,4},{6,7},{7,6},{8,9},{9,8},{10,11... | collective-permute-start | bytes 12582920 | tf_op jit(solution)/shard_map/ppermute | solution.py:41
  315.9 35.1 %collective-permute-start.57 = (bf16[2,256,512]{2,1,0:T(8,128)(2,1)}, bf16[2,256,512]{2,1,0:T(8,128)(2,1)}, u32[]{:S(2)}, u32[]{:S(2)}) collective-permute-start(bf16[2,256,512]{2,1,0:T(8,128)(2,1)} %fusion.13), channel_id=1, source_target_pairs={{6,4},{7,5},{14,12},{15,13},{22,20},{23,21},{30,28},{31,29}} | collective-permute-start | bytes 1572872 | tf_op jit(solution)/shard_map/ppermute | solution.py:210
  329.6 21.3 %collective-permute-start.56 = (bf16[2,2,2,64,512]{4,3,2,0,1:T(8,128)(2,1)}, bf16[2,2,2,64,512]{4,3,2,0,1:T(8,128)(2,1)S(1)}, u32[]{:S(2)}, u32[]{:S(2)}) collective-permute-start(bf16[2,2,2,64,512]{4,3,2,0,1:T(8,128)(2,1)} %fusion.33), channel_id=1, source_target_pairs={{0,2},{1,3},{2,0},{3,1},{4,6},{5,7},{6,4},{7,5},{8,10},{9,11},{10,... | collective-permute-start | bytes 1572872 | tf_op jit(solution)/shard_map/ppermute | solution.py:41
  330.7 20.2 %collective-permute-start.55 = (bf16[2,2,2,64,768]{4,3,1,0,2:T(8,128)(2,1)}, bf16[2,2,2,64,768]{4,3,1,0,2:T(8,128)(2,1)}, u32[]{:S(2)}, u32[]{:S(2)}) collective-permute-start(bf16[2,2,2,64,768]{4,3,1,0,2:T(8,128)(2,1)} %fusion.27), channel_id=1, source_target_pairs={{0,16},{1,17},{2,18},{3,19},{4,20},{5,21},{6,22},{7,23},{8,24},{9,... | collective-permute-start | bytes 2359304 | tf_op jit(solution)/shard_map/ppermute | solution.py:41
  333.3 18.5 %collective-permute-start.54 = (bf16[2,2,2,64,768]{4,3,1,2,0:T(8,128)(2,1)}, bf16[2,2,2,64,768]{4,3,1,2,0:T(8,128)(2,1)}, u32[]{:S(2)}, u32[]{:S(2)}) collective-permute-start(bf16[2,2,2,64,768]{4,3,1,2,0:T(8,128)(2,1)} %fusion.25), channel_id=1, source_target_pairs={{0,8},{1,9},{2,10},{3,11},{4,12},{5,13},{6,14},{7,15},{8,0},{9,1},... | collective-permute-start | bytes 2359304 | tf_op jit(solution)/shard_map/ppermute | solution.py:41
  354.7 35.9 %collective-permute-start.61 = (bf16[2,256,512]{2,1,0:T(8,128)(2,1)}, bf16[2,256,512]{2,1,0:T(8,128)(2,1)}, u32[]{:S(2)}, u32[]{:S(2)}) collective-permute-start(bf16[2,256,512]{2,1,0:T(8,128)(2,1)} %get-tuple-element.602), channel_id=1, source_target_pairs={{4,2},{5,3},{12,10},{13,11},{20,18},{21,19},{28,26},{29,27}} | collective-permute-start | bytes 1572872 | tf_op jit(solution)/shard_map/ppermute | solution.py:210
  356.3 34.3 %collective-permute-start.62 = (bf16[2,256,512]{2,1,0:T(8,128)(2,1)}, bf16[2,256,512]{2,1,0:T(8,128)(2,1)}, u32[]{:S(2)}, u32[]{:S(2)}) collective-permute-start(bf16[2,256,512]{2,1,0:T(8,128)(2,1)} %get-tuple-element.662), channel_id=1, source_target_pairs={{6,4},{7,5},{14,12},{15,13},{22,20},{23,21},{30,28},{31,29}} | collective-permute-start | bytes 1572872 | tf_op jit(solution)/shard_map/ppermute | solution.py:210
  359.6 30.9 %collective-permute-start.60 = (bf16[2,2,64,512]{3,2,1,0:T(8,128)(2,1)}, bf16[2,2,64,512]{3,2,1,0:T(8,128)(2,1)}, u32[]{:S(2)}, u32[]{:S(2)}) collective-permute-start(bf16[2,2,64,512]{3,2,1,0:T(8,128)(2,1)} %get-tuple-element.680), channel_id=1, source_target_pairs={{0,8},{1,9},{2,10},{3,11},{4,12},{5,13},{6,14},{7,15},{8,0},{9,1},... | collective-permute-start | bytes 786440 | tf_op jit(solution)/shard_map/ppermute | solution.py:41
  362.2 28.3 %collective-permute-start.59 = (bf16[2,2,64,768]{3,2,1,0:T(8,128)(2,1)}, bf16[2,2,64,768]{3,2,1,0:T(8,128)(2,1)}, u32[]{:S(2)}, u32[]{:S(2)}) collective-permute-start(bf16[2,2,64,768]{3,2,1,0:T(8,128)(2,1)} %get-tuple-element.668), channel_id=1, source_target_pairs={{0,2},{1,3},{2,0},{3,1},{4,6},{5,7},{6,4},{7,5},{8,10},{9,11},{10,... | collective-permute-start | bytes 1179656 | tf_op jit(solution)/shard_map/ppermute | solution.py:41
  364.2 26.3 %collective-permute-start.58 = (bf16[2,2,64,768]{3,2,0,1:T(8,128)(2,1)}, bf16[2,2,64,768]{3,2,0,1:T(8,128)(2,1)S(1)}, u32[]{:S(2)}, u32[]{:S(2)}) collective-permute-start(bf16[2,2,64,768]{3,2,0,1:T(8,128)(2,1)} %get-tuple-element.670), channel_id=1, source_target_pairs={{0,16},{1,17},{2,18},{3,19},{4,20},{5,21},{6,22},{7,23},{8,24},{9,... | collective-permute-start | bytes 1179656 | tf_op jit(solution)/shard_map/ppermute | solution.py:41
  390.5 23.5 %collective-permute-start.68 = (bf16[16,64,2560]{2,1,0:T(8,128)(2,1)}, bf16[16,64,2560]{2,1,0:T(8,128)(2,1)S(1)}, u32[]{:S(2)}, u32[]{:S(2)}) collective-permute-start(bf16[16,64,2560]{2,1,0:T(8,128)(2,1)} %pad_maximum_fusion.1), channel_id=1, source_target_pairs={{0,1},{1,0},{2,3},{3,2},{4,5},{5,4},{6,7},{7,6},{8,9},{9,8},{10,11... | collective-permute-start | bytes 15728648 | tf_op jit(solution)/shard_map/ppermute | solution.py:41
  394.8 19.3 %collective-permute-start.66 = (bf16[2,256,512]{2,1,0:T(8,128)(2,1)S(1)}, bf16[2,256,512]{2,1,0:T(8,128)(2,1)S(1)}, u32[]{:S(2)}, u32[]{:S(2)}) collective-permute-start(bf16[2,256,512]{2,1,0:T(8,128)(2,1)S(1)} %get-tuple-element.660), channel_id=1, source_target_pairs={{2,0},{3,1},{10,8},{11,9},{18,16},{19,17},{26,24},{27,25}} | collective-permute-start | bytes 1572872 | tf_op jit(solution)/shard_map/ppermute | solution.py:210
  396.3 17.8 %collective-permute-start.67 = (bf16[2,256,512]{2,1,0:T(8,128)(2,1)S(1)}, bf16[2,256,512]{2,1,0:T(8,128)(2,1)S(1)}, u32[]{:S(2)}, u32[]{:S(2)}) collective-permute-start(bf16[2,256,512]{2,1,0:T(8,128)(2,1)S(1)} %get-tuple-element.598), channel_id=1, source_target_pairs={{4,2},{5,3},{12,10},{13,11},{20,18},{21,19},{28,26},{29,27}} | collective-permute-start | bytes 1572872 | tf_op jit(solution)/shard_map/ppermute | solution.py:210
  415.7 29.6 %collective-permute-start.73 = (bf16[2,256,512]{2,1,0:T(8,128)(2,1)S(1)}, bf16[2,256,512]{2,1,0:T(8,128)(2,1)S(1)}, u32[]{:S(2)}, u32[]{:S(2)}) collective-permute-start(bf16[2,256,512]{2,1,0:T(8,128)(2,1)S(1)} %get-tuple-element.596), channel_id=1, source_target_pairs={{2,0},{3,1},{10,8},{11,9},{18,16},{19,17},{26,24},{27,25}} | collective-permute-start | bytes 1572872 | tf_op jit(solution)/shard_map/ppermute | solution.py:210
  417.2 32.3 %collective-permute-start.72 = (bf16[64,2048]{1,0:T(8,128)(2,1)S(1)}, bf16[64,2048]{1,0:T(8,128)(2,1)S(1)}, u32[]{:S(2)}, u32[]{:S(2)}) collective-permute-start(bf16[64,2048]{1,0:T(8,128)(2,1)S(1)} %pad_maximum_fusion.10), channel_id=1, source_target_pairs={{0,4},{1,5},{2,6},{3,7},{4,0},{5,1},{6,2},{7,3},{8,12},{9,13},{10,... | collective-permute-start | bytes 786440 | tf_op jit(solution)/shard_map/ppermute | solution.py:41
  427.5 31.9 %collective-permute-start.71 = (bf16[2,2,2,64,640]{4,3,2,0,1:T(8,128)(2,1)S(1)}, bf16[2,2,2,64,640]{4,3,2,0,1:T(8,128)(2,1)S(1)}, u32[]{:S(2)}, u32[]{:S(2)}) collective-permute-start(bf16[2,2,2,64,640]{4,3,2,0,1:T(8,128)(2,1)S(1)} %fusion.29), channel_id=1, source_target_pairs={{0,2},{1,3},{2,0},{3,1},{4,6},{5,7},{6,4},{7,5},{8,10},{9,11},{10,... | collective-permute-start | bytes 1966088 | tf_op jit(solution)/shard_map/ppermute | solution.py:41
  429.5 29.9 %collective-permute-start.70 = (bf16[2,2,2,64,896]{4,3,1,0,2:T(8,128)(2,1)S(1)}, bf16[2,2,2,64,896]{4,3,1,0,2:T(8,128)(2,1)S(1)}, u32[]{:S(2)}, u32[]{:S(2)}) collective-permute-start(bf16[2,2,2,64,896]{4,3,1,0,2:T(8,128)(2,1)S(1)} %fusion.23), channel_id=1, source_target_pairs={{0,16},{1,17},{2,18},{3,19},{4,20},{5,21},{6,22},{7,23},{8,24},{9,... | collective-permute-start | bytes 2752520 | tf_op jit(solution)/shard_map/ppermute | solution.py:41
  431.5 27.9 %collective-permute-start.69 = (bf16[2,2,2,64,1024]{4,3,1,2,0:T(8,128)(2,1)S(1)}, bf16[2,2,2,64,1024]{4,3,1,2,0:T(8,128)(2,1)S(1)}, u32[]{:S(2)}, u32[]{:S(2)}) collective-permute-start(bf16[2,2,2,64,1024]{4,3,1,2,0:T(8,128)(2,1)S(1)} %fusion.3), channel_id=1, source_target_pairs={{0,8},{1,9},{2,10},{3,11},{4,12},{5,13},{6,14},{7,15},{8,0},{9,1},... | collective-permute-start | bytes 3145736 | tf_op jit(solution)/shard_map/ppermute | solution.py:41
  460.5 18.1 %collective-permute-start.76 = (bf16[2,2,64,896]{3,2,1,0:T(8,128)(2,1)S(1)}, bf16[2,2,64,896]{3,2,1,0:T(8,128)(2,1)S(1)}, u32[]{:S(2)}, u32[]{:S(2)}) collective-permute-start(bf16[2,2,64,896]{3,2,1,0:T(8,128)(2,1)S(1)} %get-tuple-element.666), channel_id=1, source_target_pairs={{0,2},{1,3},{2,0},{3,1},{4,6},{5,7},{6,4},{7,5},{8,10},{9,11},{10,... | collective-permute-start | bytes 1376264 | tf_op jit(solution)/shard_map/ppermute | solution.py:41
  461.8 16.9 %collective-permute-start.75 = (bf16[2,2,64,1024]{3,2,0,1:T(8,128)(2,1)S(1)}, bf16[2,2,64,1024]{3,2,0,1:T(8,128)(2,1)S(1)}, u32[]{:S(2)}, u32[]{:S(2)}) collective-permute-start(bf16[2,2,64,1024]{3,2,0,1:T(8,128)(2,1)S(1)} %get-tuple-element.658), channel_id=1, source_target_pairs={{0,16},{1,17},{2,18},{3,19},{4,20},{5,21},{6,22},{7,23},{8,24},{9,... | collective-permute-start | bytes 1572872 | tf_op jit(solution)/shard_map/ppermute | solution.py:41
  463.5 15.1 %collective-permute-start.77 = (bf16[2,2,64,640]{3,2,1,0:T(8,128)(2,1)S(1)}, bf16[2,2,64,640]{3,2,1,0:T(8,128)(2,1)S(1)}, u32[]{:S(2)}, u32[]{:S(2)}) collective-permute-start(bf16[2,2,64,640]{3,2,1,0:T(8,128)(2,1)S(1)} %get-tuple-element.674), channel_id=1, source_target_pairs={{0,8},{1,9},{2,10},{3,11},{4,12},{5,13},{6,14},{7,15},{8,0},{9,1},... | collective-permute-start | bytes 983048 | tf_op jit(solution)/shard_map/ppermute | solution.py:41
  479.7 26.8 %collective-permute-start.81 = (bf16[16,64,1536]{2,1,0:T(8,128)(2,1)}, bf16[16,64,1536]{2,1,0:T(8,128)(2,1)S(1)}, u32[]{:S(2)}, u32[]{:S(2)}) collective-permute-start(bf16[16,64,1536]{2,1,0:T(8,128)(2,1)} %get-tuple-element.507), channel_id=1, source_target_pairs={{0,1},{1,0},{2,3},{3,2},{4,5},{5,4},{6,7},{7,6},{8,9},{9,8},{10,11... | collective-permute-start | bytes 9437192 | tf_op jit(solution)/shard_map/ppermute | solution.py:41
  488.5 17.9 %collective-permute-start.80 = (bf16[2,64,640]{2,1,0:T(8,128)(2,1)S(1)}, bf16[2,64,640]{2,1,0:T(8,128)(2,1)S(1)}, u32[]{:S(2)}, u32[]{:S(2)}) collective-permute-start(bf16[2,64,640]{2,1,0:T(8,128)(2,1)S(1)} %get-tuple-element.699), channel_id=1, source_target_pairs={{0,16},{1,17},{2,18},{3,19},{4,20},{5,21},{6,22},{7,23},{8,24},{9,... | collective-permute-start | bytes 491528 | tf_op jit(solution)/shard_map/ppermute | solution.py:41
  489.7 16.7 %collective-permute-start.79 = (bf16[2,64,896]{2,1,0:T(8,128)(2,1)S(1)}, bf16[2,64,896]{2,1,0:T(8,128)(2,1)S(1)}, u32[]{:S(2)}, u32[]{:S(2)}) collective-permute-start(bf16[2,64,896]{2,1,0:T(8,128)(2,1)S(1)} %get-tuple-element.682), channel_id=1, source_target_pairs={{0,8},{1,9},{2,10},{3,11},{4,12},{5,13},{6,14},{7,15},{8,0},{9,1},... | collective-permute-start | bytes 688136 | tf_op jit(solution)/shard_map/ppermute | solution.py:41
  490.9 15.5 %collective-permute-start.78 = (bf16[2,64,1024]{2,1,0:T(8,128)(2,1)S(1)}, bf16[2,64,1024]{2,1,0:T(8,128)(2,1)S(1)}, u32[]{:S(2)}, u32[]{:S(2)}) collective-permute-start(bf16[2,64,1024]{2,1,0:T(8,128)(2,1)S(1)} %get-tuple-element.678), channel_id=1, source_target_pairs={{0,2},{1,3},{2,0},{3,1},{4,6},{5,7},{6,4},{7,5},{8,10},{9,11},{10,... | collective-permute-start | bytes 786440 | tf_op jit(solution)/shard_map/ppermute | solution.py:41
  509.2 17.4 %collective-permute-start.85 = (bf16[64,2560]{1,0:T(8,128)(2,1)S(1)}, bf16[64,2560]{1,0:T(8,128)(2,1)S(1)}, u32[]{:S(2)}, u32[]{:S(2)}) collective-permute-start(bf16[64,2560]{1,0:T(8,128)(2,1)S(1)} %pad_maximum_fusion.6), channel_id=1, source_target_pairs={{0,4},{1,5},{2,6},{3,7},{4,0},{5,1},{6,2},{7,3},{8,12},{9,13},{10,... | collective-permute-start | bytes 983048 | tf_op jit(solution)/shard_map/ppermute | solution.py:41
  509.3 17.2 %collective-permute-start.84 = (bf16[2,2,2,64,384]{4,3,2,0,1:T(8,128)(2,1)S(1)}, bf16[2,2,2,64,384]{4,3,2,0,1:T(8,128)(2,1)S(1)}, u32[]{:S(2)}, u32[]{:S(2)}) collective-permute-start(bf16[2,2,2,64,384]{4,3,2,0,1:T(8,128)(2,1)S(1)} %fusion.45), channel_id=1, source_target_pairs={{0,2},{1,3},{2,0},{3,1},{4,6},{5,7},{6,4},{7,5},{8,10},{9,11},{10,... | collective-permute-start | bytes 1179656 | tf_op jit(solution)/shard_map/ppermute | solution.py:41
  509.6 17.0 %collective-permute-start.83 = (bf16[2,2,2,64,512]{4,3,1,0,2:T(8,128)(2,1)S(1)}, bf16[2,2,2,64,512]{4,3,1,0,2:T(8,128)(2,1)S(1)}, u32[]{:S(2)}, u32[]{:S(2)}) collective-permute-start(bf16[2,2,2,64,512]{4,3,1,0,2:T(8,128)(2,1)S(1)} %fusion.37), channel_id=1, source_target_pairs={{0,16},{1,17},{2,18},{3,19},{4,20},{5,21},{6,22},{7,23},{8,24},{9,... | collective-permute-start | bytes 1572872 | tf_op jit(solution)/shard_map/ppermute | solution.py:41
  511.1 15.5 %collective-permute-start.82 = (bf16[2,2,2,64,640]{4,3,2,1,0:T(8,128)(2,1)S(1)}, bf16[2,2,2,64,640]{4,3,2,1,0:T(8,128)(2,1)S(1)}, u32[]{:S(2)}, u32[]{:S(2)}) collective-permute-start(bf16[2,2,2,64,640]{4,3,2,1,0:T(8,128)(2,1)S(1)} %get-tuple-element.616), channel_id=1, source_target_pairs={{0,8},{1,9},{2,10},{3,11},{4,12},{5,13},{6,14},{7,15},{8,0},{9,1},... | collective-permute-start | bytes 1966088 | tf_op jit(solution)/shard_map/ppermute | solution.py:41
  528.2 14.9 %collective-permute-start.95 = (f32[64,512]{1,0:T(8,128)}, f32[64,512]{1,0:T(8,128)}, u32[]{:S(2)}, u32[]{:S(2)}) collective-permute-start(f32[64,512]{1,0:T(8,128)} %slice_select_fusion.7), channel_id=1, source_target_pairs={{0,1},{1,0},{2,3},{3,2},{4,5},{5,4},{6,7},{7,6},{8,9},{9,8},{10,11... | collective-permute-start | bytes 393224 | tf_op jit(solution)/shard_map/ppermute | solution.py:41
  (114 other events, 923.0 us)

commit v3 on v2

--- a/solution.py
+++ b/solution.py
@@ -1,5 +1,3 @@
-import functools
-
 import jax
 import jax.numpy as jnp
 from jax import lax
@@ -14,7 +12,7 @@
 F32 = jnp.float32
 BF16 = jnp.bfloat16
 FAR = 4
-VMEM = 56 * 1024 * 1024
+MIB = 1024 * 1024
 
 
 def mm(left, right):
@@ -45,25 +43,163 @@
     return lax.axis_index("seq") % 2 == 1
 
 
+def sync(*values):
+    return lax.optimization_barrier(values)
+
+
 def orders():
     bits = [1 << k for k in range(1, devices().bit_length() - 1)]
-    near = [bit for bit in bits if bit not in (2, FAR)] + [2]
-    return [near[turn:] + near[:turn] for turn in range(3)]
-
-
-def cut(width):
-    tiles = width // 128
-    third = tiles // 4
-    first = (tiles - third + 1) // 2
-    edges = [0, first * 128, (tiles - third) * 128, width]
-    return list(zip(edges[:-1], edges[1:]))
-
-
-def halves(values):
-    half = values.shape[-1] // 2
-    upper = upper_core()
-    low, high = values[..., :half], values[..., half:]
-    return jnp.where(upper, high, low), jnp.where(upper, low, high)
+    near = [bit for bit in bits if bit not in (2, FAR)]
+    return (near[:1] + [2] + near[1:] + [FAR], near[1:] + near[:1] + [2, FAR])
+
+
+def step(values, turn):
+    pairs = [(i, i ^ orders()[i % 2][turn]) for i in range(devices())]
+    return lax.ppermute(values, AXES, pairs)
+
+
+def chip_tables():
+    count = devices() // 2
+    me, core = place() // 2, lax.axis_index("seq") % 2
+    every = jnp.arange(count, dtype=jnp.int32)
+
+    def spread_bits(values, sources, targets):
+        return sum(((values >> s) & 1) << t for s, t in zip(sources, targets))
+
+    spots, chips = [], []
+    for order in orders():
+        sources = [bit.bit_length() - 2 for bit in order]
+        targets = list(range(len(order)))[::-1]
+        spots.append(spread_bits(every ^ me, sources, targets))
+        chips.append(spread_bits(every, targets, sources) ^ me)
+    return jnp.concatenate(
+        [
+            jnp.stack([me, core]),
+            jnp.where(core == 1, spots[1], spots[0]),
+            jnp.where(core == 1, chips[1], chips[0]),
+            jnp.where(core == 1, spots[0], spots[1]),
+        ]
+    ).astype(jnp.int32)
+
+
+def local(body, outs, *arrays, name):
+    size = sum(a.size * a.dtype.itemsize for a in arrays)
+    for shape, dtype in outs:
+        extent = jnp.dtype(dtype).itemsize
+        for length in shape:
+            extent *= length
+        size += extent
+
+    def spec(shape):
+        zeros = (0,) * len(shape)
+        return pl.BlockSpec(shape, lambda k: zeros)
+
+    return pl.pallas_call(
+        body,
+        grid=(1,),
+        out_shape=[jax.ShapeDtypeStruct(shape, dtype) for shape, dtype in outs],
+        in_specs=[
+            pl.BlockSpec(memory_space=pltpu.SMEM) if a.dtype == jnp.int32 else spec(a.shape)
+            for a in arrays
+        ],
+        out_specs=[spec(shape) for shape, _ in outs],
+        compiler_params=pltpu.CompilerParams(vmem_limit_bytes=2 * size + 4 * MIB),
+        cost_estimate=pl.CostEstimate(flops=1, bytes_accessed=1, transcendentals=0),
+        name=name,
+    )(*arrays)
+
+
+def pack(info, *weights):
+    width = sum(w.shape[1] for w in weights) // 2
+    shape = (weights[0].shape[0], width)
+
+    def body(info_ref, *refs):
+        keep, give = refs[-2:]
+        at = 0
+        for ref in refs[:-2]:
+            half = ref.shape[1] // 2
+            here = pl.multiple_of(info_ref[1] * half, 128)
+            there = pl.multiple_of((1 - info_ref[1]) * half, 128)
+            keep[:, at : at + half] = ref[:, pl.ds(here, half)]
+            give[:, at : at + half] = ref[:, pl.ds(there, half)]
+            at += half
+
+    return local(body, [(shape, BF16)] * 2, info, *weights, name="pack")
+
+
+def stack_rows(info, keep, got):
+    rows, width = keep.shape
+
+    def body(info_ref, keep_ref, got_ref, out):
+        upper = info_ref[1] == 1
+        out[:rows] = jnp.where(upper, got_ref[...], keep_ref[...])
+        out[rows:] = jnp.where(upper, keep_ref[...], got_ref[...])
+
+    return local(body, [((2 * rows, width), BF16)], info, keep, got, name="stack")[0]
+
+
+def join(part, got):
+    half = part.shape[0]
+
+    def body(part_ref, got_ref, out):
+        out[:half] = part_ref[...]
+        out[half:] = got_ref[...]
+
+    outs = [((2 * half,) + part.shape[1:], BF16)]
+    return local(body, outs, part, got, name="join")[0]
+
+
+def settle(info, *pieces):
+    lengths = [piece.shape[0] for piece in pieces]
+    chips = sum(lengths)
+
+    def body(info_ref, *refs):
+        at = 0
+        for ref, length in zip(refs, lengths):
+            for block in range(length):
+                refs[-1][info_ref[2 + chips + at]] = ref[block]
+                at += 1
+
+    outs = [((chips,) + pieces[0].shape[1:], BF16)]
+    return local(body, outs, info, *pieces, name="settle")[0]
+
+
+@jax.tree_util.register_pytree_node_class
+class Piece:
+    def __init__(self, array, start=0):
+        self.array, self.start = array, start
+
+    def tree_flatten(self):
+        return (self.array,), self.start
+
+    @classmethod
+    def tree_unflatten(cls, start, children):
+        return cls(children[0], start)
+
+
+def summed(pieces, start, stop):
+    total = None
+    for piece in pieces:
+        first, last = start - piece.start, stop - piece.start
+        if 0 <= first and last <= piece.array.shape[0]:
+            value = piece.array[first:last].astype(F32)
+            total = value if total is None else total + value
+    return total
+
+
+def span(turn):
+    length = devices() // 2 >> turn
+    return length // 2, length
+
+
+def shrink(pieces, turn, part=None):
+    start, stop = span(turn)
+    shift = start
+    if part is not None:
+        middle = (start + stop) // 2
+        start, stop = (middle, stop) if part else (start, middle)
+    send = summed(pieces, start, stop).astype(BF16)
+    return [Piece(step(send, turn), start - shift)]
 
 
 def ordered(mine, other, axis):
@@ -71,98 +207,6 @@
     return jnp.concatenate(
         [jnp.where(upper, other, mine), jnp.where(upper, mine, other)], axis=axis
     )
-
-
-def settle(info, parts, cuts, held, width):
-    chips = devices() // 2
-    rows = parts[0].shape[1]
-
-    def body(info_ref, *refs):
-        sources, target = refs[:-1], refs[-1]
-        me = info_ref[0]
-        for turn, ((start, stop), bits) in enumerate(zip(cuts, held)):
-            for far in range(chips):
-                at = sum((1 << k) for k, bit in enumerate(bits[:-1]) if far & (bit >> 1))
-                source = sources[2 * turn + (1 if far & (bits[-1] >> 1) else 0)]
-                target[far ^ me, :, start:stop] = source[at]
-
-    return pl.pallas_call(
-        body,
-        out_shape=jax.ShapeDtypeStruct((chips, rows, width), BF16),
-        in_specs=[pl.BlockSpec(memory_space=pltpu.SMEM)]
-        + [pl.BlockSpec(memory_space=pltpu.VMEM)] * len(parts),
-        out_specs=pl.BlockSpec(memory_space=pltpu.VMEM),
-        compiler_params=pltpu.CompilerParams(vmem_limit_bytes=20 * 1024 * 1024),
-        cost_estimate=pl.CostEstimate(
-            flops=0, bytes_accessed=4 * chips * rows * width, transcendentals=0
-        ),
-        name="settle",
-    )(info, *parts)
-
-
-def sync(*values):
-    return lax.optimization_barrier(values)
-
-
-def classes(piece, got):
-    pair = jnp.stack([piece, got])
-    return [pair[:, :, start:stop] for start, stop in cut(piece.shape[-1])]
-
-
-def grow(parts, turn):
-    return [swap(part, order[::-1][turn]) for part, order in zip(parts, orders())]
-
-
-def join(parts, gots):
-    return [jnp.concatenate([part, got], axis=0) for part, got in zip(parts, gots)]
-
-
-def settled(info, parts, gots, width):
-    held = [[FAR] + order[::-1] for order in orders()]
-    both = [value for pair in zip(parts, gots) for value in pair]
-    return settle(info, both, cut(width), held, width)
-
-
-def total_of(mine, got):
-    return mine.astype(F32) + got.astype(F32)
-
-
-def split_first(own, got):
-    chips, rows, width = own.shape
-    levels = chips.bit_length() - 1
-    dims = (2,) * levels + (rows, width)
-    own, got = own.reshape(dims), got.reshape(dims)
-    bits = [1 << k for k in range(levels, 0, -1)]
-    return [
-        (own[..., start:stop], got[..., start:stop], list(bits)) for start, stop in cut(width)
-    ]
-
-
-def shrink(parts, turn):
-    after = []
-    for (mine, theirs, bits), order in zip(parts, orders()):
-        bit = order[turn]
-        spot = bits.index(bit)
-
-        def pick(values, side):
-            return lax.index_in_dim(values, side, spot, False)
-
-        send = total_of(pick(mine, 1), pick(theirs, 1)).astype(BF16)
-        keep = total_of(pick(mine, 0), pick(theirs, 0)).astype(BF16)
-        after.append((keep, swap(send, bit), [other for other in bits if other != bit]))
-    return after
-
-
-def shrink_far(parts):
-    send = jnp.concatenate([total_of(m[1], t[1]).astype(BF16) for m, t, _ in parts], axis=1)
-    mine = jnp.concatenate([total_of(m[0], t[0]) for m, t, _ in parts], axis=1)
-    return mine, swap(send, FAR)
-
-
-def hold(parts, *others):
-    arrays = [(mine, theirs) for mine, theirs, _ in parts]
-    arrays, others = lax.optimization_barrier((arrays, others))
-    return ([(m, t, bits) for (m, t), (_, _, bits) in zip(arrays, parts)],) + tuple(others)
 
 
 def finish_wide(values):
@@ -181,56 +225,60 @@
     return ordered(mine, swap(give, 1), 1)
 
 
-def begin_states(carry, near_carry, own, near, reverse):
+def states_of(carry, near_carry, own, near, reverse):
     upper = upper_core()
     turned = jnp.logical_not(upper) if reverse else upper
-    first_carry = jnp.where(turned, near_carry, carry)[:, :, None, None]
-    last_carry = jnp.where(turned, carry, near_carry)[:, :, None, None]
-    first = jnp.where(turned, near, own)
-    last = jnp.where(turned, own, near)
-    joined = last_carry * first + last
-    both = first_carry * last_carry
-    rows = own.shape[1]
-    entering = [jnp.zeros_like(joined[:, 0]) for _ in range(rows)]
-    return (turned, first_carry, first, joined, both, entering)
-
-
-def hop(states, phase, reverse):
-    turned, first_carry, first, joined, both, entering = states
+    one, zero = jnp.ones_like(carry), jnp.zeros_like(carry)
+
+    def either(yes, no):
+        return jnp.where(turned, yes, no)[:, :, None, None]
+
+    passed = (either(one, near_carry), either(carry, one), (carry * near_carry)[:, :, None, None])
+    mine = (either(zero, zero), either(one, zero), either(near_carry, one))
+    theirs = (either(zero, one), either(zero, zero), either(one, carry))
+    return (passed, mine, theirs, own, near)
+
+
+def entered(arrived, row):
+    total = None
+    for arrivals in arrived:
+        if arrivals[row] is not None:
+            value = arrivals[row].astype(F32)
+            total = value if total is None else total + value
+    return total
+
+
+def hop(states, arrived, phase, reverse):
+    (a, b, c), _, _, own, near = states
     chips = lax.axis_size("seq") // 2
-    arrived = []
-    for row in range(len(entering)):
+    arrivals = []
+    for row in range(own.shape[1]):
         step = phase - row
         if not 1 <= step < chips:
-            arrived.append(None)
+            arrivals.append(None)
             continue
-        message = (joined[:, row] + both[:, row] * entering[row]).astype(BF16)
+        message = a[:, row] * own[:, row] + b[:, row] * near[:, row]
+        before = entered(arrived, row)
+        if before is not None:
+            message = message + c[:, row] * before
         source, target = (step - 1, step) if not reverse else (chips - step, chips - step - 1)
         pairs = [(2 * source + core, 2 * target + core) for core in range(2)]
-        arrived.append(lax.ppermute(message, "seq", pairs))
-    return arrived
-
-
-def land(states, arrived):
-    turned, first_carry, first, joined, both, entering = states
-    entering = [
-        e if a is None else e + a.astype(F32)
-        for e, a in zip(entering, arrived)
-    ]
-    return (turned, first_carry, first, joined, both, entering)
-
-
-def end_states(states):
-    turned, first_carry, first, joined, both, entering = states
-    entering = jnp.stack(entering, axis=1)
-    middle = (first_carry * entering + first).astype(BF16)
-    entering = entering.astype(BF16)
-    mine = jnp.where(turned, middle, entering)
-    theirs = swap(jnp.where(turned, entering, middle), 1)
-    return mine, theirs
-
-
-def call(body, grid, info, ins, outs, scratch, flops, name):
+        arrivals.append(lax.ppermute(message.astype(BF16), "seq", pairs))
+    return arrivals
+
+
+def end_states(states, arrived):
+    _, mine, theirs, own, near = states
+    before = jnp.stack([entered(arrived, row) for row in range(own.shape[1])], axis=1)
+
+    def taken(factors):
+        a, b, c = factors
+        return (a * own + b * near + c * before).astype(BF16)
+
+    return taken(mine), swap(taken(theirs), 1)
+
+
+def call(body, grid, info, ins, outs, scratch, flops, name, vmem):
     def spec(block, index):
         if block is None:
             return pl.BlockSpec(memory_space=pltpu.SMEM)
@@ -253,9 +301,9 @@
         ),
         out_shape=[jax.ShapeDtypeStruct(shape, dtype) for shape, dtype, _, _ in outs],
         compiler_params=pltpu.CompilerParams(
-            vmem_limit_bytes=VMEM, dimension_semantics=("arbitrary",)
+            vmem_limit_bytes=vmem * MIB, dimension_semantics=("arbitrary",)
         ),
-        cost_estimate=pl.CostEstimate(flops=int(flops), bytes_accessed=int(moved), transcendentals=0),
+        cost_estimate=pl.CostEstimate(flops=1, bytes_accessed=1, transcendentals=0),
         name=name,
     )(info, *[a for a, _, _ in ins])
 
@@ -338,20 +386,20 @@
     return pl.multiple_of(512 * (info[1] if own else 1 - info[1]), 512)
 
 
-def put_wide(target, info, values, start):
+def put_wide(target, info, values, start, own):
     chips, rows, _ = target.shape
     width = values.shape[1]
     values = values.astype(BF16)
     for chip in range(chips):
-        target[chip ^ info[0], :, start : start + width] = values[chip * rows : (chip + 1) * rows]
-
-
-def put_tall(target, info, values, block, start):
+        target[info[(2 if own else 2 + 2 * chips) + chip], :, start : start + width] = values[chip * rows : (chip + 1) * rows]
+
+
+def put_tall(target, info, values, block, start, own):
     chips, rows, _ = target.shape
     values = values.astype(BF16)
     share = chips // 4
     for chip in range(share):
-        at = (block * share + chip) ^ info[0]
+        at = info[(2 if own else 2 + 2 * chips) + block * share + chip]
         base = 2 * rows * chip
         target[at, :, start : start + 512] = values[base : base + rows]
         target[at, :, start + 512 : start + 1024] = values[base + rows : base + 2 * rows]
@@ -555,14 +603,14 @@
     grad_up = (slope * (nt(cot[:, own_at], own) + nt(cot[:, oth_at], oth))).astype(BF16)
     block = real(f, info)
     act_t = activated.T
-    put_tall(g_own, info, mm(act_t, cot[:, own_at]), block, 1024)
-    put_tall(g_oth, info, mm(act_t, cot[:, oth_at]), block, 1024)
+    put_tall(g_own, info, mm(act_t, cot[:, own_at]), block, 1024, True)
+    put_tall(g_oth, info, mm(act_t, cot[:, oth_at]), block, 1024, False)
     grad_w = mm(normed_t[...], grad_up)
     for step in range(4):
 
         @pl.when(f == step)
         def _():
-            put_wide(g_own if step < 2 else g_oth, info, grad_w, 512 * (step % 2))
+            put_wide(g_own if step < 2 else g_oth, info, grad_w, 512 * (step % 2), step < 2)
 
     @pl.when(f < 2)
     def _():
@@ -625,51 +673,14 @@
             state_oth[0, row] = state
 
 
-def outer_kernel(
-    info, grad_low, normed_t, mixed_t, grad_gate, g_own, g_oth,
-    norm_part, out_own, out_oth,
-):
-    h = pl.program_id(0)
-
-    @pl.when(h == 0)
-    def _():
-        norm_part[...] = jnp.zeros_like(norm_part)
-
-    block = real(h, info)
-    left = mixed_t[0]
-    put_tall(out_own, info, mm(left, grad_low[:, pl.ds(side(info, True), 512)]), block, 1024)
-    put_tall(out_oth, info, mm(left, grad_low[:, pl.ds(side(info, False), 512)]), block, 1024)
-    grad_wg = mm(normed_t[...], grad_gate[0])
-    for step in range(4):
-
-        @pl.when(h == step)
-        def _():
-            put_wide(out_own if step < 2 else out_oth, info, grad_wg, 512 * (step % 2))
-
-    @pl.when(h < 2)
-    def _():
-        norm_part[...] += nt(grad_gate[0], flat(g_own))
-
-    @pl.when(h >= 2)
-    def _():
-        norm_part[...] += nt(grad_gate[0], flat(g_oth))
-
-
 def inside_kernel(
-    info, rates, normed_t, grad_ret, query, key, value, mixing,
+    info, rates, grad_ret, query, key, value, mixing,
     cosine, sine, tall_count, wide_count, state_own, state_oth,
-    q_own, q_oth, norm_before,
-    key_part, value_part, norm_part, out_own, out_oth,
-    grad_q,
+    grad_q, key_part, value_part,
 ):
     h = pl.program_id(0)
     rate = rates[h]
     length = cosine.shape[0]
-
-    @pl.when(h == 0)
-    def _():
-        norm_part[...] = norm_before[...]
-
     for row in range(tall_count.shape[0]):
         at = slice(row * length, (row + 1) * length)
         grad = grad_ret[0, at]
@@ -679,7 +690,7 @@
 
         def set_query(state):
             total = mm(scores, key[0, at]) + nt(grad, state[0, row]) * enter
-            grad_q[at, :] = unrotated(total, cosine[...], sine[...]).astype(BF16)
+            grad_q[0, at] = unrotated(total, cosine[...], sine[...]).astype(BF16)
 
         @pl.when(h < 2)
         def _():
@@ -692,20 +703,38 @@
         key_part[0, at] = tn(scores, query[0, at])
         value_part[0, at] = tn(mixing[0, at], grad)
 
-    grad_wq = mm(normed_t[...], grad_q[...])
+
+def outer_kernel(
+    info, grad_low, normed_t, mixed_t, grad_gate, grad_q, g_own, g_oth, q_own, q_oth,
+    norm_part, out_own, out_oth,
+):
+    h = pl.program_id(0)
+
+    @pl.when(h == 0)
+    def _():
+        norm_part[...] = jnp.zeros_like(norm_part)
+
+    block = real(h, info)
+    left = mixed_t[0]
+    put_tall(out_own, info, mm(left, grad_low[:, pl.ds(side(info, True), 512)]), block, 1024, True)
+    put_tall(out_oth, info, mm(left, grad_low[:, pl.ds(side(info, False), 512)]), block, 1024, False)
+    grad_wg = mm(normed_t[...], grad_gate[0])
+    grad_wq = mm(normed_t[...], grad_q[0])
     for step in range(4):
 
         @pl.when(h == step)
         def _():
-            put_wide(out_own if step < 2 else out_oth, info, grad_wq, 256 * (step % 2))
+            target = out_own if step < 2 else out_oth
+            put_wide(target, info, grad_wg, 512 * (step % 2), step < 2)
+            put_wide(target, info, grad_wq, 2048 + 256 * (step % 2), step < 2)
 
     @pl.when(h < 2)
     def _():
-        norm_part[...] += nt(grad_q[...], flat(q_own))
+        norm_part[...] += nt(grad_gate[0], flat(g_own)) + nt(grad_q[0], flat(q_own))
 
     @pl.when(h >= 2)
     def _():
-        norm_part[...] += nt(grad_q[...], flat(q_oth))
+        norm_part[...] += nt(grad_gate[0], flat(g_oth)) + nt(grad_q[0], flat(q_oth))
 
 
 def last_kernel(
@@ -742,8 +771,8 @@
         @pl.when(h == step)
         def _():
             target = out_own if step < 2 else out_oth
-            put_wide(target, info, grad_wk, 256 * (step % 2))
-            put_wide(target, info, grad_wv, 512 + 512 * (step % 2))
+            put_wide(target, info, grad_wk, 256 * (step % 2), step < 2)
+            put_wide(target, info, grad_wv, 512 + 512 * (step % 2), step < 2)
 
 
 def input_kernel(
@@ -803,57 +832,71 @@
     tokens = rows * length
     count = devices()
     chips = count // 2
-    core = lax.axis_index("seq") % 2
-    info = jnp.stack([place() // 2, core]).astype(jnp.int32)
+    info = chip_tables()
     x = inputs.reshape(tokens, width)
     cot = cotangent.reshape(tokens, width)
 
+    upper = upper_core()
     share = w_query.shape[0]
-    upper = upper_core()
-
-    def rows_of(values):
-        return values.reshape(1, -1)
-
-    def both_cores(keep, got, axis):
-        return jnp.concatenate(
-            [jnp.where(upper, got, keep), jnp.where(upper, keep, got)], axis=axis
-        )
-
-    def top_piece(*weights):
-        pairs = [halves(w) for w in weights]
-        keep = jnp.concatenate([a for a, _ in pairs], axis=1)
-        got = swap(jnp.concatenate([b for _, b in pairs], axis=1), 1)
-        return both_cores(keep, got, 0)
-
-    def side_piece(weight):
-        keep, give = halves(weight)
-        return both_cores(keep, swap(give, 1), 1)
-
+    last = len(orders()[0]) - 1
+
+    keep, give = pack(info, w_query, w_key, w_value)
+    qkv = stack_rows(info, keep, swap(give, 1))
     vectors = [first_gain, first_bias, second_gain, second_bias, group_gain]
-    vector = jnp.concatenate(vectors)[None]
+    qkv, vectors = sync(qkv, vectors)
+    got_qkv = step(qkv[None], last)
+
     sizes = [v.shape[0] for v in vectors]
     edges = [sum(sizes[:k]) for k in range(len(sizes) + 1)]
-    vector = jnp.concatenate([vector, jnp.zeros((15, vector.shape[1]), BF16)], axis=0)
-
-    qkv = top_piece(w_query, w_key, w_value)
-    go = jnp.concatenate([top_piece(w_gate), side_piece(w_output)], axis=1)
-    ff = jnp.concatenate([top_piece(w_up), side_piece(w_down)], axis=1)
-    got_qkv = swap(qkv, FAR)
-    table = vector[None]
-    for bit in [1 << k for k in range(count.bit_length() - 1)]:
-        table = both_cores(table, swap(table, bit), 0) if bit == 1 else jnp.concatenate(
-            [
-                jnp.where((place() // bit) % 2 == 1, swapped, table)
-                if first
-                else jnp.where((place() // bit) % 2 == 1, table, swapped)
-                for swapped in [swap(table, bit)]
-                for first in (True, False)
-            ],
-            axis=0,
+    lanes = -(-edges[-1] // 128) * 128
+    table = jnp.concatenate([v.reshape(1, -1) for v in vectors], axis=1)
+    table = jnp.pad(table, ((0, 15), (0, lanes - edges[-1])))
+
+    def table_step(table, done, bit):
+        got = swap(table, bit)
+        turned = (place() // bit) % 2 == 1
+        spot = sum(1 for other in done if other > bit)
+        done.append(bit)
+        return jnp.stack(
+            [jnp.where(turned, got, table), jnp.where(turned, table, got)], axis=spot
         )
-    table = table[:, 0]
+
+    bits = [1 << k for k in range(count.bit_length() - 1)]
+    done = []
+    for bit in bits[:1] + bits[3:]:
+        table = table_step(table, done, bit)
+    got_qkv, table = sync(got_qkv, table)
+    part, got = qkv[None], got_qkv
+    for turn in range(last - 1, 1, -1):
+        part = join(part, got)
+        got = step(part, turn)
+        if turn == last - 1:
+            table = table_step(table, done, 2)
+        part, got, table, w_gate, w_up, w_output, w_down, doc_flags = sync(
+            part, got, table, w_gate, w_up, w_output, w_down, doc_flags
+        )
+
+    part = join(part, got)
+    got = step(part, 1)
+    table = table_step(table, done, FAR)
+
+    top_keep, top_give = pack(info, w_gate, w_up)
+    tall_keep, tall_give = pack(info, w_output, w_down)
+    top = stack_rows(info, top_keep, swap(top_give, 1))
+    tall_got = swap(tall_give, 1)
+    low, high = jnp.where(upper, tall_got, tall_keep), jnp.where(upper, tall_keep, tall_got)
+    go = jnp.concatenate([top[:, :1024], low[:, :512], high[:, :512]], axis=1)
+    ff = jnp.concatenate([top[:, 1024:], low[:, 512:], high[:, 512:]], axis=1)
+    go_part, ff_part = go[None], ff[None]
+    part, got, go_part, ff_part, table, doc_flags = sync(
+        part, got, go_part, ff_part, table, doc_flags
+    )
+
+    pieces = [part, got, step(part, 0), step(got, 0)]
+    go_got = step(go_part, last)
+    vector = table.reshape(count, -1, lanes)[:, 0]
     first_gain, first_bias, second_gain, second_bias, group_gain = [
-        table[:, a:b].reshape(1, -1) for a, b in zip(edges[:-1], edges[1:])
+        vector[:, a:b].reshape(1, -1) for a, b in zip(edges[:-1], edges[1:])
     ]
     group_gain = group_gain.reshape(H, 1, VH)
 
@@ -876,29 +919,6 @@
     rates_in = (rates, None, None)
     unit = 2.0 * tokens * width * 512
 
-    got_qkv, go, ff, gains, tables = sync(
-        got_qkv, go, ff, (first_gain, first_bias, second_gain, second_bias, group_gain),
-        (cosine, sine, tall_count, wide_count, carry, near_carry),
-    )
-    first_gain, first_bias, second_gain, second_bias, group_gain = gains
-    cosine, sine, tall_count, wide_count, carry, near_carry = tables
-    qkv_parts = classes(qkv, got_qkv)
-    qkv_gots = grow(qkv_parts, 0)
-    qkv_parts, qkv_gots, go = sync(qkv_parts, qkv_gots, go)
-    qkv_parts = join(qkv_parts, qkv_gots)
-    qkv_gots = grow(qkv_parts, 1)
-    got_go = swap(go, FAR)
-    qkv_parts, qkv_gots, got_go, go, ff = sync(qkv_parts, qkv_gots, got_go, go, ff)
-    levels = len(orders()[0])
-    for turn in range(2, levels - 1):
-        qkv_parts = join(qkv_parts, qkv_gots)
-        qkv_gots = grow(qkv_parts, turn)
-        qkv_parts, qkv_gots = sync(qkv_parts, qkv_gots)
-    qkv_parts = join(qkv_parts, qkv_gots)
-    qkv_gots = grow(qkv_parts, levels - 1)
-    go_parts = classes(go, got_go)
-    go_gots = grow(go_parts, 0)
-    got_ff = swap(ff, FAR)
     normed, normed_t = call(
         norm_kernel,
         1,
@@ -908,21 +928,26 @@
         [],
         unit / 100,
         "norm",
-    )
-    qkv_parts, qkv_gots, go_parts, go_gots, got_ff, ff, normed, normed_t = sync(
-        qkv_parts, qkv_gots, go_parts, go_gots, got_ff, ff, normed, normed_t
-    )
-
-    qkv_own = settled(info, qkv_parts, qkv_gots, 2048)
+        16,
+    )
+    pieces, go_part, go_got, normed, normed_t, tables, gains = sync(
+        pieces, go_part, go_got, normed, normed_t,
+        (cosine, sine, tall_count, wide_count, carry, near_carry, rates),
+        (second_gain, second_bias, group_gain),
+    )
+    cosine, sine, tall_count, wide_count, carry, near_carry, rates = tables
+    second_gain, second_bias, group_gain = gains
+    rates_in = (rates, None, None)
+
+    qkv_own = settle(info, *pieces)
     qkv_oth = swap(qkv_own, 1)
-    for turn in range(1, levels - 2):
-        go_parts = join(go_parts, go_gots)
-        go_gots = grow(go_parts, turn)
-        go_parts, go_gots = sync(go_parts, go_gots)
-    go_parts = join(go_parts, go_gots)
-    go_gots = grow(go_parts, levels - 2)
-    ff_parts = classes(ff, got_ff)
-    ff_gots = grow(ff_parts, 0)
+    go_part = join(go_part, go_got)
+    go_got = step(go_part, last - 1)
+    qkv_own, qkv_oth, go_part, go_got, ff_part = sync(qkv_own, qkv_oth, go_part, go_got, ff_part)
+
+    go_part = join(go_part, go_got)
+    go_got = step(go_part, last - 2)
+    ff_got = step(ff_part, last)
     (query, key, value, mixing, inner, sum_own, sum_oth) = call(
         project_kernel,
         H,
@@ -944,57 +969,72 @@
         [pltpu.VMEM((tokens, 1024), F32)],
         10 * unit,
         "project",
-    )
+        56,
+    )
+    go_part, go_got, ff_part, ff_got, sum_own, sum_oth = sync(
+        go_part, go_got, ff_part, ff_got, sum_own, sum_oth
+    )
+    for turn in range(last - 3, 0, -1):
+        go_part = join(go_part, go_got)
+        go_got = step(go_part, turn)
+        ff_part = join(ff_part, ff_got)
+        ff_got = step(ff_part, turn + 2)
+        go_part, go_got, ff_part, ff_got = sync(go_part, go_got, ff_part, ff_got)
     sum_near = swap(sum_oth, 1)
-    go_parts, go_gots, ff_parts, ff_gots, sum_own, sum_near = sync(
-        go_parts, go_gots, ff_parts, ff_gots, sum_own, sum_near
-    )
-
-    states = begin_states(carry, near_carry, sum_own, sum_near, False)
-    arrived = hop(states, 1, False)
-    go_parts = join(go_parts, go_gots)
-    go_gots = grow(go_parts, levels - 1)
-    for turn in range(1, levels - 2):
-        ff_parts = join(ff_parts, ff_gots)
-        ff_gots = grow(ff_parts, turn)
-        ff_parts, ff_gots = sync(ff_parts, ff_gots)
-    states, arrived, go_parts, go_gots = sync(states, arrived, go_parts, go_gots)
-    states = land(states, arrived)
-
-    arrived = hop(states, 2, False)
-    go_own = settled(info, go_parts, go_gots, 2048)
+    ff_part = join(ff_part, ff_got)
+    ff_got = step(ff_part, 2)
+    sum_own, sum_near, go_part, go_got, ff_part, ff_got = sync(
+        sum_own, sum_near, go_part, go_got, ff_part, ff_got
+    )
+
+    states = states_of(carry, near_carry, sum_own, sum_near, False)
+    phases = lax.axis_size("seq") // 2 - 1 + rows - 1
+    arrivals = hop(states, [], 1, False)
+    go_first = step(go_part, 0)
+    states, arrivals, go_part, go_got, go_first = sync(
+        states, arrivals, go_part, go_got, go_first
+    )
+    arrived = [arrivals]
+
+    arrivals = hop(states, arrived, 2, False)
+    go_second = step(go_got, 0)
+    states, arrived, arrivals, pieces, ff_part, ff_got = sync(
+        states, arrived, arrivals, [go_part, go_got, go_first, go_second], ff_part, ff_got
+    )
+    arrived = arrived + [arrivals]
+
+    arrivals = hop(states, arrived, 3, False)
+    go_own = settle(info, *pieces)
     go_oth = swap(go_own, 1)
-    ff_parts = join(ff_parts, ff_gots)
-    ff_gots = grow(ff_parts, levels - 2)
-    states, arrived, go_own, go_oth, ff_parts, ff_gots = sync(
-        states, arrived, go_own, go_oth, ff_parts, ff_gots
-    )
-    states = land(states, arrived)
-
-    arrived = hop(states, 3, False)
-    ff_parts = join(ff_parts, ff_gots)
-    ff_gots = grow(ff_parts, levels - 1)
-    (gate,) = call(
-        gate_kernel,
-        H,
-        info,
-        [whole(normed), columns(go_own, 512, 0, True), columns(go_oth, 512, 0, False)],
-        [head_out(per_head + (VH,), F32)],
-        [],
-        4 * unit,
-        "gate",
-    )
-    states, arrived, gate, ff_parts, ff_gots = sync(states, arrived, gate, ff_parts, ff_gots)
-    states = land(states, arrived)
-
-    phases = lax.axis_size("seq") // 2 - 1 + rows - 1
-    ff_own = settled(info, ff_parts, ff_gots, 2048)
-    ff_oth = swap(ff_own, 1)
+    ff_part = join(ff_part, ff_got)
+    ff_got = step(ff_part, 1)
+    states, arrived, arrivals, go_own, go_oth, normed, ff_part, ff_got = sync(
+        states, arrived, arrivals, go_own, go_oth, normed, ff_part, ff_got
+    )
+    arrived = arrived + [arrivals]
+
     for phase in range(4, phases + 1):
-        arrived = hop(states, phase, False)
-        states, arrived = sync(states, arrived)
-        states = land(states, arrived)
-    state_own, state_oth = end_states(states)
+        arrivals = hop(states, arrived, phase, False)
+        if phase == 4:
+            ff_first = step(ff_part, 0)
+            (gate,) = call(
+                gate_kernel,
+                H,
+                info,
+                [whole(normed), columns(go_own, 512, 0, True), columns(go_oth, 512, 0, False)],
+                [head_out(per_head + (VH,), F32)],
+                [],
+                4 * unit,
+                "gate",
+                20,
+            )
+        states, arrived, arrivals, gate, ff_part, ff_got, ff_first = sync(
+            states, arrived, arrivals, gate, ff_part, ff_got, ff_first
+        )
+        arrived = arrived + [arrivals]
+    state_own, state_oth = end_states(states, arrived)
+    state_own, state_oth, ff_got = sync(state_own, state_oth, ff_got)
+    ff_second = step(ff_got, 0)
 
     retained, mixed_t, hidden, normed_second, normed_second_t = call(
         mix_kernel,
@@ -1013,7 +1053,11 @@
         [],
         5 * unit,
         "mix",
-    )
+        32,
+    )
+    ff_second, hidden = sync(ff_second, hidden)
+    ff_own = settle(info, ff_part, ff_got, ff_first, ff_second)
+    ff_oth = swap(ff_own, 1)
     output, grad_hidden, grad_low, grad_second_gain, grad_second_bias, ff_g_own, ff_g_oth = call(
         feed_kernel,
         4,
@@ -1036,6 +1080,7 @@
         ],
         24 * unit,
         "feed",
+        48,
     )
 
     ff_g_got = swap(ff_g_oth, 1)
@@ -1058,84 +1103,95 @@
         [],
         5 * unit,
         "unmix",
+        32,
+    )
+    ff_g_own, ff_g_got, gstate_own, gstate_oth, grad_gate, grad_ret = sync(
+        ff_g_own, ff_g_got, gstate_own, gstate_oth, grad_gate, grad_ret
     )
     gstate_near = swap(gstate_oth, 1)
-    gstate_own, gstate_near, ff_g_own, ff_g_got, grad_gate, grad_ret = sync(
-        gstate_own, gstate_near, ff_g_own, ff_g_got, grad_gate, grad_ret
-    )
-
-    states = begin_states(carry, near_carry, gstate_own, gstate_near, True)
-    arrived = hop(states, 1, True)
-    ff_sums = shrink(split_first(ff_g_own, ff_g_got), 0)
+    ff_sum = [Piece(ff_g_own), Piece(ff_g_got)]
+    gstate_own, gstate_near, grad_gate, grad_ret = sync(
+        gstate_own, gstate_near, grad_gate, grad_ret
+    )
+
+    states = states_of(carry, near_carry, gstate_own, gstate_near, True)
+    arrived = []
+    arrivals = hop(states, arrived, 1, True)
+    ff_first = shrink(ff_sum, 0, 1)
+    grad_q, key_part, value_part = call(
+        inside_kernel,
+        H,
+        info,
+        [
+            rates_in, head_in(grad_ret),
+            head_in(query), head_in(key), head_in(value), head_in(mixing),
+            whole(cosine), whole(sine), whole(tall_count), whole(wide_count),
+            own_in(state_own), other_in(state_oth),
+        ],
+        [
+            head_out(per_head + (QK,), BF16),
+            head_out(per_head + (QK,), F32), head_out(per_head + (VH,), F32),
+        ],
+        [],
+        3 * unit,
+        "inside",
+        24,
+    )
+    states, arrivals, ff_sum, ff_first, grad_q, key_part, value_part = sync(
+        states, arrivals, ff_sum, ff_first, grad_q, key_part, value_part
+    )
+    arrived = arrived + [arrivals]
+
+    arrivals = hop(states, arrived, 2, True)
+    ff_sum = ff_sum + ff_first + shrink(ff_sum, 0, 0)
     norm_part, go_g_own, go_g_oth = call(
         outer_kernel,
         H,
         info,
         [
             whole(grad_low), whole(normed_t), head_in(mixed_t), head_in(grad_gate),
+            head_in(grad_q),
             columns(go_own, 512, 0, True), columns(go_oth, 512, 0, False),
+            columns(qkv_own, 256, 0, True), columns(qkv_oth, 256, 0, False),
         ],
         [
             whole_out((tokens, width), F32),
-            whole_out(grad_shape + (2048,), BF16), whole_out(grad_shape + (2048,), BF16),
+            whole_out(grad_shape + (2560,), BF16), whole_out(grad_shape + (2560,), BF16),
         ],
         [],
-        12 * unit,
+        16 * unit,
         "outer",
-    )
-    ff_sums, states, arrived, norm_part, go_g_own, go_g_oth = hold(
-        ff_sums, states, arrived, norm_part, go_g_own, go_g_oth
-    )
-    states = land(states, arrived)
-
-    arrived = hop(states, 2, True)
-    ff_sums = shrink(ff_sums, 1)
-    key_part, value_part, norm_part, q_g_own, q_g_oth = call(
-        inside_kernel,
-        H,
-        info,
-        [
-            rates_in, whole(normed_t), head_in(grad_ret),
-            head_in(query), head_in(key), head_in(value), head_in(mixing),
-            whole(cosine), whole(sine), whole(tall_count), whole(wide_count),
-            own_in(state_own), other_in(state_oth),
-            columns(qkv_own, 256, 0, True), columns(qkv_oth, 256, 0, False), whole(norm_part),
-        ],
-        [
-            head_out(per_head + (QK,), F32), head_out(per_head + (VH,), F32),
-            whole_out((tokens, width), F32),
-            whole_out(grad_shape + (512,), BF16), whole_out(grad_shape + (512,), BF16),
-        ],
-        [pltpu.VMEM((tokens, QK), BF16)],
-        7 * unit,
-        "inside",
-    )
-    go_g_own = jnp.concatenate([go_g_own, q_g_own], axis=2)
-    go_g_oth = jnp.concatenate([go_g_oth, q_g_oth], axis=2)
-    ff_sums, states, arrived, key_part, value_part, norm_part, go_g_own, go_g_oth = hold(
-        ff_sums, states, arrived, key_part, value_part, norm_part, go_g_own, go_g_oth
-    )
-    states = land(states, arrived)
-
-    arrived = hop(states, 3, True)
+        44,
+    )
+    states, arrived, arrivals, ff_sum, norm_part, go_g_own, go_g_oth = sync(
+        states, arrived, arrivals, ff_sum, norm_part, go_g_own, go_g_oth
+    )
+    arrived = arrived + [arrivals]
+
+    arrivals = hop(states, arrived, 3, True)
     go_g_got = swap(go_g_oth, 1)
-    for turn in range(2, levels):
-        ff_sums = shrink(ff_sums, turn)
-    ff_sums, states, arrived, go_g_own, go_g_got = hold(
-        ff_sums, states, arrived, go_g_own, go_g_got
-    )
-    states = land(states, arrived)
-
-    ff_far = shrink_far(ff_sums)
-    go_sums = shrink(split_first(go_g_own, go_g_got), 0)
+    ff_sum = ff_sum + shrink(ff_sum, 1)
+    states, arrived, arrivals, go_g_own, go_g_got, ff_sum = sync(
+        states, arrived, arrivals, go_g_own, go_g_got, ff_sum
+    )
+    arrived = arrived + [arrivals]
+
+    go_sum = [Piece(go_g_own), Piece(go_g_got)]
     for phase in range(4, phases + 1):
-        arrived = hop(states, phase, True)
-        states, arrived = sync(states, arrived)
-        states = land(states, arrived)
-    after_own, after_oth = end_states(states)
-    go_sums, ff_far, after_own, after_oth = hold(go_sums, ff_far, after_own, after_oth)
-
-    go_sums = shrink(go_sums, 1)
+        arrivals = hop(states, arrived, phase, True)
+        if phase == 4:
+            go_first = shrink(go_sum, 0, 1)
+            ff_sum = ff_sum + shrink(ff_sum, 2)
+        states, arrived, arrivals, go_sum, go_first, ff_sum = sync(
+            states, arrived, arrivals, go_sum, go_first, ff_sum
+        )
+        arrived = arrived + [arrivals]
+    after_own, after_oth = end_states(states, arrived)
+    after_own, after_oth, go_sum, ff_sum = sync(after_own, after_oth, go_sum, ff_sum)
+    go_sum = go_sum + go_first + shrink(go_sum, 0, 0)
+    for turn in range(3, last + 1):
+        ff_sum = ff_sum + shrink(ff_sum, turn)
+
     grad_k, grad_v, kv_g_own, kv_g_oth = call(
         last_kernel,
         H,
@@ -1152,16 +1208,16 @@
         [],
         8 * unit,
         "last",
-    )
-    go_sums, kv_g_own, kv_g_oth, grad_k, grad_v = hold(
-        go_sums, kv_g_own, kv_g_oth, grad_k, grad_v
+        32,
+    )
+    ff_sum, go_sum, kv_g_own, kv_g_oth, grad_k, grad_v = sync(
+        ff_sum, go_sum, kv_g_own, kv_g_oth, grad_k, grad_v
     )
     kv_g_got = swap(kv_g_oth, 1)
-    for turn in range(2, levels):
-        go_sums = shrink(go_sums, turn)
-    go_sums, kv_g_own, kv_g_got = hold(go_sums, kv_g_own, kv_g_got)
-    kv_sums = shrink(split_first(kv_g_own, kv_g_got), 0)
-    go_far = shrink_far(go_sums)
+    kv_g_own, kv_g_got, go_sum = sync(kv_g_own, kv_g_got, go_sum)
+    kv_sum = [Piece(kv_g_own), Piece(kv_g_got)]
+    kv_first = shrink(kv_sum, 0, 1)
+    go_next = shrink(go_sum, 1)
     input_grad, grad_first_gain, grad_first_bias = call(
         input_kernel,
         H,
@@ -1179,26 +1235,45 @@
         [pltpu.VMEM((tokens, width), F32)],
         6 * unit,
         "input",
-    )
-    kv_sums, go_far, input_grad, grad_first_gain, grad_first_bias = hold(
-        kv_sums, go_far, input_grad, grad_first_gain, grad_first_bias
+        56,
+    )
+    kv_sum, kv_first, go_sum, go_next, ff_sum, input_grad, grad_first_gain, grad_first_bias = sync(
+        kv_sum, kv_first, go_sum, go_next, ff_sum, input_grad, grad_first_gain, grad_first_bias
     )
     small = [grad_first_gain, grad_first_bias, grad_second_gain, grad_second_bias, grad_group_gain]
     small = jnp.concatenate([part.reshape(count, -1) for part in small], axis=1)
-    small = jnp.pad(small, ((0, 0), (0, 1024 - edges[-1]))).reshape(count, 8, 128)
-    kv_sums = shrink(kv_sums, 1)
-    spread_small = lax.all_to_all(small, AXES, 0, 0, tiled=True)
-    kv_sums, spread_small = hold(kv_sums, spread_small)
-    for turn in range(2, levels):
-        kv_sums = shrink(kv_sums, turn)
-    summed = jnp.sum(spread_small, axis=0).reshape(-1)
-    small = [summed[a:b] for a, b in zip(edges[:-1], edges[1:])]
-    kv_far = shrink_far(kv_sums)
-
-    def whole_sum(far):
-        return far[0] + far[1].astype(F32)
-
-    ff_grad, go_grad, kv_grad = whole_sum(ff_far), whole_sum(go_far), whole_sum(kv_far)
+    small = jnp.pad(small, ((0, 0), (0, lanes - edges[-1])))
+    small = small.reshape((2,) * len(bits) + (1, lanes))
+
+    def small_step(small, bit):
+        turned = (place() // bit) % 2 == 1
+        got = swap(jnp.where(turned, small[0], small[1]), bit)
+        return jnp.where(turned, small[1], small[0]) + got
+
+    kv_sum = kv_sum + kv_first
+    go_sum = go_sum + go_next
+    kv_second, kv_next = shrink(kv_sum, 0, 0), shrink(kv_sum, 1)
+    go_next = shrink(go_sum, 2)
+    for bit in bits[:1:-1]:
+        small = small_step(small, bit)
+    kv_sum, kv_second, kv_next, go_sum, go_next, small = sync(
+        kv_sum, kv_second, kv_next, go_sum, go_next, small
+    )
+    kv_sum = kv_sum + kv_second + kv_next
+    go_sum = go_sum + go_next
+    kv_next = shrink(kv_sum, 2)
+    for turn in range(3, last + 1):
+        go_sum = go_sum + shrink(go_sum, turn)
+    for bit in bits[1::-1]:
+        small = small_step(small, bit)
+    ff_grad = summed(ff_sum, 0, 1)[0]
+    kv_sum, kv_next, small, ff_grad = sync(kv_sum, kv_next, small, ff_grad)
+    kv_sum = kv_sum + kv_next
+    for turn in range(3, last + 1):
+        kv_sum = kv_sum + shrink(kv_sum, turn)
+    small = [small[0, a:b] for a, b in zip(edges[:-1], edges[1:])]
+
+    go_grad, kv_grad = summed(go_sum, 0, 1)[0], summed(kv_sum, 0, 1)[0]
     ff_mine, ff_got = finish_wide(ff_grad[:, :1024])
     go_mine, go_got = finish_wide(jnp.concatenate([go_grad[:, :1024], go_grad[:, 2048:]], axis=1))
     kv_mine, kv_got = finish_wide(kv_grad)

time: 583 us -> 508 us (0.87)
  starting transfers between devices: 139 us -> 80.8 us
  waiting for transfers between devices: 157 us -> 196 us
  Pallas kernels: 156 us -> 128 us
  other arithmetic: 78 us -> 60.4 us
  local copies, waits for them, and re-layouts: 39.8 us -> 31.2 us
    ppermute x12 -> x42, waiting for transfers between devices: 27.5 us -> 162 us  [the longest x30 118 us: step(): return lax.ppermute(values, AXES, pairs)]
    ppermute x86 -> x29, waiting for transfers between devices: 129 us -> 33.6 us  [swap(): return lax.ppermute(values, AXES, [(i, i ^ bit) for i in range(devices())])]
    ppermute x86 -> x29, starting transfers between devices: 107 us -> 36.2 us  [swap(): return lax.ppermute(values, AXES, [(i, i ^ bit) for i in range(devices())])]
    pallas_call x10, Pallas kernels: 150 us -> 120 us  [call(): pl.pallas_call(body, grid_spec=pltpu.PrefetchScalarGridSpec(num_scalar_pr...]
    ppermute x12 -> x42, starting transfers between devices: 28.9 us -> 44.5 us  [the longest x30 27.4 us: step(): return lax.ppermute(values, AXES, pairs)]
    unnamed x147 -> x157, local copies, waits for them, and re-layouts: 9.31 us -> 22.7 us
    concatenate x14 -> x0, other arithmetic: 9.1 us -> none  [the longest x1 5.35 us: per_device(): go_g_oth = jnp.concatenate([go_g_oth, q_g_oth], axis=2)]
    concatenate x19 -> x2, local copies, waits for them, and re-layouts: 9.6 us -> 0.89 us  [the longest x1 0.81 us: per_device(): table = jnp.concatenate([v.reshape(1, -1) for v in vectors], axis=1)]
  transfers between devices with their start and end apart: 99 -> 71, of which waited for: 38 -> 34; matrix products, arithmetic and copies ran while one was open for 16% -> 10% of each run, Pallas kernels for 18% -> 19%
where the time goes in v3:
time: 508 us; the launch traced here: 498 us
  waiting for transfers between devices  196 us (39%)
  Pallas kernels  128 us (25%)
  starting transfers between devices  80.8 us (16%)
  other arithmetic  60.4 us (12%)
  local copies, waits for them, and re-layouts  31.2 us (6%)
    pallas_call x10, Pallas kernels, call(): pl.pallas_call(body, grid_spec=pltpu.PrefetchScalarGridSpec(num_scalar_pr...  120 us
    ppermute x30, waiting for transfers between devices, step(): return lax.ppermute(values, AXES, pairs)  118 us
    ppermute x12, waiting for transfers between devices, hop(): arrivals.append(lax.ppermute(message.astype(BF16), 'seq', pairs))  43.9 us
    ppermute x29, starting transfers between devices, swap(): return lax.ppermute(values, AXES, [(i, i ^ bit) for i in range(devices())])  36.2 us
    ppermute x29, waiting for transfers between devices, swap(): return lax.ppermute(values, AXES, [(i, i ^ bit) for i in range(devices())])  33.6 us
    ppermute x30, starting transfers between devices, step(): return lax.ppermute(values, AXES, pairs)  27.4 us
    convert_element_type x14, other arithmetic, shrink(): send = summed(pieces, start, stop).astype(BF16)  25.8 us
    unnamed x157, local copies, waits for them, and re-layouts  22.7 us
  transfers between devices with their start and end apart: 71, of which 34 were waited for; matrix products, arithmetic and copies ran while one was open for 10% of the time, Pallas kernels for 19%

profile of v3, /device:TPU:1, one launch (start us, length us, event | category | flops | bytes accessed | tf_op | source)
XLA Modules:
  0.0 498.4 jit_solution(14250669195077848054)
XLA Ops:
  15.5 11.3 %collective-permute-done.1.got_ref = bf16[1,64,2048]{2,1,0:T(8,128)(2,1)S(1)} collective-permute-done((bf16[1,64,2048]{2,1,0:T(8,128)(2,1)S(1)}, bf16[1,64,2048]{2,1,0:T(8,128)(2,1)S(1)}, u32[]{:S(2)}, u32[]{:S(2)}) %collective-permute-start.1) | collective-permute-done | bytes 262176 | tf_op jit(solution)/shard_map/ppermute | solution.py:58
  29.7 7.0 %collective-permute-done.6 = bf16[2,2,2,16,256]{4,3,2,1,0:T(8,128)(2,1)S(1)} collective-permute-done((bf16[2,2,2,16,256]{4,3,2,1,0:T(8,128)(2,1)S(1)}, bf16[2,2,2,16,256]{4,3,2,1,0:T(8,128)(2,1)S(1)}, u32[]{:S(2)}, u32[]{:S(2)}) %collective-permute-start.6) | collective-permute-done | bytes 65568 | tf_op jit(solution)/shard_map/ppermute | solution.py:39
  36.8 2.9 collective-permute-start.10
  42.9 2.7 collective-permute-done.10
  46.4 9.4 %collective-permute-done.7.refs_1_ = bf16[4,64,2048]{2,1,0:T(8,128)(2,1)} collective-permute-done((bf16[4,64,2048]{2,1,0:T(8,128)(2,1)S(1)}, bf16[4,64,2048]{2,1,0:T(8,128)(2,1)}, u32[]{:S(2)}, u32[]{:S(2)}) %collective-permute-start.7) | collective-permute-done | bytes 1048608 | tf_op jit(solution)/shard_map/ppermute | solution.py:58
  59.0 2.9 collective-permute-start.14
  67.0 5.1 %collective-permute-done.13.got_ref = bf16[1,64,2048]{2,1,0:T(8,128)(2,1)S(1)} collective-permute-done((bf16[1,64,2048]{2,1,0:T(8,128)(2,1)S(1)}, bf16[1,64,2048]{2,1,0:T(8,128)(2,1)S(1)}, u32[]{:S(2)}, u32[]{:S(2)}) %collective-permute-start.13) | collective-permute-done | bytes 262176 | tf_op jit(solution)/shard_map/ppermute | solution.py:58
  72.1 8.9 %collective-permute-done.12.refs_3_ = bf16[4,64,2048]{2,1,0:T(8,128)(2,1)} collective-permute-done((bf16[4,64,2048]{2,1,0:T(8,128)(2,1)}, bf16[4,64,2048]{2,1,0:T(8,128)(2,1)}, u32[]{:S(2)}, u32[]{:S(2)}) %collective-permute-start.12) | collective-permute-done | bytes 1048608 | tf_op jit(solution)/shard_map/ppermute | solution.py:58
  85.3 3.3 collective-permute-start.15
  89.9 8.0 %collective-permute-done.16.got_ref = bf16[2,64,2048]{2,1,0:T(8,128)(2,1)S(1)} collective-permute-done((bf16[2,64,2048]{2,1,0:T(8,128)(2,1)S(1)}, bf16[2,64,2048]{2,1,0:T(8,128)(2,1)S(1)}, u32[]{:S(2)}, u32[]{:S(2)}) %collective-permute-start.16) | collective-permute-done | bytes 524320 | tf_op jit(solution)/shard_map/ppermute | solution.py:58
  102.4 15.4 %project.1 = (bf16[4,512,256]{2,1,0:T(8,128)(2,1)}, bf16[4,512,256]{2,1,0:T(8,128)(2,1)}, bf16[4,512,512]{2,1,0:T(8,128)(2,1)}, bf16[4,512,256]{2,1,0:T(8,128)(2...) custom-call(s32[50]{0:T(128)} %copy-done.42, f32[4]{0:T(128)} %copy-done.54, ...), custom_call_target="tpu_custom_call" | custom-call | flops 1 | bytes 1 | tf_op jit(solution)/shard_map/project/pallas_call | solution.py:293
  117.8 3.5 collective-permute-start.19
  121.7 8.0 %collective-permute-done.20.got_ref = bf16[2,64,2048]{2,1,0:T(8,128)(2,1)S(1)} collective-permute-done((bf16[2,64,2048]{2,1,0:T(8,128)(2,1)S(1)}, bf16[2,64,2048]{2,1,0:T(8,128)(2,1)S(1)}, u32[]{:S(2)}, u32[]{:S(2)}) %collective-permute-start.20) | collective-permute-done | bytes 524320 | tf_op jit(solution)/shard_map/ppermute | solution.py:58
  130.2 2.7 fusion.50
  132.9 3.4 collective-permute-start.21
  136.3 9.3 %collective-permute-done.21 = bf16[2,256,512]{2,1,0:T(8,128)(2,1)} collective-permute-done((bf16[2,256,512]{2,1,0:T(8,128)(2,1)}, bf16[2,256,512]{2,1,0:T(8,128)(2,1)}, u32[]{:S(2)}, u32[]{:S(2)}) %collective-permute-start.21) | collective-permute-done | bytes 524320 | tf_op jit(solution)/shard_map/ppermute | solution.py:266
  147.6 3.0 fusion.41
  151.2 4.8 collective-permute-start.24
  156.0 9.4 %collective-permute-done.24 = bf16[2,256,512]{2,1,0:T(8,128)(2,1)S(1)} collective-permute-done((bf16[2,256,512]{2,1,0:T(8,128)(2,1)S(1)}, bf16[2,256,512]{2,1,0:T(8,128)(2,1)S(1)}, u32[]{:S(2)}, u32[]{:S(2)}) %collective-permute-start.24) | collective-permute-done | bytes 524320 | tf_op jit(solution)/shard_map/ppermute | solution.py:266
  167.3 2.7 collective-permute-start.28
  175.6 8.5 %collective-permute-done.29.refs_1_ = bf16[4,64,2048]{2,1,0:T(8,128)(2,1)S(1)} collective-permute-done((bf16[4,64,2048]{2,1,0:T(8,128)(2,1)S(1)}, bf16[4,64,2048]{2,1,0:T(8,128)(2,1)S(1)}, u32[]{:S(2)}, u32[]{:S(2)}) %collective-permute-start.29) | collective-permute-done | bytes 1048608 | tf_op jit(solution)/shard_map/ppermute | solution.py:58
  188.0 3.8 gate.1
  191.9 6.4 %collective-permute-done.31.refs_2_ = bf16[4,64,2048]{2,1,0:T(8,128)(2,1)S(1)} collective-permute-done((bf16[4,64,2048]{2,1,0:T(8,128)(2,1)S(1)}, bf16[4,64,2048]{2,1,0:T(8,128)(2,1)S(1)}, u32[]{:S(2)}, u32[]{:S(2)}) %collective-permute-start.31) | collective-permute-done | bytes 1048608 | tf_op jit(solution)/shard_map/ppermute | solution.py:58
  199.8 2.7 add_convert_fusion.8
  207.1 11.7 %mix.1 = (f32[4,512,512]{2,1,0:T(8,128)S(1)}, bf16[4,512,512]{2,1,0:T(8,128)(2,1)S(1)}, f32[512,1024]{1,0:T(8,128)S(1)}, bf16[512,1024]{1,0:T(8,128)(2,1)S(1)}, bf16[1024,512]{1,0:T(8,128)(2,1)S(1)}) custom-call(s32[50]{0:T(128)S(1)} %copy-done.43, f32[4]{0:T(128)S(1)} %copy-done.55, bf16[512,1024]{1,0:T(8,128)(2,1)S(1)} %bitcast.340, ...), custom_call_target="tpu_custom_call" | custom-call | flops 1 | bytes 1 | tf_op jit(solution)/shard_map/mix/pallas_call | solution.py:293
  225.6 6.8 %collective-permute-done.34.up_oth.down_oth = bf16[16,64,2048]{2,1,0:T(8,128)(2,1)S(1)} collective-permute-done((bf16[16,64,2048]{2,1,0:T(8,128)(2,1)S(1)}, bf16[16,64,2048]{2,1,0:T(8,128)(2,1)S(1)}, u32[]{:S(2)}, u32[]{:S(2)}) %collective-permute-start.34) | collective-permute-done | bytes 4194336 | tf_op jit(solution)/shard_map/ppermute | solution.py:39
  236.8 27.8 %feed.1 = (bf16[512,1024]{1,0:T(8,128)(2,1)}, f32[512,1024]{1,0:T(8,128)}, bf16[512,1024]{1,0:T(8,128)(2,1)S(1)}, f32[1,1024]{1,0:T(1,128)S(1)}, f32[1,1024]{1,0...) custom-call(s32[50]{0:T(128)S(1)} %copy-done.43, f32[512,1024]{1,0:T(8,128)} %copy-done.32, ...), custom_call_target="tpu_custom_call" | custom-call | flops 1 | bytes 1 | tf_op jit(solution)/shard_map/feed/pallas_call | solution.py:293
  267.0 10.3 %unmix.1 = (bf16[4,512,512]{2,1,0:T(8,128)(2,1)S(1)}, bf16[4,512,512]{2,1,0:T(8,128)(2,1)S(1)}, f32[4,1,512]{2,1,0:T(1,128)S(1)}, f32[2,2,256,512]{3,2,1,0:T(8,128)S(1)}, f32[2,2,256,512]{3,2,1,0:T(8,128)S(1)}) custom-call(s32[50]{0:T(128)S(1)} %copy-done.43, f32[4]{0:T(128)S(1)} %copy-done.55, bf16[512,1024]{1,0:T(8,128)(2,1)S(1)} %get-tuple-element.503.grad_low, ...), custom_call_target="tpu_custom_call" | custom-call | flops 1 | bytes 1 | tf_op jit(solution)/shard_map/unmix/pallas_call | solution.py:293
  282.7 7.6 %inside.1 = (bf16[4,512,256]{2,1,0:T(8,128)(2,1)S(1)}, f32[4,512,256]{2,1,0:T(8,128)S(1)}, f32[4,512,512]{2,1,0:T(8,128)S(1)}) custom-call(s32[50]{0:T(128)S(1)} %copy-done.43, f32[4]{0:T(128)S(1)} %copy-done.55, bf16[4,512,512]{2,1,0:T(8,128)(2,1)S(1)} %get-tuple-element.517.grad_ret, bf16[4,512,256]{2,1,0:T(8,128)(2,1)S(1)} %copy-done.7, ...), custom_call_target="tpu_custom_call" | custom-call | flops 1 | bytes 1 | tf_op jit(solution)/shard_map/inside/pallas_call | solution.py:293
  290.4 4.0 collective-permute-done.38
  300.4 17.9 %outer.1 = (f32[512,1024]{1,0:T(8,128)S(1)}, bf16[16,64,2560]{2,1,0:T(8,128)(2,1)}, bf16[16,64,2560]{2,1,0:T(8,128)(2,1)}) custom-call(s32[50]{0:T(128)S(1)} %copy-done.43, bf16[512,1024]{1,0:T(8,128)(2,1)S(1)} %get-tuple-element.503.grad_low, bf16[1024,512]{1,0:T(8,128)(2,1)S(1)} %copy-done.21, bf16[4,512,512]{2,1,0:T(8,128)(2,1)S(1)} %copy-done.31, ...), custom_call_target="tpu_custom_call" | custom-call | flops 1 | bytes 1 | tf_op jit(solution)/shard_map/outer/pallas_call | solution.py:293
  328.1 17.1 %collective-permute-done.42 = bf16[2,256,512]{2,1,0:T(8,128)(2,1)S(1)} collective-permute-done((bf16[2,256,512]{2,1,0:T(8,128)(2,1)S(1)}, bf16[2,256,512]{2,1,0:T(8,128)(2,1)S(1)}, u32[]{:S(2)}, u32[]{:S(2)}) %collective-permute-start.42) | collective-permute-done | bytes 524320 | tf_op jit(solution)/shard_map/ppermute | solution.py:266
  348.5 5.5 %collective-permute-start.48 = (bf16[2,64,2048]{2,1,0:T(8,128)(2,1)S(1)}, bf16[2,64,2048]{2,1,0:T(8,128)(2,1)S(1)}, u32[]{:S(2)}, u32[]{:S(2)}) collective-permute-start(bf16[2,64,2048]{2,1,0:T(8,128)(2,1)S(1)} %add_convert_fusion.14), channel_id=1, source_target_pairs={{0,16},{1,3},{2,18},{3,1},{4,20},{5,7},{6,22},{7,5},{8,24},{9,11},... | collective-permute-start | bytes 1572872 | tf_op jit(solution)/shard_map/ppermute | solution.py:58
  356.5 4.3 collective-permute-done.48
  360.8 8.1 %collective-permute-done.46 = bf16[2,256,512]{2,1,0:T(8,128)(2,1)S(1)} collective-permute-done((bf16[2,256,512]{2,1,0:T(8,128)(2,1)S(1)}, bf16[2,256,512]{2,1,0:T(8,128)(2,1)S(1)}, u32[]{:S(2)}, u32[]{:S(2)}) %collective-permute-start.46) | collective-permute-done | bytes 524320 | tf_op jit(solution)/shard_map/ppermute | solution.py:266
  370.3 3.6 collective-permute-start.49
  378.9 9.1 %last.1 = (bf16[4,512,256]{2,1,0:T(8,128)(2,1)S(1)}, bf16[4,512,512]{2,1,0:T(8,128)(2,1)S(1)}, bf16[16,64,1536]{2,1,0:T(8,128)(2,1)S(1)}, bf16[16,64,1536]{2,1,0:T(8,128)(2,1)S(1)}) custom-call(s32[50]{0:T(128)S(1)} %copy-done.43, f32[4]{0:T(128)S(1)} %copy-done.55, bf16[1024,512]{1,0:T(8,128)(2,1)S(1)} %copy-done.21, bf16[4,512,256]{2,1,0:T(8,128)(2,1)S(1)} %copy-done.17, ...), custom_call_target="tpu_custom_call" | custom-call | flops 1 | bytes 1 | tf_op jit(solution)/shard_map/last/pallas_call | solution.py:293
  389.0 3.9 collective-permute-done.50
  394.8 5.3 %collective-permute-done.52 = bf16[16,64,1536]{2,1,0:T(8,128)(2,1)S(1)} collective-permute-done((bf16[16,64,1536]{2,1,0:T(8,128)(2,1)S(1)}, bf16[16,64,1536]{2,1,0:T(8,128)(2,1)S(1)}, u32[]{:S(2)}, u32[]{:S(2)}) %collective-permute-start.52) | collective-permute-done | bytes 3145760 | tf_op jit(solution)/shard_map/ppermute | solution.py:39
  400.1 4.4 add_convert_fusion
  408.8 13.5 %input.1 = (f32[512,1024]{1,0:T(8,128)}, f32[1,1024]{1,0:T(1,128)}, f32[1,1024]{1,0:T(1,128)}) custom-call(s32[50]{0:T(128)} %copy-done.42, bf16[512,1024]{1,0:T(8,128)(2,1)} %bitcast.338, bf16[1,1024]{1,0:T(2,128)(2,1)} %copy-done.53, f32[512,1024]{1,0:T(8,128)} %get-tuple-element.643.grad_hidden, f32[512,1024]{1,0:T(8,128)} %copy-done.26, ...), custom_call_target="tpu_custom_call" | custom-call | flops 1 | bytes 1 | tf_op jit(solution)/shard_map/input/pallas_call | solution.py:293
  422.3 7.4 %collective-permute-done.54 = bf16[4,64,2560]{2,1,0:T(8,128)(2,1)} collective-permute-done((bf16[4,64,2560]{2,1,0:T(8,128)(2,1)}, bf16[4,64,2560]{2,1,0:T(8,128)(2,1)}, u32[]{:S(2)}, u32[]{:S(2)}) %collective-permute-start.54) | collective-permute-done | bytes 1310752 | tf_op jit(solution)/shard_map/ppermute | solution.py:58
  433.5 2.9 add_convert_fusion.13
  444.4 3.1 collective-permute-done.60
  449.5 3.9 collective-permute-done.55
  453.4 4.9 collective-permute-done.56
  464.6 13.6 %collective-permute-done.64 = bf16[1,64,2560]{2,1,0:T(8,128)(2,1)S(1)} collective-permute-done((bf16[1,64,2560]{2,1,0:T(8,128)(2,1)S(1)}, bf16[1,64,2560]{2,1,0:T(8,128)(2,1)S(1)}, u32[]{:S(2)}, u32[]{:S(2)}) %collective-permute-start.64) | collective-permute-done | bytes 327712 | tf_op jit(solution)/shard_map/ppermute | solution.py:58
  485.6 7.9 %collective-permute-done.66 = bf16[1,64,1536]{2,1,0:T(8,128)(2,1)S(1)} collective-permute-done((bf16[1,64,1536]{2,1,0:T(8,128)(2,1)S(1)}, bf16[1,64,1536]{2,1,0:T(8,128)(2,1)S(1)}, u32[]{:S(2)}, u32[]{:S(2)}) %collective-permute-start.66) | collective-permute-done | bytes 196640 | tf_op jit(solution)/shard_map/ppermute | solution.py:58
  (425 shorter events, 146.2 us)
Async XLA Ops:
  13.2 13.7 %collective-permute-start.1 = (bf16[1,64,2048]{2,1,0:T(8,128)(2,1)S(1)}, bf16[1,64,2048]{2,1,0:T(8,128)(2,1)S(1)}, u32[]{:S(2)}, u32[]{:S(2)}) collective-permute-start(bf16[1,64,2048]{2,1,0:T(8,128)(2,1)S(1)} %bitcast.341), channel_id=1, source_target_pairs={{0,4},{1,5},{2,6},{3,7},{4,0},{5,1},{6,2},{7,3},{8,12},{9,13},{10,... | collective-permute-start | bytes 786440 | tf_op jit(solution)/shard_map/ppermute | solution.py:58
  26.9 9.9 %collective-permute-start.5 = (bf16[2,64,2048]{2,1,0:T(8,128)(2,1)S(1)}, bf16[2,64,2048]{2,1,0:T(8,128)(2,1)S(1)}, u32[]{:S(2)}, u32[]{:S(2)}) collective-permute-start(bf16[2,64,2048]{2,1,0:T(8,128)(2,1)S(1)} %join.6.part_ref), channel_id=1, source_target_pairs={{0,16},{1,3},{2,18},{3,1},{4,20},{5,7},{6,22},{7,5},{8,24},{9,11},... | collective-permute-start | bytes 1572872 | tf_op jit(solution)/shard_map/ppermute | solution.py:58
  29.7 7.0 %collective-permute-start.6 = (bf16[2,2,2,16,256]{4,3,2,1,0:T(8,128)(2,1)S(1)}, bf16[2,2,2,16,256]{4,3,2,1,0:T(8,128)(2,1)S(1)}, u32[]{:S(2)}, u32[]{:S(2)}) collective-permute-start(bf16[2,2,2,16,256]{4,3,2,1,0:T(8,128)(2,1)S(1)} %pad_maximum_fusion.12), channel_id=1, source_target_pairs={{0,2},{1,3},{2,0},{3,1},{4,6},{5,7},{6,4},{7,5},{8,10},{9,11},{10,... | collective-permute-start | bytes 196616 | tf_op jit(solution)/shard_map/ppermute | solution.py:39
  36.8 8.8 %collective-permute-start.10 = (bf16[2,2,2,2,16,256]{5,4,3,1,0,2:T(8,128)(2,1)S(1)}, bf16[2,2,2,2,16,256]{5,4,3,1,0,2:T(8,128)(2,1)S(1)}, u32[]{:S(2)}, u32[]{:S(2)}) collective-permute-start(bf16[2,2,2,2,16,256]{5,4,3,1,0,2:T(8,128)(2,1)S(1)} %pad_maximum_fusion.9), channel_id=1, source_target_pairs={{0,4},{1,5},{2,6},{3,7},{4,0},{5,1},{6,2},{7,3},{8,12},{9,13},{10,... | collective-permute-start | bytes 393224 | tf_op jit(solution)/shard_map/ppermute | solution.py:39
  41.7 14.1 %collective-permute-start.7 = (bf16[4,64,2048]{2,1,0:T(8,128)(2,1)S(1)}, bf16[4,64,2048]{2,1,0:T(8,128)(2,1)}, u32[]{:S(2)}, u32[]{:S(2)}) collective-permute-start(bf16[4,64,2048]{2,1,0:T(8,128)(2,1)S(1)} %join.7.refs_0_), channel_id=1, source_target_pairs={{0,2},{1,9},{2,0},{3,11},{4,6},{5,13},{6,4},{7,15},{8,10},{9,1},{1... | collective-permute-start | bytes 3145736 | tf_op jit(solution)/shard_map/ppermute | solution.py:58
  55.8 16.4 %collective-permute-start.11 = (bf16[4,64,2048]{2,1,0:T(8,128)(2,1)S(1)}, bf16[4,64,2048]{2,1,0:T(8,128)(2,1)}, u32[]{:S(2)}, u32[]{:S(2)}) collective-permute-start(bf16[4,64,2048]{2,1,0:T(8,128)(2,1)S(1)} %join.7.refs_0_), channel_id=1, source_target_pairs={{0,8},{1,17},{2,10},{3,19},{4,12},{5,21},{6,14},{7,23},{8,0},{9,25... | collective-permute-start | bytes 3145736 | tf_op jit(solution)/shard_map/ppermute | solution.py:58
  56.0 25.1 %collective-permute-start.12 = (bf16[4,64,2048]{2,1,0:T(8,128)(2,1)}, bf16[4,64,2048]{2,1,0:T(8,128)(2,1)}, u32[]{:S(2)}, u32[]{:S(2)}) collective-permute-start(bf16[4,64,2048]{2,1,0:T(8,128)(2,1)} %collective-permute-done.7.refs_1_), channel_id=1, source_target_pairs={{0,8},{1,17},{2,10},{3,19},{4,12},{5,21},{6,14},{7,23},{8,0},{9,25... | collective-permute-start | bytes 3145736 | tf_op jit(solution)/shard_map/ppermute | solution.py:58
  58.6 13.6 %collective-permute-start.13 = (bf16[1,64,2048]{2,1,0:T(8,128)(2,1)S(1)}, bf16[1,64,2048]{2,1,0:T(8,128)(2,1)S(1)}, u32[]{:S(2)}, u32[]{:S(2)}) collective-permute-start(bf16[1,64,2048]{2,1,0:T(8,128)(2,1)S(1)} %maximum_bitcast_fusion.part_ref), channel_id=1, source_target_pairs={{0,4},{1,5},{2,6},{3,7},{4,0},{5,1},{6,2},{7,3},{8,12},{9,13},{10,... | collective-permute-start | bytes 786440 | tf_op jit(solution)/shard_map/ppermute | solution.py:58
  59.0 8.0 %collective-permute-start.14 = (f32[2]{0:T(128)S(1)}, f32[2]{0:T(128)S(1)}, u32[]{:S(2)}, u32[]{:S(2)}) collective-permute-start(f32[2]{0:T(128)S(1)} %fusion.66), channel_id=1, source_target_pairs={{0,1},{1,0},{2,3},{3,2},{4,5},{5,4},{6,7},{7,6},{8,9},{9,8},{10,11... | collective-permute-start | bytes 32 | tf_op jit(solution)/shard_map/ppermute | solution.py:39
  85.3 12.7 %collective-permute-start.15 = (bf16[16,64,2048]{2,1,0:T(8,128)(2,1)S(1)}, bf16[16,64,2048]{2,1,0:T(8,128)(2,1)S(1)}, u32[]{:S(2)}, u32[]{:S(2)}) collective-permute-start(bf16[16,64,2048]{2,1,0:T(8,128)(2,1)S(1)} %settle.3.q_own.k_own.v_own), channel_id=1, source_target_pairs={{0,1},{1,0},{2,3},{3,2},{4,5},{5,4},{6,7},{7,6},{8,9},{9,8},{10,11... | collective-permute-start | bytes 12582920 | tf_op jit(solution)/shard_map/ppermute | solution.py:39
  89.6 8.4 %collective-permute-start.16 = (bf16[2,64,2048]{2,1,0:T(8,128)(2,1)S(1)}, bf16[2,64,2048]{2,1,0:T(8,128)(2,1)S(1)}, u32[]{:S(2)}, u32[]{:S(2)}) collective-permute-start(bf16[2,64,2048]{2,1,0:T(8,128)(2,1)S(1)} %join.8.part_ref), channel_id=1, source_target_pairs={{0,16},{1,3},{2,18},{3,1},{4,20},{5,7},{6,22},{7,5},{8,24},{9,11},... | collective-permute-start | bytes 1572872 | tf_op jit(solution)/shard_map/ppermute | solution.py:58
  99.9 17.9 %collective-permute-start.17 = (bf16[4,64,2048]{2,1,0:T(8,128)(2,1)S(1)}, bf16[4,64,2048]{2,1,0:T(8,128)(2,1)}, u32[]{:S(2)}, u32[]{:S(2)}) collective-permute-start(bf16[4,64,2048]{2,1,0:T(8,128)(2,1)S(1)} %join.9.refs_0_), channel_id=1, source_target_pairs={{0,2},{1,9},{2,0},{3,11},{4,6},{5,13},{6,4},{7,15},{8,10},{9,1},{1... | collective-permute-start | bytes 3145736 | tf_op jit(solution)/shard_map/ppermute | solution.py:58
  101.1 16.7 %collective-permute-start.18 = (bf16[1,64,2048]{2,1,0:T(8,128)(2,1)S(1)}, bf16[1,64,2048]{2,1,0:T(8,128)(2,1)S(1)}, u32[]{:S(2)}, u32[]{:S(2)}) collective-permute-start(bf16[1,64,2048]{2,1,0:T(8,128)(2,1)S(1)} %maximum_bitcast_fusion.1.part_ref), channel_id=1, source_target_pairs={{0,4},{1,5},{2,6},{3,7},{4,0},{5,1},{6,2},{7,3},{8,12},{9,13},{10,... | collective-permute-start | bytes 786440 | tf_op jit(solution)/shard_map/ppermute | solution.py:58
  117.8 11.9 %collective-permute-start.19 = (f32[2,2,256,512]{3,2,1,0:T(8,128)}, f32[2,2,256,512]{3,2,1,0:T(8,128)}, u32[]{:S(2)}, u32[]{:S(2)}) collective-permute-start(f32[2,2,256,512]{3,2,1,0:T(8,128)} %get-tuple-element.402), channel_id=1, source_target_pairs={{0,1},{1,0},{2,3},{3,2},{4,5},{5,4},{6,7},{7,6},{8,9},{9,8},{10,11... | collective-permute-start | bytes 6291464 | tf_op jit(solution)/shard_map/ppermute | solution.py:39
  121.3 8.4 %collective-permute-start.20 = (bf16[2,64,2048]{2,1,0:T(8,128)(2,1)S(1)}, bf16[2,64,2048]{2,1,0:T(8,128)(2,1)S(1)}, u32[]{:S(2)}, u32[]{:S(2)}) collective-permute-start(bf16[2,64,2048]{2,1,0:T(8,128)(2,1)S(1)} %join.10.part_ref), channel_id=1, source_target_pairs={{0,16},{1,3},{2,18},{3,1},{4,20},{5,7},{6,22},{7,5},{8,24},{9,11},... | collective-permute-start | bytes 1572872 | tf_op jit(solution)/shard_map/ppermute | solution.py:58
  129.7 15.8 %collective-permute-start.22 = (bf16[4,64,2048]{2,1,0:T(8,128)(2,1)S(1)}, bf16[4,64,2048]{2,1,0:T(8,128)(2,1)}, u32[]{:S(2)}, u32[]{:S(2)}) collective-permute-start(bf16[4,64,2048]{2,1,0:T(8,128)(2,1)S(1)} %join.9.refs_0_), channel_id=1, source_target_pairs={{0,8},{1,17},{2,10},{3,19},{4,12},{5,21},{6,14},{7,23},{8,0},{9,25... | collective-permute-start | bytes 3145736 | tf_op jit(solution)/shard_map/ppermute | solution.py:58
  132.9 12.7 %collective-permute-start.21 = (bf16[2,256,512]{2,1,0:T(8,128)(2,1)}, bf16[2,256,512]{2,1,0:T(8,128)(2,1)}, u32[]{:S(2)}, u32[]{:S(2)}) collective-permute-start(bf16[2,256,512]{2,1,0:T(8,128)(2,1)} %fusion.50), channel_id=1, source_target_pairs={{0,2},{1,3},{8,10},{9,11},{16,18},{17,19},{24,26},{25,27}} | collective-permute-start | bytes 1572872 | tf_op jit(solution)/shard_map/ppermute | solution.py:266
  145.8 19.7 %collective-permute-start.25 = (bf16[4,64,2048]{2,1,0:T(8,128)(2,1)}, bf16[4,64,2048]{2,1,0:T(8,128)(2,1)S(1)}, u32[]{:S(2)}, u32[]{:S(2)}) collective-permute-start(bf16[4,64,2048]{2,1,0:T(8,128)(2,1)} %collective-permute-done.17.refs_1_), channel_id=1, source_target_pairs={{0,8},{1,17},{2,10},{3,19},{4,12},{5,21},{6,14},{7,23},{8,0},{9,25... | collective-permute-start | bytes 3145736 | tf_op jit(solution)/shard_map/ppermute | solution.py:58
  151.2 14.2 %collective-permute-start.24 = (bf16[2,256,512]{2,1,0:T(8,128)(2,1)S(1)}, bf16[2,256,512]{2,1,0:T(8,128)(2,1)S(1)}, u32[]{:S(2)}, u32[]{:S(2)}) collective-permute-start(bf16[2,256,512]{2,1,0:T(8,128)(2,1)S(1)} %get-tuple-element.756), channel_id=1, source_target_pairs={{0,2},{1,3},{8,10},{9,11},{16,18},{17,19},{24,26},{25,27}} | collective-permute-start | bytes 1572872 | tf_op jit(solution)/shard_map/ppermute | solution.py:266
  167.3 16.8 %collective-permute-start.28 = (bf16[16,64,2048]{2,1,0:T(8,128)(2,1)S(1)}, bf16[16,64,2048]{2,1,0:T(8,128)(2,1)S(1)}, u32[]{:S(2)}, u32[]{:S(2)}) collective-permute-start(bf16[16,64,2048]{2,1,0:T(8,128)(2,1)S(1)} %settle.4.own.wo_own.g_own), channel_id=1, source_target_pairs={{0,1},{1,0},{2,3},{3,2},{4,5},{5,4},{6,7},{7,6},{8,9},{9,8},{10,11... | collective-permute-start | bytes 12582920 | tf_op jit(solution)/shard_map/ppermute | solution.py:39
  170.1 14.0 %collective-permute-start.29 = (bf16[4,64,2048]{2,1,0:T(8,128)(2,1)S(1)}, bf16[4,64,2048]{2,1,0:T(8,128)(2,1)S(1)}, u32[]{:S(2)}, u32[]{:S(2)}) collective-permute-start(bf16[4,64,2048]{2,1,0:T(8,128)(2,1)S(1)} %join.11.refs_0_), channel_id=1, source_target_pairs={{0,2},{1,9},{2,0},{3,11},{4,6},{5,13},{6,4},{7,15},{8,10},{9,1},{1... | collective-permute-start | bytes 3145736 | tf_op jit(solution)/shard_map/ppermute | solution.py:58
  184.3 14.0 %collective-permute-start.31 = (bf16[4,64,2048]{2,1,0:T(8,128)(2,1)S(1)}, bf16[4,64,2048]{2,1,0:T(8,128)(2,1)S(1)}, u32[]{:S(2)}, u32[]{:S(2)}) collective-permute-start(bf16[4,64,2048]{2,1,0:T(8,128)(2,1)S(1)} %join.11.refs_0_), channel_id=1, source_target_pairs={{0,8},{1,17},{2,10},{3,19},{4,12},{5,21},{6,14},{7,23},{8,0},{9,25... | collective-permute-start | bytes 3145736 | tf_op jit(solution)/shard_map/ppermute | solution.py:58
  207.0 13.9 %collective-permute-start.33 = (bf16[4,64,2048]{2,1,0:T(8,128)(2,1)S(1)}, bf16[4,64,2048]{2,1,0:T(8,128)(2,1)S(1)}, u32[]{:S(2)}, u32[]{:S(2)}) collective-permute-start(bf16[4,64,2048]{2,1,0:T(8,128)(2,1)S(1)} %collective-permute-done.29.refs_1_), channel_id=1, source_target_pairs={{0,8},{1,17},{2,10},{3,19},{4,12},{5,21},{6,14},{7,23},{8,0},{9,25... | collective-permute-start | bytes 3145736 | tf_op jit(solution)/shard_map/ppermute | solution.py:58
  224.0 8.3 %collective-permute-start.34 = (bf16[16,64,2048]{2,1,0:T(8,128)(2,1)S(1)}, bf16[16,64,2048]{2,1,0:T(8,128)(2,1)S(1)}, u32[]{:S(2)}, u32[]{:S(2)}) collective-permute-start(bf16[16,64,2048]{2,1,0:T(8,128)(2,1)S(1)} %settle.5.up_own.down_own), channel_id=1, source_target_pairs={{0,1},{1,0},{2,3},{3,2},{4,5},{5,4},{6,7},{7,6},{8,9},{9,8},{10,11... | collective-permute-start | bytes 12582920 | tf_op jit(solution)/shard_map/ppermute | solution.py:39
  264.5 12.8 %collective-permute-start.35 = (bf16[16,64,2048]{2,1,0:T(8,128)(2,1)}, bf16[16,64,2048]{2,1,0:T(8,128)(2,1)S(1)}, u32[]{:S(2)}, u32[]{:S(2)}) collective-permute-start(bf16[16,64,2048]{2,1,0:T(8,128)(2,1)} %get-tuple-element.502), channel_id=1, source_target_pairs={{0,1},{1,0},{2,3},{3,2},{4,5},{5,4},{6,7},{7,6},{8,9},{9,8},{10,11... | collective-permute-start | bytes 12582920 | tf_op jit(solution)/shard_map/ppermute | solution.py:39
  280.3 14.0 %collective-permute-start.38 = (bf16[4,64,2048]{2,1,0:T(8,128)(2,1)S(1)}, bf16[4,64,2048]{2,1,0:T(8,128)(2,1)S(1)}, u32[]{:S(2)}, u32[]{:S(2)}) collective-permute-start(bf16[4,64,2048]{2,1,0:T(8,128)(2,1)S(1)} %add_convert_fusion.7), channel_id=1, source_target_pairs={{0,8},{1,17},{2,10},{3,19},{4,12},{5,21},{6,14},{7,23},{8,0},{9,25... | collective-permute-start | bytes 3145736 | tf_op jit(solution)/shard_map/ppermute | solution.py:58
  281.9 12.4 %collective-permute-start.37 = (bf16[2,256,512]{2,1,0:T(8,128)(2,1)S(1)}, bf16[2,256,512]{2,1,0:T(8,128)(2,1)S(1)}, u32[]{:S(2)}, u32[]{:S(2)}) collective-permute-start(bf16[2,256,512]{2,1,0:T(8,128)(2,1)S(1)} %fusion.24), channel_id=1, source_target_pairs={{6,4},{7,5},{14,12},{15,13},{22,20},{23,21},{30,28},{31,29}} | collective-permute-start | bytes 1572872 | tf_op jit(solution)/shard_map/ppermute | solution.py:266
  296.6 21.6 %collective-permute-start.41 = (bf16[4,64,2048]{2,1,0:T(8,128)(2,1)S(1)}, bf16[4,64,2048]{2,1,0:T(8,128)(2,1)S(1)}, u32[]{:S(2)}, u32[]{:S(2)}) collective-permute-start(bf16[4,64,2048]{2,1,0:T(8,128)(2,1)S(1)} %add_convert_fusion.6), channel_id=1, source_target_pairs={{0,8},{1,17},{2,10},{3,19},{4,12},{5,21},{6,14},{7,23},{8,0},{9,25... | collective-permute-start | bytes 3145736 | tf_op jit(solution)/shard_map/ppermute | solution.py:58
  299.0 19.3 %collective-permute-start.39 = (bf16[2,256,512]{2,1,0:T(8,128)(2,1)}, bf16[2,256,512]{2,1,0:T(8,128)(2,1)S(1)}, u32[]{:S(2)}, u32[]{:S(2)}) collective-permute-start(bf16[2,256,512]{2,1,0:T(8,128)(2,1)} %get-tuple-element.755), channel_id=1, source_target_pairs={{4,2},{5,3},{12,10},{13,11},{20,18},{21,19},{28,26},{29,27}} | collective-permute-start | bytes 1572872 | tf_op jit(solution)/shard_map/ppermute | solution.py:266
  299.7 18.6 %collective-permute-start.40 = (bf16[2,256,512]{2,1,0:T(8,128)(2,1)S(1)}, bf16[2,256,512]{2,1,0:T(8,128)(2,1)S(1)}, u32[]{:S(2)}, u32[]{:S(2)}) collective-permute-start(bf16[2,256,512]{2,1,0:T(8,128)(2,1)S(1)} %get-tuple-element.754), channel_id=1, source_target_pairs={{6,4},{7,5},{14,12},{15,13},{22,20},{23,21},{30,28},{31,29}} | collective-permute-start | bytes 1572872 | tf_op jit(solution)/shard_map/ppermute | solution.py:266
  319.3 25.9 %collective-permute-start.44 = (bf16[16,64,2560]{2,1,0:T(8,128)(2,1)}, bf16[16,64,2560]{2,1,0:T(8,128)(2,1)S(1)}, u32[]{:S(2)}, u32[]{:S(2)}) collective-permute-start(bf16[16,64,2560]{2,1,0:T(8,128)(2,1)} %get-tuple-element.561), channel_id=1, source_target_pairs={{0,1},{1,0},{2,3},{3,2},{4,5},{5,4},{6,7},{7,6},{8,9},{9,8},{10,11... | collective-permute-start | bytes 15728648 | tf_op jit(solution)/shard_map/ppermute | solution.py:39
  323.5 21.7 %collective-permute-start.45 = (bf16[4,64,2048]{2,1,0:T(8,128)(2,1)S(1)}, bf16[4,64,2048]{2,1,0:T(8,128)(2,1)S(1)}, u32[]{:S(2)}, u32[]{:S(2)}) collective-permute-start(bf16[4,64,2048]{2,1,0:T(8,128)(2,1)S(1)} %add_convert_fusion.5), channel_id=1, source_target_pairs={{0,2},{1,9},{2,0},{3,11},{4,6},{5,13},{6,4},{7,15},{8,10},{9,1},{1... | collective-permute-start | bytes 3145736 | tf_op jit(solution)/shard_map/ppermute | solution.py:58
  325.8 19.4 %collective-permute-start.42 = (bf16[2,256,512]{2,1,0:T(8,128)(2,1)S(1)}, bf16[2,256,512]{2,1,0:T(8,128)(2,1)S(1)}, u32[]{:S(2)}, u32[]{:S(2)}) collective-permute-start(bf16[2,256,512]{2,1,0:T(8,128)(2,1)S(1)} %get-tuple-element.759), channel_id=1, source_target_pairs={{2,0},{3,1},{10,8},{11,9},{18,16},{19,17},{26,24},{27,25}} | collective-permute-start | bytes 1572872 | tf_op jit(solution)/shard_map/ppermute | solution.py:266
  327.4 17.8 %collective-permute-start.43 = (bf16[2,256,512]{2,1,0:T(8,128)(2,1)S(1)}, bf16[2,256,512]{2,1,0:T(8,128)(2,1)S(1)}, u32[]{:S(2)}, u32[]{:S(2)}) collective-permute-start(bf16[2,256,512]{2,1,0:T(8,128)(2,1)S(1)} %get-tuple-element.758), channel_id=1, source_target_pairs={{4,2},{5,3},{12,10},{13,11},{20,18},{21,19},{28,26},{29,27}} | collective-permute-start | bytes 1572872 | tf_op jit(solution)/shard_map/ppermute | solution.py:266
  345.6 23.3 %collective-permute-start.47 = (bf16[4,64,2560]{2,1,0:T(8,128)(2,1)S(1)}, bf16[4,64,2560]{2,1,0:T(8,128)(2,1)S(1)}, u32[]{:S(2)}, u32[]{:S(2)}) collective-permute-start(bf16[4,64,2560]{2,1,0:T(8,128)(2,1)S(1)} %add_convert_fusion.2), channel_id=1, source_target_pairs={{0,8},{1,17},{2,10},{3,19},{4,12},{5,21},{6,14},{7,23},{8,0},{9,25... | collective-permute-start | bytes 3932168 | tf_op jit(solution)/shard_map/ppermute | solution.py:58
  348.5 12.4 %collective-permute-start.48 = (bf16[2,64,2048]{2,1,0:T(8,128)(2,1)S(1)}, bf16[2,64,2048]{2,1,0:T(8,128)(2,1)S(1)}, u32[]{:S(2)}, u32[]{:S(2)}) collective-permute-start(bf16[2,64,2048]{2,1,0:T(8,128)(2,1)S(1)} %add_convert_fusion.14), channel_id=1, source_target_pairs={{0,16},{1,3},{2,18},{3,1},{4,20},{5,7},{6,22},{7,5},{8,24},{9,11},... | collective-permute-start | bytes 1572872 | tf_op jit(solution)/shard_map/ppermute | solution.py:58
  354.9 14.0 %collective-permute-start.46 = (bf16[2,256,512]{2,1,0:T(8,128)(2,1)S(1)}, bf16[2,256,512]{2,1,0:T(8,128)(2,1)S(1)}, u32[]{:S(2)}, u32[]{:S(2)}) collective-permute-start(bf16[2,256,512]{2,1,0:T(8,128)(2,1)S(1)} %fusion.3), channel_id=1, source_target_pairs={{2,0},{3,1},{10,8},{11,9},{18,16},{19,17},{26,24},{27,25}} | collective-permute-start | bytes 1572872 | tf_op jit(solution)/shard_map/ppermute | solution.py:266
  376.6 16.8 %collective-permute-start.51 = (bf16[4,64,2560]{2,1,0:T(8,128)(2,1)S(1)}, bf16[4,64,2560]{2,1,0:T(8,128)(2,1)S(1)}, u32[]{:S(2)}, u32[]{:S(2)}) collective-permute-start(bf16[4,64,2560]{2,1,0:T(8,128)(2,1)S(1)} %add_convert_fusion.1), channel_id=1, source_target_pairs={{0,8},{1,17},{2,10},{3,19},{4,12},{5,21},{6,14},{7,23},{8,0},{9,25... | collective-permute-start | bytes 3932168 | tf_op jit(solution)/shard_map/ppermute | solution.py:58
  378.8 14.2 %collective-permute-start.50 = (bf16[1,64,2048]{2,1,0:T(8,128)(2,1)S(1)}, bf16[1,64,2048]{2,1,0:T(8,128)(2,1)S(1)}, u32[]{:S(2)}, u32[]{:S(2)}) collective-permute-start(bf16[1,64,2048]{2,1,0:T(8,128)(2,1)S(1)} %add_convert_fusion.17), channel_id=1, source_target_pairs={{0,4},{1,5},{2,6},{3,7},{4,0},{5,1},{6,2},{7,3},{8,12},{9,13},{10,... | collective-permute-start | bytes 786440 | tf_op jit(solution)/shard_map/ppermute | solution.py:58
  404.5 25.2 %collective-permute-start.54 = (bf16[4,64,2560]{2,1,0:T(8,128)(2,1)}, bf16[4,64,2560]{2,1,0:T(8,128)(2,1)}, u32[]{:S(2)}, u32[]{:S(2)}) collective-permute-start(bf16[4,64,2560]{2,1,0:T(8,128)(2,1)} %add_convert_fusion), channel_id=1, source_target_pairs={{0,2},{1,9},{2,0},{3,11},{4,6},{5,13},{6,4},{7,15},{8,10},{9,1},{1... | collective-permute-start | bytes 3932168 | tf_op jit(solution)/shard_map/ppermute | solution.py:58
  405.9 16.4 %collective-permute-start.53 = (bf16[4,64,1536]{2,1,0:T(8,128)(2,1)}, bf16[4,64,1536]{2,1,0:T(8,128)(2,1)}, u32[]{:S(2)}, u32[]{:S(2)}) collective-permute-start(bf16[4,64,1536]{2,1,0:T(8,128)(2,1)} %add_convert_fusion.12), channel_id=1, source_target_pairs={{0,8},{1,17},{2,10},{3,19},{4,12},{5,21},{6,14},{7,23},{8,0},{9,25... | collective-permute-start | bytes 2359304 | tf_op jit(solution)/shard_map/ppermute | solution.py:58
  436.4 13.1 %collective-permute-start.57 = (bf16[2,64,2560]{2,1,0:T(8,128)(2,1)}, bf16[2,64,2560]{2,1,0:T(8,128)(2,1)S(1)}, u32[]{:S(2)}, u32[]{:S(2)}) collective-permute-start(bf16[2,64,2560]{2,1,0:T(8,128)(2,1)} %add_convert_fusion.13), channel_id=1, source_target_pairs={{0,16},{1,3},{2,18},{3,1},{4,20},{5,7},{6,22},{7,5},{8,24},{9,11},... | collective-permute-start | bytes 1966088 | tf_op jit(solution)/shard_map/ppermute | solution.py:58
  439.4 14.0 %collective-permute-start.55 = (bf16[4,64,1536]{2,1,0:T(8,128)(2,1)S(1)}, bf16[4,64,1536]{2,1,0:T(8,128)(2,1)S(1)}, u32[]{:S(2)}, u32[]{:S(2)}) collective-permute-start(bf16[4,64,1536]{2,1,0:T(8,128)(2,1)S(1)} %get-tuple-element.749), channel_id=1, source_target_pairs={{0,8},{1,17},{2,10},{3,19},{4,12},{5,21},{6,14},{7,23},{8,0},{9,25... | collective-permute-start | bytes 2359304 | tf_op jit(solution)/shard_map/ppermute | solution.py:58
  440.4 18.0 %collective-permute-start.56 = (bf16[4,64,1536]{2,1,0:T(8,128)(2,1)S(1)}, bf16[4,64,1536]{2,1,0:T(8,128)(2,1)S(1)}, u32[]{:S(2)}, u32[]{:S(2)}) collective-permute-start(bf16[4,64,1536]{2,1,0:T(8,128)(2,1)S(1)} %get-tuple-element.748), channel_id=1, source_target_pairs={{0,2},{1,9},{2,0},{3,11},{4,6},{5,13},{6,4},{7,15},{8,10},{9,1},{1... | collective-permute-start | bytes 2359304 | tf_op jit(solution)/shard_map/ppermute | solution.py:58
  460.6 17.6 %collective-permute-start.64 = (bf16[1,64,2560]{2,1,0:T(8,128)(2,1)S(1)}, bf16[1,64,2560]{2,1,0:T(8,128)(2,1)S(1)}, u32[]{:S(2)}, u32[]{:S(2)}) collective-permute-start(bf16[1,64,2560]{2,1,0:T(8,128)(2,1)S(1)} %add_convert_fusion.16), channel_id=1, source_target_pairs={{0,4},{1,5},{2,6},{3,7},{4,0},{5,1},{6,2},{7,3},{8,12},{9,13},{10,... | collective-permute-start | bytes 983048 | tf_op jit(solution)/shard_map/ppermute | solution.py:58
  463.1 17.2 %collective-permute-start.61 = (bf16[2,64,1536]{2,1,0:T(8,128)(2,1)S(1)}, bf16[2,64,1536]{2,1,0:T(8,128)(2,1)S(1)}, u32[]{:S(2)}, u32[]{:S(2)}) collective-permute-start(bf16[2,64,1536]{2,1,0:T(8,128)(2,1)S(1)} %add_convert_fusion.15), channel_id=1, source_target_pairs={{0,16},{1,3},{2,18},{3,1},{4,20},{5,7},{6,22},{7,5},{8,24},{9,11},... | collective-permute-start | bytes 1179656 | tf_op jit(solution)/shard_map/ppermute | solution.py:58
  481.9 11.6 %collective-permute-start.66 = (bf16[1,64,1536]{2,1,0:T(8,128)(2,1)S(1)}, bf16[1,64,1536]{2,1,0:T(8,128)(2,1)S(1)}, u32[]{:S(2)}, u32[]{:S(2)}) collective-permute-start(bf16[1,64,1536]{2,1,0:T(8,128)(2,1)S(1)} %add_convert_fusion.18), channel_id=1, source_target_pairs={{0,4},{1,5},{2,6},{3,7},{4,0},{5,1},{6,2},{7,3},{8,12},{9,13},{10,... | collective-permute-start | bytes 589832 | tf_op jit(solution)/shard_map/ppermute | solution.py:58
  483.2 11.9 %collective-permute-start.65 = (f32[32,1536]{1,0:T(8,128)S(1)}, f32[32,1536]{1,0:T(8,128)S(1)}, u32[]{:S(2)}, u32[]{:S(2)}) collective-permute-start(f32[32,1536]{1,0:T(8,128)S(1)} %get-tuple-element.779), channel_id=1, source_target_pairs={{0,1},{1,0},{2,3},{3,2},{4,5},{5,4},{6,7},{7,6},{8,9},{9,8},{10,11... | collective-permute-start | bytes 589832 | tf_op jit(solution)/shard_map/ppermute | solution.py:39
  (101 other events, 952.6 us)

commit v4 on v3

--- a/solution.py
+++ b/solution.py
@@ -12,6 +12,7 @@
 F32 = jnp.float32
 BF16 = jnp.bfloat16
 FAR = 4
+LONE, EDGE, EVEN = range(3)
 MIB = 1024 * 1024
 
 
@@ -47,18 +48,23 @@
     return lax.optimization_barrier(values)
 
 
-def orders():
+def orders(kind):
     bits = [1 << k for k in range(1, devices().bit_length() - 1)]
     near = [bit for bit in bits if bit not in (2, FAR)]
-    return (near[:1] + [2] + near[1:] + [FAR], near[1:] + near[:1] + [2, FAR])
-
-
-def step(values, turn):
-    pairs = [(i, i ^ orders()[i % 2][turn]) for i in range(devices())]
+    turned = near[1:] + near[:1]
+    return {
+        LONE: (near[:1] + [2] + near[1:] + [FAR], turned + [2, FAR]),
+        EDGE: (near + [2, FAR], turned + [2, FAR]),
+        EVEN: (near[:1] + [2] + near[1:] + [FAR], turned[:1] + [2] + turned[1:] + [FAR]),
+    }[kind]
+
+
+def step(values, turn, kind):
+    pairs = [(i, i ^ orders(kind)[i % 2][turn]) for i in range(devices())]
     return lax.ppermute(values, AXES, pairs)
 
 
-def chip_tables():
+def chip_tables(kind):
     count = devices() // 2
     me, core = place() // 2, lax.axis_index("seq") % 2
     every = jnp.arange(count, dtype=jnp.int32)
@@ -67,17 +73,19 @@
         return sum(((values >> s) & 1) << t for s, t in zip(sources, targets))
 
     spots, chips = [], []
-    for order in orders():
+    for order in orders(kind):
         sources = [bit.bit_length() - 2 for bit in order]
         targets = list(range(len(order)))[::-1]
         spots.append(spread_bits(every ^ me, sources, targets))
         chips.append(spread_bits(every, targets, sources) ^ me)
+    swapped = core == 1
     return jnp.concatenate(
         [
             jnp.stack([me, core]),
-            jnp.where(core == 1, spots[1], spots[0]),
-            jnp.where(core == 1, chips[1], chips[0]),
-            jnp.where(core == 1, spots[0], spots[1]),
+            jnp.where(swapped, spots[1], spots[0]),
+            jnp.where(swapped, spots[0], spots[1]),
+            jnp.where(swapped, chips[1], chips[0]),
+            jnp.where(swapped, chips[0], chips[1]),
         ]
     ).astype(jnp.int32)
 
@@ -149,7 +157,7 @@
     return local(body, outs, part, got, name="join")[0]
 
 
-def settle(info, *pieces):
+def settle(info, pieces, own):
     lengths = [piece.shape[0] for piece in pieces]
     chips = sum(lengths)
 
@@ -157,7 +165,7 @@
         at = 0
         for ref, length in zip(refs, lengths):
             for block in range(length):
-                refs[-1][info_ref[2 + chips + at]] = ref[block]
+                refs[-1][info_ref[2 + (2 if own else 3) * chips + at]] = ref[block]
                 at += 1
 
     outs = [((chips,) + pieces[0].shape[1:], BF16)]
@@ -192,14 +200,21 @@
     return length // 2, length
 
 
-def shrink(pieces, turn, part=None):
+def upper_part(pieces, turn, part=None):
     start, stop = span(turn)
     shift = start
     if part is not None:
         middle = (start + stop) // 2
         start, stop = (middle, stop) if part else (start, middle)
-    send = summed(pieces, start, stop).astype(BF16)
-    return [Piece(step(send, turn), start - shift)]
+    return Piece(summed(pieces, start, stop).astype(BF16), start - shift)
+
+
+def send(piece, turn, kind):
+    return [Piece(step(piece.array, turn, kind), piece.start)]
+
+
+def shrink(pieces, turn, kind, part=None):
+    return send(upper_part(pieces, turn, part), turn, kind)
 
 
 def ordered(mine, other, axis):
@@ -225,51 +240,71 @@
     return ordered(mine, swap(give, 1), 1)
 
 
-def states_of(carry, near_carry, own, near, reverse):
+def phase_count(rows):
+    return lax.axis_size("seq") // 2 - 1 + rows - 1
+
+
+def chip_place(reverse):
+    chips = lax.axis_size("seq") // 2
+    at = lax.axis_index("seq") // 2
+    return chips - 1 - at if reverse else at
+
+
+def row_at(phase, rows, reverse):
+    return jnp.clip(phase - 1 - chip_place(reverse), 0, rows - 1)
+
+
+def factors_of(carry, near_carry, reverse):
+    rows = carry.shape[0]
     upper = upper_core()
     turned = jnp.logical_not(upper) if reverse else upper
     one, zero = jnp.ones_like(carry), jnp.zeros_like(carry)
 
     def either(yes, no):
-        return jnp.where(turned, yes, no)[:, :, None, None]
-
-    passed = (either(one, near_carry), either(carry, one), (carry * near_carry)[:, :, None, None])
+        return jnp.where(turned, yes, no)
+
+    table = (either(one, near_carry), either(carry, one), carry * near_carry)
+    passed = []
+    for phase in range(1, phase_count(rows) + 1):
+        row = row_at(phase, rows, reverse)
+        passed.append([
+            sum(jnp.where(row == k, factor[k], 0.0) for k in range(rows))[:, None, None]
+            for factor in table
+        ])
     mine = (either(zero, zero), either(one, zero), either(near_carry, one))
     theirs = (either(zero, one), either(zero, zero), either(one, carry))
-    return (passed, mine, theirs, own, near)
-
-
-def entered(arrived, row):
-    total = None
-    for arrivals in arrived:
-        if arrivals[row] is not None:
-            value = arrivals[row].astype(F32)
-            total = value if total is None else total + value
-    return total
+    return passed, [[f[:, :, None, None] for f in side] for side in (mine, theirs)]
 
 
 def hop(states, arrived, phase, reverse):
-    (a, b, c), _, _, own, near = states
+    passed, _, own, near = states
+    rows = own.shape[0]
+    row = row_at(phase, rows, reverse)
+    a, b, c = passed[phase - 1]
+    message = a * lax.dynamic_index_in_dim(own, row, 0, False)
+    message = message + b * lax.dynamic_index_in_dim(near, row, 0, False)
+    if arrived:
+        message = message + c * arrived[-1].astype(F32)
     chips = lax.axis_size("seq") // 2
-    arrivals = []
-    for row in range(own.shape[1]):
-        step = phase - row
-        if not 1 <= step < chips:
-            arrivals.append(None)
-            continue
-        message = a[:, row] * own[:, row] + b[:, row] * near[:, row]
-        before = entered(arrived, row)
-        if before is not None:
-            message = message + c[:, row] * before
-        source, target = (step - 1, step) if not reverse else (chips - step, chips - step - 1)
-        pairs = [(2 * source + core, 2 * target + core) for core in range(2)]
-        arrivals.append(lax.ppermute(message.astype(BF16), "seq", pairs))
-    return arrivals
-
-
-def end_states(states, arrived):
-    _, mine, theirs, own, near = states
-    before = jnp.stack([entered(arrived, row) for row in range(own.shape[1])], axis=1)
+    pairs = []
+    for at in range(chips - 1):
+        if 0 <= phase - 1 - at < rows:
+            source, target = (chips - 1 - at, chips - 2 - at) if reverse else (at, at + 1)
+            pairs += [(2 * source + core, 2 * target + core) for core in range(2)]
+    return lax.ppermute(message.astype(BF16), "seq", pairs)
+
+
+def end_states(states, arrived, reverse):
+    _, (mine, theirs), own, near = states
+    at = chip_place(reverse)
+    chips = lax.axis_size("seq") // 2
+    before = []
+    for row in range(own.shape[0]):
+        value = jnp.zeros_like(arrived[0])
+        for other in range(1, chips):
+            value = jnp.where(at == other, arrived[row + other - 1], value)
+        before.append(value.astype(F32))
+    before = jnp.stack(before)
 
     def taken(factors):
         a, b, c = factors
@@ -279,9 +314,11 @@
 
 
 def call(body, grid, info, ins, outs, scratch, flops, name, vmem):
-    def spec(block, index):
+    def spec(shape, block, index, once):
         if block is None:
             return pl.BlockSpec(memory_space=pltpu.SMEM)
+        if once and block == shape and name == "feed":
+            return pl.BlockSpec(block, index, pipeline_mode=pl.Buffered(1))
         return pl.BlockSpec(block, index)
 
     moved = sum(a.size * a.dtype.itemsize for a, _, _ in ins)
@@ -295,8 +332,8 @@
         grid_spec=pltpu.PrefetchScalarGridSpec(
             num_scalar_prefetch=1,
             grid=(grid,),
-            in_specs=[spec(block, index) for _, block, index in ins],
-            out_specs=[spec(block, index) for _, _, block, index in outs],
+            in_specs=[spec(a.shape, block, index, True) for a, block, index in ins],
+            out_specs=[spec(shape, block, index, False) for shape, _, block, index in outs],
             scratch_shapes=scratch,
         ),
         out_shape=[jax.ShapeDtypeStruct(shape, dtype) for shape, dtype, _, _ in outs],
@@ -328,24 +365,27 @@
     return (shape, dtype, (1,) + shape[1:], lambda h, info: (h,) + rest)
 
 
+def state_block(shape, own):
+    block = (shape[0], 1) + shape[2:]
+    if own:
+        return block, lambda h, info: (0, jnp.minimum(h, 1), 0, 0)
+    return block, lambda h, info: (0, jnp.maximum(h - 2, 0), 0, 0)
+
+
 def own_in(array):
-    rest = (0,) * (array.ndim - 1)
-    return (array, (1,) + array.shape[1:], lambda h, info: (jnp.minimum(h, 1),) + rest)
+    return (array,) + state_block(array.shape, True)
 
 
 def other_in(array):
-    rest = (0,) * (array.ndim - 1)
-    return (array, (1,) + array.shape[1:], lambda h, info: (jnp.maximum(h - 2, 0),) + rest)
+    return (array,) + state_block(array.shape, False)
 
 
 def own_out(shape, dtype):
-    rest = (0,) * (len(shape) - 1)
-    return (shape, dtype, (1,) + shape[1:], lambda h, info: (jnp.minimum(h, 1),) + rest)
+    return (shape, dtype) + state_block(shape, True)
 
 
 def other_out(shape, dtype):
-    rest = (0,) * (len(shape) - 1)
-    return (shape, dtype, (1,) + shape[1:], lambda h, info: (jnp.maximum(h - 2, 0),) + rest)
+    return (shape, dtype) + state_block(shape, False)
 
 
 def real(h, info):
@@ -391,7 +431,7 @@
     width = values.shape[1]
     values = values.astype(BF16)
     for chip in range(chips):
-        target[info[(2 if own else 2 + 2 * chips) + chip], :, start : start + width] = values[chip * rows : (chip + 1) * rows]
+        target[info[(2 if own else 2 + chips) + chip], :, start : start + width] = values[chip * rows : (chip + 1) * rows]
 
 
 def put_tall(target, info, values, block, start, own):
@@ -399,7 +439,7 @@
     values = values.astype(BF16)
     share = chips // 4
     for chip in range(share):
-        at = info[(2 if own else 2 + 2 * chips) + block * share + chip]
+        at = info[(2 if own else 2 + chips) + block * share + chip]
         base = 2 * rows * chip
         target[at, :, start : start + 512] = values[base : base + rows]
         target[at, :, start + 512 : start + 1024] = values[base + rows : base + 2 * rows]
@@ -502,11 +542,11 @@
 
         @pl.when(h < 2)
         def _():
-            sum_own[0, row] = summary
+            sum_own[row, 0] = summary
 
         @pl.when(h >= 2)
         def _():
-            sum_oth[0, row] = summary
+            sum_oth[row, 0] = summary
 
 
 def gate_kernel(info, normed, own, oth, out):
@@ -540,11 +580,11 @@
 
         @pl.when(h < 2)
         def _():
-            retained[0, at] = inner[0, at] + mm(entered, state_own[0, row])
+            retained[0, at] = inner[0, at] + mm(entered, state_own[row, 0])
 
         @pl.when(h >= 2)
         def _():
-            retained[0, at] = inner[0, at] + mm(entered, state_oth[0, row])
+            retained[0, at] = inner[0, at] + mm(entered, state_oth[row, 0])
 
     normal, _ = norm_parts(retained[0], 1.0)
     pre = gate[0]
@@ -666,11 +706,11 @@
 
         @pl.when(h < 2)
         def _():
-            state_own[0, row] = state
+            state_own[row, 0] = state
 
         @pl.when(h >= 2)
         def _():
-            state_oth[0, row] = state
+            state_oth[row, 0] = state
 
 
 def inside_kernel(
@@ -689,7 +729,7 @@
         enter = enter_of(rate, tall_count[row])
 
         def set_query(state):
-            total = mm(scores, key[0, at]) + nt(grad, state[0, row]) * enter
+            total = mm(scores, key[0, at]) + nt(grad, state[row, 0]) * enter
             grad_q[0, at] = unrotated(total, cosine[...], sine[...]).astype(BF16)
 
         @pl.when(h < 2)
@@ -705,15 +745,9 @@
 
 
 def outer_kernel(
-    info, grad_low, normed_t, mixed_t, grad_gate, grad_q, g_own, g_oth, q_own, q_oth,
-    norm_part, out_own, out_oth,
+    info, grad_low, normed_t, mixed_t, grad_gate, grad_q, out_own, out_oth,
 ):
     h = pl.program_id(0)
-
-    @pl.when(h == 0)
-    def _():
-        norm_part[...] = jnp.zeros_like(norm_part)
-
     block = real(h, info)
     left = mixed_t[0]
     put_tall(out_own, info, mm(left, grad_low[:, pl.ds(side(info, True), 512)]), block, 1024, True)
@@ -727,14 +761,6 @@
             target = out_own if step < 2 else out_oth
             put_wide(target, info, grad_wg, 512 * (step % 2), step < 2)
             put_wide(target, info, grad_wq, 2048 + 256 * (step % 2), step < 2)
-
-    @pl.when(h < 2)
-    def _():
-        norm_part[...] += nt(grad_gate[0], flat(g_own)) + nt(grad_q[0], flat(q_own))
-
-    @pl.when(h >= 2)
-    def _():
-        norm_part[...] += nt(grad_gate[0], flat(g_oth)) + nt(grad_q[0], flat(q_oth))
 
 
 def last_kernel(
@@ -751,7 +777,7 @@
         weighted = (key[0, at].astype(F32) * leave).astype(BF16)
 
         def set_both(state):
-            low = state[0, row]
+            low = state[row, 0]
             grad_v[0, at] = (value_part[0, at] + mm(weighted, low)).astype(BF16)
             total = key_part[0, at] + nt(value[0, at], low) * leave
             grad_k[0, at] = (unrotated(total, cosine[...], sine[...]) * QK**-0.5).astype(BF16)
@@ -776,22 +802,29 @@
 
 
 def input_kernel(
-    info, x, gain, grad_hidden, norm_part, grad_k, grad_v, k_own, k_oth, v_own, v_oth,
+    info, x, gain, grad_hidden, grad_q, grad_k, grad_v, grad_gate,
+    q_own, q_oth, k_own, k_oth, v_own, v_oth, g_own, g_oth,
     input_grad, grad_gain, grad_bias, norm_sum,
 ):
     h = pl.program_id(0)
 
     @pl.when(h == 0)
     def _():
-        norm_sum[...] = norm_part[...]
+        norm_sum[...] = jnp.zeros_like(norm_sum)
+
+    def add(wq, wk, wv, wg):
+        norm_sum[...] += (
+            nt(grad_q[0], flat(wq)) + nt(grad_k[0], flat(wk))
+            + nt(grad_v[0], flat(wv)) + nt(grad_gate[0], flat(wg))
+        )
 
     @pl.when(h < 2)
     def _():
-        norm_sum[...] += nt(grad_k[0], flat(k_own)) + nt(grad_v[0], flat(v_own))
+        add(q_own, k_own, v_own, g_own)
 
     @pl.when(h >= 2)
     def _():
-        norm_sum[...] += nt(grad_k[0], flat(k_oth)) + nt(grad_v[0], flat(v_oth))
+        add(q_oth, k_oth, v_oth, g_oth)
 
     @pl.when(h == 3)
     def _():
@@ -832,19 +865,19 @@
     tokens = rows * length
     count = devices()
     chips = count // 2
-    info = chip_tables()
+    info, info_edge = chip_tables(LONE), chip_tables(EDGE)
     x = inputs.reshape(tokens, width)
     cot = cotangent.reshape(tokens, width)
 
     upper = upper_core()
     share = w_query.shape[0]
-    last = len(orders()[0]) - 1
+    last = len(orders(LONE)[0]) - 1
 
     keep, give = pack(info, w_query, w_key, w_value)
     qkv = stack_rows(info, keep, swap(give, 1))
     vectors = [first_gain, first_bias, second_gain, second_bias, group_gain]
     qkv, vectors = sync(qkv, vectors)
-    got_qkv = step(qkv[None], last)
+    got_qkv = step(qkv[None], last, LONE)
 
     sizes = [v.shape[0] for v in vectors]
     edges = [sum(sizes[:k]) for k in range(len(sizes) + 1)]
@@ -863,13 +896,13 @@
 
     bits = [1 << k for k in range(count.bit_length() - 1)]
     done = []
-    for bit in bits[:1] + bits[3:]:
+    for bit in (1, FAR):
         table = table_step(table, done, bit)
     got_qkv, table = sync(got_qkv, table)
     part, got = qkv[None], got_qkv
     for turn in range(last - 1, 1, -1):
         part = join(part, got)
-        got = step(part, turn)
+        got = step(part, turn, LONE)
         if turn == last - 1:
             table = table_step(table, done, 2)
         part, got, table, w_gate, w_up, w_output, w_down, doc_flags = sync(
@@ -877,8 +910,9 @@
         )
 
     part = join(part, got)
-    got = step(part, 1)
-    table = table_step(table, done, FAR)
+    got = step(part, 1, LONE)
+    for bit in bits[:2:-1]:
+        table = table_step(table, done, bit)
 
     top_keep, top_give = pack(info, w_gate, w_up)
     tall_keep, tall_give = pack(info, w_output, w_down)
@@ -892,8 +926,9 @@
         part, got, go_part, ff_part, table, doc_flags
     )
 
-    pieces = [part, got, step(part, 0), step(got, 0)]
-    go_got = step(go_part, last)
+    pieces = [part, got, step(part, 0, LONE), step(got, 0, LONE)]
+    go_got = step(go_part, last, EDGE)
+    ff_got = step(ff_part, last, EDGE)
     vector = table.reshape(count, -1, lanes)[:, 0]
     first_gain, first_bias, second_gain, second_bias, group_gain = [
         vector[:, a:b].reshape(1, -1) for a, b in zip(edges[:-1], edges[1:])
@@ -911,10 +946,12 @@
     open_row = (counts[:, -1] == 0).astype(F32)
     near_row = swap(open_row, 1)
     decay = jnp.exp(rates[:2] * float(length))
-    carry, near_carry = decay[:, None] * open_row[None], decay[:, None] * near_row[None]
+    carry, near_carry = decay[None] * open_row[:, None], decay[None] * near_row[:, None]
+    ahead = factors_of(carry, near_carry, False)
+    behind = factors_of(carry, near_carry, True)
 
     per_head = (H, tokens)
-    state_shape = (2, rows, QK, VH)
+    state_shape = (rows, 2, QK, VH)
     grad_shape = (chips, 2 * share)
     rates_in = (rates, None, None)
     unit = 2.0 * tokens * width * 512
@@ -930,24 +967,27 @@
         "norm",
         16,
     )
-    pieces, go_part, go_got, normed, normed_t, tables, gains = sync(
-        pieces, go_part, go_got, normed, normed_t,
-        (cosine, sine, tall_count, wide_count, carry, near_carry, rates),
+    pieces, go_part, go_got, ff_part, ff_got, normed, normed_t, tables, gains = sync(
+        pieces, go_part, go_got, ff_part, ff_got, normed, normed_t,
+        (cosine, sine, tall_count, wide_count, ahead, behind, rates),
         (second_gain, second_bias, group_gain),
     )
-    cosine, sine, tall_count, wide_count, carry, near_carry, rates = tables
+    cosine, sine, tall_count, wide_count, ahead, behind, rates = tables
     second_gain, second_bias, group_gain = gains
     rates_in = (rates, None, None)
 
-    qkv_own = settle(info, *pieces)
+    qkv_own = settle(info, pieces, True)
     qkv_oth = swap(qkv_own, 1)
     go_part = join(go_part, go_got)
-    go_got = step(go_part, last - 1)
-    qkv_own, qkv_oth, go_part, go_got, ff_part = sync(qkv_own, qkv_oth, go_part, go_got, ff_part)
+    go_got = step(go_part, last - 1, EDGE)
+    qkv_own, qkv_oth, go_part, go_got, ff_part, ff_got = sync(
+        qkv_own, qkv_oth, go_part, go_got, ff_part, ff_got
+    )
 
     go_part = join(go_part, go_got)
-    go_got = step(go_part, last - 2)
-    ff_got = step(ff_part, last)
+    go_got = step(go_part, last - 2, EDGE)
+    ff_part = join(ff_part, ff_got)
+    ff_got = step(ff_part, last - 1, EDGE)
     (query, key, value, mixing, inner, sum_own, sum_oth) = call(
         project_kernel,
         H,
@@ -976,65 +1016,70 @@
     )
     for turn in range(last - 3, 0, -1):
         go_part = join(go_part, go_got)
-        go_got = step(go_part, turn)
+        go_got = step(go_part, turn, EDGE)
         ff_part = join(ff_part, ff_got)
-        ff_got = step(ff_part, turn + 2)
+        ff_got = step(ff_part, turn + 1, EDGE)
         go_part, go_got, ff_part, ff_got = sync(go_part, go_got, ff_part, ff_got)
     sum_near = swap(sum_oth, 1)
-    ff_part = join(ff_part, ff_got)
-    ff_got = step(ff_part, 2)
     sum_own, sum_near, go_part, go_got, ff_part, ff_got = sync(
         sum_own, sum_near, go_part, go_got, ff_part, ff_got
     )
 
-    states = states_of(carry, near_carry, sum_own, sum_near, False)
-    phases = lax.axis_size("seq") // 2 - 1 + rows - 1
+    states = tuple(ahead) + (sum_own, sum_near)
+    phases = phase_count(rows)
     arrivals = hop(states, [], 1, False)
-    go_first = step(go_part, 0)
+    go_first = step(go_part, 0, EDGE)
     states, arrivals, go_part, go_got, go_first = sync(
         states, arrivals, go_part, go_got, go_first
     )
     arrived = [arrivals]
 
     arrivals = hop(states, arrived, 2, False)
-    go_second = step(go_got, 0)
+    go_second = step(go_got, 0, EDGE)
     states, arrived, arrivals, pieces, ff_part, ff_got = sync(
         states, arrived, arrivals, [go_part, go_got, go_first, go_second], ff_part, ff_got
     )
     arrived = arrived + [arrivals]
 
     arrivals = hop(states, arrived, 3, False)
-    go_own = settle(info, *pieces)
-    go_oth = swap(go_own, 1)
     ff_part = join(ff_part, ff_got)
-    ff_got = step(ff_part, 1)
-    states, arrived, arrivals, go_own, go_oth, normed, ff_part, ff_got = sync(
-        states, arrived, arrivals, go_own, go_oth, normed, ff_part, ff_got
+    ff_got = step(ff_part, 1, EDGE)
+    states, arrived, arrivals, pieces, ff_part, ff_got = sync(
+        states, arrived, arrivals, pieces, ff_part, ff_got
     )
     arrived = arrived + [arrivals]
 
     for phase in range(4, phases + 1):
         arrivals = hop(states, arrived, phase, False)
         if phase == 4:
-            ff_first = step(ff_part, 0)
-            (gate,) = call(
-                gate_kernel,
-                H,
-                info,
-                [whole(normed), columns(go_own, 512, 0, True), columns(go_oth, 512, 0, False)],
-                [head_out(per_head + (VH,), F32)],
-                [],
-                4 * unit,
-                "gate",
-                20,
+            ff_first = step(ff_part, 0, EDGE)
+            ff_others = [swap(ff_part, 1), swap(ff_got, 1)]
+            go_own = settle(info_edge, pieces, True)
+            go_oth = swap(go_own, 1)
+        states, arrived, arrivals, go_own, go_oth, normed, ff_part, ff_got, ff_first, ff_others = (
+            sync(
+                states, arrived, arrivals, go_own, go_oth, normed, ff_part, ff_got, ff_first,
+                ff_others,
             )
-        states, arrived, arrivals, gate, ff_part, ff_got, ff_first = sync(
-            states, arrived, arrivals, gate, ff_part, ff_got, ff_first
         )
         arrived = arrived + [arrivals]
-    state_own, state_oth = end_states(states, arrived)
-    state_own, state_oth, ff_got = sync(state_own, state_oth, ff_got)
-    ff_second = step(ff_got, 0)
+    state_own, state_oth = end_states(states, arrived, False)
+    (gate,) = call(
+        gate_kernel,
+        H,
+        info,
+        [whole(normed), columns(go_own, 512, 0, True), columns(go_oth, 512, 0, False)],
+        [head_out(per_head + (VH,), F32)],
+        [],
+        4 * unit,
+        "gate",
+        20,
+    )
+    state_own, state_oth, gate, ff_got, ff_first = sync(
+        state_own, state_oth, gate, ff_got, ff_first
+    )
+    ff_second = step(ff_got, 0, EDGE)
+    ff_others = ff_others + [swap(ff_first, 1)]
 
     retained, mixed_t, hidden, normed_second, normed_second_t = call(
         mix_kernel,
@@ -1055,13 +1100,14 @@
         "mix",
         32,
     )
-    ff_second, hidden = sync(ff_second, hidden)
-    ff_own = settle(info, ff_part, ff_got, ff_first, ff_second)
-    ff_oth = swap(ff_own, 1)
+    ff_second, ff_others, hidden = sync(ff_second, ff_others, hidden)
+    ff_others = ff_others + [swap(ff_second, 1)]
+    ff_own = settle(info_edge, [ff_part, ff_got, ff_first, ff_second], True)
+    ff_oth = settle(info_edge, ff_others, False)
     output, grad_hidden, grad_low, grad_second_gain, grad_second_bias, ff_g_own, ff_g_oth = call(
         feed_kernel,
         4,
-        info,
+        info_edge,
         [
             whole(hidden), whole(normed_second), whole(normed_second_t), whole(cot),
             whole(second_gain),
@@ -1110,14 +1156,16 @@
     )
     gstate_near = swap(gstate_oth, 1)
     ff_sum = [Piece(ff_g_own), Piece(ff_g_got)]
-    gstate_own, gstate_near, grad_gate, grad_ret = sync(
-        gstate_own, gstate_near, grad_gate, grad_ret
-    )
-
-    states = states_of(carry, near_carry, gstate_own, gstate_near, True)
+    ff_first = upper_part(ff_sum, 0, 1)
+    gstate_own, gstate_near, grad_gate, grad_ret, ff_sum, ff_first = sync(
+        gstate_own, gstate_near, grad_gate, grad_ret, ff_sum, ff_first
+    )
+
+    states = tuple(behind) + (gstate_own, gstate_near)
     arrived = []
     arrivals = hop(states, arrived, 1, True)
-    ff_first = shrink(ff_sum, 0, 1)
+    ff_first = send(ff_first, 0, EDGE)
+    ff_second = upper_part(ff_sum, 0, 0)
     grad_q, key_part, value_part = call(
         inside_kernel,
         H,
@@ -1137,40 +1185,38 @@
         "inside",
         24,
     )
-    states, arrivals, ff_sum, ff_first, grad_q, key_part, value_part = sync(
-        states, arrivals, ff_sum, ff_first, grad_q, key_part, value_part
+    states, arrivals, ff_sum, ff_first, ff_second, grad_q, key_part, value_part = sync(
+        states, arrivals, ff_sum, ff_first, ff_second, grad_q, key_part, value_part
     )
     arrived = arrived + [arrivals]
 
     arrivals = hop(states, arrived, 2, True)
-    ff_sum = ff_sum + ff_first + shrink(ff_sum, 0, 0)
-    norm_part, go_g_own, go_g_oth = call(
+    ff_sum = ff_sum + ff_first
+    ff_second = send(ff_second, 0, EDGE)
+    ff_next = upper_part(ff_sum, 1)
+    go_g_own, go_g_oth = call(
         outer_kernel,
         H,
         info,
         [
             whole(grad_low), whole(normed_t), head_in(mixed_t), head_in(grad_gate),
             head_in(grad_q),
-            columns(go_own, 512, 0, True), columns(go_oth, 512, 0, False),
-            columns(qkv_own, 256, 0, True), columns(qkv_oth, 256, 0, False),
-        ],
-        [
-            whole_out((tokens, width), F32),
-            whole_out(grad_shape + (2560,), BF16), whole_out(grad_shape + (2560,), BF16),
-        ],
+        ],
+        [whole_out(grad_shape + (2560,), BF16), whole_out(grad_shape + (2560,), BF16)],
         [],
-        16 * unit,
+        11 * unit,
         "outer",
         44,
     )
-    states, arrived, arrivals, ff_sum, norm_part, go_g_own, go_g_oth = sync(
-        states, arrived, arrivals, ff_sum, norm_part, go_g_own, go_g_oth
-    )
+    states, arrived, arrivals, ff_sum, ff_second, ff_next, go_g_own, go_g_oth = sync(
+        states, arrived, arrivals, ff_sum, ff_second, ff_next, go_g_own, go_g_oth
+    )
+    ff_sum = ff_sum + ff_second
     arrived = arrived + [arrivals]
 
     arrivals = hop(states, arrived, 3, True)
     go_g_got = swap(go_g_oth, 1)
-    ff_sum = ff_sum + shrink(ff_sum, 1)
+    ff_sum = ff_sum + send(ff_next, 1, EDGE)
     states, arrived, arrivals, go_g_own, go_g_got, ff_sum = sync(
         states, arrived, arrivals, go_g_own, go_g_got, ff_sum
     )
@@ -1180,17 +1226,21 @@
     for phase in range(4, phases + 1):
         arrivals = hop(states, arrived, phase, True)
         if phase == 4:
-            go_first = shrink(go_sum, 0, 1)
-            ff_sum = ff_sum + shrink(ff_sum, 2)
-        states, arrived, arrivals, go_sum, go_first, ff_sum = sync(
-            states, arrived, arrivals, go_sum, go_first, ff_sum
+            go_first = shrink(go_sum, 0, LONE, 1)
+            go_second = upper_part(go_sum, 0, 0)
+            ff_next = upper_part(ff_sum, 2)
+        states, arrived, arrivals, go_sum, go_first, go_second, ff_sum, ff_next = sync(
+            states, arrived, arrivals, go_sum, go_first, go_second, ff_sum, ff_next
         )
         arrived = arrived + [arrivals]
-    after_own, after_oth = end_states(states, arrived)
-    after_own, after_oth, go_sum, ff_sum = sync(after_own, after_oth, go_sum, ff_sum)
-    go_sum = go_sum + go_first + shrink(go_sum, 0, 0)
-    for turn in range(3, last + 1):
-        ff_sum = ff_sum + shrink(ff_sum, turn)
+    after_own, after_oth = end_states(states, arrived, True)
+    after_own, after_oth, go_sum, go_first, go_second, ff_sum, ff_next = sync(
+        after_own, after_oth, go_sum, go_first, go_second, ff_sum, ff_next
+    )
+    go_sum = go_sum + go_first
+    go_next = upper_part(go_sum, 1)
+    go_second = send(go_second, 0, LONE)
+    ff_sum = ff_sum + send(ff_next, 2, EDGE)
 
     grad_k, grad_v, kv_g_own, kv_g_oth = call(
         last_kernel,
@@ -1210,23 +1260,32 @@
         "last",
         32,
     )
-    ff_sum, go_sum, kv_g_own, kv_g_oth, grad_k, grad_v = sync(
-        ff_sum, go_sum, kv_g_own, kv_g_oth, grad_k, grad_v
-    )
+    ff_sum, go_sum, go_second, go_next, kv_g_own, kv_g_oth, grad_k, grad_v = sync(
+        ff_sum, go_sum, go_second, go_next, kv_g_own, kv_g_oth, grad_k, grad_v
+    )
+    go_sum = go_sum + go_second
     kv_g_got = swap(kv_g_oth, 1)
-    kv_g_own, kv_g_got, go_sum = sync(kv_g_own, kv_g_got, go_sum)
+    ff_next = upper_part(ff_sum, 3)
+    kv_g_own, kv_g_got, go_sum, ff_sum, ff_next = sync(
+        kv_g_own, kv_g_got, go_sum, ff_sum, ff_next
+    )
     kv_sum = [Piece(kv_g_own), Piece(kv_g_got)]
-    kv_first = shrink(kv_sum, 0, 1)
-    go_next = shrink(go_sum, 1)
+    kv_first, kv_second = shrink(kv_sum, 0, LONE, 1), shrink(kv_sum, 0, LONE, 0)
+    go_next = send(go_next, 1, LONE)
+    ff_sum = ff_sum + send(ff_next, 3, EDGE)
+    for turn in range(4, last + 1):
+        ff_sum = ff_sum + shrink(ff_sum, turn, EDGE)
     input_grad, grad_first_gain, grad_first_bias = call(
         input_kernel,
         H,
         info,
         [
-            whole(x), whole(first_gain), whole(grad_hidden), whole(norm_part),
-            head_in(grad_k), head_in(grad_v),
+            whole(x), whole(first_gain), whole(grad_hidden), head_in(grad_q),
+            head_in(grad_k), head_in(grad_v), head_in(grad_gate),
+            columns(qkv_own, 256, 0, True), columns(qkv_oth, 256, 0, False),
             columns(qkv_own, 256, 2, True), columns(qkv_oth, 256, 2, False),
             columns(qkv_own, 512, 2, True), columns(qkv_oth, 512, 2, False),
+            columns(go_own, 512, 0, True), columns(go_oth, 512, 0, False),
         ],
         [
             whole_out((tokens, width), F32), whole_out((1, width), F32),
@@ -1237,41 +1296,42 @@
         "input",
         56,
     )
-    kv_sum, kv_first, go_sum, go_next, ff_sum, input_grad, grad_first_gain, grad_first_bias = sync(
-        kv_sum, kv_first, go_sum, go_next, ff_sum, input_grad, grad_first_gain, grad_first_bias
-    )
-    small = [grad_first_gain, grad_first_bias, grad_second_gain, grad_second_bias, grad_group_gain]
-    small = jnp.concatenate([part.reshape(count, -1) for part in small], axis=1)
-    small = jnp.pad(small, ((0, 0), (0, lanes - edges[-1])))
-    small = small.reshape((2,) * len(bits) + (1, lanes))
-
-    def small_step(small, bit):
-        turned = (place() // bit) % 2 == 1
-        got = swap(jnp.where(turned, small[0], small[1]), bit)
-        return jnp.where(turned, small[1], small[0]) + got
-
-    kv_sum = kv_sum + kv_first
+    kv_sum, kv_first, kv_second, go_sum, go_next, ff_sum, input_grad, sums = sync(
+        kv_sum, kv_first, kv_second, go_sum, go_next, ff_sum, input_grad,
+        (grad_first_gain, grad_first_bias),
+    )
+    grad_first_gain, grad_first_bias = sums
+    small = jnp.concatenate(
+        [
+            grad_first_gain, grad_first_bias, grad_second_gain, grad_second_bias,
+            grad_group_gain.reshape(-1, width), jnp.zeros((2, width), F32),
+        ],
+        axis=0,
+    )
+
+    kv_sum = kv_sum + kv_first + kv_second
     go_sum = go_sum + go_next
-    kv_second, kv_next = shrink(kv_sum, 0, 0), shrink(kv_sum, 1)
-    go_next = shrink(go_sum, 2)
-    for bit in bits[:1:-1]:
-        small = small_step(small, bit)
-    kv_sum, kv_second, kv_next, go_sum, go_next, small = sync(
-        kv_sum, kv_second, kv_next, go_sum, go_next, small
-    )
-    kv_sum = kv_sum + kv_second + kv_next
+    kv_next = shrink(kv_sum, 1, LONE)
+    go_next = shrink(go_sum, 2, LONE)
+    for bit in bits[:2:-1]:
+        small = small + swap(small, bit)
+    kv_sum, kv_next, go_sum, go_next, small = sync(kv_sum, kv_next, go_sum, go_next, small)
+    kv_sum = kv_sum + kv_next
     go_sum = go_sum + go_next
-    kv_next = shrink(kv_sum, 2)
+    kv_next = shrink(kv_sum, 2, LONE)
     for turn in range(3, last + 1):
-        go_sum = go_sum + shrink(go_sum, turn)
-    for bit in bits[1::-1]:
-        small = small_step(small, bit)
+        go_sum = go_sum + shrink(go_sum, turn, LONE)
+    small = small + swap(small, bits[2])
     ff_grad = summed(ff_sum, 0, 1)[0]
     kv_sum, kv_next, small, ff_grad = sync(kv_sum, kv_next, small, ff_grad)
     kv_sum = kv_sum + kv_next
     for turn in range(3, last + 1):
-        kv_sum = kv_sum + shrink(kv_sum, turn)
-    small = [small[0, a:b] for a, b in zip(edges[:-1], edges[1:])]
+        kv_sum = kv_sum + shrink(kv_sum, turn, LONE)
+    for bit in bits[1::-1]:
+        small = small + swap(small, bit)
+    group = small[4:6].reshape(-1)
+    small = lax.dynamic_slice_in_dim(small, place() * sizes[0], sizes[0], 1)
+    group = lax.dynamic_slice_in_dim(group, place() * sizes[4], sizes[4], 0)
 
     go_grad, kv_grad = summed(go_sum, 0, 1)[0], summed(kv_sum, 0, 1)[0]
     ff_mine, ff_got = finish_wide(ff_grad[:, :1024])
@@ -1290,7 +1350,7 @@
         wide(kv_mine, kv_got, 0, 512),
         wide(kv_mine, kv_got, 512, 1536),
         wide(go_mine, go_got, 0, 1024),
-        small[4],
+        group,
         finish_tall(go_grad[:, 1024:2048]),
         small[2],
         small[3],

time: 508 us -> 484 us (0.953)
  waiting for transfers between devices: 196 us -> 164 us
  Pallas kernels: 128 us -> 135 us
    ppermute x30, waiting for transfers between devices: 118 us -> 74.9 us  [step(): return lax.ppermute(values, AXES, pairs)]
    pallas_call x14 -> x15, Pallas kernels: 7.92 us -> 14.9 us  [local(): pl.pallas_call(body, grid=(1,), out_shape=[jax.ShapeDtypeStruct(shape, dt...]
    ppermute x12 -> x8, waiting for transfers between devices: 43.9 us -> 50.4 us  [hop(): return lax.ppermute(message.astype(BF16), 'seq', pairs)]
    ppermute x29 -> x32, waiting for transfers between devices: 33.6 us -> 39.1 us  [swap(): return lax.ppermute(values, AXES, [(i, i ^ bit) for i in range(devices())])]
    ppermute x29 -> x32, starting transfers between devices: 36.2 us -> 41.2 us  [swap(): return lax.ppermute(values, AXES, [(i, i ^ bit) for i in range(devices())])]
    ppermute x12 -> x8, starting transfers between devices: 17.1 us -> 14.6 us  [hop(): return lax.ppermute(message.astype(BF16), 'seq', pairs)]
    convert_element_type x22 -> x21, other arithmetic: 39.2 us -> 37.6 us  [the longest x13 29.6 us: upper_part(): return Piece(summed(pieces, start, stop).astype(BF16), start - shift)]
    unnamed x157 -> x229, local copies, waits for them, and re-layouts: 22.7 us -> 22.9 us
  transfers between devices with their start and end apart: 71 -> 70, of which waited for: 34 -> 25; matrix products, arithmetic and copies ran while one was open for 10% -> 10% of each run, Pallas kernels for 19% -> 21%
where the time goes in v4:
time: 484 us; the launch traced here: 475 us
  waiting for transfers between devices  164 us (34%)
  Pallas kernels  135 us (28%)
  starting transfers between devices  84.9 us (18%)
  other arithmetic  60.3 us (12%)
  local copies, waits for them, and re-layouts  27.1 us (6%)
    pallas_call x10, Pallas kernels, call(): pl.pallas_call(body, grid_spec=pltpu.PrefetchScalarGridSpec(num_scalar_pr...  120 us
    ppermute x30, waiting for transfers between devices, step(): return lax.ppermute(values, AXES, pairs)  74.9 us
    ppermute x8, waiting for transfers between devices, hop(): return lax.ppermute(message.astype(BF16), 'seq', pairs)  50.4 us
    ppermute x32, starting transfers between devices, swap(): return lax.ppermute(values, AXES, [(i, i ^ bit) for i in range(devices())])  41.2 us
    ppermute x32, waiting for transfers between devices, swap(): return lax.ppermute(values, AXES, [(i, i ^ bit) for i in range(devices())])  39.1 us
    convert_element_type x13, other arithmetic, upper_part(): return Piece(summed(pieces, start, stop).astype(BF16), start - shift)  29.6 us
    ppermute x30, starting transfers between devices, step(): return lax.ppermute(values, AXES, pairs)  29.2 us
    unnamed x229, local copies, waits for them, and re-layouts  22.9 us
  transfers between devices with their start and end apart: 70, of which 25 were waited for; matrix products, arithmetic and copies ran while one was open for 10% of the time, Pallas kernels for 21%

profile of v4, /device:TPU:1, one launch (start us, length us, event | category | flops | bytes accessed | tf_op | source)
XLA Modules:
  0.0 475.0 jit_solution(7373815646581920116)
XLA Ops:
  8.3 3.7 collective-permute-start.3
  13.1 12.9 %collective-permute-done.1.got_ref = bf16[1,64,2048]{2,1,0:T(8,128)(2,1)S(1)} collective-permute-done((bf16[1,64,2048]{2,1,0:T(8,128)(2,1)S(1)}, bf16[1,64,2048]{2,1,0:T(8,128)(2,1)S(1)}, u32[]{:S(2)}, u32[]{:S(2)}) %collective-permute-start.1) | collective-permute-done | bytes 262176 | tf_op jit(solution)/shard_map/ppermute | solution.py:64
  27.8 7.4 %collective-permute-done.5 = bf16[2,2,16,256]{3,2,1,0:T(8,128)(2,1)S(1)} collective-permute-done((bf16[2,2,16,256]{3,2,1,0:T(8,128)(2,1)S(1)}, bf16[2,2,16,256]{3,2,1,0:T(8,128)(2,1)S(1)}, u32[]{:S(2)}, u32[]{:S(2)}) %collective-permute-start.5) | collective-permute-done | bytes 32800 | tf_op jit(solution)/shard_map/ppermute | solution.py:40
  43.1 13.4 %collective-permute-done.10 = bf16[2,2,2,2,16,256]{5,4,3,1,2,0:T(8,128)(2,1)S(1)} collective-permute-done((bf16[2,2,2,2,16,256]{5,4,3,1,2,0:T(8,128)(2,1)S(1)}, bf16[2,2,2,2,16,256]{5,4,3,1,2,0:T(8,128)(2,1)S(1)}, u32[]{:S(2)}, u32[]{:S(2)}) %collective-permute-start.10) | collective-permute-done | bytes 131104 | tf_op jit(solution)/shard_map/ppermute | solution.py:40
  60.1 2.4 collective-permute-start.14
  62.4 2.6 norm.1
  68.7 11.1 %collective-permute-done.13.got_ref = bf16[1,64,2048]{2,1,0:T(8,128)(2,1)S(1)} collective-permute-done((bf16[1,64,2048]{2,1,0:T(8,128)(2,1)}, bf16[1,64,2048]{2,1,0:T(8,128)(2,1)S(1)}, u32[]{:S(2)}, u32[]{:S(2)}) %collective-permute-start.13) | collective-permute-done | bytes 262176 | tf_op jit(solution)/shard_map/ppermute | solution.py:64
  79.8 5.6 %collective-permute-done.14.got_ref = bf16[1,64,2048]{2,1,0:T(8,128)(2,1)S(1)} collective-permute-done((bf16[1,64,2048]{2,1,0:T(8,128)(2,1)S(1)}, bf16[1,64,2048]{2,1,0:T(8,128)(2,1)S(1)}, u32[]{:S(2)}, u32[]{:S(2)}) %collective-permute-start.14) | collective-permute-done | bytes 262176 | tf_op jit(solution)/shard_map/ppermute | solution.py:64
  91.1 13.5 %collective-permute-done.17.got_ref = bf16[2,64,2048]{2,1,0:T(8,128)(2,1)S(1)} collective-permute-done((bf16[2,64,2048]{2,1,0:T(8,128)(2,1)S(1)}, bf16[2,64,2048]{2,1,0:T(8,128)(2,1)S(1)}, u32[]{:S(2)}, u32[]{:S(2)}) %collective-permute-start.17) | collective-permute-done | bytes 524320 | tf_op jit(solution)/shard_map/ppermute | solution.py:64
  107.7 15.4 %project.1 = (bf16[4,512,256]{2,1,0:T(8,128)(2,1)}, bf16[4,512,256]{2,1,0:T(8,128)(2,1)}, bf16[4,512,512]{2,1,0:T(8,128)(2,1)}, bf16[4,512,256]{2,1,0:T(8,128)(2...) custom-call(s32[66]{0:T(128)} %copy-done.48, f32[4]{0:T(128)} %copy-done.60, ...), custom_call_target="tpu_custom_call" | custom-call | flops 1 | bytes 1 | tf_op jit(solution)/shard_map/project/pallas_call | solution.py:330
  124.1 4.0 collective-permute-done.20
  130.5 3.5 collective-permute-start.21
  134.0 10.1 %collective-permute-done.21 = bf16[2,256,512]{2,1,0:T(8,128)(2,1)S(1)} collective-permute-done((bf16[2,256,512]{2,1,0:T(8,128)(2,1)S(1)}, bf16[2,256,512]{2,1,0:T(8,128)(2,1)S(1)}, u32[]{:S(2)}, u32[]{:S(2)}) %collective-permute-start.21) | collective-permute-done | bytes 524320 | tf_op jit(solution)/shard_map/ppermute | solution.py:294
  146.7 4.1 collective-permute-start.23
  150.9 8.9 %collective-permute-done.23 = bf16[2,256,512]{2,1,0:T(8,128)(2,1)S(1)} collective-permute-done((bf16[2,256,512]{2,1,0:T(8,128)(2,1)S(1)}, bf16[2,256,512]{2,1,0:T(8,128)(2,1)S(1)}, u32[]{:S(2)}, u32[]{:S(2)}) %collective-permute-start.23) | collective-permute-done | bytes 524320 | tf_op jit(solution)/shard_map/ppermute | solution.py:294
  161.1 3.9 collective-permute-start.26
  167.7 9.8 %collective-permute-done.26.refs_1_ = bf16[4,64,2048]{2,1,0:T(8,128)(2,1)} collective-permute-done((bf16[4,64,2048]{2,1,0:T(8,128)(2,1)S(1)}, bf16[4,64,2048]{2,1,0:T(8,128)(2,1)}, u32[]{:S(2)}, u32[]{:S(2)}) %collective-permute-start.26) | collective-permute-done | bytes 1048608 | tf_op jit(solution)/shard_map/ppermute | solution.py:64
  180.0 3.7 settle.5.own.wo_own.g_own
  187.7 2.2 fusion.21
  191.3 8.1 %collective-permute-done.29.refs_2_ = bf16[4,64,2048]{2,1,0:T(8,128)(2,1)} collective-permute-done((bf16[4,64,2048]{2,1,0:T(8,128)(2,1)S(1)}, bf16[4,64,2048]{2,1,0:T(8,128)(2,1)}, u32[]{:S(2)}, u32[]{:S(2)}) %collective-permute-start.29) | collective-permute-done | bytes 1048608 | tf_op jit(solution)/shard_map/ppermute | solution.py:64
  201.2 2.6 fusion.3
  205.0 6.0 %gate.1 = f32[4,512,512]{2,1,0:T(8,128)S(1)} custom-call(s32[66]{0:T(128)S(1)} %copy-done.49, bf16[512,1024]{1,0:T(8,128)(2,1)S(1)} %copy-done.20, bf16[16,64,2048]{2,1,0:T(8,128)(2,1)} %settle.5.own.wo_own.g_own, bf16[16,64,2048]{2,1,0:T(8,128)(2,1)} %collective-permute-done.28.oth.wo_oth.g_oth), custom_call_target="tpu_custom_call" | custom-call | flops 1 | bytes 1 | tf_op jit(solution)/shard_map/gate/pallas_call | solution.py:330
  215.3 11.8 %mix.1 = (f32[4,512,512]{2,1,0:T(8,128)S(1)}, bf16[4,512,512]{2,1,0:T(8,128)(2,1)S(1)}, f32[512,1024]{1,0:T(8,128)S(1)}, bf16[512,1024]{1,0:T(8,128)(2,1)S(1)}, bf16[1024,512]{1,0:T(8,128)(2,1)S(1)}) custom-call(s32[66]{0:T(128)S(1)} %copy-done.49, f32[4]{0:T(128)S(1)} %copy-done.61, bf16[512,1024]{1,0:T(8,128)(2,1)S(1)} %bitcast.251, ...), custom_call_target="tpu_custom_call" | custom-call | flops 1 | bytes 1 | tf_op jit(solution)/shard_map/mix/pallas_call | solution.py:330
  228.2 3.4 settle.6.up_own.down_own
  237.4 27.7 %feed.1 = (bf16[512,1024]{1,0:T(8,128)(2,1)}, f32[512,1024]{1,0:T(8,128)}, bf16[512,1024]{1,0:T(8,128)(2,1)S(1)}, f32[1,1024]{1,0:T(1,128)S(1)}, f32[1,1024]{1,0...) custom-call(s32[66]{0:T(128)S(1)} %concatenate.46.info_ref.info, f32[512,1024]{1,0:T(8,128)} %copy-done.36, ...), custom_call_target="tpu_custom_call" | custom-call | flops 1 | bytes 1 | tf_op jit(solution)/shard_map/feed/pallas_call | solution.py:330
  265.2 2.2 copy-done.17
  267.3 10.4 %unmix.1 = (bf16[4,512,512]{2,1,0:T(8,128)(2,1)S(1)}, bf16[4,512,512]{2,1,0:T(8,128)(2,1)S(1)}, f32[4,1,512]{2,1,0:T(1,128)S(1)}, f32[2,2,256,512]{3,2,1,0:T(8,128)S(1)}, f32[2,2,256,512]{3,2,1,0:T(8,128)S(1)}) custom-call(s32[66]{0:T(128)S(1)} %copy-done.49, f32[4]{0:T(128)S(1)} %copy-done.61, bf16[512,1024]{1,0:T(8,128)(2,1)S(1)} %get-tuple-element.615.grad_low, ...), custom_call_target="tpu_custom_call" | custom-call | flops 1 | bytes 1 | tf_op jit(solution)/shard_map/unmix/pallas_call | solution.py:330
  278.4 2.5 add_convert_fusion.5
  283.6 7.9 %inside.1 = (bf16[4,512,256]{2,1,0:T(8,128)(2,1)S(1)}, f32[4,512,256]{2,1,0:T(8,128)S(1)}, f32[4,512,512]{2,1,0:T(8,128)S(1)}) custom-call(s32[66]{0:T(128)S(1)} %copy-done.49, f32[4]{0:T(128)S(1)} %copy-done.61, bf16[4,512,512]{2,1,0:T(8,128)(2,1)S(1)} %get-tuple-element.632.grad_ret, bf16[4,512,256]{2,1,0:T(8,128)(2,1)S(1)} %copy-done.6, ...), custom_call_target="tpu_custom_call" | custom-call | flops 1 | bytes 1 | tf_op jit(solution)/shard_map/inside/pallas_call | solution.py:330
  292.9 3.4 add_convert_fusion.4
  298.8 11.4 %outer.1 = (bf16[16,64,2560]{2,1,0:T(8,128)(2,1)}, bf16[16,64,2560]{2,1,0:T(8,128)(2,1)}) custom-call(s32[66]{0:T(128)S(1)} %copy-done.49, bf16[512,1024]{1,0:T(8,128)(2,1)S(1)} %get-tuple-element.615.grad_low, bf16[1024,512]{1,0:T(8,128)(2,1)S(1)} %copy-done.23, bf16[4,512,512]{2,1,0:T(8,128)(2,1)S(1)} %copy-done.35, ...), custom_call_target="tpu_custom_call" | custom-call | flops 1 | bytes 1 | tf_op jit(solution)/shard_map/outer/pallas_call | solution.py:330
  310.2 2.2 add_convert_fusion.3
  316.1 19.7 %collective-permute-done.42 = bf16[2,256,512]{2,1,0:T(8,128)(2,1)S(1)} collective-permute-done((bf16[2,256,512]{2,1,0:T(8,128)(2,1)S(1)}, bf16[2,256,512]{2,1,0:T(8,128)(2,1)S(1)}, u32[]{:S(2)}, u32[]{:S(2)}) %collective-permute-start.42) | collective-permute-done | bytes 524320 | tf_op jit(solution)/shard_map/ppermute | solution.py:294
  335.8 2.7 add_convert_fusion.1
  338.6 2.4 collective-permute-start.46
  345.5 11.7 %collective-permute-done.45 = bf16[2,256,512]{2,1,0:T(8,128)(2,1)} collective-permute-done((bf16[2,256,512]{2,1,0:T(8,128)(2,1)}, bf16[2,256,512]{2,1,0:T(8,128)(2,1)}, u32[]{:S(2)}, u32[]{:S(2)}) %collective-permute-start.45) | collective-permute-done | bytes 524320 | tf_op jit(solution)/shard_map/ppermute | solution.py:294
  361.5 2.3 collective-permute-done.47.state_oth
  366.1 9.6 %last.1 = (bf16[4,512,256]{2,1,0:T(8,128)(2,1)S(1)}, bf16[4,512,512]{2,1,0:T(8,128)(2,1)S(1)}, bf16[16,64,1536]{2,1,0:T(8,128)(2,1)S(1)}, bf16[16,64,1536]{2,1,0:T(8,128)(2,1)S(1)}) custom-call(s32[66]{0:T(128)S(1)} %copy-done.49, f32[4]{0:T(128)S(1)} %copy-done.61, bf16[1024,512]{1,0:T(8,128)(2,1)S(1)} %copy-done.24, bf16[4,512,256]{2,1,0:T(8,128)(2,1)S(1)} %copy-done.18, ...), custom_call_target="tpu_custom_call" | custom-call | flops 1 | bytes 1 | tf_op jit(solution)/shard_map/last/pallas_call | solution.py:330
  376.6 4.5 add_convert_fusion
  385.1 3.4 collective-permute-done.50
  392.4 17.5 %input.1 = (f32[512,1024]{1,0:T(8,128)}, f32[1,1024]{1,0:T(1,128)}, f32[1,1024]{1,0:T(1,128)}) custom-call(s32[66]{0:T(128)} %copy-done.48, bf16[512,1024]{1,0:T(8,128)(2,1)} %bitcast.249, bf16[1,1024]{1,0:T(2,128)(2,1)} %copy-done.59, f32[512,1024]{1,0:T(8,128)} %get-tuple-element.769.grad_hidden, bf16[4,512,256]{2,1,0:T(8,128)(2,1)} %copy-done.21, ...), custom_call_target="tpu_custom_call" | custom-call | flops 1 | bytes 1 | tf_op jit(solution)/shard_map/input/pallas_call | solution.py:330
  410.1 2.4 add_convert_fusion.6
  413.5 2.6 add_convert_fusion.9
  422.7 3.1 collective-permute-done.58
  434.7 6.7 %collective-permute-done.63 = bf16[1,64,2560]{2,1,0:T(8,128)(2,1)S(1)} collective-permute-done((bf16[1,64,2560]{2,1,0:T(8,128)(2,1)S(1)}, bf16[1,64,2560]{2,1,0:T(8,128)(2,1)S(1)}, u32[]{:S(2)}, u32[]{:S(2)}) %collective-permute-start.63) | collective-permute-done | bytes 327712 | tf_op jit(solution)/shard_map/ppermute | solution.py:64
  443.0 12.9 %collective-permute-start.67 = (f32[64,512]{1,0:T(8,128)S(1)}, f32[64,512]{1,0:T(8,128)S(1)}, u32[]{:S(2)}, u32[]{:S(2)}) collective-permute-start(f32[64,512]{1,0:T(8,128)S(1)} %slice_select_fusion.1), channel_id=1, source_target_pairs={{0,1},{1,0},{2,3},{3,2},{4,5},{5,4},{6,7},{7,6},{8,9},{9,8},{10,11... | collective-permute-start | bytes 393224 | tf_op jit(solution)/shard_map/ppermute | solution.py:40
  457.8 2.2 collective-permute-start.65
  464.3 5.1 %collective-permute-done.65 = bf16[1,64,1536]{2,1,0:T(8,128)(2,1)S(1)} collective-permute-done((bf16[1,64,1536]{2,1,0:T(8,128)(2,1)S(1)}, bf16[1,64,1536]{2,1,0:T(8,128)(2,1)S(1)}, u32[]{:S(2)}, u32[]{:S(2)}) %collective-permute-start.65) | collective-permute-done | bytes 196640 | tf_op jit(solution)/shard_map/ppermute | solution.py:64
  (466 shorter events, 125.1 us)
Async XLA Ops:
  12.0 14.0 %collective-permute-start.1 = (bf16[1,64,2048]{2,1,0:T(8,128)(2,1)S(1)}, bf16[1,64,2048]{2,1,0:T(8,128)(2,1)S(1)}, u32[]{:S(2)}, u32[]{:S(2)}) collective-permute-start(bf16[1,64,2048]{2,1,0:T(8,128)(2,1)S(1)} %bitcast.252), channel_id=1, source_target_pairs={{0,4},{1,5},{2,6},{3,7},{4,0},{5,1},{6,2},{7,3},{8,12},{9,13},{10,... | collective-permute-start | bytes 786440 | tf_op jit(solution)/shard_map/ppermute | solution.py:64
  26.1 9.1 %collective-permute-start.4 = (bf16[2,64,2048]{2,1,0:T(8,128)(2,1)S(1)}, bf16[2,64,2048]{2,1,0:T(8,128)(2,1)S(1)}, u32[]{:S(2)}, u32[]{:S(2)}) collective-permute-start(bf16[2,64,2048]{2,1,0:T(8,128)(2,1)S(1)} %join.6.part_ref), channel_id=1, source_target_pairs={{0,16},{1,3},{2,18},{3,1},{4,20},{5,7},{6,22},{7,5},{8,24},{9,11},... | collective-permute-start | bytes 1572872 | tf_op jit(solution)/shard_map/ppermute | solution.py:64
  26.2 8.9 %collective-permute-start.5 = (bf16[2,2,16,256]{3,2,1,0:T(8,128)(2,1)S(1)}, bf16[2,2,16,256]{3,2,1,0:T(8,128)(2,1)S(1)}, u32[]{:S(2)}, u32[]{:S(2)}) collective-permute-start(bf16[2,2,16,256]{3,2,1,0:T(8,128)(2,1)S(1)} %pad_maximum_fusion.13), channel_id=1, source_target_pairs={{0,2},{1,3},{2,0},{3,1},{4,6},{5,7},{6,4},{7,5},{8,10},{9,11},{10,... | collective-permute-start | bytes 98312 | tf_op jit(solution)/shard_map/ppermute | solution.py:40
  40.0 16.6 %collective-permute-start.6 = (bf16[4,64,2048]{2,1,0:T(8,128)(2,1)S(1)}, bf16[4,64,2048]{2,1,0:T(8,128)(2,1)}, u32[]{:S(2)}, u32[]{:S(2)}) collective-permute-start(bf16[4,64,2048]{2,1,0:T(8,128)(2,1)S(1)} %join.7.refs_0_), channel_id=1, source_target_pairs={{0,2},{1,9},{2,0},{3,11},{4,6},{5,13},{6,4},{7,15},{8,10},{9,1},{1... | collective-permute-start | bytes 3145736 | tf_op jit(solution)/shard_map/ppermute | solution.py:64
  41.4 15.2 %collective-permute-start.10 = (bf16[2,2,2,2,16,256]{5,4,3,1,2,0:T(8,128)(2,1)S(1)}, bf16[2,2,2,2,16,256]{5,4,3,1,2,0:T(8,128)(2,1)S(1)}, u32[]{:S(2)}, u32[]{:S(2)}) collective-permute-start(bf16[2,2,2,2,16,256]{5,4,3,1,2,0:T(8,128)(2,1)S(1)} %pad_maximum_fusion.9), channel_id=1, source_target_pairs={{0,8},{1,9},{2,10},{3,11},{4,12},{5,13},{6,14},{7,15},{8,0},{9,1},... | collective-permute-start | bytes 393224 | tf_op jit(solution)/shard_map/ppermute | solution.py:40
  58.3 27.1 %collective-permute-start.11 = (bf16[4,64,2048]{2,1,0:T(8,128)(2,1)S(1)}, bf16[4,64,2048]{2,1,0:T(8,128)(2,1)}, u32[]{:S(2)}, u32[]{:S(2)}) collective-permute-start(bf16[4,64,2048]{2,1,0:T(8,128)(2,1)S(1)} %join.7.refs_0_), channel_id=1, source_target_pairs={{0,8},{1,17},{2,10},{3,19},{4,12},{5,21},{6,14},{7,23},{8,0},{9,25... | collective-permute-start | bytes 3145736 | tf_op jit(solution)/shard_map/ppermute | solution.py:64
  58.6 26.8 %collective-permute-start.12 = (bf16[4,64,2048]{2,1,0:T(8,128)(2,1)}, bf16[4,64,2048]{2,1,0:T(8,128)(2,1)}, u32[]{:S(2)}, u32[]{:S(2)}) collective-permute-start(bf16[4,64,2048]{2,1,0:T(8,128)(2,1)} %collective-permute-done.6.refs_1_), channel_id=1, source_target_pairs={{0,8},{1,17},{2,10},{3,19},{4,12},{5,21},{6,14},{7,23},{8,0},{9,25... | collective-permute-start | bytes 3145736 | tf_op jit(solution)/shard_map/ppermute | solution.py:64
  60.0 19.7 %collective-permute-start.13 = (bf16[1,64,2048]{2,1,0:T(8,128)(2,1)}, bf16[1,64,2048]{2,1,0:T(8,128)(2,1)S(1)}, u32[]{:S(2)}, u32[]{:S(2)}) collective-permute-start(bf16[1,64,2048]{2,1,0:T(8,128)(2,1)} %maximum_bitcast_fusion.part_ref), channel_id=1, source_target_pairs={{0,4},{1,5},{2,6},{3,7},{4,0},{5,1},{6,2},{7,3},{8,12},{9,13},{10,... | collective-permute-start | bytes 786440 | tf_op jit(solution)/shard_map/ppermute | solution.py:64
  60.1 25.3 %collective-permute-start.14 = (bf16[1,64,2048]{2,1,0:T(8,128)(2,1)S(1)}, bf16[1,64,2048]{2,1,0:T(8,128)(2,1)S(1)}, u32[]{:S(2)}, u32[]{:S(2)}) collective-permute-start(bf16[1,64,2048]{2,1,0:T(8,128)(2,1)S(1)} %maximum_bitcast_fusion.1.part_ref), channel_id=1, source_target_pairs={{0,4},{1,5},{2,6},{3,7},{4,0},{5,1},{6,2},{7,3},{8,12},{9,13},{10,... | collective-permute-start | bytes 786440 | tf_op jit(solution)/shard_map/ppermute | solution.py:64
  89.6 15.1 %collective-permute-start.16 = (bf16[16,64,2048]{2,1,0:T(8,128)(2,1)S(1)}, bf16[16,64,2048]{2,1,0:T(8,128)(2,1)S(1)}, u32[]{:S(2)}, u32[]{:S(2)}) collective-permute-start(bf16[16,64,2048]{2,1,0:T(8,128)(2,1)S(1)} %settle.4.q_own.k_own.v_own), channel_id=1, source_target_pairs={{0,1},{1,0},{2,3},{3,2},{4,5},{5,4},{6,7},{7,6},{8,9},{9,8},{10,11... | collective-permute-start | bytes 12582920 | tf_op jit(solution)/shard_map/ppermute | solution.py:40
  91.0 13.6 %collective-permute-start.17 = (bf16[2,64,2048]{2,1,0:T(8,128)(2,1)S(1)}, bf16[2,64,2048]{2,1,0:T(8,128)(2,1)S(1)}, u32[]{:S(2)}, u32[]{:S(2)}) collective-permute-start(bf16[2,64,2048]{2,1,0:T(8,128)(2,1)S(1)} %join.8.part_ref), channel_id=1, source_target_pairs={{0,2},{1,3},{2,0},{3,1},{4,6},{5,7},{6,4},{7,5},{8,10},{9,11},{10,... | collective-permute-start | bytes 1572872 | tf_op jit(solution)/shard_map/ppermute | solution.py:64
  104.7 18.5 %collective-permute-start.18 = (bf16[4,64,2048]{2,1,0:T(8,128)(2,1)S(1)}, bf16[4,64,2048]{2,1,0:T(8,128)(2,1)}, u32[]{:S(2)}, u32[]{:S(2)}) collective-permute-start(bf16[4,64,2048]{2,1,0:T(8,128)(2,1)S(1)} %join.9.refs_0_), channel_id=1, source_target_pairs={{0,16},{1,9},{2,18},{3,11},{4,20},{5,13},{6,22},{7,15},{8,24},{9,1... | collective-permute-start | bytes 3145736 | tf_op jit(solution)/shard_map/ppermute | solution.py:64
  106.7 16.5 %collective-permute-start.19 = (bf16[2,64,2048]{2,1,0:T(8,128)(2,1)S(1)}, bf16[2,64,2048]{2,1,0:T(8,128)(2,1)S(1)}, u32[]{:S(2)}, u32[]{:S(2)}) collective-permute-start(bf16[2,64,2048]{2,1,0:T(8,128)(2,1)S(1)} %join.10.part_ref), channel_id=1, source_target_pairs={{0,2},{1,3},{2,0},{3,1},{4,6},{5,7},{6,4},{7,5},{8,10},{9,11},{10,... | collective-permute-start | bytes 1572872 | tf_op jit(solution)/shard_map/ppermute | solution.py:64
  128.1 15.9 %collective-permute-start.22 = (bf16[4,64,2048]{2,1,0:T(8,128)(2,1)S(1)}, bf16[4,64,2048]{2,1,0:T(8,128)(2,1)S(1)}, u32[]{:S(2)}, u32[]{:S(2)}) collective-permute-start(bf16[4,64,2048]{2,1,0:T(8,128)(2,1)S(1)} %join.9.refs_0_), channel_id=1, source_target_pairs={{0,8},{1,17},{2,10},{3,19},{4,12},{5,21},{6,14},{7,23},{8,0},{9,25... | collective-permute-start | bytes 3145736 | tf_op jit(solution)/shard_map/ppermute | solution.py:64
  130.5 13.6 %collective-permute-start.21 = (bf16[2,256,512]{2,1,0:T(8,128)(2,1)S(1)}, bf16[2,256,512]{2,1,0:T(8,128)(2,1)S(1)}, u32[]{:S(2)}, u32[]{:S(2)}) collective-permute-start(bf16[2,256,512]{2,1,0:T(8,128)(2,1)S(1)} %fusion.29), channel_id=1, source_target_pairs={{0,2},{1,3},{8,10},{9,11},{16,18},{17,19},{24,26},{25,27}} | collective-permute-start | bytes 1572872 | tf_op jit(solution)/shard_map/ppermute | solution.py:294
  145.1 14.7 %collective-permute-start.24 = (bf16[4,64,2048]{2,1,0:T(8,128)(2,1)}, bf16[4,64,2048]{2,1,0:T(8,128)(2,1)S(1)}, u32[]{:S(2)}, u32[]{:S(2)}) collective-permute-start(bf16[4,64,2048]{2,1,0:T(8,128)(2,1)} %collective-permute-done.18.refs_1_), channel_id=1, source_target_pairs={{0,8},{1,17},{2,10},{3,19},{4,12},{5,21},{6,14},{7,23},{8,0},{9,25... | collective-permute-start | bytes 3145736 | tf_op jit(solution)/shard_map/ppermute | solution.py:64
  146.7 13.0 %collective-permute-start.23 = (bf16[2,256,512]{2,1,0:T(8,128)(2,1)S(1)}, bf16[2,256,512]{2,1,0:T(8,128)(2,1)S(1)}, u32[]{:S(2)}, u32[]{:S(2)}) collective-permute-start(bf16[2,256,512]{2,1,0:T(8,128)(2,1)S(1)} %fusion.27), channel_id=1, source_target_pairs={{0,2},{1,3},{2,4},{3,5},{8,10},{9,11},{10,12},{11,13},{16,18},{17,... | collective-permute-start | bytes 1572872 | tf_op jit(solution)/shard_map/ppermute | solution.py:294
  161.1 16.5 %collective-permute-start.26 = (bf16[4,64,2048]{2,1,0:T(8,128)(2,1)S(1)}, bf16[4,64,2048]{2,1,0:T(8,128)(2,1)}, u32[]{:S(2)}, u32[]{:S(2)}) collective-permute-start(bf16[4,64,2048]{2,1,0:T(8,128)(2,1)S(1)} %join.11.refs_0_), channel_id=1, source_target_pairs={{0,16},{1,9},{2,18},{3,11},{4,20},{5,13},{6,22},{7,15},{8,24},{9,1... | collective-permute-start | bytes 3145736 | tf_op jit(solution)/shard_map/ppermute | solution.py:64
  183.6 15.8 %collective-permute-start.28 = (bf16[16,64,2048]{2,1,0:T(8,128)(2,1)}, bf16[16,64,2048]{2,1,0:T(8,128)(2,1)}, u32[]{:S(2)}, u32[]{:S(2)}) collective-permute-start(bf16[16,64,2048]{2,1,0:T(8,128)(2,1)} %settle.5.own.wo_own.g_own), channel_id=1, source_target_pairs={{0,1},{1,0},{2,3},{3,2},{4,5},{5,4},{6,7},{7,6},{8,9},{9,8},{10,11... | collective-permute-start | bytes 12582920 | tf_op jit(solution)/shard_map/ppermute | solution.py:40
  185.4 14.0 %collective-permute-start.29 = (bf16[4,64,2048]{2,1,0:T(8,128)(2,1)S(1)}, bf16[4,64,2048]{2,1,0:T(8,128)(2,1)}, u32[]{:S(2)}, u32[]{:S(2)}) collective-permute-start(bf16[4,64,2048]{2,1,0:T(8,128)(2,1)S(1)} %join.11.refs_0_), channel_id=1, source_target_pairs={{0,8},{1,17},{2,10},{3,19},{4,12},{5,21},{6,14},{7,23},{8,0},{9,25... | collective-permute-start | bytes 3145736 | tf_op jit(solution)/shard_map/ppermute | solution.py:64
  185.6 13.8 %collective-permute-start.30 = (bf16[4,64,2048]{2,1,0:T(8,128)(2,1)S(1)}, bf16[4,64,2048]{2,1,0:T(8,128)(2,1)S(1)}, u32[]{:S(2)}, u32[]{:S(2)}) collective-permute-start(bf16[4,64,2048]{2,1,0:T(8,128)(2,1)S(1)} %join.11.refs_0_), channel_id=1, source_target_pairs={{0,1},{1,0},{2,3},{3,2},{4,5},{5,4},{6,7},{7,6},{8,9},{9,8},{10,11... | collective-permute-start | bytes 3145736 | tf_op jit(solution)/shard_map/ppermute | solution.py:40
  187.6 11.8 %collective-permute-start.31 = (bf16[4,64,2048]{2,1,0:T(8,128)(2,1)}, bf16[4,64,2048]{2,1,0:T(8,128)(2,1)}, u32[]{:S(2)}, u32[]{:S(2)}) collective-permute-start(bf16[4,64,2048]{2,1,0:T(8,128)(2,1)} %collective-permute-done.26.refs_1_), channel_id=1, source_target_pairs={{0,1},{1,0},{2,3},{3,2},{4,5},{5,4},{6,7},{7,6},{8,9},{9,8},{10,11... | collective-permute-start | bytes 3145736 | tf_op jit(solution)/shard_map/ppermute | solution.py:40
  203.8 9.2 %collective-permute-start.32 = (bf16[2,2,256,512]{3,2,1,0:T(8,128)(2,1)S(1)}, bf16[2,2,256,512]{3,2,1,0:T(8,128)(2,1)S(1)}, u32[]{:S(2)}, u32[]{:S(2)}) collective-permute-start(bf16[2,2,256,512]{3,2,1,0:T(8,128)(2,1)S(1)} %get-tuple-element.860), channel_id=1, source_target_pairs={{0,1},{1,0},{2,3},{3,2},{4,5},{5,4},{6,7},{7,6},{8,9},{9,8},{10,11... | collective-permute-start | bytes 3145736 | tf_op jit(solution)/shard_map/ppermute | solution.py:40
  213.1 14.2 %collective-permute-start.33 = (bf16[4,64,2048]{2,1,0:T(8,128)(2,1)}, bf16[4,64,2048]{2,1,0:T(8,128)(2,1)S(1)}, u32[]{:S(2)}, u32[]{:S(2)}) collective-permute-start(bf16[4,64,2048]{2,1,0:T(8,128)(2,1)} %collective-permute-done.26.refs_1_), channel_id=1, source_target_pairs={{0,8},{1,17},{2,10},{3,19},{4,12},{5,21},{6,14},{7,23},{8,0},{9,25... | collective-permute-start | bytes 3145736 | tf_op jit(solution)/shard_map/ppermute | solution.py:64
  213.4 13.9 %collective-permute-start.34 = (bf16[4,64,2048]{2,1,0:T(8,128)(2,1)}, bf16[4,64,2048]{2,1,0:T(8,128)(2,1)S(1)}, u32[]{:S(2)}, u32[]{:S(2)}) collective-permute-start(bf16[4,64,2048]{2,1,0:T(8,128)(2,1)} %collective-permute-done.29.refs_2_), channel_id=1, source_target_pairs={{0,1},{1,0},{2,3},{3,2},{4,5},{5,4},{6,7},{7,6},{8,9},{9,8},{10,11... | collective-permute-start | bytes 3145736 | tf_op jit(solution)/shard_map/ppermute | solution.py:40
  265.1 12.8 %collective-permute-start.36 = (bf16[16,64,2048]{2,1,0:T(8,128)(2,1)}, bf16[16,64,2048]{2,1,0:T(8,128)(2,1)S(1)}, u32[]{:S(2)}, u32[]{:S(2)}) collective-permute-start(bf16[16,64,2048]{2,1,0:T(8,128)(2,1)} %get-tuple-element.614), channel_id=1, source_target_pairs={{0,1},{1,0},{2,3},{3,2},{4,5},{5,4},{6,7},{7,6},{8,9},{9,8},{10,11... | collective-permute-start | bytes 12582920 | tf_op jit(solution)/shard_map/ppermute | solution.py:40
  282.2 14.1 %collective-permute-start.39 = (bf16[4,64,2048]{2,1,0:T(8,128)(2,1)S(1)}, bf16[4,64,2048]{2,1,0:T(8,128)(2,1)S(1)}, u32[]{:S(2)}, u32[]{:S(2)}) collective-permute-start(bf16[4,64,2048]{2,1,0:T(8,128)(2,1)S(1)} %add_convert_fusion.5), channel_id=1, source_target_pairs={{0,8},{1,17},{2,10},{3,19},{4,12},{5,21},{6,14},{7,23},{8,0},{9,25... | collective-permute-start | bytes 3145736 | tf_op jit(solution)/shard_map/ppermute | solution.py:64
  282.8 13.5 %collective-permute-start.38 = (bf16[2,256,512]{2,1,0:T(8,128)(2,1)S(1)}, bf16[2,256,512]{2,1,0:T(8,128)(2,1)S(1)}, u32[]{:S(2)}, u32[]{:S(2)}) collective-permute-start(bf16[2,256,512]{2,1,0:T(8,128)(2,1)S(1)} %fusion.18), channel_id=1, source_target_pairs={{6,4},{7,5},{14,12},{15,13},{22,20},{23,21},{30,28},{31,29}} | collective-permute-start | bytes 1572872 | tf_op jit(solution)/shard_map/ppermute | solution.py:294
  296.3 16.2 %collective-permute-start.41 = (bf16[4,64,2048]{2,1,0:T(8,128)(2,1)}, bf16[4,64,2048]{2,1,0:T(8,128)(2,1)}, u32[]{:S(2)}, u32[]{:S(2)}) collective-permute-start(bf16[4,64,2048]{2,1,0:T(8,128)(2,1)} %add_convert_fusion.4), channel_id=1, source_target_pairs={{0,8},{1,17},{2,10},{3,19},{4,12},{5,21},{6,14},{7,23},{8,0},{9,25... | collective-permute-start | bytes 3145736 | tf_op jit(solution)/shard_map/ppermute | solution.py:64
  297.9 14.5 %collective-permute-start.40 = (bf16[2,256,512]{2,1,0:T(8,128)(2,1)S(1)}, bf16[2,256,512]{2,1,0:T(8,128)(2,1)S(1)}, u32[]{:S(2)}, u32[]{:S(2)}) collective-permute-start(bf16[2,256,512]{2,1,0:T(8,128)(2,1)S(1)} %fusion.16), channel_id=1, source_target_pairs={{6,4},{7,5},{4,2},{5,3},{14,12},{15,13},{12,10},{13,11},{22,20},{2... | collective-permute-start | bytes 1572872 | tf_op jit(solution)/shard_map/ppermute | solution.py:294
  312.5 23.3 %collective-permute-start.43 = (bf16[16,64,2560]{2,1,0:T(8,128)(2,1)}, bf16[16,64,2560]{2,1,0:T(8,128)(2,1)S(1)}, u32[]{:S(2)}, u32[]{:S(2)}) collective-permute-start(bf16[16,64,2560]{2,1,0:T(8,128)(2,1)} %get-tuple-element.684), channel_id=1, source_target_pairs={{0,1},{1,0},{2,3},{3,2},{4,5},{5,4},{6,7},{7,6},{8,9},{9,8},{10,11... | collective-permute-start | bytes 15728648 | tf_op jit(solution)/shard_map/ppermute | solution.py:40
  313.4 22.4 %collective-permute-start.44 = (bf16[4,64,2048]{2,1,0:T(8,128)(2,1)S(1)}, bf16[4,64,2048]{2,1,0:T(8,128)(2,1)S(1)}, u32[]{:S(2)}, u32[]{:S(2)}) collective-permute-start(bf16[4,64,2048]{2,1,0:T(8,128)(2,1)S(1)} %add_convert_fusion.3), channel_id=1, source_target_pairs={{0,16},{1,9},{2,18},{3,11},{4,20},{5,13},{6,22},{7,15},{8,24},{9,1... | collective-permute-start | bytes 3145736 | tf_op jit(solution)/shard_map/ppermute | solution.py:64
  314.8 21.0 %collective-permute-start.42 = (bf16[2,256,512]{2,1,0:T(8,128)(2,1)S(1)}, bf16[2,256,512]{2,1,0:T(8,128)(2,1)S(1)}, u32[]{:S(2)}, u32[]{:S(2)}) collective-permute-start(bf16[2,256,512]{2,1,0:T(8,128)(2,1)S(1)} %fusion.13), channel_id=1, source_target_pairs={{4,2},{5,3},{2,0},{3,1},{12,10},{13,11},{10,8},{11,9},{20,18},{21,... | collective-permute-start | bytes 1572872 | tf_op jit(solution)/shard_map/ppermute | solution.py:294
  338.6 18.7 %collective-permute-start.46 = (bf16[4,64,2560]{2,1,0:T(8,128)(2,1)}, bf16[4,64,2560]{2,1,0:T(8,128)(2,1)}, u32[]{:S(2)}, u32[]{:S(2)}) collective-permute-start(bf16[4,64,2560]{2,1,0:T(8,128)(2,1)} %get-tuple-element.855), channel_id=1, source_target_pairs={{0,8},{1,17},{2,10},{3,19},{4,12},{5,21},{6,14},{7,23},{8,0},{9,25... | collective-permute-start | bytes 3932168 | tf_op jit(solution)/shard_map/ppermute | solution.py:64
  342.2 15.1 %collective-permute-start.45 = (bf16[2,256,512]{2,1,0:T(8,128)(2,1)}, bf16[2,256,512]{2,1,0:T(8,128)(2,1)}, u32[]{:S(2)}, u32[]{:S(2)}) collective-permute-start(bf16[2,256,512]{2,1,0:T(8,128)(2,1)} %fusion.10), channel_id=1, source_target_pairs={{2,0},{3,1},{10,8},{11,9},{18,16},{19,17},{26,24},{27,25}} | collective-permute-start | bytes 1572872 | tf_op jit(solution)/shard_map/ppermute | solution.py:294
  363.7 17.4 %collective-permute-start.49 = (bf16[4,64,2560]{2,1,0:T(8,128)(2,1)}, bf16[4,64,2560]{2,1,0:T(8,128)(2,1)S(1)}, u32[]{:S(2)}, u32[]{:S(2)}) collective-permute-start(bf16[4,64,2560]{2,1,0:T(8,128)(2,1)} %get-tuple-element.738), channel_id=1, source_target_pairs={{0,8},{1,17},{2,10},{3,19},{4,12},{5,21},{6,14},{7,23},{8,0},{9,25... | collective-permute-start | bytes 3932168 | tf_op jit(solution)/shard_map/ppermute | solution.py:64
  364.5 16.6 %collective-permute-start.48 = (bf16[2,64,2048]{2,1,0:T(8,128)(2,1)S(1)}, bf16[2,64,2048]{2,1,0:T(8,128)(2,1)S(1)}, u32[]{:S(2)}, u32[]{:S(2)}) collective-permute-start(bf16[2,64,2048]{2,1,0:T(8,128)(2,1)S(1)} %add_convert_fusion.10), channel_id=1, source_target_pairs={{0,2},{1,3},{2,0},{3,1},{4,6},{5,7},{6,4},{7,5},{8,10},{9,11},{10,... | collective-permute-start | bytes 1572872 | tf_op jit(solution)/shard_map/ppermute | solution.py:64
  383.3 26.6 %collective-permute-start.53 = (bf16[4,64,2560]{2,1,0:T(8,128)(2,1)S(1)}, bf16[4,64,2560]{2,1,0:T(8,128)(2,1)}, u32[]{:S(2)}, u32[]{:S(2)}) collective-permute-start(bf16[4,64,2560]{2,1,0:T(8,128)(2,1)S(1)} %add_convert_fusion), channel_id=1, source_target_pairs={{0,2},{1,9},{2,0},{3,11},{4,6},{5,13},{6,4},{7,15},{8,10},{9,1},{1... | collective-permute-start | bytes 3932168 | tf_op jit(solution)/shard_map/ppermute | solution.py:64
  390.2 19.8 %collective-permute-start.51 = (bf16[4,64,1536]{2,1,0:T(8,128)(2,1)}, bf16[4,64,1536]{2,1,0:T(8,128)(2,1)}, u32[]{:S(2)}, u32[]{:S(2)}) collective-permute-start(bf16[4,64,1536]{2,1,0:T(8,128)(2,1)} %get-tuple-element.857), channel_id=1, source_target_pairs={{0,8},{1,17},{2,10},{3,19},{4,12},{5,21},{6,14},{7,23},{8,0},{9,25... | collective-permute-start | bytes 2359304 | tf_op jit(solution)/shard_map/ppermute | solution.py:64
  390.7 19.4 %collective-permute-start.52 = (bf16[4,64,1536]{2,1,0:T(8,128)(2,1)}, bf16[4,64,1536]{2,1,0:T(8,128)(2,1)}, u32[]{:S(2)}, u32[]{:S(2)}) collective-permute-start(bf16[4,64,1536]{2,1,0:T(8,128)(2,1)} %get-tuple-element.856), channel_id=1, source_target_pairs={{0,8},{1,17},{2,10},{3,19},{4,12},{5,21},{6,14},{7,23},{8,0},{9,25... | collective-permute-start | bytes 2359304 | tf_op jit(solution)/shard_map/ppermute | solution.py:64
  391.6 18.3 %collective-permute-start.54 = (bf16[1,64,2048]{2,1,0:T(8,128)(2,1)S(1)}, bf16[1,64,2048]{2,1,0:T(8,128)(2,1)S(1)}, u32[]{:S(2)}, u32[]{:S(2)}) collective-permute-start(bf16[1,64,2048]{2,1,0:T(8,128)(2,1)S(1)} %add_convert_fusion.13), channel_id=1, source_target_pairs={{0,4},{1,5},{2,6},{3,7},{4,0},{5,1},{6,2},{7,3},{8,12},{9,13},{10,... | collective-permute-start | bytes 786440 | tf_op jit(solution)/shard_map/ppermute | solution.py:64
  412.5 15.1 %collective-permute-start.55 = (bf16[4,64,1536]{2,1,0:T(8,128)(2,1)}, bf16[4,64,1536]{2,1,0:T(8,128)(2,1)}, u32[]{:S(2)}, u32[]{:S(2)}) collective-permute-start(bf16[4,64,1536]{2,1,0:T(8,128)(2,1)} %add_convert_fusion.6), channel_id=1, source_target_pairs={{0,2},{1,9},{2,0},{3,11},{4,6},{5,13},{6,4},{7,15},{8,10},{9,1},{1... | collective-permute-start | bytes 2359304 | tf_op jit(solution)/shard_map/ppermute | solution.py:64
  416.1 11.5 %collective-permute-start.56 = (bf16[2,64,2560]{2,1,0:T(8,128)(2,1)}, bf16[2,64,2560]{2,1,0:T(8,128)(2,1)}, u32[]{:S(2)}, u32[]{:S(2)}) collective-permute-start(bf16[2,64,2560]{2,1,0:T(8,128)(2,1)} %add_convert_fusion.9), channel_id=1, source_target_pairs={{0,16},{1,3},{2,18},{3,1},{4,20},{5,7},{6,22},{7,5},{8,24},{9,11},... | collective-permute-start | bytes 1966088 | tf_op jit(solution)/shard_map/ppermute | solution.py:64
  430.9 10.5 %collective-permute-start.63 = (bf16[1,64,2560]{2,1,0:T(8,128)(2,1)S(1)}, bf16[1,64,2560]{2,1,0:T(8,128)(2,1)S(1)}, u32[]{:S(2)}, u32[]{:S(2)}) collective-permute-start(bf16[1,64,2560]{2,1,0:T(8,128)(2,1)S(1)} %add_convert_fusion.12), channel_id=1, source_target_pairs={{0,4},{1,5},{2,6},{3,7},{4,0},{5,1},{6,2},{7,3},{8,12},{9,13},{10,... | collective-permute-start | bytes 983048 | tf_op jit(solution)/shard_map/ppermute | solution.py:64
  432.9 23.0 %collective-permute-start.59 = (bf16[2,64,1536]{2,1,0:T(8,128)(2,1)S(1)}, bf16[2,64,1536]{2,1,0:T(8,128)(2,1)S(1)}, u32[]{:S(2)}, u32[]{:S(2)}) collective-permute-start(bf16[2,64,1536]{2,1,0:T(8,128)(2,1)S(1)} %add_convert_fusion.11), channel_id=1, source_target_pairs={{0,16},{1,3},{2,18},{3,1},{4,20},{5,7},{6,22},{7,5},{8,24},{9,11},... | collective-permute-start | bytes 1179656 | tf_op jit(solution)/shard_map/ppermute | solution.py:64
  443.0 17.7 %collective-permute-start.67 = (f32[64,512]{1,0:T(8,128)S(1)}, f32[64,512]{1,0:T(8,128)S(1)}, u32[]{:S(2)}, u32[]{:S(2)}) collective-permute-start(f32[64,512]{1,0:T(8,128)S(1)} %slice_select_fusion.1), channel_id=1, source_target_pairs={{0,1},{1,0},{2,3},{3,2},{4,5},{5,4},{6,7},{7,6},{8,9},{9,8},{10,11... | collective-permute-start | bytes 393224 | tf_op jit(solution)/shard_map/ppermute | solution.py:40
  457.8 11.7 %collective-permute-start.65 = (bf16[1,64,1536]{2,1,0:T(8,128)(2,1)S(1)}, bf16[1,64,1536]{2,1,0:T(8,128)(2,1)S(1)}, u32[]{:S(2)}, u32[]{:S(2)}) collective-permute-start(bf16[1,64,1536]{2,1,0:T(8,128)(2,1)S(1)} %add_convert_fusion.14), channel_id=1, source_target_pairs={{0,4},{1,5},{2,6},{3,7},{4,0},{5,1},{6,2},{7,3},{8,12},{9,13},{10,... | collective-permute-start | bytes 589832 | tf_op jit(solution)/shard_map/ppermute | solution.py:64
  460.8 10.9 %collective-permute-start.64 = (f32[32,1536]{1,0:T(8,128)S(1)}, f32[32,1536]{1,0:T(8,128)S(1)}, u32[]{:S(2)}, u32[]{:S(2)}) collective-permute-start(f32[32,1536]{1,0:T(8,128)S(1)} %get-tuple-element.883), channel_id=1, source_target_pairs={{0,1},{1,0},{2,3},{3,2},{4,5},{5,4},{6,7},{7,6},{8,9},{9,8},{10,11... | collective-permute-start | bytes 589832 | tf_op jit(solution)/shard_map/ppermute | solution.py:40
  (135 other events, 1646.0 us)

commit v5 on v4

--- a/solution.py
+++ b/solution.py
@@ -900,13 +900,14 @@
         table = table_step(table, done, bit)
     got_qkv, table = sync(got_qkv, table)
     part, got = qkv[None], got_qkv
+    start = lax.axis_index("seq") * length
     for turn in range(last - 1, 1, -1):
         part = join(part, got)
         got = step(part, turn, LONE)
         if turn == last - 1:
             table = table_step(table, done, 2)
-        part, got, table, w_gate, w_up, w_output, w_down, doc_flags = sync(
-            part, got, table, w_gate, w_up, w_output, w_down, doc_flags
+        part, got, table, w_gate, w_up, w_output, w_down, doc_flags, start = sync(
+            part, got, table, w_gate, w_up, w_output, w_down, doc_flags, start
         )
 
     part = join(part, got)
@@ -935,7 +936,7 @@
     ]
     group_gain = group_gain.reshape(H, 1, VH)
 
-    positions = lax.axis_index("seq") * length + jnp.arange(length, dtype=jnp.int32)
+    positions = start + jnp.arange(length, dtype=jnp.int32)
     frequency = 10000.0 ** (-jnp.arange(QK // 2, dtype=F32) / (QK // 2))
     angles = positions.astype(F32)[:, None] * frequency[None, :]
     cosine, sine = jnp.cos(angles), jnp.sin(angles)
@@ -1044,8 +1045,10 @@
     arrivals = hop(states, arrived, 3, False)
     ff_part = join(ff_part, ff_got)
     ff_got = step(ff_part, 1, EDGE)
-    states, arrived, arrivals, pieces, ff_part, ff_got = sync(
-        states, arrived, arrivals, pieces, ff_part, ff_got
+    go_own = settle(info_edge, pieces, True)
+    go_oth = swap(go_own, 1)
+    states, arrived, arrivals, go_own, go_oth, normed, ff_part, ff_got = sync(
+        states, arrived, arrivals, go_own, go_oth, normed, ff_part, ff_got
     )
     arrived = arrived + [arrivals]
 
@@ -1054,30 +1057,23 @@
         if phase == 4:
             ff_first = step(ff_part, 0, EDGE)
             ff_others = [swap(ff_part, 1), swap(ff_got, 1)]
-            go_own = settle(info_edge, pieces, True)
-            go_oth = swap(go_own, 1)
-        states, arrived, arrivals, go_own, go_oth, normed, ff_part, ff_got, ff_first, ff_others = (
-            sync(
-                states, arrived, arrivals, go_own, go_oth, normed, ff_part, ff_got, ff_first,
-                ff_others,
+            (gate,) = call(
+                gate_kernel,
+                H,
+                info,
+                [whole(normed), columns(go_own, 512, 0, True), columns(go_oth, 512, 0, False)],
+                [head_out(per_head + (VH,), F32)],
+                [],
+                4 * unit,
+                "gate",
+                20,
             )
+        states, arrived, arrivals, gate, ff_part, ff_got, ff_first, ff_others = sync(
+            states, arrived, arrivals, gate, ff_part, ff_got, ff_first, ff_others
         )
         arrived = arrived + [arrivals]
     state_own, state_oth = end_states(states, arrived, False)
-    (gate,) = call(
-        gate_kernel,
-        H,
-        info,
-        [whole(normed), columns(go_own, 512, 0, True), columns(go_oth, 512, 0, False)],
-        [head_out(per_head + (VH,), F32)],
-        [],
-        4 * unit,
-        "gate",
-        20,
-    )
-    state_own, state_oth, gate, ff_got, ff_first = sync(
-        state_own, state_oth, gate, ff_got, ff_first
-    )
+    state_own, state_oth, ff_got, ff_first = sync(state_own, state_oth, ff_got, ff_first)
     ff_second = step(ff_got, 0, EDGE)
     ff_others = ff_others + [swap(ff_first, 1)]
 
@@ -1313,21 +1309,20 @@
     go_sum = go_sum + go_next
     kv_next = shrink(kv_sum, 1, LONE)
     go_next = shrink(go_sum, 2, LONE)
-    for bit in bits[:2:-1]:
-        small = small + swap(small, bit)
+    small = small + swap(small, FAR)
     kv_sum, kv_next, go_sum, go_next, small = sync(kv_sum, kv_next, go_sum, go_next, small)
     kv_sum = kv_sum + kv_next
     go_sum = go_sum + go_next
     kv_next = shrink(kv_sum, 2, LONE)
     for turn in range(3, last + 1):
         go_sum = go_sum + shrink(go_sum, turn, LONE)
-    small = small + swap(small, bits[2])
+    small = small + swap(small, 2)
     ff_grad = summed(ff_sum, 0, 1)[0]
     kv_sum, kv_next, small, ff_grad = sync(kv_sum, kv_next, small, ff_grad)
     kv_sum = kv_sum + kv_next
     for turn in range(3, last + 1):
         kv_sum = kv_sum + shrink(kv_sum, turn, LONE)
-    for bit in bits[1::-1]:
+    for bit in bits[3:] + bits[:1]:
         small = small + swap(small, bit)
     group = small[4:6].reshape(-1)
     small = lax.dynamic_slice_in_dim(small, place() * sizes[0], sizes[0], 1)

time: 484 us -> 473 us (0.977)
  other arithmetic: 60.3 us -> 54.8 us
    ppermute x30, waiting for transfers between devices: 74.9 us -> 68.4 us  [step(): return lax.ppermute(values, AXES, pairs)]
    ppermute x32, waiting for transfers between devices: 39.1 us -> 45.3 us  [swap(): return lax.ppermute(values, AXES, [(i, i ^ bit) for i in range(devices())])]
    ppermute x30, starting transfers between devices: 29.2 us -> 23.3 us  [step(): return lax.ppermute(values, AXES, pairs)]
    convert_element_type x13, other arithmetic: 29.6 us -> 24.4 us  [upper_part(): return Piece(summed(pieces, start, stop).astype(BF16), start - shift)]
  transfers between devices with their start and end apart: 70 -> 70, of which waited for: 25 -> 30; matrix products, arithmetic and copies ran while one was open for 10% -> 9% of each run, Pallas kernels for 21% -> 21%
where the time goes in v5:
time: 473 us; the launch traced here: 465 us
  waiting for transfers between devices  166 us (35%)
  Pallas kernels  131 us (28%)
  starting transfers between devices  80.9 us (17%)
  other arithmetic  54.8 us (12%)
  local copies, waits for them, and re-layouts  28.6 us (6%)
    pallas_call x10, Pallas kernels, call(): pl.pallas_call(body, grid_spec=pltpu.PrefetchScalarGridSpec(num_scalar_pr...  119 us
    ppermute x30, waiting for transfers between devices, step(): return lax.ppermute(values, AXES, pairs)  68.4 us
    ppermute x8, waiting for transfers between devices, hop(): return lax.ppermute(message.astype(BF16), 'seq', pairs)  52.4 us
    ppermute x32, waiting for transfers between devices, swap(): return lax.ppermute(values, AXES, [(i, i ^ bit) for i in range(devices())])  45.3 us
    ppermute x32, starting transfers between devices, swap(): return lax.ppermute(values, AXES, [(i, i ^ bit) for i in range(devices())])  42.8 us
    unnamed x229, local copies, waits for them, and re-layouts  24.5 us
    convert_element_type x13, other arithmetic, upper_part(): return Piece(summed(pieces, start, stop).astype(BF16), start - shift)  24.4 us
    ppermute x30, starting transfers between devices, step(): return lax.ppermute(values, AXES, pairs)  23.3 us
  transfers between devices with their start and end apart: 70, of which 30 were waited for; matrix products, arithmetic and copies ran while one was open for 9% of the time, Pallas kernels for 21%

profile of v5, /device:TPU:1, one launch (start us, length us, event | category | flops | bytes accessed | tf_op | source)
XLA Modules:
  0.0 464.8 jit_solution(3330891581689719217)
XLA Ops:
  8.0 3.5 collective-permute-start.3
  12.7 12.7 %collective-permute-done.1.got_ref = bf16[1,64,2048]{2,1,0:T(8,128)(2,1)S(1)} collective-permute-done((bf16[1,64,2048]{2,1,0:T(8,128)(2,1)S(1)}, bf16[1,64,2048]{2,1,0:T(8,128)(2,1)S(1)}, u32[]{:S(2)}, u32[]{:S(2)}) %collective-permute-start.1) | collective-permute-done | bytes 262176 | tf_op jit(solution)/shard_map/ppermute | solution.py:64
  27.0 7.5 %collective-permute-done.5 = bf16[2,2,16,256]{3,2,1,0:T(8,128)(2,1)S(1)} collective-permute-done((bf16[2,2,16,256]{3,2,1,0:T(8,128)(2,1)S(1)}, bf16[2,2,16,256]{3,2,1,0:T(8,128)(2,1)S(1)}, u32[]{:S(2)}, u32[]{:S(2)}) %collective-permute-start.5) | collective-permute-done | bytes 32800 | tf_op jit(solution)/shard_map/ppermute | solution.py:40
  43.5 12.2 %collective-permute-done.10 = bf16[2,2,2,2,16,256]{5,4,3,1,2,0:T(8,128)(2,1)S(1)} collective-permute-done((bf16[2,2,2,2,16,256]{5,4,3,1,2,0:T(8,128)(2,1)S(1)}, bf16[2,2,2,2,16,256]{5,4,3,1,2,0:T(8,128)(2,1)S(1)}, u32[]{:S(2)}, u32[]{:S(2)}) %collective-permute-start.10) | collective-permute-done | bytes 131104 | tf_op jit(solution)/shard_map/ppermute | solution.py:40
  59.1 2.4 collective-permute-start.14
  61.5 2.6 norm.1
  67.8 11.1 %collective-permute-done.13.got_ref = bf16[1,64,2048]{2,1,0:T(8,128)(2,1)S(1)} collective-permute-done((bf16[1,64,2048]{2,1,0:T(8,128)(2,1)}, bf16[1,64,2048]{2,1,0:T(8,128)(2,1)S(1)}, u32[]{:S(2)}, u32[]{:S(2)}) %collective-permute-start.13) | collective-permute-done | bytes 262176 | tf_op jit(solution)/shard_map/ppermute | solution.py:64
  78.8 5.6 %collective-permute-done.14.got_ref = bf16[1,64,2048]{2,1,0:T(8,128)(2,1)S(1)} collective-permute-done((bf16[1,64,2048]{2,1,0:T(8,128)(2,1)S(1)}, bf16[1,64,2048]{2,1,0:T(8,128)(2,1)S(1)}, u32[]{:S(2)}, u32[]{:S(2)}) %collective-permute-start.14) | collective-permute-done | bytes 262176 | tf_op jit(solution)/shard_map/ppermute | solution.py:64
  90.2 13.5 %collective-permute-done.17.got_ref = bf16[2,64,2048]{2,1,0:T(8,128)(2,1)S(1)} collective-permute-done((bf16[2,64,2048]{2,1,0:T(8,128)(2,1)S(1)}, bf16[2,64,2048]{2,1,0:T(8,128)(2,1)S(1)}, u32[]{:S(2)}, u32[]{:S(2)}) %collective-permute-start.17) | collective-permute-done | bytes 524320 | tf_op jit(solution)/shard_map/ppermute | solution.py:64
  106.8 15.5 %project.1 = (bf16[4,512,256]{2,1,0:T(8,128)(2,1)}, bf16[4,512,256]{2,1,0:T(8,128)(2,1)}, bf16[4,512,512]{2,1,0:T(8,128)(2,1)}, bf16[4,512,256]{2,1,0:T(8,128)(2...) custom-call(s32[66]{0:T(128)} %copy-done.44, f32[4]{0:T(128)} %copy-done.56, ...), custom_call_target="tpu_custom_call" | custom-call | flops 1 | bytes 1 | tf_op jit(solution)/shard_map/project/pallas_call | solution.py:330
  123.2 4.0 collective-permute-done.20
  129.5 3.4 collective-permute-start.21
  132.9 10.1 %collective-permute-done.21 = bf16[2,256,512]{2,1,0:T(8,128)(2,1)S(1)} collective-permute-done((bf16[2,256,512]{2,1,0:T(8,128)(2,1)S(1)}, bf16[2,256,512]{2,1,0:T(8,128)(2,1)S(1)}, u32[]{:S(2)}, u32[]{:S(2)}) %collective-permute-start.21) | collective-permute-done | bytes 524320 | tf_op jit(solution)/shard_map/ppermute | solution.py:294
  146.6 4.9 %collective-permute-start.23 = (bf16[2,256,512]{2,1,0:T(8,128)(2,1)}, bf16[2,256,512]{2,1,0:T(8,128)(2,1)}, u32[]{:S(2)}, u32[]{:S(2)}) collective-permute-start(bf16[2,256,512]{2,1,0:T(8,128)(2,1)} %fusion.27), channel_id=1, source_target_pairs={{0,2},{1,3},{2,4},{3,5},{8,10},{9,11},{10,12},{11,13},{16,18},{17,... | collective-permute-start | bytes 1572872 | tf_op jit(solution)/shard_map/ppermute | solution.py:294
  151.6 8.3 %collective-permute-done.23 = bf16[2,256,512]{2,1,0:T(8,128)(2,1)} collective-permute-done((bf16[2,256,512]{2,1,0:T(8,128)(2,1)}, bf16[2,256,512]{2,1,0:T(8,128)(2,1)}, u32[]{:S(2)}, u32[]{:S(2)}) %collective-permute-start.23) | collective-permute-done | bytes 524320 | tf_op jit(solution)/shard_map/ppermute | solution.py:294
  163.1 3.3 collective-permute-start.26
  170.9 10.2 %collective-permute-done.27.refs_1_ = bf16[4,64,2048]{2,1,0:T(8,128)(2,1)} collective-permute-done((bf16[4,64,2048]{2,1,0:T(8,128)(2,1)S(1)}, bf16[4,64,2048]{2,1,0:T(8,128)(2,1)}, u32[]{:S(2)}, u32[]{:S(2)}) %collective-permute-start.27) | collective-permute-done | bytes 1048608 | tf_op jit(solution)/shard_map/ppermute | solution.py:64
  183.4 2.4 collective-permute-start.30
  188.6 2.2 copy-done.2
  190.8 2.2 copy-done.4
  193.0 3.8 gate.1
  197.2 2.9 select_bitcast_fusion.3
  201.8 2.3 collective-permute-done.32.state_oth
  205.7 11.8 %mix.1 = (f32[4,512,512]{2,1,0:T(8,128)S(1)}, bf16[4,512,512]{2,1,0:T(8,128)(2,1)S(1)}, f32[512,1024]{1,0:T(8,128)S(1)}, bf16[512,1024]{1,0:T(8,128)(2,1)S(1)}, bf16[1024,512]{1,0:T(8,128)(2,1)S(1)}) custom-call(s32[66]{0:T(128)S(1)} %copy-done.45, f32[4]{0:T(128)S(1)} %copy-done.57, bf16[512,1024]{1,0:T(8,128)(2,1)S(1)} %bitcast.251, ...), custom_call_target="tpu_custom_call" | custom-call | flops 1 | bytes 1 | tf_op jit(solution)/shard_map/mix/pallas_call | solution.py:330
  219.5 2.6 settle.6.up_own.down_own
  228.1 27.7 %feed.1 = (bf16[512,1024]{1,0:T(8,128)(2,1)}, f32[512,1024]{1,0:T(8,128)}, bf16[512,1024]{1,0:T(8,128)(2,1)S(1)}, f32[1,1024]{1,0:T(1,128)S(1)}, f32[1,1024]{1,0...) custom-call(s32[66]{0:T(128)S(1)} %concatenate.46.info_ref.info, f32[512,1024]{1,0:T(8,128)} %copy-done.38, ...), custom_call_target="tpu_custom_call" | custom-call | flops 1 | bytes 1 | tf_op jit(solution)/shard_map/feed/pallas_call | solution.py:330
  258.1 11.1 %unmix.1 = (bf16[4,512,512]{2,1,0:T(8,128)(2,1)S(1)}, bf16[4,512,512]{2,1,0:T(8,128)(2,1)S(1)}, f32[4,1,512]{2,1,0:T(1,128)S(1)}, f32[2,2,256,512]{3,2,1,0:T(8,128)S(1)}, f32[2,2,256,512]{3,2,1,0:T(8,128)S(1)}) custom-call(s32[66]{0:T(128)S(1)} %copy-done.45, f32[4]{0:T(128)S(1)} %copy-done.57, bf16[512,1024]{1,0:T(8,128)(2,1)S(1)} %get-tuple-element.609.grad_low, ...), custom_call_target="tpu_custom_call" | custom-call | flops 1 | bytes 1 | tf_op jit(solution)/shard_map/unmix/pallas_call | solution.py:330
  270.3 3.3 collective-permute-done.37
  275.0 7.8 %inside.1 = (bf16[4,512,256]{2,1,0:T(8,128)(2,1)S(1)}, f32[4,512,256]{2,1,0:T(8,128)S(1)}, f32[4,512,512]{2,1,0:T(8,128)S(1)}) custom-call(s32[66]{0:T(128)S(1)} %copy-done.45, f32[4]{0:T(128)S(1)} %copy-done.57, bf16[4,512,512]{2,1,0:T(8,128)(2,1)S(1)} %get-tuple-element.626.grad_ret, bf16[4,512,256]{2,1,0:T(8,128)(2,1)S(1)} %copy-done.10, ...), custom_call_target="tpu_custom_call" | custom-call | flops 1 | bytes 1 | tf_op jit(solution)/shard_map/inside/pallas_call | solution.py:330
  284.6 3.0 collective-permute-done.39
  289.9 11.4 %outer.1 = (bf16[16,64,2560]{2,1,0:T(8,128)(2,1)}, bf16[16,64,2560]{2,1,0:T(8,128)(2,1)}) custom-call(s32[66]{0:T(128)S(1)} %copy-done.45, bf16[512,1024]{1,0:T(8,128)(2,1)S(1)} %get-tuple-element.609.grad_low, bf16[1024,512]{1,0:T(8,128)(2,1)S(1)} %copy-done.27, bf16[4,512,512]{2,1,0:T(8,128)(2,1)S(1)} %copy-done.37, ...), custom_call_target="tpu_custom_call" | custom-call | flops 1 | bytes 1 | tf_op jit(solution)/shard_map/outer/pallas_call | solution.py:330
  301.3 2.2 add_convert_fusion.3
  307.9 22.9 %collective-permute-done.42 = bf16[2,256,512]{2,1,0:T(8,128)(2,1)S(1)} collective-permute-done((bf16[2,256,512]{2,1,0:T(8,128)(2,1)S(1)}, bf16[2,256,512]{2,1,0:T(8,128)(2,1)S(1)}, u32[]{:S(2)}, u32[]{:S(2)}) %collective-permute-start.42) | collective-permute-done | bytes 524320 | tf_op jit(solution)/shard_map/ppermute | solution.py:294
  330.9 2.7 add_convert_fusion.1
  339.2 11.1 %collective-permute-done.45 = bf16[2,256,512]{2,1,0:T(8,128)(2,1)} collective-permute-done((bf16[2,256,512]{2,1,0:T(8,128)(2,1)}, bf16[2,256,512]{2,1,0:T(8,128)(2,1)}, u32[]{:S(2)}, u32[]{:S(2)}) %collective-permute-start.45) | collective-permute-done | bytes 524320 | tf_op jit(solution)/shard_map/ppermute | solution.py:294
  355.4 2.3 collective-permute-done.47.state_oth
  359.8 9.6 %last.1 = (bf16[4,512,256]{2,1,0:T(8,128)(2,1)S(1)}, bf16[4,512,512]{2,1,0:T(8,128)(2,1)S(1)}, bf16[16,64,1536]{2,1,0:T(8,128)(2,1)S(1)}, bf16[16,64,1536]{2,1,0:T(8,128)(2,1)S(1)}) custom-call(s32[66]{0:T(128)S(1)} %copy-done.45, f32[4]{0:T(128)S(1)} %copy-done.57, bf16[1024,512]{1,0:T(8,128)(2,1)S(1)} %copy-done.28, bf16[4,512,256]{2,1,0:T(8,128)(2,1)S(1)} %copy-done.22, ...), custom_call_target="tpu_custom_call" | custom-call | flops 1 | bytes 1 | tf_op jit(solution)/shard_map/last/pallas_call | solution.py:330
  370.3 4.5 add_convert_fusion
  378.6 2.6 collective-permute-done.50
  385.3 17.5 %input.1 = (f32[512,1024]{1,0:T(8,128)}, f32[1,1024]{1,0:T(1,128)}, f32[1,1024]{1,0:T(1,128)}) custom-call(s32[66]{0:T(128)} %copy-done.44, bf16[512,1024]{1,0:T(8,128)(2,1)} %bitcast.249, bf16[1,1024]{1,0:T(2,128)(2,1)} %copy-done.55, f32[512,1024]{1,0:T(8,128)} %get-tuple-element.763.grad_hidden, bf16[4,512,256]{2,1,0:T(8,128)(2,1)} %copy-done.25, ...), custom_call_target="tpu_custom_call" | custom-call | flops 1 | bytes 1 | tf_op jit(solution)/shard_map/input/pallas_call | solution.py:330
  402.8 2.4 add_convert_fusion.6
  406.4 2.6 add_convert_fusion.9
  413.0 6.2 %collective-permute-done.57 = f32[8,1024]{1,0:T(8,128)S(1)} collective-permute-done((f32[8,1024]{1,0:T(8,128)S(1)}, f32[8,1024]{1,0:T(8,128)S(1)}, u32[]{:S(2)}, u32[]{:S(2)}) %collective-permute-start.57) | collective-permute-done | bytes 32800 | tf_op jit(solution)/shard_map/ppermute | solution.py:40
  421.2 2.5 collective-permute-start.59
  425.2 2.3 collective-permute-start.63
  429.0 6.9 %collective-permute-done.63 = bf16[1,64,2560]{2,1,0:T(8,128)(2,1)S(1)} collective-permute-done((bf16[1,64,2560]{2,1,0:T(8,128)(2,1)S(1)}, bf16[1,64,2560]{2,1,0:T(8,128)(2,1)S(1)}, u32[]{:S(2)}, u32[]{:S(2)}) %collective-permute-start.63) | collective-permute-done | bytes 327712 | tf_op jit(solution)/shard_map/ppermute | solution.py:64
  437.5 8.9 %collective-permute-start.67 = (f32[64,512]{1,0:T(8,128)S(1)}, f32[64,512]{1,0:T(8,128)S(1)}, u32[]{:S(2)}, u32[]{:S(2)}) collective-permute-start(f32[64,512]{1,0:T(8,128)S(1)} %slice_select_fusion.1), channel_id=1, source_target_pairs={{0,1},{1,0},{2,3},{3,2},{4,5},{5,4},{6,7},{7,6},{8,9},{9,8},{10,11... | collective-permute-start | bytes 393224 | tf_op jit(solution)/shard_map/ppermute | solution.py:40
  452.6 2.4 collective-permute-start.62
  (466 shorter events, 127.0 us)
Async XLA Ops:
  11.6 13.8 %collective-permute-start.1 = (bf16[1,64,2048]{2,1,0:T(8,128)(2,1)S(1)}, bf16[1,64,2048]{2,1,0:T(8,128)(2,1)S(1)}, u32[]{:S(2)}, u32[]{:S(2)}) collective-permute-start(bf16[1,64,2048]{2,1,0:T(8,128)(2,1)S(1)} %bitcast.252), channel_id=1, source_target_pairs={{0,4},{1,5},{2,6},{3,7},{4,0},{5,1},{6,2},{7,3},{8,12},{9,13},{10,... | collective-permute-start | bytes 786440 | tf_op jit(solution)/shard_map/ppermute | solution.py:64
  39.1 16.6 %collective-permute-start.6 = (bf16[4,64,2048]{2,1,0:T(8,128)(2,1)S(1)}, bf16[4,64,2048]{2,1,0:T(8,128)(2,1)}, u32[]{:S(2)}, u32[]{:S(2)}) collective-permute-start(bf16[4,64,2048]{2,1,0:T(8,128)(2,1)S(1)} %join.7.refs_0_), channel_id=1, source_target_pairs={{0,2},{1,9},{2,0},{3,11},{4,6},{5,13},{6,4},{7,15},{8,10},{9,1},{1... | collective-permute-start | bytes 3145736 | tf_op jit(solution)/shard_map/ppermute | solution.py:64
  41.7 14.0 %collective-permute-start.10 = (bf16[2,2,2,2,16,256]{5,4,3,1,2,0:T(8,128)(2,1)S(1)}, bf16[2,2,2,2,16,256]{5,4,3,1,2,0:T(8,128)(2,1)S(1)}, u32[]{:S(2)}, u32[]{:S(2)}) collective-permute-start(bf16[2,2,2,2,16,256]{5,4,3,1,2,0:T(8,128)(2,1)S(1)} %pad_maximum_fusion.9), channel_id=1, source_target_pairs={{0,8},{1,9},{2,10},{3,11},{4,12},{5,13},{6,14},{7,15},{8,0},{9,1},... | collective-permute-start | bytes 393224 | tf_op jit(solution)/shard_map/ppermute | solution.py:40
  57.4 27.0 %collective-permute-start.11 = (bf16[4,64,2048]{2,1,0:T(8,128)(2,1)S(1)}, bf16[4,64,2048]{2,1,0:T(8,128)(2,1)}, u32[]{:S(2)}, u32[]{:S(2)}) collective-permute-start(bf16[4,64,2048]{2,1,0:T(8,128)(2,1)S(1)} %join.7.refs_0_), channel_id=1, source_target_pairs={{0,8},{1,17},{2,10},{3,19},{4,12},{5,21},{6,14},{7,23},{8,0},{9,25... | collective-permute-start | bytes 3145736 | tf_op jit(solution)/shard_map/ppermute | solution.py:64
  57.6 26.8 %collective-permute-start.12 = (bf16[4,64,2048]{2,1,0:T(8,128)(2,1)}, bf16[4,64,2048]{2,1,0:T(8,128)(2,1)}, u32[]{:S(2)}, u32[]{:S(2)}) collective-permute-start(bf16[4,64,2048]{2,1,0:T(8,128)(2,1)} %collective-permute-done.6.refs_1_), channel_id=1, source_target_pairs={{0,8},{1,17},{2,10},{3,19},{4,12},{5,21},{6,14},{7,23},{8,0},{9,25... | collective-permute-start | bytes 3145736 | tf_op jit(solution)/shard_map/ppermute | solution.py:64
  59.1 19.7 %collective-permute-start.13 = (bf16[1,64,2048]{2,1,0:T(8,128)(2,1)}, bf16[1,64,2048]{2,1,0:T(8,128)(2,1)S(1)}, u32[]{:S(2)}, u32[]{:S(2)}) collective-permute-start(bf16[1,64,2048]{2,1,0:T(8,128)(2,1)} %maximum_bitcast_fusion.part_ref), channel_id=1, source_target_pairs={{0,4},{1,5},{2,6},{3,7},{4,0},{5,1},{6,2},{7,3},{8,12},{9,13},{10,... | collective-permute-start | bytes 786440 | tf_op jit(solution)/shard_map/ppermute | solution.py:64
  59.1 25.3 %collective-permute-start.14 = (bf16[1,64,2048]{2,1,0:T(8,128)(2,1)S(1)}, bf16[1,64,2048]{2,1,0:T(8,128)(2,1)S(1)}, u32[]{:S(2)}, u32[]{:S(2)}) collective-permute-start(bf16[1,64,2048]{2,1,0:T(8,128)(2,1)S(1)} %maximum_bitcast_fusion.1.part_ref), channel_id=1, source_target_pairs={{0,4},{1,5},{2,6},{3,7},{4,0},{5,1},{6,2},{7,3},{8,12},{9,13},{10,... | collective-permute-start | bytes 786440 | tf_op jit(solution)/shard_map/ppermute | solution.py:64
  88.6 15.1 %collective-permute-start.16 = (bf16[16,64,2048]{2,1,0:T(8,128)(2,1)S(1)}, bf16[16,64,2048]{2,1,0:T(8,128)(2,1)S(1)}, u32[]{:S(2)}, u32[]{:S(2)}) collective-permute-start(bf16[16,64,2048]{2,1,0:T(8,128)(2,1)S(1)} %settle.4.q_own.k_own.v_own), channel_id=1, source_target_pairs={{0,1},{1,0},{2,3},{3,2},{4,5},{5,4},{6,7},{7,6},{8,9},{9,8},{10,11... | collective-permute-start | bytes 12582920 | tf_op jit(solution)/shard_map/ppermute | solution.py:40
  90.1 13.6 %collective-permute-start.17 = (bf16[2,64,2048]{2,1,0:T(8,128)(2,1)S(1)}, bf16[2,64,2048]{2,1,0:T(8,128)(2,1)S(1)}, u32[]{:S(2)}, u32[]{:S(2)}) collective-permute-start(bf16[2,64,2048]{2,1,0:T(8,128)(2,1)S(1)} %join.8.part_ref), channel_id=1, source_target_pairs={{0,2},{1,3},{2,0},{3,1},{4,6},{5,7},{6,4},{7,5},{8,10},{9,11},{10,... | collective-permute-start | bytes 1572872 | tf_op jit(solution)/shard_map/ppermute | solution.py:64
  103.8 18.5 %collective-permute-start.18 = (bf16[4,64,2048]{2,1,0:T(8,128)(2,1)S(1)}, bf16[4,64,2048]{2,1,0:T(8,128)(2,1)}, u32[]{:S(2)}, u32[]{:S(2)}) collective-permute-start(bf16[4,64,2048]{2,1,0:T(8,128)(2,1)S(1)} %join.9.refs_0_), channel_id=1, source_target_pairs={{0,16},{1,9},{2,18},{3,11},{4,20},{5,13},{6,22},{7,15},{8,24},{9,1... | collective-permute-start | bytes 3145736 | tf_op jit(solution)/shard_map/ppermute | solution.py:64
  105.7 16.5 %collective-permute-start.19 = (bf16[2,64,2048]{2,1,0:T(8,128)(2,1)S(1)}, bf16[2,64,2048]{2,1,0:T(8,128)(2,1)S(1)}, u32[]{:S(2)}, u32[]{:S(2)}) collective-permute-start(bf16[2,64,2048]{2,1,0:T(8,128)(2,1)S(1)} %join.10.part_ref), channel_id=1, source_target_pairs={{0,2},{1,3},{2,0},{3,1},{4,6},{5,7},{6,4},{7,5},{8,10},{9,11},{10,... | collective-permute-start | bytes 1572872 | tf_op jit(solution)/shard_map/ppermute | solution.py:64
  127.2 15.8 %collective-permute-start.22 = (bf16[4,64,2048]{2,1,0:T(8,128)(2,1)S(1)}, bf16[4,64,2048]{2,1,0:T(8,128)(2,1)S(1)}, u32[]{:S(2)}, u32[]{:S(2)}) collective-permute-start(bf16[4,64,2048]{2,1,0:T(8,128)(2,1)S(1)} %join.9.refs_0_), channel_id=1, source_target_pairs={{0,8},{1,17},{2,10},{3,19},{4,12},{5,21},{6,14},{7,23},{8,0},{9,25... | collective-permute-start | bytes 3145736 | tf_op jit(solution)/shard_map/ppermute | solution.py:64
  129.5 13.5 %collective-permute-start.21 = (bf16[2,256,512]{2,1,0:T(8,128)(2,1)S(1)}, bf16[2,256,512]{2,1,0:T(8,128)(2,1)S(1)}, u32[]{:S(2)}, u32[]{:S(2)}) collective-permute-start(bf16[2,256,512]{2,1,0:T(8,128)(2,1)S(1)} %fusion.29), channel_id=1, source_target_pairs={{0,2},{1,3},{8,10},{9,11},{16,18},{17,19},{24,26},{25,27}} | collective-permute-start | bytes 1572872 | tf_op jit(solution)/shard_map/ppermute | solution.py:294
  144.1 15.8 %collective-permute-start.24 = (bf16[4,64,2048]{2,1,0:T(8,128)(2,1)}, bf16[4,64,2048]{2,1,0:T(8,128)(2,1)}, u32[]{:S(2)}, u32[]{:S(2)}) collective-permute-start(bf16[4,64,2048]{2,1,0:T(8,128)(2,1)} %collective-permute-done.18.refs_1_), channel_id=1, source_target_pairs={{0,8},{1,17},{2,10},{3,19},{4,12},{5,21},{6,14},{7,23},{8,0},{9,25... | collective-permute-start | bytes 3145736 | tf_op jit(solution)/shard_map/ppermute | solution.py:64
  146.6 13.3 %collective-permute-start.23 = (bf16[2,256,512]{2,1,0:T(8,128)(2,1)}, bf16[2,256,512]{2,1,0:T(8,128)(2,1)}, u32[]{:S(2)}, u32[]{:S(2)}) collective-permute-start(bf16[2,256,512]{2,1,0:T(8,128)(2,1)} %fusion.27), channel_id=1, source_target_pairs={{0,2},{1,3},{2,4},{3,5},{8,10},{9,11},{10,12},{11,13},{16,18},{17,... | collective-permute-start | bytes 1572872 | tf_op jit(solution)/shard_map/ppermute | solution.py:294
  163.1 17.9 %collective-permute-start.26 = (bf16[16,64,2048]{2,1,0:T(8,128)(2,1)S(1)}, bf16[16,64,2048]{2,1,0:T(8,128)(2,1)S(1)}, u32[]{:S(2)}, u32[]{:S(2)}) collective-permute-start(bf16[16,64,2048]{2,1,0:T(8,128)(2,1)S(1)} %settle.5.own.wo_own.g_own), channel_id=1, source_target_pairs={{0,1},{1,0},{2,3},{3,2},{4,5},{5,4},{6,7},{7,6},{8,9},{9,8},{10,11... | collective-permute-start | bytes 12582920 | tf_op jit(solution)/shard_map/ppermute | solution.py:40
  166.5 14.6 %collective-permute-start.27 = (bf16[4,64,2048]{2,1,0:T(8,128)(2,1)S(1)}, bf16[4,64,2048]{2,1,0:T(8,128)(2,1)}, u32[]{:S(2)}, u32[]{:S(2)}) collective-permute-start(bf16[4,64,2048]{2,1,0:T(8,128)(2,1)S(1)} %join.11.refs_0_), channel_id=1, source_target_pairs={{0,16},{1,9},{2,18},{3,11},{4,20},{5,13},{6,22},{7,15},{8,24},{9,1... | collective-permute-start | bytes 3145736 | tf_op jit(solution)/shard_map/ppermute | solution.py:64
  183.2 14.0 %collective-permute-start.29 = (bf16[4,64,2048]{2,1,0:T(8,128)(2,1)S(1)}, bf16[4,64,2048]{2,1,0:T(8,128)(2,1)}, u32[]{:S(2)}, u32[]{:S(2)}) collective-permute-start(bf16[4,64,2048]{2,1,0:T(8,128)(2,1)S(1)} %join.11.refs_0_), channel_id=1, source_target_pairs={{0,8},{1,17},{2,10},{3,19},{4,12},{5,21},{6,14},{7,23},{8,0},{9,25... | collective-permute-start | bytes 3145736 | tf_op jit(solution)/shard_map/ppermute | solution.py:64
  183.4 13.8 %collective-permute-start.30 = (bf16[4,64,2048]{2,1,0:T(8,128)(2,1)S(1)}, bf16[4,64,2048]{2,1,0:T(8,128)(2,1)}, u32[]{:S(2)}, u32[]{:S(2)}) collective-permute-start(bf16[4,64,2048]{2,1,0:T(8,128)(2,1)S(1)} %join.11.refs_0_), channel_id=1, source_target_pairs={{0,1},{1,0},{2,3},{3,2},{4,5},{5,4},{6,7},{7,6},{8,9},{9,8},{10,11... | collective-permute-start | bytes 3145736 | tf_op jit(solution)/shard_map/ppermute | solution.py:40
  185.8 11.4 %collective-permute-start.31 = (bf16[4,64,2048]{2,1,0:T(8,128)(2,1)}, bf16[4,64,2048]{2,1,0:T(8,128)(2,1)}, u32[]{:S(2)}, u32[]{:S(2)}) collective-permute-start(bf16[4,64,2048]{2,1,0:T(8,128)(2,1)} %collective-permute-done.27.refs_1_), channel_id=1, source_target_pairs={{0,1},{1,0},{2,3},{3,2},{4,5},{5,4},{6,7},{7,6},{8,9},{9,8},{10,11... | collective-permute-start | bytes 3145736 | tf_op jit(solution)/shard_map/ppermute | solution.py:40
  187.0 9.9 %collective-permute-start.28 = (bf16[2,256,512]{2,1,0:T(8,128)(2,1)}, bf16[2,256,512]{2,1,0:T(8,128)(2,1)}, u32[]{:S(2)}, u32[]{:S(2)}) collective-permute-start(bf16[2,256,512]{2,1,0:T(8,128)(2,1)} %fusion.21), channel_id=1, source_target_pairs={{4,6},{5,7},{12,14},{13,15},{20,22},{21,23},{28,30},{29,31}} | collective-permute-start | bytes 1572872 | tf_op jit(solution)/shard_map/ppermute | solution.py:294
  204.1 14.2 %collective-permute-start.33 = (bf16[4,64,2048]{2,1,0:T(8,128)(2,1)}, bf16[4,64,2048]{2,1,0:T(8,128)(2,1)S(1)}, u32[]{:S(2)}, u32[]{:S(2)}) collective-permute-start(bf16[4,64,2048]{2,1,0:T(8,128)(2,1)} %collective-permute-done.27.refs_1_), channel_id=1, source_target_pairs={{0,8},{1,17},{2,10},{3,19},{4,12},{5,21},{6,14},{7,23},{8,0},{9,25... | collective-permute-start | bytes 3145736 | tf_op jit(solution)/shard_map/ppermute | solution.py:64
  204.4 13.9 %collective-permute-start.34 = (bf16[4,64,2048]{2,1,0:T(8,128)(2,1)}, bf16[4,64,2048]{2,1,0:T(8,128)(2,1)S(1)}, u32[]{:S(2)}, u32[]{:S(2)}) collective-permute-start(bf16[4,64,2048]{2,1,0:T(8,128)(2,1)} %collective-permute-done.29.refs_2_), channel_id=1, source_target_pairs={{0,1},{1,0},{2,3},{3,2},{4,5},{5,4},{6,7},{7,6},{8,9},{9,8},{10,11... | collective-permute-start | bytes 3145736 | tf_op jit(solution)/shard_map/ppermute | solution.py:40
  255.8 13.5 %collective-permute-start.36 = (bf16[16,64,2048]{2,1,0:T(8,128)(2,1)}, bf16[16,64,2048]{2,1,0:T(8,128)(2,1)S(1)}, u32[]{:S(2)}, u32[]{:S(2)}) collective-permute-start(bf16[16,64,2048]{2,1,0:T(8,128)(2,1)} %get-tuple-element.608), channel_id=1, source_target_pairs={{0,1},{1,0},{2,3},{3,2},{4,5},{5,4},{6,7},{7,6},{8,9},{9,8},{10,11... | collective-permute-start | bytes 12582920 | tf_op jit(solution)/shard_map/ppermute | solution.py:40
  273.6 13.9 %collective-permute-start.39 = (bf16[4,64,2048]{2,1,0:T(8,128)(2,1)S(1)}, bf16[4,64,2048]{2,1,0:T(8,128)(2,1)S(1)}, u32[]{:S(2)}, u32[]{:S(2)}) collective-permute-start(bf16[4,64,2048]{2,1,0:T(8,128)(2,1)S(1)} %add_convert_fusion.5), channel_id=1, source_target_pairs={{0,8},{1,17},{2,10},{3,19},{4,12},{5,21},{6,14},{7,23},{8,0},{9,25... | collective-permute-start | bytes 3145736 | tf_op jit(solution)/shard_map/ppermute | solution.py:64
  274.3 10.3 %collective-permute-start.38 = (bf16[2,256,512]{2,1,0:T(8,128)(2,1)S(1)}, bf16[2,256,512]{2,1,0:T(8,128)(2,1)S(1)}, u32[]{:S(2)}, u32[]{:S(2)}) collective-permute-start(bf16[2,256,512]{2,1,0:T(8,128)(2,1)S(1)} %fusion.18), channel_id=1, source_target_pairs={{6,4},{7,5},{14,12},{15,13},{22,20},{23,21},{30,28},{31,29}} | collective-permute-start | bytes 1572872 | tf_op jit(solution)/shard_map/ppermute | solution.py:294
  287.6 15.9 %collective-permute-start.41 = (bf16[4,64,2048]{2,1,0:T(8,128)(2,1)S(1)}, bf16[4,64,2048]{2,1,0:T(8,128)(2,1)S(1)}, u32[]{:S(2)}, u32[]{:S(2)}) collective-permute-start(bf16[4,64,2048]{2,1,0:T(8,128)(2,1)S(1)} %add_convert_fusion.4), channel_id=1, source_target_pairs={{0,8},{1,17},{2,10},{3,19},{4,12},{5,21},{6,14},{7,23},{8,0},{9,25... | collective-permute-start | bytes 3145736 | tf_op jit(solution)/shard_map/ppermute | solution.py:64
  289.1 14.4 %collective-permute-start.40 = (bf16[2,256,512]{2,1,0:T(8,128)(2,1)}, bf16[2,256,512]{2,1,0:T(8,128)(2,1)S(1)}, u32[]{:S(2)}, u32[]{:S(2)}) collective-permute-start(bf16[2,256,512]{2,1,0:T(8,128)(2,1)} %fusion.16), channel_id=1, source_target_pairs={{6,4},{7,5},{4,2},{5,3},{14,12},{15,13},{12,10},{13,11},{22,20},{2... | collective-permute-start | bytes 1572872 | tf_op jit(solution)/shard_map/ppermute | solution.py:294
  303.5 27.3 %collective-permute-start.43 = (bf16[16,64,2560]{2,1,0:T(8,128)(2,1)}, bf16[16,64,2560]{2,1,0:T(8,128)(2,1)S(1)}, u32[]{:S(2)}, u32[]{:S(2)}) collective-permute-start(bf16[16,64,2560]{2,1,0:T(8,128)(2,1)} %get-tuple-element.678), channel_id=1, source_target_pairs={{0,1},{1,0},{2,3},{3,2},{4,5},{5,4},{6,7},{7,6},{8,9},{9,8},{10,11... | collective-permute-start | bytes 15728648 | tf_op jit(solution)/shard_map/ppermute | solution.py:40
  305.3 25.6 %collective-permute-start.44 = (bf16[4,64,2048]{2,1,0:T(8,128)(2,1)S(1)}, bf16[4,64,2048]{2,1,0:T(8,128)(2,1)S(1)}, u32[]{:S(2)}, u32[]{:S(2)}) collective-permute-start(bf16[4,64,2048]{2,1,0:T(8,128)(2,1)S(1)} %add_convert_fusion.3), channel_id=1, source_target_pairs={{0,16},{1,9},{2,18},{3,11},{4,20},{5,13},{6,22},{7,15},{8,24},{9,1... | collective-permute-start | bytes 3145736 | tf_op jit(solution)/shard_map/ppermute | solution.py:64
  306.6 24.2 %collective-permute-start.42 = (bf16[2,256,512]{2,1,0:T(8,128)(2,1)S(1)}, bf16[2,256,512]{2,1,0:T(8,128)(2,1)S(1)}, u32[]{:S(2)}, u32[]{:S(2)}) collective-permute-start(bf16[2,256,512]{2,1,0:T(8,128)(2,1)S(1)} %fusion.13), channel_id=1, source_target_pairs={{4,2},{5,3},{2,0},{3,1},{12,10},{13,11},{10,8},{11,9},{20,18},{21,... | collective-permute-start | bytes 1572872 | tf_op jit(solution)/shard_map/ppermute | solution.py:294
  334.4 17.1 %collective-permute-start.46 = (bf16[4,64,2560]{2,1,0:T(8,128)(2,1)}, bf16[4,64,2560]{2,1,0:T(8,128)(2,1)}, u32[]{:S(2)}, u32[]{:S(2)}) collective-permute-start(bf16[4,64,2560]{2,1,0:T(8,128)(2,1)} %get-tuple-element.849), channel_id=1, source_target_pairs={{0,8},{1,17},{2,10},{3,19},{4,12},{5,21},{6,14},{7,23},{8,0},{9,25... | collective-permute-start | bytes 3932168 | tf_op jit(solution)/shard_map/ppermute | solution.py:64
  335.9 14.4 %collective-permute-start.45 = (bf16[2,256,512]{2,1,0:T(8,128)(2,1)}, bf16[2,256,512]{2,1,0:T(8,128)(2,1)}, u32[]{:S(2)}, u32[]{:S(2)}) collective-permute-start(bf16[2,256,512]{2,1,0:T(8,128)(2,1)} %fusion.10), channel_id=1, source_target_pairs={{2,0},{3,1},{10,8},{11,9},{18,16},{19,17},{26,24},{27,25}} | collective-permute-start | bytes 1572872 | tf_op jit(solution)/shard_map/ppermute | solution.py:294
  357.6 17.2 %collective-permute-start.49 = (bf16[4,64,2560]{2,1,0:T(8,128)(2,1)}, bf16[4,64,2560]{2,1,0:T(8,128)(2,1)S(1)}, u32[]{:S(2)}, u32[]{:S(2)}) collective-permute-start(bf16[4,64,2560]{2,1,0:T(8,128)(2,1)} %get-tuple-element.732), channel_id=1, source_target_pairs={{0,8},{1,17},{2,10},{3,19},{4,12},{5,21},{6,14},{7,23},{8,0},{9,25... | collective-permute-start | bytes 3932168 | tf_op jit(solution)/shard_map/ppermute | solution.py:64
  358.6 16.2 %collective-permute-start.48 = (bf16[2,64,2048]{2,1,0:T(8,128)(2,1)S(1)}, bf16[2,64,2048]{2,1,0:T(8,128)(2,1)S(1)}, u32[]{:S(2)}, u32[]{:S(2)}) collective-permute-start(bf16[2,64,2048]{2,1,0:T(8,128)(2,1)S(1)} %add_convert_fusion.10), channel_id=1, source_target_pairs={{0,2},{1,3},{2,0},{3,1},{4,6},{5,7},{6,4},{7,5},{8,10},{9,11},{10,... | collective-permute-start | bytes 1572872 | tf_op jit(solution)/shard_map/ppermute | solution.py:64
  375.9 26.9 %collective-permute-start.53 = (bf16[4,64,2560]{2,1,0:T(8,128)(2,1)S(1)}, bf16[4,64,2560]{2,1,0:T(8,128)(2,1)}, u32[]{:S(2)}, u32[]{:S(2)}) collective-permute-start(bf16[4,64,2560]{2,1,0:T(8,128)(2,1)S(1)} %add_convert_fusion), channel_id=1, source_target_pairs={{0,2},{1,9},{2,0},{3,11},{4,6},{5,13},{6,4},{7,15},{8,10},{9,1},{1... | collective-permute-start | bytes 3932168 | tf_op jit(solution)/shard_map/ppermute | solution.py:64
  382.7 20.0 %collective-permute-start.51 = (bf16[4,64,1536]{2,1,0:T(8,128)(2,1)}, bf16[4,64,1536]{2,1,0:T(8,128)(2,1)}, u32[]{:S(2)}, u32[]{:S(2)}) collective-permute-start(bf16[4,64,1536]{2,1,0:T(8,128)(2,1)} %get-tuple-element.851), channel_id=1, source_target_pairs={{0,8},{1,17},{2,10},{3,19},{4,12},{5,21},{6,14},{7,23},{8,0},{9,25... | collective-permute-start | bytes 2359304 | tf_op jit(solution)/shard_map/ppermute | solution.py:64
  383.7 19.1 %collective-permute-start.52 = (bf16[4,64,1536]{2,1,0:T(8,128)(2,1)}, bf16[4,64,1536]{2,1,0:T(8,128)(2,1)}, u32[]{:S(2)}, u32[]{:S(2)}) collective-permute-start(bf16[4,64,1536]{2,1,0:T(8,128)(2,1)} %get-tuple-element.850), channel_id=1, source_target_pairs={{0,8},{1,17},{2,10},{3,19},{4,12},{5,21},{6,14},{7,23},{8,0},{9,25... | collective-permute-start | bytes 2359304 | tf_op jit(solution)/shard_map/ppermute | solution.py:64
  384.2 18.6 %collective-permute-start.54 = (bf16[1,64,2048]{2,1,0:T(8,128)(2,1)S(1)}, bf16[1,64,2048]{2,1,0:T(8,128)(2,1)S(1)}, u32[]{:S(2)}, u32[]{:S(2)}) collective-permute-start(bf16[1,64,2048]{2,1,0:T(8,128)(2,1)S(1)} %add_convert_fusion.13), channel_id=1, source_target_pairs={{0,4},{1,5},{2,6},{3,7},{4,0},{5,1},{6,2},{7,3},{8,12},{9,13},{10,... | collective-permute-start | bytes 786440 | tf_op jit(solution)/shard_map/ppermute | solution.py:64
  405.2 16.0 %collective-permute-start.55 = (bf16[4,64,1536]{2,1,0:T(8,128)(2,1)}, bf16[4,64,1536]{2,1,0:T(8,128)(2,1)}, u32[]{:S(2)}, u32[]{:S(2)}) collective-permute-start(bf16[4,64,1536]{2,1,0:T(8,128)(2,1)} %add_convert_fusion.6), channel_id=1, source_target_pairs={{0,2},{1,9},{2,0},{3,11},{4,6},{5,13},{6,4},{7,15},{8,10},{9,1},{1... | collective-permute-start | bytes 2359304 | tf_op jit(solution)/shard_map/ppermute | solution.py:64
  409.0 12.2 %collective-permute-start.56 = (bf16[2,64,2560]{2,1,0:T(8,128)(2,1)}, bf16[2,64,2560]{2,1,0:T(8,128)(2,1)}, u32[]{:S(2)}, u32[]{:S(2)}) collective-permute-start(bf16[2,64,2560]{2,1,0:T(8,128)(2,1)} %add_convert_fusion.9), channel_id=1, source_target_pairs={{0,16},{1,3},{2,18},{3,1},{4,20},{5,7},{6,22},{7,5},{8,24},{9,11},... | collective-permute-start | bytes 1966088 | tf_op jit(solution)/shard_map/ppermute | solution.py:64
  425.2 10.8 %collective-permute-start.63 = (bf16[1,64,2560]{2,1,0:T(8,128)(2,1)S(1)}, bf16[1,64,2560]{2,1,0:T(8,128)(2,1)S(1)}, u32[]{:S(2)}, u32[]{:S(2)}) collective-permute-start(bf16[1,64,2560]{2,1,0:T(8,128)(2,1)S(1)} %add_convert_fusion.12), channel_id=1, source_target_pairs={{0,4},{1,5},{2,6},{3,7},{4,0},{5,1},{6,2},{7,3},{8,12},{9,13},{10,... | collective-permute-start | bytes 983048 | tf_op jit(solution)/shard_map/ppermute | solution.py:64
  428.9 17.5 %collective-permute-start.58 = (bf16[2,64,1536]{2,1,0:T(8,128)(2,1)S(1)}, bf16[2,64,1536]{2,1,0:T(8,128)(2,1)S(1)}, u32[]{:S(2)}, u32[]{:S(2)}) collective-permute-start(bf16[2,64,1536]{2,1,0:T(8,128)(2,1)S(1)} %add_convert_fusion.11), channel_id=1, source_target_pairs={{0,16},{1,3},{2,18},{3,1},{4,20},{5,7},{6,22},{7,5},{8,24},{9,11},... | collective-permute-start | bytes 1179656 | tf_op jit(solution)/shard_map/ppermute | solution.py:64
  437.5 13.0 %collective-permute-start.67 = (f32[64,512]{1,0:T(8,128)S(1)}, f32[64,512]{1,0:T(8,128)S(1)}, u32[]{:S(2)}, u32[]{:S(2)}) collective-permute-start(f32[64,512]{1,0:T(8,128)S(1)} %slice_select_fusion.1), channel_id=1, source_target_pairs={{0,1},{1,0},{2,3},{3,2},{4,5},{5,4},{6,7},{7,6},{8,9},{9,8},{10,11... | collective-permute-start | bytes 393224 | tf_op jit(solution)/shard_map/ppermute | solution.py:40
  446.4 10.6 %collective-permute-start.69 = (f32[64,512]{1,0:T(8,128)S(1)}, f32[64,512]{1,0:T(8,128)S(1)}, u32[]{:S(2)}, u32[]{:S(2)}) collective-permute-start(f32[64,512]{1,0:T(8,128)S(1)} %slice_select_fusion.7), channel_id=1, source_target_pairs={{0,1},{1,0},{2,3},{3,2},{4,5},{5,4},{6,7},{7,6},{8,9},{9,8},{10,11... | collective-permute-start | bytes 393224 | tf_op jit(solution)/shard_map/ppermute | solution.py:40
  446.5 11.2 %collective-permute-start.68 = (f32[32,1024]{1,0:T(8,128)S(1)}, f32[32,1024]{1,0:T(8,128)S(1)}, u32[]{:S(2)}, u32[]{:S(2)}) collective-permute-start(f32[32,1024]{1,0:T(8,128)S(1)} %slice_select_fusion.9), channel_id=1, source_target_pairs={{0,1},{1,0},{2,3},{3,2},{4,5},{5,4},{6,7},{7,6},{8,9},{9,8},{10,11... | collective-permute-start | bytes 393224 | tf_op jit(solution)/shard_map/ppermute | solution.py:40
  448.6 11.1 %collective-permute-start.65 = (bf16[1,64,1536]{2,1,0:T(8,128)(2,1)S(1)}, bf16[1,64,1536]{2,1,0:T(8,128)(2,1)S(1)}, u32[]{:S(2)}, u32[]{:S(2)}) collective-permute-start(bf16[1,64,1536]{2,1,0:T(8,128)(2,1)S(1)} %add_convert_fusion.14), channel_id=1, source_target_pairs={{0,4},{1,5},{2,6},{3,7},{4,0},{5,1},{6,2},{7,3},{8,12},{9,13},{10,... | collective-permute-start | bytes 589832 | tf_op jit(solution)/shard_map/ppermute | solution.py:64
  450.6 10.9 %collective-permute-start.64 = (f32[32,1536]{1,0:T(8,128)S(1)}, f32[32,1536]{1,0:T(8,128)S(1)}, u32[]{:S(2)}, u32[]{:S(2)}) collective-permute-start(f32[32,1536]{1,0:T(8,128)S(1)} %get-tuple-element.877), channel_id=1, source_target_pairs={{0,1},{1,0},{2,3},{3,2},{4,5},{5,4},{6,7},{7,6},{8,9},{9,8},{10,11... | collective-permute-start | bytes 589832 | tf_op jit(solution)/shard_map/ppermute | solution.py:40
  (135 other events, 1635.6 us)

commit v6 on v5

--- a/solution.py
+++ b/solution.py
@@ -1022,8 +1022,9 @@
         ff_got = step(ff_part, turn + 1, EDGE)
         go_part, go_got, ff_part, ff_got = sync(go_part, go_got, ff_part, ff_got)
     sum_near = swap(sum_oth, 1)
-    sum_own, sum_near, go_part, go_got, ff_part, ff_got = sync(
-        sum_own, sum_near, go_part, go_got, ff_part, ff_got
+    ff_part = join(ff_part, ff_got)
+    sum_own, sum_near, go_part, go_got, ff_part = sync(
+        sum_own, sum_near, go_part, go_got, ff_part
     )
 
     states = tuple(ahead) + (sum_own, sum_near)
@@ -1037,13 +1038,12 @@
 
     arrivals = hop(states, arrived, 2, False)
     go_second = step(go_got, 0, EDGE)
-    states, arrived, arrivals, pieces, ff_part, ff_got = sync(
-        states, arrived, arrivals, [go_part, go_got, go_first, go_second], ff_part, ff_got
+    states, arrived, arrivals, pieces, ff_part = sync(
+        states, arrived, arrivals, [go_part, go_got, go_first, go_second], ff_part
     )
     arrived = arrived + [arrivals]
 
     arrivals = hop(states, arrived, 3, False)
-    ff_part = join(ff_part, ff_got)
     ff_got = step(ff_part, 1, EDGE)
     go_own = settle(info_edge, pieces, True)
     go_oth = swap(go_own, 1)
@@ -1213,16 +1213,17 @@
     arrivals = hop(states, arrived, 3, True)
     go_g_got = swap(go_g_oth, 1)
     ff_sum = ff_sum + send(ff_next, 1, EDGE)
-    states, arrived, arrivals, go_g_own, go_g_got, ff_sum = sync(
-        states, arrived, arrivals, go_g_own, go_g_got, ff_sum
+    go_sum = [Piece(go_g_own), Piece(go_g_got)]
+    go_first = upper_part(go_sum, 0, 1)
+    states, arrived, arrivals, go_sum, go_first, ff_sum = sync(
+        states, arrived, arrivals, go_sum, go_first, ff_sum
     )
     arrived = arrived + [arrivals]
 
-    go_sum = [Piece(go_g_own), Piece(go_g_got)]
     for phase in range(4, phases + 1):
         arrivals = hop(states, arrived, phase, True)
         if phase == 4:
-            go_first = shrink(go_sum, 0, LONE, 1)
+            go_first = send(go_first, 0, LONE)
             go_second = upper_part(go_sum, 0, 0)
             ff_next = upper_part(ff_sum, 2)
         states, arrived, arrivals, go_sum, go_first, go_second, ff_sum, ff_next = sync(

time: 473 us -> 469 us (level)
  waiting for transfers between devices: 166 us -> 158 us
    ppermute x8, waiting for transfers between devices: 52.4 us -> 40.8 us  [hop(): return lax.ppermute(message.astype(BF16), 'seq', pairs)]
    unnamed x229 -> x223, local copies, waits for them, and re-layouts: 24.5 us -> 28.7 us
    convert_element_type x13 -> x14, other arithmetic: 24.4 us -> 25.8 us  [upper_part(): return Piece(summed(pieces, start, stop).astype(BF16), start - shift)]
  transfers between devices with their start and end apart: 70 -> 70, of which waited for: 30 -> 32; matrix products, arithmetic and copies ran while one was open for 9% -> 10% of each run, Pallas kernels for 21% -> 21%
where the time goes in v6:
time: 469 us; the launch traced here: 461 us
  waiting for transfers between devices  158 us (34%)
  Pallas kernels  131 us (28%)
  starting transfers between devices  82.6 us (18%)
  other arithmetic  53.1 us (11%)
  local copies, waits for them, and re-layouts  32.9 us (7%)
    pallas_call x10, Pallas kernels, call(): pl.pallas_call(body, grid_spec=pltpu.PrefetchScalarGridSpec(num_scalar_pr...  119 us
    ppermute x30, waiting for transfers between devices, step(): return lax.ppermute(values, AXES, pairs)  69.6 us
    ppermute x32, waiting for transfers between devices, swap(): return lax.ppermute(values, AXES, [(i, i ^ bit) for i in range(devices())])  47.5 us
    ppermute x32, starting transfers between devices, swap(): return lax.ppermute(values, AXES, [(i, i ^ bit) for i in range(devices())])  43.2 us
    ppermute x8, waiting for transfers between devices, hop(): return lax.ppermute(message.astype(BF16), 'seq', pairs)  40.8 us
    unnamed x223, local copies, waits for them, and re-layouts  28.7 us
    convert_element_type x14, other arithmetic, upper_part(): return Piece(summed(pieces, start, stop).astype(BF16), start - shift)  25.8 us
    ppermute x30, starting transfers between devices, step(): return lax.ppermute(values, AXES, pairs)  23.7 us
  transfers between devices with their start and end apart: 70, of which 32 were waited for; matrix products, arithmetic and copies ran while one was open for 10% of the time, Pallas kernels for 21%

profile of v6, /device:TPU:1, one launch (start us, length us, event | category | flops | bytes accessed | tf_op | source)
XLA Modules:
  0.0 460.6 jit_solution(6097590452871874965)
XLA Ops:
  8.0 3.5 collective-permute-start.3
  12.7 12.7 %collective-permute-done.1.got_ref = bf16[1,64,2048]{2,1,0:T(8,128)(2,1)S(1)} collective-permute-done((bf16[1,64,2048]{2,1,0:T(8,128)(2,1)S(1)}, bf16[1,64,2048]{2,1,0:T(8,128)(2,1)S(1)}, u32[]{:S(2)}, u32[]{:S(2)}) %collective-permute-start.1) | collective-permute-done | bytes 262176 | tf_op jit(solution)/shard_map/ppermute | solution.py:64
  27.0 7.5 %collective-permute-done.5 = bf16[2,2,16,256]{3,2,1,0:T(8,128)(2,1)S(1)} collective-permute-done((bf16[2,2,16,256]{3,2,1,0:T(8,128)(2,1)S(1)}, bf16[2,2,16,256]{3,2,1,0:T(8,128)(2,1)S(1)}, u32[]{:S(2)}, u32[]{:S(2)}) %collective-permute-start.5) | collective-permute-done | bytes 32800 | tf_op jit(solution)/shard_map/ppermute | solution.py:40
  43.5 12.2 %collective-permute-done.10 = bf16[2,2,2,2,16,256]{5,4,3,1,2,0:T(8,128)(2,1)S(1)} collective-permute-done((bf16[2,2,2,2,16,256]{5,4,3,1,2,0:T(8,128)(2,1)S(1)}, bf16[2,2,2,2,16,256]{5,4,3,1,2,0:T(8,128)(2,1)S(1)}, u32[]{:S(2)}, u32[]{:S(2)}) %collective-permute-start.10) | collective-permute-done | bytes 131104 | tf_op jit(solution)/shard_map/ppermute | solution.py:40
  59.1 2.4 collective-permute-start.14
  61.5 2.6 norm.1
  67.8 11.1 %collective-permute-done.13.got_ref = bf16[1,64,2048]{2,1,0:T(8,128)(2,1)S(1)} collective-permute-done((bf16[1,64,2048]{2,1,0:T(8,128)(2,1)}, bf16[1,64,2048]{2,1,0:T(8,128)(2,1)S(1)}, u32[]{:S(2)}, u32[]{:S(2)}) %collective-permute-start.13) | collective-permute-done | bytes 262176 | tf_op jit(solution)/shard_map/ppermute | solution.py:64
  78.8 5.6 %collective-permute-done.14.got_ref = bf16[1,64,2048]{2,1,0:T(8,128)(2,1)S(1)} collective-permute-done((bf16[1,64,2048]{2,1,0:T(8,128)(2,1)S(1)}, bf16[1,64,2048]{2,1,0:T(8,128)(2,1)S(1)}, u32[]{:S(2)}, u32[]{:S(2)}) %collective-permute-start.14) | collective-permute-done | bytes 262176 | tf_op jit(solution)/shard_map/ppermute | solution.py:64
  90.3 13.5 %collective-permute-done.17.got_ref = bf16[2,64,2048]{2,1,0:T(8,128)(2,1)S(1)} collective-permute-done((bf16[2,64,2048]{2,1,0:T(8,128)(2,1)S(1)}, bf16[2,64,2048]{2,1,0:T(8,128)(2,1)S(1)}, u32[]{:S(2)}, u32[]{:S(2)}) %collective-permute-start.17) | collective-permute-done | bytes 524320 | tf_op jit(solution)/shard_map/ppermute | solution.py:64
  106.9 15.4 %project.1 = (bf16[4,512,256]{2,1,0:T(8,128)(2,1)}, bf16[4,512,256]{2,1,0:T(8,128)(2,1)}, bf16[4,512,512]{2,1,0:T(8,128)(2,1)}, bf16[4,512,256]{2,1,0:T(8,128)(2...) custom-call(s32[66]{0:T(128)} %copy-done.48, f32[4]{0:T(128)} %copy-done.60, ...), custom_call_target="tpu_custom_call" | custom-call | flops 1 | bytes 1 | tf_op jit(solution)/shard_map/project/pallas_call | solution.py:330
  128.6 3.4 collective-permute-start.21
  132.0 9.5 %collective-permute-done.21 = bf16[2,256,512]{2,1,0:T(8,128)(2,1)S(1)} collective-permute-done((bf16[2,256,512]{2,1,0:T(8,128)(2,1)S(1)}, bf16[2,256,512]{2,1,0:T(8,128)(2,1)S(1)}, u32[]{:S(2)}, u32[]{:S(2)}) %collective-permute-start.21) | collective-permute-done | bytes 524320 | tf_op jit(solution)/shard_map/ppermute | solution.py:294
  146.1 4.9 %collective-permute-start.23 = (bf16[2,256,512]{2,1,0:T(8,128)(2,1)}, bf16[2,256,512]{2,1,0:T(8,128)(2,1)}, u32[]{:S(2)}, u32[]{:S(2)}) collective-permute-start(bf16[2,256,512]{2,1,0:T(8,128)(2,1)} %fusion.27), channel_id=1, source_target_pairs={{0,2},{1,3},{2,4},{3,5},{8,10},{9,11},{10,12},{11,13},{16,18},{17,... | collective-permute-start | bytes 1572872 | tf_op jit(solution)/shard_map/ppermute | solution.py:294
  151.1 8.8 %collective-permute-done.23 = bf16[2,256,512]{2,1,0:T(8,128)(2,1)} collective-permute-done((bf16[2,256,512]{2,1,0:T(8,128)(2,1)}, bf16[2,256,512]{2,1,0:T(8,128)(2,1)}, u32[]{:S(2)}, u32[]{:S(2)}) %collective-permute-start.23) | collective-permute-done | bytes 524320 | tf_op jit(solution)/shard_map/ppermute | solution.py:294
  163.1 2.7 collective-permute-start.26
  165.9 2.2 collective-permute-start.27
  170.4 10.1 %collective-permute-done.27.refs_1_ = bf16[4,64,2048]{2,1,0:T(8,128)(2,1)} collective-permute-done((bf16[4,64,2048]{2,1,0:T(8,128)(2,1)S(1)}, bf16[4,64,2048]{2,1,0:T(8,128)(2,1)}, u32[]{:S(2)}, u32[]{:S(2)}) %collective-permute-start.27) | collective-permute-done | bytes 1048608 | tf_op jit(solution)/shard_map/ppermute | solution.py:64
  182.4 2.9 collective-permute-start.30
  188.1 2.2 copy-done.2
  190.3 2.2 copy-done.4
  192.5 3.8 gate.1
  201.3 2.3 collective-permute-done.32.state_oth
  205.2 11.8 %mix.1 = (f32[4,512,512]{2,1,0:T(8,128)S(1)}, bf16[4,512,512]{2,1,0:T(8,128)(2,1)S(1)}, f32[512,1024]{1,0:T(8,128)S(1)}, bf16[512,1024]{1,0:T(8,128)(2,1)S(1)}, bf16[1024,512]{1,0:T(8,128)(2,1)S(1)}) custom-call(s32[66]{0:T(128)S(1)} %copy-done.49, f32[4]{0:T(128)S(1)} %copy-done.61, bf16[512,1024]{1,0:T(8,128)(2,1)S(1)} %bitcast.251, ...), custom_call_target="tpu_custom_call" | custom-call | flops 1 | bytes 1 | tf_op jit(solution)/shard_map/mix/pallas_call | solution.py:330
  218.9 2.6 settle.6.up_own.down_own
  227.5 27.7 %feed.1 = (bf16[512,1024]{1,0:T(8,128)(2,1)}, f32[512,1024]{1,0:T(8,128)}, bf16[512,1024]{1,0:T(8,128)(2,1)S(1)}, f32[1,1024]{1,0:T(1,128)S(1)}, f32[1,1024]{1,0...) custom-call(s32[66]{0:T(128)S(1)} %concatenate.46.info_ref.info, f32[512,1024]{1,0:T(8,128)} %copy-done.40, ...), custom_call_target="tpu_custom_call" | custom-call | flops 1 | bytes 1 | tf_op jit(solution)/shard_map/feed/pallas_call | solution.py:330
  257.5 11.1 %unmix.1 = (bf16[4,512,512]{2,1,0:T(8,128)(2,1)S(1)}, bf16[4,512,512]{2,1,0:T(8,128)(2,1)S(1)}, f32[4,1,512]{2,1,0:T(1,128)S(1)}, f32[2,2,256,512]{3,2,1,0:T(8,128)S(1)}, f32[2,2,256,512]{3,2,1,0:T(8,128)S(1)}) custom-call(s32[66]{0:T(128)S(1)} %copy-done.49, f32[4]{0:T(128)S(1)} %copy-done.61, bf16[512,1024]{1,0:T(8,128)(2,1)S(1)} %get-tuple-element.606.grad_low, ...), custom_call_target="tpu_custom_call" | custom-call | flops 1 | bytes 1 | tf_op jit(solution)/shard_map/unmix/pallas_call | solution.py:330
  269.8 3.3 collective-permute-done.37
  274.4 7.8 %inside.1 = (bf16[4,512,256]{2,1,0:T(8,128)(2,1)S(1)}, f32[4,512,256]{2,1,0:T(8,128)S(1)}, f32[4,512,512]{2,1,0:T(8,128)S(1)}) custom-call(s32[66]{0:T(128)S(1)} %copy-done.49, f32[4]{0:T(128)S(1)} %copy-done.61, bf16[4,512,512]{2,1,0:T(8,128)(2,1)S(1)} %get-tuple-element.623.grad_ret, bf16[4,512,256]{2,1,0:T(8,128)(2,1)S(1)} %copy-done.10, ...), custom_call_target="tpu_custom_call" | custom-call | flops 1 | bytes 1 | tf_op jit(solution)/shard_map/inside/pallas_call | solution.py:330
  284.1 3.0 collective-permute-done.39
  289.2 11.3 %outer.1 = (bf16[16,64,2560]{2,1,0:T(8,128)(2,1)}, bf16[16,64,2560]{2,1,0:T(8,128)(2,1)}) custom-call(s32[66]{0:T(128)S(1)} %copy-done.49, bf16[512,1024]{1,0:T(8,128)(2,1)S(1)} %get-tuple-element.606.grad_low, bf16[1024,512]{1,0:T(8,128)(2,1)S(1)} %copy-done.27, bf16[4,512,512]{2,1,0:T(8,128)(2,1)S(1)} %copy-done.39, ...), custom_call_target="tpu_custom_call" | custom-call | flops 1 | bytes 1 | tf_op jit(solution)/shard_map/outer/pallas_call | solution.py:330
  300.5 3.0 add_convert_fusion.3
  310.4 4.5 collective-permute-done.43
  316.9 13.7 %collective-permute-done.42 = bf16[2,256,512]{2,1,0:T(8,128)(2,1)S(1)} collective-permute-done((bf16[2,256,512]{2,1,0:T(8,128)(2,1)S(1)}, bf16[2,256,512]{2,1,0:T(8,128)(2,1)S(1)}, u32[]{:S(2)}, u32[]{:S(2)}) %collective-permute-start.42) | collective-permute-done | bytes 524320 | tf_op jit(solution)/shard_map/ppermute | solution.py:294
  336.3 8.8 %collective-permute-done.45 = bf16[2,256,512]{2,1,0:T(8,128)(2,1)S(1)} collective-permute-done((bf16[2,256,512]{2,1,0:T(8,128)(2,1)S(1)}, bf16[2,256,512]{2,1,0:T(8,128)(2,1)S(1)}, u32[]{:S(2)}, u32[]{:S(2)}) %collective-permute-start.45) | collective-permute-done | bytes 524320 | tf_op jit(solution)/shard_map/ppermute | solution.py:294
  345.1 2.3 collective-permute-done.46
  350.9 2.3 collective-permute-done.47.state_oth
  356.2 9.6 %last.1 = (bf16[4,512,256]{2,1,0:T(8,128)(2,1)S(1)}, bf16[4,512,512]{2,1,0:T(8,128)(2,1)S(1)}, bf16[16,64,1536]{2,1,0:T(8,128)(2,1)S(1)}, bf16[16,64,1536]{2,1,0:T(8,128)(2,1)S(1)}) custom-call(s32[66]{0:T(128)S(1)} %copy-done.49, f32[4]{0:T(128)S(1)} %copy-done.61, bf16[1024,512]{1,0:T(8,128)(2,1)S(1)} %copy-done.28, bf16[4,512,256]{2,1,0:T(8,128)(2,1)S(1)} %copy-done.22, ...), custom_call_target="tpu_custom_call" | custom-call | flops 1 | bytes 1 | tf_op jit(solution)/shard_map/last/pallas_call | solution.py:330
  366.8 4.1 add_convert_fusion
  374.1 3.0 collective-permute-done.50
  380.9 17.5 %input.1 = (f32[512,1024]{1,0:T(8,128)}, f32[1,1024]{1,0:T(1,128)}, f32[1,1024]{1,0:T(1,128)}) custom-call(s32[66]{0:T(128)} %copy-done.48, bf16[512,1024]{1,0:T(8,128)(2,1)} %bitcast.249, bf16[1,1024]{1,0:T(2,128)(2,1)} %copy-done.59, f32[512,1024]{1,0:T(8,128)} %get-tuple-element.761.grad_hidden, bf16[4,512,256]{2,1,0:T(8,128)(2,1)} %copy-done.25, ...), custom_call_target="tpu_custom_call" | custom-call | flops 1 | bytes 1 | tf_op jit(solution)/shard_map/input/pallas_call | solution.py:330
  398.5 2.4 add_convert_fusion.6
  402.0 2.6 add_convert_fusion.9
  409.0 6.2 %collective-permute-done.57 = f32[8,1024]{1,0:T(8,128)S(1)} collective-permute-done((f32[8,1024]{1,0:T(8,128)S(1)}, f32[8,1024]{1,0:T(8,128)S(1)}, u32[]{:S(2)}, u32[]{:S(2)}) %collective-permute-start.57) | collective-permute-done | bytes 32800 | tf_op jit(solution)/shard_map/ppermute | solution.py:40
  416.6 2.9 collective-permute-start.59
  421.0 2.5 collective-permute-start.63
  425.0 6.8 %collective-permute-done.63 = bf16[1,64,2560]{2,1,0:T(8,128)(2,1)S(1)} collective-permute-done((bf16[1,64,2560]{2,1,0:T(8,128)(2,1)S(1)}, bf16[1,64,2560]{2,1,0:T(8,128)(2,1)S(1)}, u32[]{:S(2)}, u32[]{:S(2)}) %collective-permute-start.63) | collective-permute-done | bytes 327712 | tf_op jit(solution)/shard_map/ppermute | solution.py:64
  433.4 8.3 %collective-permute-start.67 = (f32[64,512]{1,0:T(8,128)S(1)}, f32[64,512]{1,0:T(8,128)S(1)}, u32[]{:S(2)}, u32[]{:S(2)}) collective-permute-start(f32[64,512]{1,0:T(8,128)S(1)} %slice_select_fusion.1), channel_id=1, source_target_pairs={{0,1},{1,0},{2,3},{3,2},{4,5},{5,4},{6,7},{7,6},{8,9},{9,8},{10,11... | collective-permute-start | bytes 393224 | tf_op jit(solution)/shard_map/ppermute | solution.py:40
  447.9 2.3 collective-permute-start.62
  (461 shorter events, 134.8 us)
Async XLA Ops:
  11.6 13.8 %collective-permute-start.1 = (bf16[1,64,2048]{2,1,0:T(8,128)(2,1)S(1)}, bf16[1,64,2048]{2,1,0:T(8,128)(2,1)S(1)}, u32[]{:S(2)}, u32[]{:S(2)}) collective-permute-start(bf16[1,64,2048]{2,1,0:T(8,128)(2,1)S(1)} %bitcast.252), channel_id=1, source_target_pairs={{0,4},{1,5},{2,6},{3,7},{4,0},{5,1},{6,2},{7,3},{8,12},{9,13},{10,... | collective-permute-start | bytes 786440 | tf_op jit(solution)/shard_map/ppermute | solution.py:64
  39.1 16.6 %collective-permute-start.6 = (bf16[4,64,2048]{2,1,0:T(8,128)(2,1)S(1)}, bf16[4,64,2048]{2,1,0:T(8,128)(2,1)}, u32[]{:S(2)}, u32[]{:S(2)}) collective-permute-start(bf16[4,64,2048]{2,1,0:T(8,128)(2,1)S(1)} %join.7.refs_0_), channel_id=1, source_target_pairs={{0,2},{1,9},{2,0},{3,11},{4,6},{5,13},{6,4},{7,15},{8,10},{9,1},{1... | collective-permute-start | bytes 3145736 | tf_op jit(solution)/shard_map/ppermute | solution.py:64
  41.7 14.0 %collective-permute-start.10 = (bf16[2,2,2,2,16,256]{5,4,3,1,2,0:T(8,128)(2,1)S(1)}, bf16[2,2,2,2,16,256]{5,4,3,1,2,0:T(8,128)(2,1)S(1)}, u32[]{:S(2)}, u32[]{:S(2)}) collective-permute-start(bf16[2,2,2,2,16,256]{5,4,3,1,2,0:T(8,128)(2,1)S(1)} %pad_maximum_fusion.9), channel_id=1, source_target_pairs={{0,8},{1,9},{2,10},{3,11},{4,12},{5,13},{6,14},{7,15},{8,0},{9,1},... | collective-permute-start | bytes 393224 | tf_op jit(solution)/shard_map/ppermute | solution.py:40
  57.4 27.0 %collective-permute-start.11 = (bf16[4,64,2048]{2,1,0:T(8,128)(2,1)S(1)}, bf16[4,64,2048]{2,1,0:T(8,128)(2,1)}, u32[]{:S(2)}, u32[]{:S(2)}) collective-permute-start(bf16[4,64,2048]{2,1,0:T(8,128)(2,1)S(1)} %join.7.refs_0_), channel_id=1, source_target_pairs={{0,8},{1,17},{2,10},{3,19},{4,12},{5,21},{6,14},{7,23},{8,0},{9,25... | collective-permute-start | bytes 3145736 | tf_op jit(solution)/shard_map/ppermute | solution.py:64
  57.6 26.8 %collective-permute-start.12 = (bf16[4,64,2048]{2,1,0:T(8,128)(2,1)}, bf16[4,64,2048]{2,1,0:T(8,128)(2,1)}, u32[]{:S(2)}, u32[]{:S(2)}) collective-permute-start(bf16[4,64,2048]{2,1,0:T(8,128)(2,1)} %collective-permute-done.6.refs_1_), channel_id=1, source_target_pairs={{0,8},{1,17},{2,10},{3,19},{4,12},{5,21},{6,14},{7,23},{8,0},{9,25... | collective-permute-start | bytes 3145736 | tf_op jit(solution)/shard_map/ppermute | solution.py:64
  59.1 19.7 %collective-permute-start.13 = (bf16[1,64,2048]{2,1,0:T(8,128)(2,1)}, bf16[1,64,2048]{2,1,0:T(8,128)(2,1)S(1)}, u32[]{:S(2)}, u32[]{:S(2)}) collective-permute-start(bf16[1,64,2048]{2,1,0:T(8,128)(2,1)} %maximum_bitcast_fusion.part_ref), channel_id=1, source_target_pairs={{0,4},{1,5},{2,6},{3,7},{4,0},{5,1},{6,2},{7,3},{8,12},{9,13},{10,... | collective-permute-start | bytes 786440 | tf_op jit(solution)/shard_map/ppermute | solution.py:64
  59.1 25.3 %collective-permute-start.14 = (bf16[1,64,2048]{2,1,0:T(8,128)(2,1)S(1)}, bf16[1,64,2048]{2,1,0:T(8,128)(2,1)S(1)}, u32[]{:S(2)}, u32[]{:S(2)}) collective-permute-start(bf16[1,64,2048]{2,1,0:T(8,128)(2,1)S(1)} %maximum_bitcast_fusion.1.part_ref), channel_id=1, source_target_pairs={{0,4},{1,5},{2,6},{3,7},{4,0},{5,1},{6,2},{7,3},{8,12},{9,13},{10,... | collective-permute-start | bytes 786440 | tf_op jit(solution)/shard_map/ppermute | solution.py:64
  88.7 15.1 %collective-permute-start.16 = (bf16[16,64,2048]{2,1,0:T(8,128)(2,1)S(1)}, bf16[16,64,2048]{2,1,0:T(8,128)(2,1)S(1)}, u32[]{:S(2)}, u32[]{:S(2)}) collective-permute-start(bf16[16,64,2048]{2,1,0:T(8,128)(2,1)S(1)} %settle.4.q_own.k_own.v_own), channel_id=1, source_target_pairs={{0,1},{1,0},{2,3},{3,2},{4,5},{5,4},{6,7},{7,6},{8,9},{9,8},{10,11... | collective-permute-start | bytes 12582920 | tf_op jit(solution)/shard_map/ppermute | solution.py:40
  90.2 13.6 %collective-permute-start.17 = (bf16[2,64,2048]{2,1,0:T(8,128)(2,1)S(1)}, bf16[2,64,2048]{2,1,0:T(8,128)(2,1)S(1)}, u32[]{:S(2)}, u32[]{:S(2)}) collective-permute-start(bf16[2,64,2048]{2,1,0:T(8,128)(2,1)S(1)} %join.8.part_ref), channel_id=1, source_target_pairs={{0,2},{1,3},{2,0},{3,1},{4,6},{5,7},{6,4},{7,5},{8,10},{9,11},{10,... | collective-permute-start | bytes 1572872 | tf_op jit(solution)/shard_map/ppermute | solution.py:64
  103.9 19.3 %collective-permute-start.18 = (bf16[4,64,2048]{2,1,0:T(8,128)(2,1)S(1)}, bf16[4,64,2048]{2,1,0:T(8,128)(2,1)}, u32[]{:S(2)}, u32[]{:S(2)}) collective-permute-start(bf16[4,64,2048]{2,1,0:T(8,128)(2,1)S(1)} %join.9.refs_0_), channel_id=1, source_target_pairs={{0,16},{1,9},{2,18},{3,11},{4,20},{5,13},{6,22},{7,15},{8,24},{9,1... | collective-permute-start | bytes 3145736 | tf_op jit(solution)/shard_map/ppermute | solution.py:64
  105.9 16.5 %collective-permute-start.19 = (bf16[2,64,2048]{2,1,0:T(8,128)(2,1)S(1)}, bf16[2,64,2048]{2,1,0:T(8,128)(2,1)S(1)}, u32[]{:S(2)}, u32[]{:S(2)}) collective-permute-start(bf16[2,64,2048]{2,1,0:T(8,128)(2,1)S(1)} %join.10.part_ref), channel_id=1, source_target_pairs={{0,2},{1,3},{2,0},{3,1},{4,6},{5,7},{6,4},{7,5},{8,10},{9,11},{10,... | collective-permute-start | bytes 1572872 | tf_op jit(solution)/shard_map/ppermute | solution.py:64
  128.1 13.9 %collective-permute-start.22 = (bf16[4,64,2048]{2,1,0:T(8,128)(2,1)S(1)}, bf16[4,64,2048]{2,1,0:T(8,128)(2,1)S(1)}, u32[]{:S(2)}, u32[]{:S(2)}) collective-permute-start(bf16[4,64,2048]{2,1,0:T(8,128)(2,1)S(1)} %join.9.refs_0_), channel_id=1, source_target_pairs={{0,8},{1,17},{2,10},{3,19},{4,12},{5,21},{6,14},{7,23},{8,0},{9,25... | collective-permute-start | bytes 3145736 | tf_op jit(solution)/shard_map/ppermute | solution.py:64
  128.6 12.9 %collective-permute-start.21 = (bf16[2,256,512]{2,1,0:T(8,128)(2,1)S(1)}, bf16[2,256,512]{2,1,0:T(8,128)(2,1)S(1)}, u32[]{:S(2)}, u32[]{:S(2)}) collective-permute-start(bf16[2,256,512]{2,1,0:T(8,128)(2,1)S(1)} %fusion.29), channel_id=1, source_target_pairs={{0,2},{1,3},{8,10},{9,11},{16,18},{17,19},{24,26},{25,27}} | collective-permute-start | bytes 1572872 | tf_op jit(solution)/shard_map/ppermute | solution.py:294
  143.0 16.9 %collective-permute-start.24 = (bf16[4,64,2048]{2,1,0:T(8,128)(2,1)}, bf16[4,64,2048]{2,1,0:T(8,128)(2,1)}, u32[]{:S(2)}, u32[]{:S(2)}) collective-permute-start(bf16[4,64,2048]{2,1,0:T(8,128)(2,1)} %collective-permute-done.18.refs_1_), channel_id=1, source_target_pairs={{0,8},{1,17},{2,10},{3,19},{4,12},{5,21},{6,14},{7,23},{8,0},{9,25... | collective-permute-start | bytes 3145736 | tf_op jit(solution)/shard_map/ppermute | solution.py:64
  146.1 13.9 %collective-permute-start.23 = (bf16[2,256,512]{2,1,0:T(8,128)(2,1)}, bf16[2,256,512]{2,1,0:T(8,128)(2,1)}, u32[]{:S(2)}, u32[]{:S(2)}) collective-permute-start(bf16[2,256,512]{2,1,0:T(8,128)(2,1)} %fusion.27), channel_id=1, source_target_pairs={{0,2},{1,3},{2,4},{3,5},{8,10},{9,11},{10,12},{11,13},{16,18},{17,... | collective-permute-start | bytes 1572872 | tf_op jit(solution)/shard_map/ppermute | solution.py:294
  163.1 17.3 %collective-permute-start.26 = (bf16[16,64,2048]{2,1,0:T(8,128)(2,1)S(1)}, bf16[16,64,2048]{2,1,0:T(8,128)(2,1)S(1)}, u32[]{:S(2)}, u32[]{:S(2)}) collective-permute-start(bf16[16,64,2048]{2,1,0:T(8,128)(2,1)S(1)} %settle.5.own.wo_own.g_own), channel_id=1, source_target_pairs={{0,1},{1,0},{2,3},{3,2},{4,5},{5,4},{6,7},{7,6},{8,9},{9,8},{10,11... | collective-permute-start | bytes 12582920 | tf_op jit(solution)/shard_map/ppermute | solution.py:40
  165.9 14.6 %collective-permute-start.27 = (bf16[4,64,2048]{2,1,0:T(8,128)(2,1)S(1)}, bf16[4,64,2048]{2,1,0:T(8,128)(2,1)}, u32[]{:S(2)}, u32[]{:S(2)}) collective-permute-start(bf16[4,64,2048]{2,1,0:T(8,128)(2,1)S(1)} %join.11.refs_0_), channel_id=1, source_target_pairs={{0,16},{1,9},{2,18},{3,11},{4,20},{5,13},{6,22},{7,15},{8,24},{9,1... | collective-permute-start | bytes 3145736 | tf_op jit(solution)/shard_map/ppermute | solution.py:64
  182.4 14.0 %collective-permute-start.29 = (bf16[4,64,2048]{2,1,0:T(8,128)(2,1)S(1)}, bf16[4,64,2048]{2,1,0:T(8,128)(2,1)}, u32[]{:S(2)}, u32[]{:S(2)}) collective-permute-start(bf16[4,64,2048]{2,1,0:T(8,128)(2,1)S(1)} %join.11.refs_0_), channel_id=1, source_target_pairs={{0,8},{1,17},{2,10},{3,19},{4,12},{5,21},{6,14},{7,23},{8,0},{9,25... | collective-permute-start | bytes 3145736 | tf_op jit(solution)/shard_map/ppermute | solution.py:64
  182.4 14.0 %collective-permute-start.30 = (bf16[4,64,2048]{2,1,0:T(8,128)(2,1)S(1)}, bf16[4,64,2048]{2,1,0:T(8,128)(2,1)}, u32[]{:S(2)}, u32[]{:S(2)}) collective-permute-start(bf16[4,64,2048]{2,1,0:T(8,128)(2,1)S(1)} %join.11.refs_0_), channel_id=1, source_target_pairs={{0,1},{1,0},{2,3},{3,2},{4,5},{5,4},{6,7},{7,6},{8,9},{9,8},{10,11... | collective-permute-start | bytes 3145736 | tf_op jit(solution)/shard_map/ppermute | solution.py:40
  185.3 11.2 %collective-permute-start.31 = (bf16[4,64,2048]{2,1,0:T(8,128)(2,1)}, bf16[4,64,2048]{2,1,0:T(8,128)(2,1)}, u32[]{:S(2)}, u32[]{:S(2)}) collective-permute-start(bf16[4,64,2048]{2,1,0:T(8,128)(2,1)} %collective-permute-done.27.refs_1_), channel_id=1, source_target_pairs={{0,1},{1,0},{2,3},{3,2},{4,5},{5,4},{6,7},{7,6},{8,9},{9,8},{10,11... | collective-permute-start | bytes 3145736 | tf_op jit(solution)/shard_map/ppermute | solution.py:40
  186.5 9.9 %collective-permute-start.28 = (bf16[2,256,512]{2,1,0:T(8,128)(2,1)}, bf16[2,256,512]{2,1,0:T(8,128)(2,1)}, u32[]{:S(2)}, u32[]{:S(2)}) collective-permute-start(bf16[2,256,512]{2,1,0:T(8,128)(2,1)} %fusion.21), channel_id=1, source_target_pairs={{4,6},{5,7},{12,14},{13,15},{20,22},{21,23},{28,30},{29,31}} | collective-permute-start | bytes 1572872 | tf_op jit(solution)/shard_map/ppermute | solution.py:294
  203.6 14.2 %collective-permute-start.33 = (bf16[4,64,2048]{2,1,0:T(8,128)(2,1)}, bf16[4,64,2048]{2,1,0:T(8,128)(2,1)S(1)}, u32[]{:S(2)}, u32[]{:S(2)}) collective-permute-start(bf16[4,64,2048]{2,1,0:T(8,128)(2,1)} %collective-permute-done.27.refs_1_), channel_id=1, source_target_pairs={{0,8},{1,17},{2,10},{3,19},{4,12},{5,21},{6,14},{7,23},{8,0},{9,25... | collective-permute-start | bytes 3145736 | tf_op jit(solution)/shard_map/ppermute | solution.py:64
  203.6 14.1 %collective-permute-start.34 = (bf16[4,64,2048]{2,1,0:T(8,128)(2,1)}, bf16[4,64,2048]{2,1,0:T(8,128)(2,1)S(1)}, u32[]{:S(2)}, u32[]{:S(2)}) collective-permute-start(bf16[4,64,2048]{2,1,0:T(8,128)(2,1)} %collective-permute-done.29.refs_2_), channel_id=1, source_target_pairs={{0,1},{1,0},{2,3},{3,2},{4,5},{5,4},{6,7},{7,6},{8,9},{9,8},{10,11... | collective-permute-start | bytes 3145736 | tf_op jit(solution)/shard_map/ppermute | solution.py:40
  255.3 13.5 %collective-permute-start.36 = (bf16[16,64,2048]{2,1,0:T(8,128)(2,1)}, bf16[16,64,2048]{2,1,0:T(8,128)(2,1)S(1)}, u32[]{:S(2)}, u32[]{:S(2)}) collective-permute-start(bf16[16,64,2048]{2,1,0:T(8,128)(2,1)} %get-tuple-element.605), channel_id=1, source_target_pairs={{0,1},{1,0},{2,3},{3,2},{4,5},{5,4},{6,7},{7,6},{8,9},{9,8},{10,11... | collective-permute-start | bytes 12582920 | tf_op jit(solution)/shard_map/ppermute | solution.py:40
  273.1 13.9 %collective-permute-start.39 = (bf16[4,64,2048]{2,1,0:T(8,128)(2,1)S(1)}, bf16[4,64,2048]{2,1,0:T(8,128)(2,1)S(1)}, u32[]{:S(2)}, u32[]{:S(2)}) collective-permute-start(bf16[4,64,2048]{2,1,0:T(8,128)(2,1)S(1)} %add_convert_fusion.5), channel_id=1, source_target_pairs={{0,8},{1,17},{2,10},{3,19},{4,12},{5,21},{6,14},{7,23},{8,0},{9,25... | collective-permute-start | bytes 3145736 | tf_op jit(solution)/shard_map/ppermute | solution.py:64
  273.7 10.4 %collective-permute-start.38 = (bf16[2,256,512]{2,1,0:T(8,128)(2,1)S(1)}, bf16[2,256,512]{2,1,0:T(8,128)(2,1)S(1)}, u32[]{:S(2)}, u32[]{:S(2)}) collective-permute-start(bf16[2,256,512]{2,1,0:T(8,128)(2,1)S(1)} %fusion.18), channel_id=1, source_target_pairs={{6,4},{7,5},{14,12},{15,13},{22,20},{23,21},{30,28},{31,29}} | collective-permute-start | bytes 1572872 | tf_op jit(solution)/shard_map/ppermute | solution.py:294
  287.1 16.4 %collective-permute-start.41 = (bf16[4,64,2048]{2,1,0:T(8,128)(2,1)S(1)}, bf16[4,64,2048]{2,1,0:T(8,128)(2,1)S(1)}, u32[]{:S(2)}, u32[]{:S(2)}) collective-permute-start(bf16[4,64,2048]{2,1,0:T(8,128)(2,1)S(1)} %add_convert_fusion.4), channel_id=1, source_target_pairs={{0,8},{1,17},{2,10},{3,19},{4,12},{5,21},{6,14},{7,23},{8,0},{9,25... | collective-permute-start | bytes 3145736 | tf_op jit(solution)/shard_map/ppermute | solution.py:64
  287.7 15.8 %collective-permute-start.40 = (bf16[2,256,512]{2,1,0:T(8,128)(2,1)S(1)}, bf16[2,256,512]{2,1,0:T(8,128)(2,1)}, u32[]{:S(2)}, u32[]{:S(2)}) collective-permute-start(bf16[2,256,512]{2,1,0:T(8,128)(2,1)S(1)} %fusion.16), channel_id=1, source_target_pairs={{6,4},{7,5},{4,2},{5,3},{14,12},{15,13},{12,10},{13,11},{22,20},{2... | collective-permute-start | bytes 1572872 | tf_op jit(solution)/shard_map/ppermute | solution.py:294
  304.5 10.4 %collective-permute-start.43 = (bf16[16,64,2560]{2,1,0:T(8,128)(2,1)}, bf16[16,64,2560]{2,1,0:T(8,128)(2,1)}, u32[]{:S(2)}, u32[]{:S(2)}) collective-permute-start(bf16[16,64,2560]{2,1,0:T(8,128)(2,1)} %get-tuple-element.675), channel_id=1, source_target_pairs={{0,1},{1,0},{2,3},{3,2},{4,5},{5,4},{6,7},{7,6},{8,9},{9,8},{10,11... | collective-permute-start | bytes 15728648 | tf_op jit(solution)/shard_map/ppermute | solution.py:40
  306.3 24.4 %collective-permute-start.44 = (bf16[4,64,2048]{2,1,0:T(8,128)(2,1)}, bf16[4,64,2048]{2,1,0:T(8,128)(2,1)}, u32[]{:S(2)}, u32[]{:S(2)}) collective-permute-start(bf16[4,64,2048]{2,1,0:T(8,128)(2,1)} %add_convert_fusion.3), channel_id=1, source_target_pairs={{0,16},{1,9},{2,18},{3,11},{4,20},{5,13},{6,22},{7,15},{8,24},{9,1... | collective-permute-start | bytes 3145736 | tf_op jit(solution)/shard_map/ppermute | solution.py:64
  309.0 21.7 %collective-permute-start.42 = (bf16[2,256,512]{2,1,0:T(8,128)(2,1)S(1)}, bf16[2,256,512]{2,1,0:T(8,128)(2,1)S(1)}, u32[]{:S(2)}, u32[]{:S(2)}) collective-permute-start(bf16[2,256,512]{2,1,0:T(8,128)(2,1)S(1)} %fusion.13), channel_id=1, source_target_pairs={{4,2},{5,3},{2,0},{3,1},{12,10},{13,11},{10,8},{11,9},{20,18},{21,... | collective-permute-start | bytes 1572872 | tf_op jit(solution)/shard_map/ppermute | solution.py:294
  330.6 16.8 %collective-permute-start.46 = (bf16[4,64,2560]{2,1,0:T(8,128)(2,1)S(1)}, bf16[4,64,2560]{2,1,0:T(8,128)(2,1)S(1)}, u32[]{:S(2)}, u32[]{:S(2)}) collective-permute-start(bf16[4,64,2560]{2,1,0:T(8,128)(2,1)S(1)} %add_convert_fusion.2), channel_id=1, source_target_pairs={{0,8},{1,17},{2,10},{3,19},{4,12},{5,21},{6,14},{7,23},{8,0},{9,25... | collective-permute-start | bytes 3932168 | tf_op jit(solution)/shard_map/ppermute | solution.py:64
  331.0 14.0 %collective-permute-start.45 = (bf16[2,256,512]{2,1,0:T(8,128)(2,1)S(1)}, bf16[2,256,512]{2,1,0:T(8,128)(2,1)S(1)}, u32[]{:S(2)}, u32[]{:S(2)}) collective-permute-start(bf16[2,256,512]{2,1,0:T(8,128)(2,1)S(1)} %fusion.10), channel_id=1, source_target_pairs={{2,0},{3,1},{10,8},{11,9},{18,16},{19,17},{26,24},{27,25}} | collective-permute-start | bytes 1572872 | tf_op jit(solution)/shard_map/ppermute | solution.py:294
  353.1 17.8 %collective-permute-start.49 = (bf16[4,64,2560]{2,1,0:T(8,128)(2,1)S(1)}, bf16[4,64,2560]{2,1,0:T(8,128)(2,1)S(1)}, u32[]{:S(2)}, u32[]{:S(2)}) collective-permute-start(bf16[4,64,2560]{2,1,0:T(8,128)(2,1)S(1)} %add_convert_fusion.1), channel_id=1, source_target_pairs={{0,8},{1,17},{2,10},{3,19},{4,12},{5,21},{6,14},{7,23},{8,0},{9,25... | collective-permute-start | bytes 3932168 | tf_op jit(solution)/shard_map/ppermute | solution.py:64
  354.1 16.8 %collective-permute-start.48 = (bf16[2,64,2048]{2,1,0:T(8,128)(2,1)S(1)}, bf16[2,64,2048]{2,1,0:T(8,128)(2,1)S(1)}, u32[]{:S(2)}, u32[]{:S(2)}) collective-permute-start(bf16[2,64,2048]{2,1,0:T(8,128)(2,1)S(1)} %add_convert_fusion.10), channel_id=1, source_target_pairs={{0,2},{1,3},{2,0},{3,1},{4,6},{5,7},{6,4},{7,5},{8,10},{9,11},{10,... | collective-permute-start | bytes 1572872 | tf_op jit(solution)/shard_map/ppermute | solution.py:64
  371.8 26.6 %collective-permute-start.53 = (bf16[4,64,2560]{2,1,0:T(8,128)(2,1)S(1)}, bf16[4,64,2560]{2,1,0:T(8,128)(2,1)}, u32[]{:S(2)}, u32[]{:S(2)}) collective-permute-start(bf16[4,64,2560]{2,1,0:T(8,128)(2,1)S(1)} %add_convert_fusion), channel_id=1, source_target_pairs={{0,2},{1,9},{2,0},{3,11},{4,6},{5,13},{6,4},{7,15},{8,10},{9,1},{1... | collective-permute-start | bytes 3932168 | tf_op jit(solution)/shard_map/ppermute | solution.py:64
  378.6 19.7 %collective-permute-start.51 = (bf16[4,64,1536]{2,1,0:T(8,128)(2,1)}, bf16[4,64,1536]{2,1,0:T(8,128)(2,1)}, u32[]{:S(2)}, u32[]{:S(2)}) collective-permute-start(bf16[4,64,1536]{2,1,0:T(8,128)(2,1)} %get-tuple-element.847), channel_id=1, source_target_pairs={{0,8},{1,17},{2,10},{3,19},{4,12},{5,21},{6,14},{7,23},{8,0},{9,25... | collective-permute-start | bytes 2359304 | tf_op jit(solution)/shard_map/ppermute | solution.py:64
  380.0 18.5 %collective-permute-start.52 = (bf16[4,64,1536]{2,1,0:T(8,128)(2,1)}, bf16[4,64,1536]{2,1,0:T(8,128)(2,1)}, u32[]{:S(2)}, u32[]{:S(2)}) collective-permute-start(bf16[4,64,1536]{2,1,0:T(8,128)(2,1)} %get-tuple-element.846), channel_id=1, source_target_pairs={{0,8},{1,17},{2,10},{3,19},{4,12},{5,21},{6,14},{7,23},{8,0},{9,25... | collective-permute-start | bytes 2359304 | tf_op jit(solution)/shard_map/ppermute | solution.py:64
  380.1 18.2 %collective-permute-start.54 = (bf16[1,64,2048]{2,1,0:T(8,128)(2,1)S(1)}, bf16[1,64,2048]{2,1,0:T(8,128)(2,1)S(1)}, u32[]{:S(2)}, u32[]{:S(2)}) collective-permute-start(bf16[1,64,2048]{2,1,0:T(8,128)(2,1)S(1)} %add_convert_fusion.13), channel_id=1, source_target_pairs={{0,4},{1,5},{2,6},{3,7},{4,0},{5,1},{6,2},{7,3},{8,12},{9,13},{10,... | collective-permute-start | bytes 786440 | tf_op jit(solution)/shard_map/ppermute | solution.py:64
  401.0 15.7 %collective-permute-start.55 = (bf16[4,64,1536]{2,1,0:T(8,128)(2,1)}, bf16[4,64,1536]{2,1,0:T(8,128)(2,1)}, u32[]{:S(2)}, u32[]{:S(2)}) collective-permute-start(bf16[4,64,1536]{2,1,0:T(8,128)(2,1)} %add_convert_fusion.6), channel_id=1, source_target_pairs={{0,2},{1,9},{2,0},{3,11},{4,6},{5,13},{6,4},{7,15},{8,10},{9,1},{1... | collective-permute-start | bytes 2359304 | tf_op jit(solution)/shard_map/ppermute | solution.py:64
  404.6 12.1 %collective-permute-start.56 = (bf16[2,64,2560]{2,1,0:T(8,128)(2,1)}, bf16[2,64,2560]{2,1,0:T(8,128)(2,1)}, u32[]{:S(2)}, u32[]{:S(2)}) collective-permute-start(bf16[2,64,2560]{2,1,0:T(8,128)(2,1)} %add_convert_fusion.9), channel_id=1, source_target_pairs={{0,16},{1,3},{2,18},{3,1},{4,20},{5,7},{6,22},{7,5},{8,24},{9,11},... | collective-permute-start | bytes 1966088 | tf_op jit(solution)/shard_map/ppermute | solution.py:64
  421.0 10.8 %collective-permute-start.63 = (bf16[1,64,2560]{2,1,0:T(8,128)(2,1)S(1)}, bf16[1,64,2560]{2,1,0:T(8,128)(2,1)S(1)}, u32[]{:S(2)}, u32[]{:S(2)}) collective-permute-start(bf16[1,64,2560]{2,1,0:T(8,128)(2,1)S(1)} %add_convert_fusion.12), channel_id=1, source_target_pairs={{0,4},{1,5},{2,6},{3,7},{4,0},{5,1},{6,2},{7,3},{8,12},{9,13},{10,... | collective-permute-start | bytes 983048 | tf_op jit(solution)/shard_map/ppermute | solution.py:64
  424.9 16.7 %collective-permute-start.58 = (bf16[2,64,1536]{2,1,0:T(8,128)(2,1)S(1)}, bf16[2,64,1536]{2,1,0:T(8,128)(2,1)S(1)}, u32[]{:S(2)}, u32[]{:S(2)}) collective-permute-start(bf16[2,64,1536]{2,1,0:T(8,128)(2,1)S(1)} %add_convert_fusion.11), channel_id=1, source_target_pairs={{0,16},{1,3},{2,18},{3,1},{4,20},{5,7},{6,22},{7,5},{8,24},{9,11},... | collective-permute-start | bytes 1179656 | tf_op jit(solution)/shard_map/ppermute | solution.py:64
  433.4 12.8 %collective-permute-start.67 = (f32[64,512]{1,0:T(8,128)S(1)}, f32[64,512]{1,0:T(8,128)S(1)}, u32[]{:S(2)}, u32[]{:S(2)}) collective-permute-start(f32[64,512]{1,0:T(8,128)S(1)} %slice_select_fusion.1), channel_id=1, source_target_pairs={{0,1},{1,0},{2,3},{3,2},{4,5},{5,4},{6,7},{7,6},{8,9},{9,8},{10,11... | collective-permute-start | bytes 393224 | tf_op jit(solution)/shard_map/ppermute | solution.py:40
  441.7 10.6 %collective-permute-start.69 = (f32[64,512]{1,0:T(8,128)S(1)}, f32[64,512]{1,0:T(8,128)S(1)}, u32[]{:S(2)}, u32[]{:S(2)}) collective-permute-start(f32[64,512]{1,0:T(8,128)S(1)} %slice_select_fusion.7), channel_id=1, source_target_pairs={{0,1},{1,0},{2,3},{3,2},{4,5},{5,4},{6,7},{7,6},{8,9},{9,8},{10,11... | collective-permute-start | bytes 393224 | tf_op jit(solution)/shard_map/ppermute | solution.py:40
  441.8 11.2 %collective-permute-start.68 = (f32[32,1024]{1,0:T(8,128)S(1)}, f32[32,1024]{1,0:T(8,128)S(1)}, u32[]{:S(2)}, u32[]{:S(2)}) collective-permute-start(f32[32,1024]{1,0:T(8,128)S(1)} %slice_select_fusion.9), channel_id=1, source_target_pairs={{0,1},{1,0},{2,3},{3,2},{4,5},{5,4},{6,7},{7,6},{8,9},{9,8},{10,11... | collective-permute-start | bytes 393224 | tf_op jit(solution)/shard_map/ppermute | solution.py:40
  444.0 11.4 %collective-permute-start.65 = (bf16[1,64,1536]{2,1,0:T(8,128)(2,1)S(1)}, bf16[1,64,1536]{2,1,0:T(8,128)(2,1)S(1)}, u32[]{:S(2)}, u32[]{:S(2)}) collective-permute-start(bf16[1,64,1536]{2,1,0:T(8,128)(2,1)S(1)} %add_convert_fusion.14), channel_id=1, source_target_pairs={{0,4},{1,5},{2,6},{3,7},{4,0},{5,1},{6,2},{7,3},{8,12},{9,13},{10,... | collective-permute-start | bytes 589832 | tf_op jit(solution)/shard_map/ppermute | solution.py:64
  446.3 10.9 %collective-permute-start.64 = (f32[32,1536]{1,0:T(8,128)S(1)}, f32[32,1536]{1,0:T(8,128)S(1)}, u32[]{:S(2)}, u32[]{:S(2)}) collective-permute-start(f32[32,1536]{1,0:T(8,128)S(1)} %get-tuple-element.873), channel_id=1, source_target_pairs={{0,1},{1,0},{2,3},{3,2},{4,5},{5,4},{6,7},{7,6},{8,9},{9,8},{10,11... | collective-permute-start | bytes 589832 | tf_op jit(solution)/shard_map/ppermute | solution.py:40
  (132 other events, 1433.9 us)

commit v7 on v6

--- a/solution.py
+++ b/solution.py
@@ -505,7 +505,7 @@
 def project_kernel(
     info, rates, normed, cosine, sine, tall_count, wide_count,
     q_own, k_own, v_own, q_oth, k_oth, v_oth,
-    q_out, k_out, v_out, mix_out, inner_out, sum_own, sum_oth, pre,
+    q_out, k_out, v_out, mix_out, sum_own, sum_oth, pre,
 ):
     h = pl.program_id(0)
 
@@ -536,7 +536,6 @@
         v_out[0, at] = value
         mixing = (nt(query, key) * mask_of(rate, count, wide_count[row])).astype(BF16)
         mix_out[0, at] = mixing
-        inner_out[0, at] = mm(mixing, value)
         weighted = (key.astype(F32) * leave_of(rate, count)).astype(BF16)
         summary = tn(weighted, value)
 
@@ -562,7 +561,7 @@
 
 
 def mix_kernel(
-    info, rates, x, gain, second_gain, second_bias, tall_count, query, inner, gate,
+    info, rates, x, gain, second_gain, second_bias, tall_count, query, value, mixing, gate,
     state_own, state_oth, wo_own, wo_oth,
     retained, mixed_t, hidden, normed, normed_t,
 ):
@@ -578,13 +577,15 @@
         at = slice(row * length, (row + 1) * length)
         entered = (query[0, at].astype(F32) * enter_of(rate, tall_count[row])).astype(BF16)
 
+        inner = mm(mixing[0, at], value[0, at])
+
         @pl.when(h < 2)
         def _():
-            retained[0, at] = inner[0, at] + mm(entered, state_own[row, 0])
+            retained[0, at] = inner + mm(entered, state_own[row, 0])
 
         @pl.when(h >= 2)
         def _():
-            retained[0, at] = inner[0, at] + mm(entered, state_oth[row, 0])
+            retained[0, at] = inner + mm(entered, state_oth[row, 0])
 
     normal, _ = norm_parts(retained[0], 1.0)
     pre = gate[0]
@@ -989,7 +990,7 @@
     go_got = step(go_part, last - 2, EDGE)
     ff_part = join(ff_part, ff_got)
     ff_got = step(ff_part, last - 1, EDGE)
-    (query, key, value, mixing, inner, sum_own, sum_oth) = call(
+    (query, key, value, mixing, sum_own, sum_oth) = call(
         project_kernel,
         H,
         info,
@@ -1004,7 +1005,6 @@
         [
             head_out(per_head + (QK,), BF16), head_out(per_head + (QK,), BF16),
             head_out(per_head + (VH,), BF16), head_out(per_head + (length,), BF16),
-            head_out(per_head + (VH,), F32),
             own_out(state_shape, F32), other_out(state_shape, F32),
         ],
         [pltpu.VMEM((tokens, 1024), F32)],
@@ -1083,7 +1083,8 @@
         info,
         [
             rates_in, whole(x), real_in(group_gain), whole(second_gain), whole(second_bias),
-            whole(tall_count), head_in(query), head_in(inner), head_in(gate),
+            whole(tall_count), head_in(query), head_in(value),
+            head_in(mixing), head_in(gate),
             own_in(state_own), other_in(state_oth), tall(go_own), tall(go_oth),
         ],
         [

time: 469 us -> 475 us (1.013)
  local copies, waits for them, and re-layouts: 32.9 us -> 40.1 us
    unnamed x223 -> x233, local copies, waits for them, and re-layouts: 28.7 us -> 34.3 us
  transfers between devices with their start and end apart: 70 -> 70, of which waited for: 32 -> 32; matrix products, arithmetic and copies ran while one was open for 10% -> 11% of each run, Pallas kernels for 21% -> 20%
where the time goes in v7:
time: 475 us; the launch traced here: 466 us
  waiting for transfers between devices  160 us (34%)
  Pallas kernels  128 us (27%)
  starting transfers between devices  79.1 us (17%)
  other arithmetic  57 us (12%)
  local copies, waits for them, and re-layouts  40.1 us (8%)
    pallas_call x10, Pallas kernels, call(): pl.pallas_call(body, grid_spec=pltpu.PrefetchScalarGridSpec(num_scalar_pr...  117 us
    ppermute x30, waiting for transfers between devices, step(): return lax.ppermute(values, AXES, pairs)  70.6 us
    ppermute x32, waiting for transfers between devices, swap(): return lax.ppermute(values, AXES, [(i, i ^ bit) for i in range(devices())])  46.2 us
    ppermute x8, waiting for transfers between devices, hop(): return lax.ppermute(message.astype(BF16), 'seq', pairs)  42.8 us
    ppermute x32, starting transfers between devices, swap(): return lax.ppermute(values, AXES, [(i, i ^ bit) for i in range(devices())])  40.7 us
    unnamed x233, local copies, waits for them, and re-layouts  34.3 us
    convert_element_type x14, other arithmetic, upper_part(): return Piece(summed(pieces, start, stop).astype(BF16), start - shift)  28.1 us
    ppermute x30, starting transfers between devices, step(): return lax.ppermute(values, AXES, pairs)  22.6 us
  transfers between devices with their start and end apart: 70, of which 32 were waited for; matrix products, arithmetic and copies ran while one was open for 11% of the time, Pallas kernels for 20%

profile of v7, /device:TPU:1, one launch (start us, length us, event | category | flops | bytes accessed | tf_op | source)
XLA Modules:
  0.0 466.4 jit_solution(5382531470347965434)
XLA Ops:
  8.0 3.5 collective-permute-start.3
  12.7 12.7 %collective-permute-done.1.got_ref = bf16[1,64,2048]{2,1,0:T(8,128)(2,1)S(1)} collective-permute-done((bf16[1,64,2048]{2,1,0:T(8,128)(2,1)S(1)}, bf16[1,64,2048]{2,1,0:T(8,128)(2,1)S(1)}, u32[]{:S(2)}, u32[]{:S(2)}) %collective-permute-start.1) | collective-permute-done | bytes 262176 | tf_op jit(solution)/shard_map/ppermute | solution.py:64
  27.6 7.0 %collective-permute-done.5 = bf16[2,2,16,256]{3,2,1,0:T(8,128)(2,1)S(1)} collective-permute-done((bf16[2,2,16,256]{3,2,1,0:T(8,128)(2,1)S(1)}, bf16[2,2,16,256]{3,2,1,0:T(8,128)(2,1)S(1)}, u32[]{:S(2)}, u32[]{:S(2)}) %collective-permute-start.5) | collective-permute-done | bytes 32800 | tf_op jit(solution)/shard_map/ppermute | solution.py:40
  43.5 12.2 %collective-permute-done.10 = bf16[2,2,2,2,16,256]{5,4,3,1,2,0:T(8,128)(2,1)S(1)} collective-permute-done((bf16[2,2,2,2,16,256]{5,4,3,1,2,0:T(8,128)(2,1)S(1)}, bf16[2,2,2,2,16,256]{5,4,3,1,2,0:T(8,128)(2,1)S(1)}, u32[]{:S(2)}, u32[]{:S(2)}) %collective-permute-start.10) | collective-permute-done | bytes 131104 | tf_op jit(solution)/shard_map/ppermute | solution.py:40
  62.0 2.4 collective-permute-start.14
  64.4 2.6 norm.1
  71.5 10.2 %collective-permute-done.13.got_ref = bf16[1,64,2048]{2,1,0:T(8,128)(2,1)S(1)} collective-permute-done((bf16[1,64,2048]{2,1,0:T(8,128)(2,1)}, bf16[1,64,2048]{2,1,0:T(8,128)(2,1)S(1)}, u32[]{:S(2)}, u32[]{:S(2)}) %collective-permute-start.13) | collective-permute-done | bytes 262176 | tf_op jit(solution)/shard_map/ppermute | solution.py:64
  81.7 5.6 %collective-permute-done.14.got_ref = bf16[1,64,2048]{2,1,0:T(8,128)(2,1)S(1)} collective-permute-done((bf16[1,64,2048]{2,1,0:T(8,128)(2,1)S(1)}, bf16[1,64,2048]{2,1,0:T(8,128)(2,1)S(1)}, u32[]{:S(2)}, u32[]{:S(2)}) %collective-permute-start.14) | collective-permute-done | bytes 262176 | tf_op jit(solution)/shard_map/ppermute | solution.py:64
  91.9 13.5 %collective-permute-done.17.got_ref = bf16[2,64,2048]{2,1,0:T(8,128)(2,1)S(1)} collective-permute-done((bf16[2,64,2048]{2,1,0:T(8,128)(2,1)S(1)}, bf16[2,64,2048]{2,1,0:T(8,128)(2,1)S(1)}, u32[]{:S(2)}, u32[]{:S(2)}) %collective-permute-start.17) | collective-permute-done | bytes 524320 | tf_op jit(solution)/shard_map/ppermute | solution.py:64
  108.6 14.2 %project.1 = (bf16[4,512,256]{2,1,0:T(8,128)(2,1)}, bf16[4,512,256]{2,1,0:T(8,128)(2,1)}, bf16[4,512,512]{2,1,0:T(8,128)(2,1)}, bf16[4,512,256]{2,1,0:T(8,128)(2...) custom-call(s32[66]{0:T(128)} %copy-done.58, f32[4]{0:T(128)} %copy-done.65, bf16[512,1024]{1,0:T(8,128)(2,1)} %copy-done.29, ...), custom_call_target="tpu_custom_call" | custom-call | flops 1 | bytes 1 | tf_op jit(solution)/shard_map/project/pallas_call | solution.py:330
  123.8 3.9 collective-permute-done.20
  128.3 3.4 collective-permute-start.21
  131.7 9.5 %collective-permute-done.21 = bf16[2,256,512]{2,1,0:T(8,128)(2,1)S(1)} collective-permute-done((bf16[2,256,512]{2,1,0:T(8,128)(2,1)S(1)}, bf16[2,256,512]{2,1,0:T(8,128)(2,1)S(1)}, u32[]{:S(2)}, u32[]{:S(2)}) %collective-permute-start.21) | collective-permute-done | bytes 524320 | tf_op jit(solution)/shard_map/ppermute | solution.py:294
  144.7 4.9 %collective-permute-start.23 = (bf16[2,256,512]{2,1,0:T(8,128)(2,1)}, bf16[2,256,512]{2,1,0:T(8,128)(2,1)}, u32[]{:S(2)}, u32[]{:S(2)}) collective-permute-start(bf16[2,256,512]{2,1,0:T(8,128)(2,1)} %fusion.27), channel_id=1, source_target_pairs={{0,2},{1,3},{2,4},{3,5},{8,10},{9,11},{10,12},{11,13},{16,18},{17,... | collective-permute-start | bytes 1572872 | tf_op jit(solution)/shard_map/ppermute | solution.py:294
  149.8 8.8 %collective-permute-done.23 = bf16[2,256,512]{2,1,0:T(8,128)(2,1)} collective-permute-done((bf16[2,256,512]{2,1,0:T(8,128)(2,1)}, bf16[2,256,512]{2,1,0:T(8,128)(2,1)}, u32[]{:S(2)}, u32[]{:S(2)}) %collective-permute-start.23) | collective-permute-done | bytes 524320 | tf_op jit(solution)/shard_map/ppermute | solution.py:294
  160.5 2.7 collective-permute-start.26
  167.7 10.0 %collective-permute-done.27.refs_1_ = bf16[4,64,2048]{2,1,0:T(8,128)(2,1)S(1)} collective-permute-done((bf16[4,64,2048]{2,1,0:T(8,128)(2,1)S(1)}, bf16[4,64,2048]{2,1,0:T(8,128)(2,1)S(1)}, u32[]{:S(2)}, u32[]{:S(2)}) %collective-permute-start.27) | collective-permute-done | bytes 1048608 | tf_op jit(solution)/shard_map/ppermute | solution.py:64
  179.7 2.8 collective-permute-start.30
  185.3 2.2 copy-done.2
  187.5 2.2 copy-done.4
  189.7 3.8 gate.1
  197.7 2.3 collective-permute-done.32.state_oth
  200.0 2.4 collective-permute-start.34
  202.5 12.4 %mix.1 = (f32[4,512,512]{2,1,0:T(8,128)S(1)}, bf16[4,512,512]{2,1,0:T(8,128)(2,1)S(1)}, f32[512,1024]{1,0:T(8,128)S(1)}, bf16[512,1024]{1,0:T(8,128)(2,1)S(1)}, bf16[1024,512]{1,0:T(8,128)(2,1)S(1)}) custom-call(s32[66]{0:T(128)S(1)} %copy-done.59, f32[4]{0:T(128)S(1)} %copy-done.66, bf16[512,1024]{1,0:T(8,128)(2,1)S(1)} %bitcast.251, ...), custom_call_target="tpu_custom_call" | custom-call | flops 1 | bytes 1 | tf_op jit(solution)/shard_map/mix/pallas_call | solution.py:330
  230.7 27.4 %feed.1 = (bf16[512,1024]{1,0:T(8,128)(2,1)}, f32[512,1024]{1,0:T(8,128)}, bf16[512,1024]{1,0:T(8,128)(2,1)S(1)}, f32[1,1024]{1,0:T(1,128)S(1)}, f32[1,1024]{1,0...) custom-call(s32[66]{0:T(128)S(1)} %concatenate.46.info_ref.info, f32[512,1024]{1,0:T(8,128)} %copy-done.43, ...), custom_call_target="tpu_custom_call" | custom-call | flops 1 | bytes 1 | tf_op jit(solution)/shard_map/feed/pallas_call | solution.py:330
  259.0 2.2 copy-done.26
  261.2 11.0 %unmix.1 = (bf16[4,512,512]{2,1,0:T(8,128)(2,1)S(1)}, bf16[4,512,512]{2,1,0:T(8,128)(2,1)S(1)}, f32[4,1,512]{2,1,0:T(1,128)S(1)}, f32[2,2,256,512]{3,2,1,0:T(8,128)S(1)}, f32[2,2,256,512]{3,2,1,0:T(8,128)S(1)}) custom-call(s32[66]{0:T(128)S(1)} %copy-done.59, f32[4]{0:T(128)S(1)} %copy-done.66, bf16[512,1024]{1,0:T(8,128)(2,1)S(1)} %get-tuple-element.606.grad_low, ...), custom_call_target="tpu_custom_call" | custom-call | flops 1 | bytes 1 | tf_op jit(solution)/shard_map/unmix/pallas_call | solution.py:330
  279.5 7.7 %inside.1 = (bf16[4,512,256]{2,1,0:T(8,128)(2,1)S(1)}, f32[4,512,256]{2,1,0:T(8,128)S(1)}, f32[4,512,512]{2,1,0:T(8,128)S(1)}) custom-call(s32[66]{0:T(128)S(1)} %copy-done.59, f32[4]{0:T(128)S(1)} %copy-done.66, bf16[4,512,512]{2,1,0:T(8,128)(2,1)S(1)} %get-tuple-element.623.grad_ret, bf16[4,512,256]{2,1,0:T(8,128)(2,1)S(1)} %copy-done.11, ...), custom_call_target="tpu_custom_call" | custom-call | flops 1 | bytes 1 | tf_op jit(solution)/shard_map/inside/pallas_call | solution.py:330
  289.0 3.3 collective-permute-done.39
  294.3 11.3 %outer.1 = (bf16[16,64,2560]{2,1,0:T(8,128)(2,1)}, bf16[16,64,2560]{2,1,0:T(8,128)(2,1)}) custom-call(s32[66]{0:T(128)S(1)} %copy-done.59, bf16[512,1024]{1,0:T(8,128)(2,1)S(1)} %get-tuple-element.606.grad_low, bf16[1024,512]{1,0:T(8,128)(2,1)S(1)} %copy-done.33, bf16[4,512,512]{2,1,0:T(8,128)(2,1)S(1)} %copy-done.42, ...), custom_call_target="tpu_custom_call" | custom-call | flops 1 | bytes 1 | tf_op jit(solution)/shard_map/outer/pallas_call | solution.py:330
  305.6 2.8 add_convert_fusion.3
  312.3 2.2 fusion.13
  316.0 3.2 collective-permute-done.43
  321.2 14.9 %collective-permute-done.42 = bf16[2,256,512]{2,1,0:T(8,128)(2,1)S(1)} collective-permute-done((bf16[2,256,512]{2,1,0:T(8,128)(2,1)S(1)}, bf16[2,256,512]{2,1,0:T(8,128)(2,1)S(1)}, u32[]{:S(2)}, u32[]{:S(2)}) %collective-permute-start.42) | collective-permute-done | bytes 524320 | tf_op jit(solution)/shard_map/ppermute | solution.py:294
  342.8 9.5 %collective-permute-done.45 = bf16[2,256,512]{2,1,0:T(8,128)(2,1)S(1)} collective-permute-done((bf16[2,256,512]{2,1,0:T(8,128)(2,1)S(1)}, bf16[2,256,512]{2,1,0:T(8,128)(2,1)S(1)}, u32[]{:S(2)}, u32[]{:S(2)}) %collective-permute-start.45) | collective-permute-done | bytes 524320 | tf_op jit(solution)/shard_map/ppermute | solution.py:294
  356.2 2.3 collective-permute-done.47.state_oth
  361.3 9.5 %last.1 = (bf16[4,512,256]{2,1,0:T(8,128)(2,1)S(1)}, bf16[4,512,512]{2,1,0:T(8,128)(2,1)S(1)}, bf16[16,64,1536]{2,1,0:T(8,128)(2,1)S(1)}, bf16[16,64,1536]{2,1,0:T(8,128)(2,1)S(1)}) custom-call(s32[66]{0:T(128)S(1)} %copy-done.59, f32[4]{0:T(128)S(1)} %copy-done.66, bf16[1024,512]{1,0:T(8,128)(2,1)S(1)} %copy-done.33, bf16[4,512,256]{2,1,0:T(8,128)(2,1)S(1)} %copy-done.28, ...), custom_call_target="tpu_custom_call" | custom-call | flops 1 | bytes 1 | tf_op jit(solution)/shard_map/last/pallas_call | solution.py:330
  371.8 5.2 %add_convert_fusion = bf16[4,64,2560]{2,1,0:T(8,128)(2,1)} fusion(bf16[4,64,2560]{2,1,0:T(8,128)(2,1)S(1)} %collective-permute-done.46, bf16[16,64,2560]{2,1,0:T(8,128)(2,1)} %collective-permute-done.43, bf16[16,64,2560]{2,1,0:T(8,128)(2,1)} %get-tuple-element.791), kind=kLoop, calls=%fused_computation.4 | loop fusion | flops 3932160 | bytes 5242880 | tf_op jit(solution)/shard_map/convert_element_type | solution.py:209
  380.7 2.6 collective-permute-done.50
  386.8 17.5 %input.1 = (f32[512,1024]{1,0:T(8,128)}, f32[1,1024]{1,0:T(1,128)}, f32[1,1024]{1,0:T(1,128)}) custom-call(s32[66]{0:T(128)} %copy-done.58, bf16[512,1024]{1,0:T(8,128)(2,1)} %bitcast.249, bf16[1,1024]{1,0:T(2,128)(2,1)} %copy-done.64, f32[512,1024]{1,0:T(8,128)} %get-tuple-element.759.grad_hidden, bf16[4,512,256]{2,1,0:T(8,128)(2,1)} %copy-done.31, ...), custom_call_target="tpu_custom_call" | custom-call | flops 1 | bytes 1 | tf_op jit(solution)/shard_map/input/pallas_call | solution.py:330
  404.8 2.3 add_convert_fusion.6
  408.6 2.7 add_convert_fusion.9
  414.5 5.3 %collective-permute-done.57 = f32[8,1024]{1,0:T(8,128)S(1)} collective-permute-done((f32[8,1024]{1,0:T(8,128)S(1)}, f32[8,1024]{1,0:T(8,128)S(1)}, u32[]{:S(2)}, u32[]{:S(2)}) %collective-permute-start.57) | collective-permute-done | bytes 32800 | tf_op jit(solution)/shard_map/ppermute | solution.py:40
  419.8 3.4 collective-permute-done.56
  423.2 3.6 collective-permute-start.59
  431.0 9.0 %collective-permute-done.63 = bf16[1,64,2560]{2,1,0:T(8,128)(2,1)S(1)} collective-permute-done((bf16[1,64,2560]{2,1,0:T(8,128)(2,1)S(1)}, bf16[1,64,2560]{2,1,0:T(8,128)(2,1)S(1)}, u32[]{:S(2)}, u32[]{:S(2)}) %collective-permute-start.63) | collective-permute-done | bytes 327712 | tf_op jit(solution)/shard_map/ppermute | solution.py:64
  441.6 6.5 %collective-permute-start.67 = (f32[64,512]{1,0:T(8,128)S(1)}, f32[64,512]{1,0:T(8,128)S(1)}, u32[]{:S(2)}, u32[]{:S(2)}) collective-permute-start(f32[64,512]{1,0:T(8,128)S(1)} %slice_select_fusion.1), channel_id=1, source_target_pairs={{0,1},{1,0},{2,3},{3,2},{4,5},{5,4},{6,7},{7,6},{8,9},{9,8},{10,11... | collective-permute-start | bytes 393224 | tf_op jit(solution)/shard_map/ppermute | solution.py:40
  454.2 2.4 collective-permute-start.62
  (471 shorter events, 140.5 us)
Async XLA Ops:
  11.6 13.8 %collective-permute-start.1 = (bf16[1,64,2048]{2,1,0:T(8,128)(2,1)S(1)}, bf16[1,64,2048]{2,1,0:T(8,128)(2,1)S(1)}, u32[]{:S(2)}, u32[]{:S(2)}) collective-permute-start(bf16[1,64,2048]{2,1,0:T(8,128)(2,1)S(1)} %bitcast.252), channel_id=1, source_target_pairs={{0,4},{1,5},{2,6},{3,7},{4,0},{5,1},{6,2},{7,3},{8,12},{9,13},{10,... | collective-permute-start | bytes 786440 | tf_op jit(solution)/shard_map/ppermute | solution.py:64
  39.1 17.3 %collective-permute-start.6 = (bf16[4,64,2048]{2,1,0:T(8,128)(2,1)S(1)}, bf16[4,64,2048]{2,1,0:T(8,128)(2,1)S(1)}, u32[]{:S(2)}, u32[]{:S(2)}) collective-permute-start(bf16[4,64,2048]{2,1,0:T(8,128)(2,1)S(1)} %join.7.refs_0_), channel_id=1, source_target_pairs={{0,2},{1,9},{2,0},{3,11},{4,6},{5,13},{6,4},{7,15},{8,10},{9,1},{1... | collective-permute-start | bytes 3145736 | tf_op jit(solution)/shard_map/ppermute | solution.py:64
  41.7 14.0 %collective-permute-start.10 = (bf16[2,2,2,2,16,256]{5,4,3,1,2,0:T(8,128)(2,1)S(1)}, bf16[2,2,2,2,16,256]{5,4,3,1,2,0:T(8,128)(2,1)S(1)}, u32[]{:S(2)}, u32[]{:S(2)}) collective-permute-start(bf16[2,2,2,2,16,256]{5,4,3,1,2,0:T(8,128)(2,1)S(1)} %pad_maximum_fusion.9), channel_id=1, source_target_pairs={{0,8},{1,9},{2,10},{3,11},{4,12},{5,13},{6,14},{7,15},{8,0},{9,1},... | collective-permute-start | bytes 393224 | tf_op jit(solution)/shard_map/ppermute | solution.py:40
  60.3 27.0 %collective-permute-start.11 = (bf16[4,64,2048]{2,1,0:T(8,128)(2,1)S(1)}, bf16[4,64,2048]{2,1,0:T(8,128)(2,1)}, u32[]{:S(2)}, u32[]{:S(2)}) collective-permute-start(bf16[4,64,2048]{2,1,0:T(8,128)(2,1)S(1)} %join.7.refs_0_), channel_id=1, source_target_pairs={{0,8},{1,17},{2,10},{3,19},{4,12},{5,21},{6,14},{7,23},{8,0},{9,25... | collective-permute-start | bytes 3145736 | tf_op jit(solution)/shard_map/ppermute | solution.py:64
  60.5 26.8 %collective-permute-start.12 = (bf16[4,64,2048]{2,1,0:T(8,128)(2,1)S(1)}, bf16[4,64,2048]{2,1,0:T(8,128)(2,1)}, u32[]{:S(2)}, u32[]{:S(2)}) collective-permute-start(bf16[4,64,2048]{2,1,0:T(8,128)(2,1)S(1)} %collective-permute-done.6.refs_1_), channel_id=1, source_target_pairs={{0,8},{1,17},{2,10},{3,19},{4,12},{5,21},{6,14},{7,23},{8,0},{9,25... | collective-permute-start | bytes 3145736 | tf_op jit(solution)/shard_map/ppermute | solution.py:64
  62.0 19.7 %collective-permute-start.13 = (bf16[1,64,2048]{2,1,0:T(8,128)(2,1)}, bf16[1,64,2048]{2,1,0:T(8,128)(2,1)S(1)}, u32[]{:S(2)}, u32[]{:S(2)}) collective-permute-start(bf16[1,64,2048]{2,1,0:T(8,128)(2,1)} %maximum_bitcast_fusion.part_ref), channel_id=1, source_target_pairs={{0,4},{1,5},{2,6},{3,7},{4,0},{5,1},{6,2},{7,3},{8,12},{9,13},{10,... | collective-permute-start | bytes 786440 | tf_op jit(solution)/shard_map/ppermute | solution.py:64
  62.0 25.3 %collective-permute-start.14 = (bf16[1,64,2048]{2,1,0:T(8,128)(2,1)S(1)}, bf16[1,64,2048]{2,1,0:T(8,128)(2,1)S(1)}, u32[]{:S(2)}, u32[]{:S(2)}) collective-permute-start(bf16[1,64,2048]{2,1,0:T(8,128)(2,1)S(1)} %maximum_bitcast_fusion.1.part_ref), channel_id=1, source_target_pairs={{0,4},{1,5},{2,6},{3,7},{4,0},{5,1},{6,2},{7,3},{8,12},{9,13},{10,... | collective-permute-start | bytes 786440 | tf_op jit(solution)/shard_map/ppermute | solution.py:64
  91.3 14.1 %collective-permute-start.16 = (bf16[16,64,2048]{2,1,0:T(8,128)(2,1)S(1)}, bf16[16,64,2048]{2,1,0:T(8,128)(2,1)S(1)}, u32[]{:S(2)}, u32[]{:S(2)}) collective-permute-start(bf16[16,64,2048]{2,1,0:T(8,128)(2,1)S(1)} %settle.4.q_own.k_own.v_own), channel_id=1, source_target_pairs={{0,1},{1,0},{2,3},{3,2},{4,5},{5,4},{6,7},{7,6},{8,9},{9,8},{10,11... | collective-permute-start | bytes 12582920 | tf_op jit(solution)/shard_map/ppermute | solution.py:40
  91.8 13.6 %collective-permute-start.17 = (bf16[2,64,2048]{2,1,0:T(8,128)(2,1)S(1)}, bf16[2,64,2048]{2,1,0:T(8,128)(2,1)S(1)}, u32[]{:S(2)}, u32[]{:S(2)}) collective-permute-start(bf16[2,64,2048]{2,1,0:T(8,128)(2,1)S(1)} %join.8.part_ref), channel_id=1, source_target_pairs={{0,2},{1,3},{2,0},{3,1},{4,6},{5,7},{6,4},{7,5},{8,10},{9,11},{10,... | collective-permute-start | bytes 1572872 | tf_op jit(solution)/shard_map/ppermute | solution.py:64
  105.5 17.3 %collective-permute-start.18 = (bf16[4,64,2048]{2,1,0:T(8,128)(2,1)S(1)}, bf16[4,64,2048]{2,1,0:T(8,128)(2,1)}, u32[]{:S(2)}, u32[]{:S(2)}) collective-permute-start(bf16[4,64,2048]{2,1,0:T(8,128)(2,1)S(1)} %join.9.refs_0_), channel_id=1, source_target_pairs={{0,16},{1,9},{2,18},{3,11},{4,20},{5,13},{6,22},{7,15},{8,24},{9,1... | collective-permute-start | bytes 3145736 | tf_op jit(solution)/shard_map/ppermute | solution.py:64
  107.5 15.3 %collective-permute-start.19 = (bf16[2,64,2048]{2,1,0:T(8,128)(2,1)S(1)}, bf16[2,64,2048]{2,1,0:T(8,128)(2,1)S(1)}, u32[]{:S(2)}, u32[]{:S(2)}) collective-permute-start(bf16[2,64,2048]{2,1,0:T(8,128)(2,1)S(1)} %join.10.part_ref), channel_id=1, source_target_pairs={{0,2},{1,3},{2,0},{3,1},{4,6},{5,7},{6,4},{7,5},{8,10},{9,11},{10,... | collective-permute-start | bytes 1572872 | tf_op jit(solution)/shard_map/ppermute | solution.py:64
  127.7 13.9 %collective-permute-start.22 = (bf16[4,64,2048]{2,1,0:T(8,128)(2,1)S(1)}, bf16[4,64,2048]{2,1,0:T(8,128)(2,1)S(1)}, u32[]{:S(2)}, u32[]{:S(2)}) collective-permute-start(bf16[4,64,2048]{2,1,0:T(8,128)(2,1)S(1)} %join.9.refs_0_), channel_id=1, source_target_pairs={{0,8},{1,17},{2,10},{3,19},{4,12},{5,21},{6,14},{7,23},{8,0},{9,25... | collective-permute-start | bytes 3145736 | tf_op jit(solution)/shard_map/ppermute | solution.py:64
  128.3 12.9 %collective-permute-start.21 = (bf16[2,256,512]{2,1,0:T(8,128)(2,1)S(1)}, bf16[2,256,512]{2,1,0:T(8,128)(2,1)S(1)}, u32[]{:S(2)}, u32[]{:S(2)}) collective-permute-start(bf16[2,256,512]{2,1,0:T(8,128)(2,1)S(1)} %fusion.29), channel_id=1, source_target_pairs={{0,2},{1,3},{8,10},{9,11},{16,18},{17,19},{24,26},{25,27}} | collective-permute-start | bytes 1572872 | tf_op jit(solution)/shard_map/ppermute | solution.py:294
  141.7 16.9 %collective-permute-start.24 = (bf16[4,64,2048]{2,1,0:T(8,128)(2,1)}, bf16[4,64,2048]{2,1,0:T(8,128)(2,1)}, u32[]{:S(2)}, u32[]{:S(2)}) collective-permute-start(bf16[4,64,2048]{2,1,0:T(8,128)(2,1)} %collective-permute-done.18.refs_1_), channel_id=1, source_target_pairs={{0,8},{1,17},{2,10},{3,19},{4,12},{5,21},{6,14},{7,23},{8,0},{9,25... | collective-permute-start | bytes 3145736 | tf_op jit(solution)/shard_map/ppermute | solution.py:64
  144.7 13.9 %collective-permute-start.23 = (bf16[2,256,512]{2,1,0:T(8,128)(2,1)}, bf16[2,256,512]{2,1,0:T(8,128)(2,1)}, u32[]{:S(2)}, u32[]{:S(2)}) collective-permute-start(bf16[2,256,512]{2,1,0:T(8,128)(2,1)} %fusion.27), channel_id=1, source_target_pairs={{0,2},{1,3},{2,4},{3,5},{8,10},{9,11},{10,12},{11,13},{16,18},{17,... | collective-permute-start | bytes 1572872 | tf_op jit(solution)/shard_map/ppermute | solution.py:294
  160.5 17.2 %collective-permute-start.26 = (bf16[16,64,2048]{2,1,0:T(8,128)(2,1)S(1)}, bf16[16,64,2048]{2,1,0:T(8,128)(2,1)S(1)}, u32[]{:S(2)}, u32[]{:S(2)}) collective-permute-start(bf16[16,64,2048]{2,1,0:T(8,128)(2,1)S(1)} %settle.5.own.wo_own.g_own), channel_id=1, source_target_pairs={{0,1},{1,0},{2,3},{3,2},{4,5},{5,4},{6,7},{7,6},{8,9},{9,8},{10,11... | collective-permute-start | bytes 12582920 | tf_op jit(solution)/shard_map/ppermute | solution.py:40
  163.2 14.5 %collective-permute-start.27 = (bf16[4,64,2048]{2,1,0:T(8,128)(2,1)S(1)}, bf16[4,64,2048]{2,1,0:T(8,128)(2,1)S(1)}, u32[]{:S(2)}, u32[]{:S(2)}) collective-permute-start(bf16[4,64,2048]{2,1,0:T(8,128)(2,1)S(1)} %join.11.refs_0_), channel_id=1, source_target_pairs={{0,16},{1,9},{2,18},{3,11},{4,20},{5,13},{6,22},{7,15},{8,24},{9,1... | collective-permute-start | bytes 3145736 | tf_op jit(solution)/shard_map/ppermute | solution.py:64
  179.6 14.0 %collective-permute-start.29 = (bf16[4,64,2048]{2,1,0:T(8,128)(2,1)S(1)}, bf16[4,64,2048]{2,1,0:T(8,128)(2,1)}, u32[]{:S(2)}, u32[]{:S(2)}) collective-permute-start(bf16[4,64,2048]{2,1,0:T(8,128)(2,1)S(1)} %join.11.refs_0_), channel_id=1, source_target_pairs={{0,8},{1,17},{2,10},{3,19},{4,12},{5,21},{6,14},{7,23},{8,0},{9,25... | collective-permute-start | bytes 3145736 | tf_op jit(solution)/shard_map/ppermute | solution.py:64
  179.7 14.0 %collective-permute-start.30 = (bf16[4,64,2048]{2,1,0:T(8,128)(2,1)S(1)}, bf16[4,64,2048]{2,1,0:T(8,128)(2,1)}, u32[]{:S(2)}, u32[]{:S(2)}) collective-permute-start(bf16[4,64,2048]{2,1,0:T(8,128)(2,1)S(1)} %join.11.refs_0_), channel_id=1, source_target_pairs={{0,1},{1,0},{2,3},{3,2},{4,5},{5,4},{6,7},{7,6},{8,9},{9,8},{10,11... | collective-permute-start | bytes 3145736 | tf_op jit(solution)/shard_map/ppermute | solution.py:40
  182.5 11.2 %collective-permute-start.31 = (bf16[4,64,2048]{2,1,0:T(8,128)(2,1)S(1)}, bf16[4,64,2048]{2,1,0:T(8,128)(2,1)}, u32[]{:S(2)}, u32[]{:S(2)}) collective-permute-start(bf16[4,64,2048]{2,1,0:T(8,128)(2,1)S(1)} %collective-permute-done.27.refs_1_), channel_id=1, source_target_pairs={{0,1},{1,0},{2,3},{3,2},{4,5},{5,4},{6,7},{7,6},{8,9},{9,8},{10,11... | collective-permute-start | bytes 3145736 | tf_op jit(solution)/shard_map/ppermute | solution.py:40
  183.7 9.9 %collective-permute-start.28 = (bf16[2,256,512]{2,1,0:T(8,128)(2,1)}, bf16[2,256,512]{2,1,0:T(8,128)(2,1)}, u32[]{:S(2)}, u32[]{:S(2)}) collective-permute-start(bf16[2,256,512]{2,1,0:T(8,128)(2,1)} %fusion.21), channel_id=1, source_target_pairs={{4,6},{5,7},{12,14},{13,15},{20,22},{21,23},{28,30},{29,31}} | collective-permute-start | bytes 1572872 | tf_op jit(solution)/shard_map/ppermute | solution.py:294
  200.0 20.4 %collective-permute-start.33 = (bf16[4,64,2048]{2,1,0:T(8,128)(2,1)S(1)}, bf16[4,64,2048]{2,1,0:T(8,128)(2,1)S(1)}, u32[]{:S(2)}, u32[]{:S(2)}) collective-permute-start(bf16[4,64,2048]{2,1,0:T(8,128)(2,1)S(1)} %copy-done.45), channel_id=1, source_target_pairs={{0,8},{1,17},{2,10},{3,19},{4,12},{5,21},{6,14},{7,23},{8,0},{9,25... | collective-permute-start | bytes 3145736 | tf_op jit(solution)/shard_map/ppermute | solution.py:64
  200.0 20.4 %collective-permute-start.34 = (bf16[4,64,2048]{2,1,0:T(8,128)(2,1)}, bf16[4,64,2048]{2,1,0:T(8,128)(2,1)S(1)}, u32[]{:S(2)}, u32[]{:S(2)}) collective-permute-start(bf16[4,64,2048]{2,1,0:T(8,128)(2,1)} %collective-permute-done.29.refs_2_), channel_id=1, source_target_pairs={{0,1},{1,0},{2,3},{3,2},{4,5},{5,4},{6,7},{7,6},{8,9},{9,8},{10,11... | collective-permute-start | bytes 3145736 | tf_op jit(solution)/shard_map/ppermute | solution.py:40
  258.7 13.5 %collective-permute-start.36 = (bf16[16,64,2048]{2,1,0:T(8,128)(2,1)}, bf16[16,64,2048]{2,1,0:T(8,128)(2,1)S(1)}, u32[]{:S(2)}, u32[]{:S(2)}) collective-permute-start(bf16[16,64,2048]{2,1,0:T(8,128)(2,1)} %get-tuple-element.605), channel_id=1, source_target_pairs={{0,1},{1,0},{2,3},{3,2},{4,5},{5,4},{6,7},{7,6},{8,9},{9,8},{10,11... | collective-permute-start | bytes 12582920 | tf_op jit(solution)/shard_map/ppermute | solution.py:40
  278.4 13.9 %collective-permute-start.39 = (bf16[4,64,2048]{2,1,0:T(8,128)(2,1)S(1)}, bf16[4,64,2048]{2,1,0:T(8,128)(2,1)S(1)}, u32[]{:S(2)}, u32[]{:S(2)}) collective-permute-start(bf16[4,64,2048]{2,1,0:T(8,128)(2,1)S(1)} %add_convert_fusion.5), channel_id=1, source_target_pairs={{0,8},{1,17},{2,10},{3,19},{4,12},{5,21},{6,14},{7,23},{8,0},{9,25... | collective-permute-start | bytes 3145736 | tf_op jit(solution)/shard_map/ppermute | solution.py:64
  278.8 10.2 %collective-permute-start.38 = (bf16[2,256,512]{2,1,0:T(8,128)(2,1)S(1)}, bf16[2,256,512]{2,1,0:T(8,128)(2,1)S(1)}, u32[]{:S(2)}, u32[]{:S(2)}) collective-permute-start(bf16[2,256,512]{2,1,0:T(8,128)(2,1)S(1)} %fusion.18), channel_id=1, source_target_pairs={{6,4},{7,5},{14,12},{15,13},{22,20},{23,21},{30,28},{31,29}} | collective-permute-start | bytes 1572872 | tf_op jit(solution)/shard_map/ppermute | solution.py:294
  292.3 16.0 %collective-permute-start.41 = (bf16[4,64,2048]{2,1,0:T(8,128)(2,1)S(1)}, bf16[4,64,2048]{2,1,0:T(8,128)(2,1)S(1)}, u32[]{:S(2)}, u32[]{:S(2)}) collective-permute-start(bf16[4,64,2048]{2,1,0:T(8,128)(2,1)S(1)} %add_convert_fusion.4), channel_id=1, source_target_pairs={{0,8},{1,17},{2,10},{3,19},{4,12},{5,21},{6,14},{7,23},{8,0},{9,25... | collective-permute-start | bytes 3145736 | tf_op jit(solution)/shard_map/ppermute | solution.py:64
  292.8 15.6 %collective-permute-start.40 = (bf16[2,256,512]{2,1,0:T(8,128)(2,1)S(1)}, bf16[2,256,512]{2,1,0:T(8,128)(2,1)}, u32[]{:S(2)}, u32[]{:S(2)}) collective-permute-start(bf16[2,256,512]{2,1,0:T(8,128)(2,1)S(1)} %fusion.16), channel_id=1, source_target_pairs={{6,4},{7,5},{4,2},{5,3},{14,12},{15,13},{12,10},{13,11},{22,20},{2... | collective-permute-start | bytes 1572872 | tf_op jit(solution)/shard_map/ppermute | solution.py:294
  309.4 9.8 %collective-permute-start.43 = (bf16[16,64,2560]{2,1,0:T(8,128)(2,1)}, bf16[16,64,2560]{2,1,0:T(8,128)(2,1)}, u32[]{:S(2)}, u32[]{:S(2)}) collective-permute-start(bf16[16,64,2560]{2,1,0:T(8,128)(2,1)} %get-tuple-element.673), channel_id=1, source_target_pairs={{0,1},{1,0},{2,3},{3,2},{4,5},{5,4},{6,7},{7,6},{8,9},{9,8},{10,11... | collective-permute-start | bytes 15728648 | tf_op jit(solution)/shard_map/ppermute | solution.py:40
  310.5 25.5 %collective-permute-start.44 = (bf16[4,64,2048]{2,1,0:T(8,128)(2,1)}, bf16[4,64,2048]{2,1,0:T(8,128)(2,1)}, u32[]{:S(2)}, u32[]{:S(2)}) collective-permute-start(bf16[4,64,2048]{2,1,0:T(8,128)(2,1)} %add_convert_fusion.3), channel_id=1, source_target_pairs={{0,16},{1,9},{2,18},{3,11},{4,20},{5,13},{6,22},{7,15},{8,24},{9,1... | collective-permute-start | bytes 3145736 | tf_op jit(solution)/shard_map/ppermute | solution.py:64
  314.5 21.6 %collective-permute-start.42 = (bf16[2,256,512]{2,1,0:T(8,128)(2,1)S(1)}, bf16[2,256,512]{2,1,0:T(8,128)(2,1)S(1)}, u32[]{:S(2)}, u32[]{:S(2)}) collective-permute-start(bf16[2,256,512]{2,1,0:T(8,128)(2,1)S(1)} %fusion.13), channel_id=1, source_target_pairs={{4,2},{5,3},{2,0},{3,1},{12,10},{13,11},{10,8},{11,9},{20,18},{21,... | collective-permute-start | bytes 1572872 | tf_op jit(solution)/shard_map/ppermute | solution.py:294
  336.1 16.8 %collective-permute-start.46 = (bf16[4,64,2560]{2,1,0:T(8,128)(2,1)S(1)}, bf16[4,64,2560]{2,1,0:T(8,128)(2,1)S(1)}, u32[]{:S(2)}, u32[]{:S(2)}) collective-permute-start(bf16[4,64,2560]{2,1,0:T(8,128)(2,1)S(1)} %add_convert_fusion.2), channel_id=1, source_target_pairs={{0,8},{1,17},{2,10},{3,19},{4,12},{5,21},{6,14},{7,23},{8,0},{9,25... | collective-permute-start | bytes 3932168 | tf_op jit(solution)/shard_map/ppermute | solution.py:64
  337.5 14.8 %collective-permute-start.45 = (bf16[2,256,512]{2,1,0:T(8,128)(2,1)S(1)}, bf16[2,256,512]{2,1,0:T(8,128)(2,1)S(1)}, u32[]{:S(2)}, u32[]{:S(2)}) collective-permute-start(bf16[2,256,512]{2,1,0:T(8,128)(2,1)S(1)} %fusion.10), channel_id=1, source_target_pairs={{2,0},{3,1},{10,8},{11,9},{18,16},{19,17},{26,24},{27,25}} | collective-permute-start | bytes 1572872 | tf_op jit(solution)/shard_map/ppermute | solution.py:294
  358.5 18.5 %collective-permute-start.49 = (bf16[4,64,2560]{2,1,0:T(8,128)(2,1)S(1)}, bf16[4,64,2560]{2,1,0:T(8,128)(2,1)S(1)}, u32[]{:S(2)}, u32[]{:S(2)}) collective-permute-start(bf16[4,64,2560]{2,1,0:T(8,128)(2,1)S(1)} %add_convert_fusion.1), channel_id=1, source_target_pairs={{0,8},{1,17},{2,10},{3,19},{4,12},{5,21},{6,14},{7,23},{8,0},{9,25... | collective-permute-start | bytes 3932168 | tf_op jit(solution)/shard_map/ppermute | solution.py:64
  359.8 17.3 %collective-permute-start.48 = (bf16[2,64,2048]{2,1,0:T(8,128)(2,1)S(1)}, bf16[2,64,2048]{2,1,0:T(8,128)(2,1)S(1)}, u32[]{:S(2)}, u32[]{:S(2)}) collective-permute-start(bf16[2,64,2048]{2,1,0:T(8,128)(2,1)S(1)} %add_convert_fusion.10), channel_id=1, source_target_pairs={{0,2},{1,3},{2,0},{3,1},{4,6},{5,7},{6,4},{7,5},{8,10},{9,11},{10,... | collective-permute-start | bytes 1572872 | tf_op jit(solution)/shard_map/ppermute | solution.py:64
  378.1 26.2 %collective-permute-start.53 = (bf16[4,64,2560]{2,1,0:T(8,128)(2,1)}, bf16[4,64,2560]{2,1,0:T(8,128)(2,1)}, u32[]{:S(2)}, u32[]{:S(2)}) collective-permute-start(bf16[4,64,2560]{2,1,0:T(8,128)(2,1)} %add_convert_fusion), channel_id=1, source_target_pairs={{0,2},{1,9},{2,0},{3,11},{4,6},{5,13},{6,4},{7,15},{8,10},{9,1},{1... | collective-permute-start | bytes 3932168 | tf_op jit(solution)/shard_map/ppermute | solution.py:64
  384.9 19.4 %collective-permute-start.51 = (bf16[4,64,1536]{2,1,0:T(8,128)(2,1)}, bf16[4,64,1536]{2,1,0:T(8,128)(2,1)}, u32[]{:S(2)}, u32[]{:S(2)}) collective-permute-start(bf16[4,64,1536]{2,1,0:T(8,128)(2,1)} %get-tuple-element.845), channel_id=1, source_target_pairs={{0,8},{1,17},{2,10},{3,19},{4,12},{5,21},{6,14},{7,23},{8,0},{9,25... | collective-permute-start | bytes 2359304 | tf_op jit(solution)/shard_map/ppermute | solution.py:64
  386.4 18.4 %collective-permute-start.52 = (bf16[4,64,1536]{2,1,0:T(8,128)(2,1)}, bf16[4,64,1536]{2,1,0:T(8,128)(2,1)}, u32[]{:S(2)}, u32[]{:S(2)}) collective-permute-start(bf16[4,64,1536]{2,1,0:T(8,128)(2,1)} %get-tuple-element.844), channel_id=1, source_target_pairs={{0,8},{1,17},{2,10},{3,19},{4,12},{5,21},{6,14},{7,23},{8,0},{9,25... | collective-permute-start | bytes 2359304 | tf_op jit(solution)/shard_map/ppermute | solution.py:64
  386.5 17.9 %collective-permute-start.54 = (bf16[1,64,2048]{2,1,0:T(8,128)(2,1)S(1)}, bf16[1,64,2048]{2,1,0:T(8,128)(2,1)S(1)}, u32[]{:S(2)}, u32[]{:S(2)}) collective-permute-start(bf16[1,64,2048]{2,1,0:T(8,128)(2,1)S(1)} %add_convert_fusion.13), channel_id=1, source_target_pairs={{0,4},{1,5},{2,6},{3,7},{4,0},{5,1},{6,2},{7,3},{8,12},{9,13},{10,... | collective-permute-start | bytes 786440 | tf_op jit(solution)/shard_map/ppermute | solution.py:64
  407.2 16.1 %collective-permute-start.55 = (bf16[4,64,1536]{2,1,0:T(8,128)(2,1)}, bf16[4,64,1536]{2,1,0:T(8,128)(2,1)}, u32[]{:S(2)}, u32[]{:S(2)}) collective-permute-start(bf16[4,64,1536]{2,1,0:T(8,128)(2,1)} %add_convert_fusion.6), channel_id=1, source_target_pairs={{0,2},{1,9},{2,0},{3,11},{4,6},{5,13},{6,4},{7,15},{8,10},{9,1},{1... | collective-permute-start | bytes 2359304 | tf_op jit(solution)/shard_map/ppermute | solution.py:64
  411.2 12.0 %collective-permute-start.56 = (bf16[2,64,2560]{2,1,0:T(8,128)(2,1)}, bf16[2,64,2560]{2,1,0:T(8,128)(2,1)}, u32[]{:S(2)}, u32[]{:S(2)}) collective-permute-start(bf16[2,64,2560]{2,1,0:T(8,128)(2,1)} %add_convert_fusion.9), channel_id=1, source_target_pairs={{0,16},{1,3},{2,18},{3,1},{4,20},{5,7},{6,22},{7,5},{8,24},{9,11},... | collective-permute-start | bytes 1966088 | tf_op jit(solution)/shard_map/ppermute | solution.py:64
  428.3 11.7 %collective-permute-start.63 = (bf16[1,64,2560]{2,1,0:T(8,128)(2,1)S(1)}, bf16[1,64,2560]{2,1,0:T(8,128)(2,1)S(1)}, u32[]{:S(2)}, u32[]{:S(2)}) collective-permute-start(bf16[1,64,2560]{2,1,0:T(8,128)(2,1)S(1)} %add_convert_fusion.12), channel_id=1, source_target_pairs={{0,4},{1,5},{2,6},{3,7},{4,0},{5,1},{6,2},{7,3},{8,12},{9,13},{10,... | collective-permute-start | bytes 983048 | tf_op jit(solution)/shard_map/ppermute | solution.py:64
  430.8 17.3 %collective-permute-start.58 = (bf16[2,64,1536]{2,1,0:T(8,128)(2,1)S(1)}, bf16[2,64,1536]{2,1,0:T(8,128)(2,1)S(1)}, u32[]{:S(2)}, u32[]{:S(2)}) collective-permute-start(bf16[2,64,1536]{2,1,0:T(8,128)(2,1)S(1)} %add_convert_fusion.11), channel_id=1, source_target_pairs={{0,16},{1,3},{2,18},{3,1},{4,20},{5,7},{6,22},{7,5},{8,24},{9,11},... | collective-permute-start | bytes 1179656 | tf_op jit(solution)/shard_map/ppermute | solution.py:64
  441.6 10.7 %collective-permute-start.67 = (f32[64,512]{1,0:T(8,128)S(1)}, f32[64,512]{1,0:T(8,128)S(1)}, u32[]{:S(2)}, u32[]{:S(2)}) collective-permute-start(f32[64,512]{1,0:T(8,128)S(1)} %slice_select_fusion.1), channel_id=1, source_target_pairs={{0,1},{1,0},{2,3},{3,2},{4,5},{5,4},{6,7},{7,6},{8,9},{9,8},{10,11... | collective-permute-start | bytes 393224 | tf_op jit(solution)/shard_map/ppermute | solution.py:40
  448.1 10.6 %collective-permute-start.69 = (f32[64,512]{1,0:T(8,128)S(1)}, f32[64,512]{1,0:T(8,128)S(1)}, u32[]{:S(2)}, u32[]{:S(2)}) collective-permute-start(f32[64,512]{1,0:T(8,128)S(1)} %slice_select_fusion.7), channel_id=1, source_target_pairs={{0,1},{1,0},{2,3},{3,2},{4,5},{5,4},{6,7},{7,6},{8,9},{9,8},{10,11... | collective-permute-start | bytes 393224 | tf_op jit(solution)/shard_map/ppermute | solution.py:40
  448.2 11.2 %collective-permute-start.68 = (f32[32,1024]{1,0:T(8,128)S(1)}, f32[32,1024]{1,0:T(8,128)S(1)}, u32[]{:S(2)}, u32[]{:S(2)}) collective-permute-start(f32[32,1024]{1,0:T(8,128)S(1)} %slice_select_fusion.9), channel_id=1, source_target_pairs={{0,1},{1,0},{2,3},{3,2},{4,5},{5,4},{6,7},{7,6},{8,9},{9,8},{10,11... | collective-permute-start | bytes 393224 | tf_op jit(solution)/shard_map/ppermute | solution.py:40
  450.2 11.1 %collective-permute-start.65 = (bf16[1,64,1536]{2,1,0:T(8,128)(2,1)S(1)}, bf16[1,64,1536]{2,1,0:T(8,128)(2,1)S(1)}, u32[]{:S(2)}, u32[]{:S(2)}) collective-permute-start(bf16[1,64,1536]{2,1,0:T(8,128)(2,1)S(1)} %add_convert_fusion.14), channel_id=1, source_target_pairs={{0,4},{1,5},{2,6},{3,7},{4,0},{5,1},{6,2},{7,3},{8,12},{9,13},{10,... | collective-permute-start | bytes 589832 | tf_op jit(solution)/shard_map/ppermute | solution.py:64
  452.3 10.8 %collective-permute-start.64 = (f32[32,1536]{1,0:T(8,128)S(1)}, f32[32,1536]{1,0:T(8,128)S(1)}, u32[]{:S(2)}, u32[]{:S(2)}) collective-permute-start(f32[32,1536]{1,0:T(8,128)S(1)} %get-tuple-element.871), channel_id=1, source_target_pairs={{0,1},{1,0},{2,3},{3,2},{4,5},{5,4},{6,7},{7,6},{8,9},{9,8},{10,11... | collective-permute-start | bytes 589832 | tf_op jit(solution)/shard_map/ppermute | solution.py:40
  (137 other events, 1545.4 us)
